TPU v7x, 32 devices: a whole 2x2x4 slice. The times are simulated.
32 devices in a mesh: row: 2 (over x), seq: 16 (over z, y, core).
Axes of the slice: x: 2, y: 2, z: 4, core: 2. Of those that a mesh axis runs over, the one named last changes fastest.
Arguments:
- tokens: bfloat16 [2, 2048, 1600], P('row', 'seq'), may hold values from -6 to 6
- doc_ids: int32 [2, 2048], P('row', 'seq'), may hold values from 0 to 8, as said below
- meta_tokens: bfloat16 [128, 1600], P(('row', 'seq')), may hold values from -6 to 6
- mixer_params: bfloat16 [22246400], P(('row', 'seq'))
- small_params: bfloat16 [81600], P(('row', 'seq'))
- ffn_params: bfloat16 [26419200], P(('row', 'seq'))
- cotangent: bfloat16 [2, 2048, 1600], P('row', 'seq'), may hold values from -6 to 6
Outputs:
- block_out: bfloat16 [2, 2048, 1600], P('row', 'seq')
- grad_tokens: float32 [2, 2048, 1600], P('row', 'seq')
- grad_meta: float32 [128, 1600], P(('row', 'seq'))
- grad_mixer: float32 [22246400], P(('row', 'seq'))
- grad_small: float32 [81600], P(('row', 'seq'))
- grad_ffn: float32 [26419200], P(('row', 'seq'))
Inputs may be any that keep to these rules, and one draw needn't show every extreme that they name: `doc_ids`: ids never fall along a row, rise by one at each document start, start at 0 and end at 8 in every row (each row holds exactly 9 documents); in one row, chosen by the seed, no document starts at positions 128 to 1920.
All inputs are finite; a program needn't handle non-finite values.
Results may differ from a plain program's by a relative error of at most 0.015.
Values may be sent and summed in bfloat16 or wider, within the bound.
A program may use at most 960 MiB of HBM per device.

v0:
```python
from functools import partial
import math

import jax
import jax.numpy as jnp
from jax import lax
from jax.sharding import PartitionSpec as P

D = 1600
HEADS = 25
GROUPS = 5
HEAD = 64
INNER = 3200
STATE = 16
CONV = 4
DT_RANK = 100
FF = 5504
REACH = 8


norm_eps = 1e-05


def entering(part, axis, combine, identity):
    place = lax.axis_index(axis)
    gathered = jax.tree.map(lambda a: lax.all_gather(a, axis), part)
    state = jax.tree.map(lambda a, e: jnp.zeros_like(a) + jnp.asarray(e, a.dtype), part, identity)

    def one(turn, state):
        return combine(
            state, jax.tree.map(lambda a: lax.dynamic_index_in_dim(a, turn, 0, False), gathered)
        )

    return lax.fori_loop(0, place, one, state)


def passed_along(value, axis, steps):
    count = lax.axis_size(axis)
    first, last = (max(0, -steps), min(count, count - steps))
    return lax.ppermute(value, axis, [(source, source + steps) for source in range(first, last)])


def carried_in(array, axis, join, neutral):
    place = lax.axis_index(axis)
    gathered = jax.tree.map(
        lambda a, kind: lax.all_gather(a.astype(kind), axis), array, (jnp.bfloat16, jnp.bfloat16)
    )
    state = jax.tree.map(lambda a, e: jnp.zeros_like(a) + jnp.asarray(e, a.dtype), array, neutral)

    def one(turn, state):
        return join(
            state,
            jax.tree.map(
                lambda a, own: lax.dynamic_index_in_dim(a, turn, 0, False).astype(own.dtype),
                gathered,
                array,
            ),
        )

    return lax.fori_loop(0, place, one, state)


def carried_in_2(array, axis, join, neutral):
    count = lax.axis_size(axis)
    place = lax.axis_index(axis)
    ahead = count - 1 - place
    gathered = jax.tree.map(
        lambda a, kind: lax.all_gather(a.astype(kind), axis),
        array,
        jax.tree.map(lambda a: jnp.bfloat16 if a.dtype == jnp.float32 else a.dtype, array),
    )
    state = jax.tree.map(lambda a, e: jnp.zeros_like(a) + jnp.asarray(e, a.dtype), array, neutral)

    def one(turn, state):
        source = count - 1 - turn
        return join(
            state,
            jax.tree.map(
                lambda a, own: lax.dynamic_index_in_dim(a, source, 0, False).astype(own.dtype),
                gathered,
                array,
            ),
        )

    return lax.fori_loop(0, ahead, one, state)


def split_flat(flat_vec, layout):
    pieces = []
    offset = 0
    for piece_shape in layout:
        piece_len = math.prod(piece_shape)
        pieces.append(flat_vec[offset : offset + piece_len].reshape(piece_shape))
        offset += piece_len
    return pieces


def mixer_layout():
    return [
        (D, HEADS * HEAD),
        (D, 2 * GROUPS * HEAD),
        (D, 2 * INNER),
        (INNER, DT_RANK + 2 * STATE),
        (DT_RANK, INNER),
        (HEADS * HEAD + INNER, D),
    ]


def small_split(flat_vec):
    width = CONV + STATE + 4
    packed_rows = flat_vec[: D * (3 + 2 * width)].reshape(D, 3 + 2 * width)
    channel_part = packed_rows[:, 3:].reshape(INNER, width)
    return (
        packed_rows[:, 0],
        packed_rows[:, 1],
        channel_part[:, 0],
        packed_rows[:, 2],
        channel_part[:, 1 : 1 + CONV].T,
        channel_part[:, 1 + CONV],
        channel_part[:, 2 + CONV],
        channel_part[:, 3 + CONV : 3 + CONV + STATE],
        channel_part[:, 3 + CONV + STATE],
    )


def small_join(grad_parts, total_len):
    g_one, g_attn, g_ssm, g_two, conv_w, conv_b, dt_bias, a_log, d_skip = grad_parts
    channel_part = jnp.concatenate(
        [g_ssm[:, None], conv_w.T, conv_b[:, None], dt_bias[:, None], a_log, d_skip[:, None]],
        axis=1,
    )
    packed_rows = jnp.concatenate(
        [g_one[:, None], g_attn[:, None], g_two[:, None], channel_part.reshape(D, -1)], axis=1
    ).reshape(-1)
    return jnp.concatenate(
        [packed_rows, jnp.zeros((total_len - packed_rows.shape[0],), jnp.float32)]
    )


def ffn_layout():
    return [(D, FF), (D, FF), (FF, D)]


def rms_norm(values, gain_vec):
    return (
        values * lax.rsqrt(jnp.mean(values * values, axis=-1, keepdims=True) + norm_eps) * gain_vec
    )


def silu_fn(values):
    return values / (1.0 + jnp.exp(-values))


def softplus_fn(values):
    return jnp.maximum(values, 0.0) + jnp.log1p(jnp.exp(-jnp.abs(values)))


def glu_piece(gate_pre, up_pre):
    return silu_fn(gate_pre) * up_pre


def dot_last(left, right):
    return jnp.einsum("...k,kn->...n", left, right, preferred_element_type=jnp.float32)


def dot_back(grads, right):
    return jnp.einsum("...n,kn->...k", grads, right, preferred_element_type=jnp.float32)


def dot_weight(left, grads):
    return jnp.einsum("...k,...n->kn", left, grads, preferred_element_type=jnp.float32)


def conv_piece(extended, conv_w, conv_b, lag_masks):
    shard_len = extended.shape[1] - (CONV - 1)
    summed = conv_b
    for j in range(CONV):
        summed = (
            summed + conv_w[j] * extended[:, CONV - 1 - j : CONV - 1 - j + shard_len] * lag_masks[j]
        )
    return silu_fn(summed)


def mix_piece(attn_out, ssm_out, g_attn, g_ssm):
    return 0.5 * jnp.concatenate([rms_norm(attn_out, g_attn), rms_norm(ssm_out, g_ssm)], axis=-1)


def ssm_local(conv_out, pre_dt, b_in, c_read, z_in, dt_bias, a_log, d_skip, keep_mask):
    delta_t = softplus_fn(pre_dt + dt_bias)
    a_mat = -jnp.exp(a_log)

    def token_step(ssm_state, inputs):
        c_t, dt_t, b_t, read_t, keep_t = inputs
        decay_now = jnp.exp(dt_t[..., None] * a_mat) * keep_t[:, None, None]
        ssm_state = decay_now * ssm_state + (dt_t * c_t)[..., None] * b_t[:, None, :]
        return (ssm_state, jnp.sum(ssm_state * read_t[:, None, :], axis=-1))

    time_major = tuple((jnp.moveaxis(v, 1, 0) for v in (conv_out, delta_t, b_in, c_read))) + (
        keep_mask.T,
    )
    start_state = jnp.zeros((conv_out.shape[0], conv_out.shape[2], a_log.shape[1]), jnp.float32)
    end_state, outputs = lax.scan(token_step, start_state, time_major)
    y_ssm = jnp.moveaxis(outputs, 0, 1) + d_skip * conv_out
    return (y_ssm * silu_fn(z_in), end_state)


def decay_from(pre_dt, dt_bias, a_log, keep_mask):
    delta_t = softplus_fn(pre_dt + dt_bias)
    keep_prefix = lax.cummin(keep_mask, axis=1)
    return (
        jnp.exp(jnp.cumsum(delta_t, axis=1)[..., None] * -jnp.exp(a_log))
        * keep_prefix[..., None, None]
    )


def carry_piece(pre_dt, c_read, z_in, carried, dt_bias, a_log, keep_mask):
    decay_table = decay_from(pre_dt, dt_bias, a_log, keep_mask)
    carry_term = jnp.sum(decay_table * carried[:, None] * c_read[:, :, None, :], axis=-1)
    return (carry_term * silu_fn(z_in), decay_table[:, -1] * carried)


def combine_docs(earlier, later):
    e_empty = earlier[3] < 0
    l_empty = later[3] < 0
    joined = jnp.maximum(
        jnp.maximum(earlier[2], later[2]), jnp.where(later[0] != earlier[1], later[3], -1)
    )
    first_id = jnp.where(e_empty, later[0], earlier[0])
    last_id = jnp.where(l_empty, earlier[1], later[1])
    inner_new = jnp.where(e_empty, later[2], jnp.where(l_empty, earlier[2], joined))
    anchor_new = jnp.where(e_empty, later[3], earlier[3])
    return (first_id, last_id, inner_new, anchor_new)


def combine_state(earlier, later):
    return (earlier[0] * later[0], later[0] * earlier[1] + later[1])


def head_views(queries, key_rows):
    key_width = GROUPS * HEAD
    q_five = queries.reshape(queries.shape[0], queries.shape[1], GROUPS, HEADS // GROUPS, HEAD)
    key_four = key_rows[..., :key_width].reshape(key_rows.shape[0], key_rows.shape[1], GROUPS, HEAD)
    val_four = key_rows[..., key_width:].reshape(key_rows.shape[0], key_rows.shape[1], GROUPS, HEAD)
    return (q_five, key_four, val_four)


def masked_scores(q_five, key_four, key_valid):
    raw_dot = jnp.einsum("rsghd,rkgd->rghsk", q_five, key_four, preferred_element_type=jnp.float32)
    return jnp.where(key_valid[:, None, None], raw_dot * HEAD ** (-0.5), -1e30)


def per_device(tokens, doc_ids, meta_tokens, mixer_params, small_params, ffn_params, cotangent):
    row_count, shard_len = doc_ids.shape
    seq_index = lax.axis_index("seq")
    positions = seq_index * shard_len + jnp.arange(shard_len, dtype=jnp.int32)
    within = doc_ids[:, 1:] != doc_ids[:, :-1]
    inner_max = jnp.max(jnp.where(within, positions[None, 1:], -1), axis=1)
    own_part = (
        doc_ids[:, 0],
        doc_ids[:, -1],
        inner_max,
        jnp.broadcast_to(positions[0], (row_count,)),
    )
    blank_ids = jnp.full((row_count,), -1, jnp.int32)
    before = entering(own_part, "seq", combine_docs, (blank_ids, blank_ids, blank_ids, blank_ids))
    prev_last = jnp.where(before[3] < 0, -1, before[1])
    doc_flags = jnp.concatenate([doc_ids[:, :1] != prev_last[:, None], within], axis=1)
    doc_first = jnp.maximum(
        lax.cummax(jnp.where(doc_flags, positions[None, :], -1), axis=1),
        jnp.maximum(before[2], 0)[:, None],
    )
    keep_mask = (positions[None, :] != doc_first).astype(jnp.float32)
    lag_masks = jnp.stack(
        [(positions[None, :] - j >= doc_first).astype(jnp.float32)[..., None] for j in range(CONV)]
    )
    mixer_full, small_full, ffn_full = (
        lax.all_gather(mixer_params, ("row", "seq"), axis=0, tiled=True),
        lax.all_gather(small_params, ("row", "seq"), axis=0, tiled=True),
        lax.all_gather(ffn_params, ("row", "seq"), axis=0, tiled=True),
    )
    w_q, w_kv, w_in, w_x, w_dt, w_out = split_flat(mixer_full, mixer_layout())
    small_list = [v.astype(jnp.float32) for v in small_split(small_full)]
    g_one, g_attn, g_ssm, g_two, conv_w, conv_b, dt_bias, a_log, d_skip = small_list
    w_gate, w_up, w_down = split_flat(ffn_full, ffn_layout())
    tokens_f = tokens.astype(jnp.float32)
    normed_f, norm_pull = jax.vjp(rms_norm, tokens_f, g_one)
    normed = normed_f.astype(jnp.bfloat16)
    queries = dot_last(normed, w_q).astype(jnp.bfloat16)
    kv_own = dot_last(normed, w_kv).astype(jnp.bfloat16)
    xz_half = dot_last(normed, w_in).astype(jnp.bfloat16)
    meta_f, meta_pull = jax.vjp(rms_norm, meta_tokens.astype(jnp.float32), g_one)
    meta_normed = meta_f.astype(jnp.bfloat16)
    meta_kv = lax.all_gather(
        dot_last(meta_normed, w_kv).astype(jnp.bfloat16), ("row", "seq"), axis=0, tiled=True
    )
    meta_count = meta_kv.shape[0]
    halo_list = []
    for k in range(REACH, 0, -1):
        halo_list.append(passed_along(kv_own, "seq", k))
    meta_rows = meta_kv[None]
    key_rows = jnp.concatenate([meta_rows] + halo_list + [kv_own], axis=1)
    key_pos = (seq_index - REACH) * shard_len + jnp.arange((REACH + 1) * shard_len, dtype=jnp.int32)
    window_ok = (
        (key_pos[None, None, :] >= doc_first[:, :, None])
        & (key_pos[None, None, :] <= positions[None, :, None])
        & (key_pos[None, None, :] > positions[None, :, None] - REACH * shard_len)
    )
    key_valid = jnp.concatenate(
        [jnp.ones((row_count, shard_len, meta_count), bool), window_ok], axis=2
    )
    q_five, key_four, val_four = head_views(queries, key_rows)
    scores = masked_scores(q_five, key_four, key_valid)
    top_score = jnp.max(scores, axis=-1, keepdims=True)
    log_total = top_score + jnp.log(jnp.sum(jnp.exp(scores - top_score), axis=-1, keepdims=True))
    prob_half = jnp.exp(scores - log_total).astype(jnp.bfloat16)
    attn_out = jnp.einsum(
        "rghsk,rkgd->rsghd", prob_half, val_four, preferred_element_type=jnp.float32
    ).reshape(row_count, shard_len, HEADS * HEAD)
    edge_prev = passed_along(xz_half[:, shard_len - (CONV - 1) :, :INNER], "seq", 1)
    extended = jnp.concatenate([edge_prev, xz_half[..., :INNER]], axis=1).astype(jnp.float32)
    conv_fn = partial(conv_piece, lag_masks=lag_masks)
    conv_out, conv_pull = jax.vjp(conv_fn, extended, conv_w, conv_b)
    conv_half = conv_out.astype(jnp.bfloat16)
    projected = dot_last(conv_half, w_x)
    rank_half = projected[..., :DT_RANK].astype(jnp.bfloat16)
    pre_dt = dot_last(rank_half, w_dt)
    c_read = projected[..., DT_RANK + STATE :]
    z_in = xz_half[..., INNER:].astype(jnp.float32)
    local_fn = partial(ssm_local, keep_mask=keep_mask)
    (zero_out, local_end), local_pull = jax.vjp(
        local_fn,
        conv_half.astype(jnp.float32),
        pre_dt,
        projected[..., DT_RANK : DT_RANK + STATE],
        c_read,
        z_in,
        dt_bias,
        a_log,
        d_skip,
    )
    decay_table = decay_from(pre_dt, dt_bias, a_log, keep_mask)
    through = decay_table[:, -1]
    identity = (jnp.ones_like(through), jnp.zeros_like(local_end))
    carried = carried_in((through, local_end), "seq", combine_state, identity)[1]
    carry_fn = partial(carry_piece, keep_mask=keep_mask)
    (carry_out, _), carry_pull = jax.vjp(carry_fn, pre_dt, c_read, z_in, carried, dt_bias, a_log)
    gate_z = silu_fn(z_in)
    ssm_out = zero_out + carry_out
    mixed_f, mix_pull = jax.vjp(mix_piece, attn_out, ssm_out, g_attn, g_ssm)
    mixed_half = mixed_f.astype(jnp.bfloat16)
    hidden = tokens_f + dot_last(mixed_half, w_out)
    second_f, second_pull = jax.vjp(rms_norm, hidden, g_two)
    second = second_f.astype(jnp.bfloat16)
    gate_pre = dot_last(second, w_gate)
    up_pre = dot_last(second, w_up)
    act_f, act_pull = jax.vjp(glu_piece, gate_pre, up_pre)
    act_half = act_f.astype(jnp.bfloat16)
    block_out = (hidden + dot_last(act_half, w_down)).astype(jnp.bfloat16)
    ffn_back = lax.all_gather(ffn_params, ("row", "seq"), axis=0, tiled=True)
    w_gate, w_up, w_down = split_flat(ffn_back, ffn_layout())
    d_act = dot_back(cotangent, w_down)
    grad_down = dot_weight(act_half, cotangent)
    d_gate, d_up = act_pull(d_act)
    gate_half = d_gate.astype(jnp.bfloat16)
    up_half = d_up.astype(jnp.bfloat16)
    grad_gate = dot_weight(second, gate_half)
    grad_up = dot_weight(second, up_half)
    d_second = dot_back(gate_half, w_gate) + dot_back(up_half, w_up)
    d_hidden, grad_g_two = second_pull(d_second)
    d_hidden = d_hidden + cotangent.astype(jnp.float32)
    ffn_vec = jnp.concatenate([grad_gate.ravel(), grad_up.ravel(), grad_down.ravel()])
    grad_ffn = lax.psum_scatter(ffn_vec, ("row", "seq"), scatter_dimension=0, tiled=True)
    mixer_back = lax.all_gather(mixer_params, ("row", "seq"), axis=0, tiled=True)
    w_q, w_kv, w_in, w_x, w_dt, w_out = split_flat(mixer_back, mixer_layout())
    branch_half = d_hidden.astype(jnp.bfloat16)
    grad_out_w = dot_weight(mixed_half, branch_half)
    d_attn, d_ssm, grad_g_attn, grad_g_ssm = mix_pull(dot_back(branch_half, w_out))
    do_half = d_attn.astype(jnp.bfloat16).reshape(q_five.shape)
    scores = masked_scores(q_five, key_four, key_valid)
    prob_full = jnp.exp(scores - log_total)
    prob_half = prob_full.astype(jnp.bfloat16)
    d_val = jnp.einsum("rghsk,rsghd->rkgd", prob_half, do_half, preferred_element_type=jnp.float32)
    d_prob = jnp.einsum("rsghd,rkgd->rghsk", do_half, val_four, preferred_element_type=jnp.float32)
    d_score = (
        prob_full * (d_prob - jnp.sum(prob_full * d_prob, axis=-1, keepdims=True)) * HEAD ** (-0.5)
    ).astype(jnp.bfloat16)
    d_query = jnp.einsum(
        "rghsk,rkgd->rsghd", d_score, key_four, preferred_element_type=jnp.float32
    ).reshape(row_count, shard_len, HEADS * HEAD)
    d_key = jnp.einsum("rghsk,rsghd->rkgd", d_score, q_five, preferred_element_type=jnp.float32)
    d_rows = jnp.concatenate(
        [
            d_key.reshape(row_count, d_key.shape[1], GROUPS * HEAD),
            d_val.reshape(row_count, d_val.shape[1], GROUPS * HEAD),
        ],
        axis=-1,
    )
    d_meta_kv = jnp.sum(d_rows[:, :meta_count], axis=0)
    d_kv = d_rows[:, meta_count + REACH * shard_len :]
    for k in range(REACH, 0, -1):
        index_from = meta_count + (REACH - k) * shard_len
        d_kv = d_kv + passed_along(
            d_rows[:, index_from : index_from + shard_len].astype(jnp.bfloat16), "seq", -k
        ).astype(jnp.float32)
    meta_back = lax.psum_scatter(d_meta_kv, ("row", "seq"), scatter_dimension=0, tiled=True).astype(
        jnp.bfloat16
    )
    kv_half = d_kv.astype(jnp.bfloat16)
    query_half = d_query.astype(jnp.bfloat16)
    d_y = d_ssm * gate_z
    d_carried_own = jnp.sum(decay_table * d_y[..., None] * c_read[:, :, None, :], axis=1)
    adjoint = carried_in_2((through, d_carried_own), "seq", combine_state, identity)[1]
    d_conv_out, d_pre_a, d_bin, d_read_a, d_zin_a, grad_bias_a, grad_alog_a, grad_d_skip = (
        local_pull((d_ssm, adjoint))
    )
    d_pre_b, d_read_b, d_zin_b, _, grad_bias_b, grad_alog_b = carry_pull((d_ssm, adjoint))
    d_pre = d_pre_a + d_pre_b
    d_read = d_read_a + d_read_b
    d_zin = d_zin_a + d_zin_b
    grad_dt_bias = grad_bias_a + grad_bias_b
    grad_a_log = grad_alog_a + grad_alog_b
    pre_half = d_pre.astype(jnp.bfloat16)
    grad_dt_w = dot_weight(rank_half, pre_half)
    d_rank = dot_back(pre_half, w_dt)
    proj_half = jnp.concatenate([d_rank, d_bin, d_read], axis=-1).astype(jnp.bfloat16)
    grad_x_w = dot_weight(conv_half, proj_half)
    d_conv_total = d_conv_out + dot_back(proj_half, w_x)
    d_extended, grad_conv_w, grad_conv_b = conv_pull(d_conv_total)
    edge_back = passed_along(d_extended[:, : CONV - 1].astype(jnp.bfloat16), "seq", -1).astype(
        jnp.float32
    )
    d_xm = d_extended[:, CONV - 1 :]
    d_xm = jnp.concatenate(
        [d_xm[:, : shard_len - (CONV - 1)], d_xm[:, shard_len - (CONV - 1) :] + edge_back], axis=1
    )
    xz_back = jnp.concatenate([d_xm, d_zin], axis=-1).astype(jnp.bfloat16)
    grad_in_w = dot_weight(normed, xz_back)
    grad_q_w = dot_weight(normed, query_half)
    grad_kv_w = dot_weight(normed, kv_half) + dot_weight(meta_normed, meta_back)
    d_normed = dot_back(xz_back, w_in) + dot_back(query_half, w_q) + dot_back(kv_half, w_kv)
    grad_from_norm, grad_g_one = norm_pull(d_normed)
    grad_tokens = d_hidden + grad_from_norm
    grad_meta, grad_g_meta = meta_pull(dot_back(meta_back, w_kv))
    mixer_vec = jnp.concatenate(
        [
            grad_q_w.ravel(),
            grad_kv_w.ravel(),
            grad_in_w.ravel(),
            grad_x_w.ravel(),
            grad_dt_w.ravel(),
            grad_out_w.ravel(),
        ]
    )
    small_parts = (
        grad_g_one + grad_g_meta,
        grad_g_attn,
        grad_g_ssm,
        grad_g_two,
        grad_conv_w,
        grad_conv_b,
        grad_dt_bias,
        grad_a_log,
        grad_d_skip,
    )
    small_vec = small_join(small_parts, small_full.shape[0])
    grad_mixer, grad_small = (
        lax.psum_scatter(mixer_vec, ("row", "seq"), scatter_dimension=0, tiled=True),
        lax.psum_scatter(small_vec, ("row", "seq"), scatter_dimension=0, tiled=True),
    )
    return (block_out, grad_tokens, grad_meta, grad_mixer, grad_small, grad_ffn)


def solution(mesh):
    in_specs = (
        P("row", "seq", None),
        P("row", "seq"),
        P(("row", "seq"), None),
        P(("row", "seq")),
        P(("row", "seq")),
        P(("row", "seq")),
        P("row", "seq", None),
    )
    out_specs = (
        P("row", "seq", None),
        P("row", "seq", None),
        P(("row", "seq"), None),
        P(("row", "seq")),
        P(("row", "seq")),
        P(("row", "seq")),
    )
    return jax.shard_map(
        per_device, mesh=mesh, in_specs=in_specs, out_specs=out_specs, check_vma=False
    )
```

profile of v0, /device:TPU:0, one launch (start us, length us, event | category | flops | bytes accessed | tf_op | source)
XLA Modules:
  0.0 7338.8 jit_solution(8425497045041278806)
XLA Ops:
  8.2 14.3 broadcast.907
  22.5 21.9 dynamic-update-slice.1
  51.8 14.4 all-reduce.20
  68.8 634.4 %all-reduce.32.cloned.1.call-done = (bf16[22246400]{0:T(1024)(128)(2,1)}, bf16[81600]{0:T(1024)(128)(2,1)}) async-done(((bf16[22246400]{0:T(1024)(128)(2,1)}, bf16[81600]{0:T(1024)(128)(2,1)}), (bf16[22246400]{0:T(1024)(128)(2,1)}, bf16[81600]{0:T(1024)(128)(2,1)})) %all-reduce.32.cloned.1.call-update) | async-done | bytes 44656016
  714.1 17.0 slice.337
  731.1 35.3 slice.284
  766.5 13.6 fusion.16
  820.0 812.4 %while.101 = (s32[]{:T(128)}, f32[1,3200,16]{1,2,0:T(8,128)S(1)}, f32[128,1,3200]{2,1,0:T(1,128)}, f32[128,1,3200,1]{2,3,1,0:T(1,128)}, f32[128,1,3200,16]{2,3,1...) while((s32[]{:T(128)}, f32[1,3200,16]{1,2,0:T(8,128)S(1)}, ...), condition=%wide.region_11.12_spmd.clone, body=%wide.region_9.11_spmd.clone.sunk | while | flops 515203 | bytes 1870007 | solution.py:202
  1644.1 19.8 reshape.1836
  1709.6 37.1 all-gather.3
  1747.5 11.2 slice.358
  1758.7 25.7 reshape.1783
  1855.1 17.9 multiply_reduce_fusion.8
  1890.3 388.7 %all-gather.16.cloned.1.call-done = bf16[32,1,825600]{2,1,0:T(2,128)(2,1)} async-done(((bf16[1,1,825600]{2,1,0:T(2,128)(2,1)}), bf16[32,1,825600]{2,1,0:T(2,128)(2,1)}) %all-gather.16.cloned.1.call-update) | async-done | bytes 52838416 | tf_op jit(solution)/shard_map/all_gather | solution.py:279
  2279.0 304.7 %reduce.78 = bf16[32,825600]{1,0:T(8,128)(2,1)} reduce(bf16[32,1,825600]{2,1,0:T(2,128)(2,1)} %all-gather.16.cloned.1.call-done, bf16[]{:T(256)} %constant.339), dimensions={1}, to_apply=%all-gather.4.reduce_sub_computation | reduce | bytes 105676800 | tf_op jit(solution)/shard_map/all_gather | solution.py:279
  2583.8 116.8 %reshape.1837 = bf16[26419200]{0:T(1024)(128)(2,1)} reshape(bf16[32,825600]{1,0:T(8,128)(2,1)} %reduce.78) | data formatting | bytes 105676800
  2700.5 35.5 fusion.151
  2736.0 29.2 slice.313
  2765.2 32.5 slice.311
  2797.8 32.5 slice.309
  2845.8 10.7 multiply_convert_fusion
  2866.2 10.2 fusion.68
  2893.9 10.3 fusion.11
  2918.4 12.7 fusion.78
  2931.1 13.7 fusion.161
  2944.9 13.8 fusion.160
  2968.1 10.7 multiply_reduce_fusion.7
  2988.1 14.4 fusion.81
  3008.1 13.3 reshape.1793
  3037.8 36.3 reshape.1798
  3074.1 36.6 reshape.1802
  3110.7 36.6 reshape.1801
  3147.3 41.5 reshape.1803
  3190.4 52.7 all-reduce.33
  3261.6 15.7 while.100
  3277.3 25.1 multiply_reduce_fusion.4
  3306.0 1032.5 %while.102 = (s32[]{:T(128)}, f32[3200,16]{0,1:T(8,128)S(1)}, f32[1,3200,16]{1,2,0:T(8,128)S(1)}, f32[128,1,3200]{2,1,0:T(1,128)}, f32[128,1,3200]{2,0,1:T(8,128...) while((s32[]{:T(128)}, f32[3200,16]{0,1:T(8,128)S(1)}, ...), condition=%wide.region_29.30_spmd.clone, body=%wide.region_24.29_spmd.clone.sunk | while | flops 873572 | bytes 2498811 | solution.py:202
  4339.8 30.8 reduce_window_sum.25
  4447.2 16.0 fusion.56
  4472.0 39.9 reshape.1795
  4511.8 27.9 constant_dynamic-update-slice_fusion.16
  4539.7 14.8 dynamic-update-slice.9
  4554.4 11.4 dynamic-update-slice.10
  4565.8 22.3 constant_dynamic-update-slice_fusion.15
  4588.2 95.4 %pad_maximum_fusion = f32[26419200]{0:T(1024)} fusion(f32[8806400]{0:T(1024)} %reshape.1803, f32[8806400]{0:T(1024)} %reshape.1802, f32[8806400]{0:T(1024)} %reshape.1801), kind=kLoop, calls=%fused_computation.53 | loop fusion | flops 52838400 | bytes 211353600 | tf_op jit(solution)/shard_map/concatenate | solution.py:371
  4685.3 12.9 fusion.25
  4701.3 1133.4 %all-reduce.30.cloned.1.call-done = (f32[22246400]{0:T(1024)}, f32[81600]{0:T(1024)}) async-done(((f32[22246400]{0:T(1024)}, f32[81600]{0:T(1024)}), (f32[22246400]{0:T(1024)}, f32[81600]{0:T(1024)})) %all-reduce.30.cloned.1.call-update) | async-done | bytes 89312016
  5840.2 1486.7 %all-reduce.28.cloned.1.call-done = f32[26419200]{0:T(1024)} async-done(((f32[26419200]{0:T(1024)}), f32[26419200]{0:T(1024)}) %all-reduce.28.cloned.1.call-update) | async-done | bytes 105676816
  (3153 shorter events, 2284.4 us)
Async XLA Ops:
  7.2 696.0 %all-reduce.32.cloned.1.call-start = ((), (), s32[]{:S(2)}) async-start(), calls=%async_computation.6 | async-start | bytes 89313280
  44.5 1809.6 %all-gather.12.cloned.1.call-start = ((), (), s32[]{:S(2)}) async-start(), calls=%async_computation.1 | async-start | bytes 1740800 | tf_op jit(solution)/shard_map/all_gather | solution.py:46
  68.2 698.3 %copy-start.101 = (f32[128]{0:T(128)}, f32[128]{0:T(128)S(1)}, u32[]{:S(2)}) copy-start(f32[128]{0:T(128)S(1)} %fusion.122) | copy-start | bytes 1540
  68.2 732.4 %copy-start.132 = (f32[128]{0:T(128)}, f32[128]{0:T(128)S(1)}, u32[]{:S(2)}) copy-start(f32[128]{0:T(128)S(1)} %get-tuple-element.1345) | copy-start | bytes 1540
  68.8 731.8 %copy-start.134 = (f32[128]{0:T(128)}, f32[128]{0:T(128)S(1)}, u32[]{:S(2)}) copy-start(f32[128]{0:T(128)S(1)} %get-tuple-element.1405) | copy-start | bytes 1540
  706.3 998.3 %copy-start.66 = (f32[1600]{0:T(1024)}, f32[1600]{0:T(1024)S(1)}, u32[]{:S(2)}) copy-start(f32[1600]{0:T(1024)S(1)} %get-tuple-element.1203) | copy-start | bytes 19204
  706.3 1146.6 %copy-start.96 = (f32[1600]{0:T(1024)}, f32[1600]{0:T(1024)S(1)}, u32[]{:S(2)}) copy-start(f32[1600]{0:T(1024)S(1)} %get-tuple-element.1202) | copy-start | bytes 19204
  714.1 86.5 %copy-start.105 = (f32[3200]{0:T(1024)}, f32[3200]{0:T(1024)S(1)}, u32[]{:S(2)}) copy-start(f32[3200]{0:T(1024)S(1)} %get-tuple-element.1191) | copy-start | bytes 38404
  714.1 86.5 %copy-start.107 = (f32[3200]{0:T(1024)}, f32[3200]{0:T(1024)S(1)}, u32[]{:S(2)}) copy-start(f32[3200]{0:T(1024)S(1)} %get-tuple-element.1192) | copy-start | bytes 38404
  714.1 86.5 %copy-start.109 = (f32[3200]{0:T(1024)}, f32[3200]{0:T(1024)S(1)}, u32[]{:S(2)}) copy-start(f32[3200]{0:T(1024)S(1)} %get-tuple-element.1193) | copy-start | bytes 38404
  782.9 14.5 collective-permute-start.8
  786.4 1089.4 %copy-start.94 = (f32[3200]{0:T(1024)}, f32[3200]{0:T(1024)S(1)}, u32[]{:S(2)}) copy-start(f32[3200]{0:T(1024)S(1)} %get-tuple-element.1198) | copy-start | bytes 38404
  786.4 1092.2 %copy-start.88 = (f32[3200]{0:T(1024)}, f32[3200]{0:T(1024)S(1)}, u32[]{:S(2)}) copy-start(f32[3200]{0:T(1024)S(1)} %get-tuple-element.1197) | copy-start | bytes 38404
  820.0 813.5 %copy-start.52 = (f32[128,3200]{1,0:T(8,128)S(1)}, f32[128,3200]{1,0:T(8,128)}, u32[]{:S(2)}) copy-start(f32[128,3200]{1,0:T(8,128)} %get-tuple-element.1399) | copy-start | bytes 4915204
  1633.1 221.0 %all-gather.10.cloned.1.call-start = ((), (), s32[]{:S(2)}) async-start(), calls=%async_computation | async-start | bytes 1740800 | tf_op jit(solution)/shard_map/all_gather | solution.py:46
  1644.0 635.0 %all-gather.16.cloned.1.call-start = ((), (), s32[]{:S(2)}) async-start(), calls=%async_computation.3 | async-start | bytes 108979200 | tf_op jit(solution)/shard_map/all_gather | solution.py:279
  1663.9 1594.5 %all-gather.14.cloned.1.call-start = ((), (), s32[]{:S(2)}) async-start(), calls=%async_computation.2 | async-start | bytes 1740800 | tf_op jit(solution)/shard_map/all_gather | solution.py:68
  1665.4 38.7 copy-start.120
  1672.0 32.1 copy-start.4
  1673.6 142.5 %collective-permute-start.7 = (bf16[1,128,640]{2,1,0:T(8,128)(2,1)}, bf16[1,128,640]{2,1,0:T(8,128)(2,1)}, u32[]{:S(2)}, u32[]{:S(2)}) collective-permute-start(bf16[1,128,640]{2,1,0:T(8,128)(2,1)} %fusion.54), channel_id=1, source_target_pairs={{0,1},{1,2},{2,3},{3,4},{4,5},{5,6},{6,7},{7,8},{8,9},{9,10},{10,1... | collective-permute-start | bytes 491528 | tf_op jit(solution)/shard_map/ppermute | solution.py:40
  1678.3 136.1 %collective-permute-start.6 = (bf16[1,128,640]{2,1,0:T(8,128)(2,1)}, bf16[1,128,640]{2,1,0:T(8,128)(2,1)}, u32[]{:S(2)}, u32[]{:S(2)}) collective-permute-start(bf16[1,128,640]{2,1,0:T(8,128)(2,1)} %fusion.54), channel_id=1, source_target_pairs={{0,2},{1,3},{2,4},{3,5},{4,6},{5,7},{6,8},{7,9},{8,10},{9,11},{10,... | collective-permute-start | bytes 491528 | tf_op jit(solution)/shard_map/ppermute | solution.py:40
  1680.6 132.3 %collective-permute-start.5 = (bf16[1,128,640]{2,1,0:T(8,128)(2,1)}, bf16[1,128,640]{2,1,0:T(8,128)(2,1)}, u32[]{:S(2)}, u32[]{:S(2)}) collective-permute-start(bf16[1,128,640]{2,1,0:T(8,128)(2,1)} %fusion.54), channel_id=1, source_target_pairs={{0,3},{1,4},{2,5},{3,6},{4,7},{5,8},{6,9},{7,10},{8,11},{9,12},{10... | collective-permute-start | bytes 491528 | tf_op jit(solution)/shard_map/ppermute | solution.py:40
  1683.2 108.2 %collective-permute-start.1 = (bf16[1,128,640]{2,1,0:T(8,128)(2,1)}, bf16[1,128,640]{2,1,0:T(8,128)(2,1)}, u32[]{:S(2)}, u32[]{:S(2)}) collective-permute-start(bf16[1,128,640]{2,1,0:T(8,128)(2,1)} %fusion.54), channel_id=1, source_target_pairs={{0,7},{1,8},{2,9},{3,10},{4,11},{5,12},{6,13},{7,14},{8,15},{16,23... | collective-permute-start | bytes 491528 | tf_op jit(solution)/shard_map/ppermute | solution.py:40
  1686.9 101.7 %collective-permute-start = (bf16[1,128,640]{2,1,0:T(8,128)(2,1)}, bf16[1,128,640]{2,1,0:T(8,128)(2,1)}, u32[]{:S(2)}, u32[]{:S(2)}) collective-permute-start(bf16[1,128,640]{2,1,0:T(8,128)(2,1)} %fusion.54), channel_id=1, source_target_pairs={{0,8},{1,9},{2,10},{3,11},{4,12},{5,13},{6,14},{7,15},{16,24},{17,... | collective-permute-start | bytes 491528 | tf_op jit(solution)/shard_map/ppermute | solution.py:40
  1709.6 117.2 %copy-start.58 = (bf16[128,1600]{0,1:T(8,128)(2,1)}, bf16[128,1600]{0,1:T(8,128)(2,1)S(1)}, u32[]{:S(2)}) copy-start(bf16[128,1600]{0,1:T(8,128)(2,1)S(1)} %convolution_convert_fusion.1) | copy-start | bytes 1228804
  1788.5 87.3 %copy-start.24 = (f32[128,1,3200]{0,2,1:T(8,128)}, f32[128,1,3200]{0,2,1:T(8,128)S(1)}, u32[]{:S(2)}) copy-start(f32[128,1,3200]{0,2,1:T(8,128)S(1)} %copy.236) | copy-start | bytes 4915204
  1788.5 9.6 collective-permute-start.2
  1791.5 13.8 collective-permute-start.3
  1798.2 13.9 collective-permute-start.4
  1890.0 693.7 %copy-start.19 = (f32[1,128,1600]{1,2,0:T(8,128)}, f32[1,128,1600]{1,2,0:T(8,128)S(1)}, u32[]{:S(2)}) copy-start(f32[1,128,1600]{1,2,0:T(8,128)S(1)} %get-tuple-element.1415) | copy-start | bytes 2457604
  1890.0 693.7 %copy-start.148 = (f32[128]{0:T(128)}, f32[128]{0:T(128)S(1)}, u32[]{:S(2)}) copy-start(f32[128]{0:T(128)S(1)} %get-tuple-element.1414) | copy-start | bytes 1540
  1890.0 693.7 %copy-start.127 = (f32[128]{0:T(128)}, f32[128]{0:T(128)S(1)}, u32[]{:S(2)}) copy-start(f32[128]{0:T(128)S(1)} %fusion.125) | copy-start | bytes 1540
  2876.8 41.7 copy-start.33
  2978.8 2855.8 %all-reduce.30.cloned.1.call-start = ((), (), s32[]{:S(2)}) async-start(), calls=%async_computation.5 | async-start | bytes 178626560
  2981.6 39.7 collective-permute-start.10
  2982.9 39.7 collective-permute-start.17
  2984.2 39.8 collective-permute-start.16
  2985.5 203.4 %collective-permute-start.15 = (bf16[1,128,640]{1,2,0:T(8,128)(2,1)}, bf16[1,128,640]{1,2,0:T(8,128)(2,1)}, u32[]{:S(2)}, u32[]{:S(2)}) collective-permute-start(bf16[1,128,640]{1,2,0:T(8,128)(2,1)} %get-tuple-element.1389), channel_id=1, source_target_pairs={{3,0},{4,1},{5,2},{6,3},{7,4},{8,5},{9,6},{10,7},{11,8},{12,9},{13... | collective-permute-start | bytes 491528 | tf_op jit(solution)/shard_map/ppermute | solution.py:40
  2986.8 202.1 %collective-permute-start.14 = (bf16[1,128,640]{1,2,0:T(8,128)(2,1)}, bf16[1,128,640]{1,2,0:T(8,128)(2,1)}, u32[]{:S(2)}, u32[]{:S(2)}) collective-permute-start(bf16[1,128,640]{1,2,0:T(8,128)(2,1)} %get-tuple-element.1390), channel_id=1, source_target_pairs={{4,0},{5,1},{6,2},{7,3},{8,4},{9,5},{10,6},{11,7},{12,8},{13,9},{1... | collective-permute-start | bytes 491528 | tf_op jit(solution)/shard_map/ppermute | solution.py:40
  3021.3 167.5 %collective-permute-start.13 = (bf16[1,128,640]{1,2,0:T(8,128)(2,1)}, bf16[1,128,640]{1,2,0:T(8,128)(2,1)}, u32[]{:S(2)}, u32[]{:S(2)}) collective-permute-start(bf16[1,128,640]{1,2,0:T(8,128)(2,1)} %get-tuple-element.1391), channel_id=1, source_target_pairs={{5,0},{6,1},{7,2},{8,3},{9,4},{10,5},{11,6},{12,7},{13,8},{14,9},{... | collective-permute-start | bytes 491528 | tf_op jit(solution)/shard_map/ppermute | solution.py:40
  3022.6 166.2 %collective-permute-start.12 = (bf16[1,128,640]{1,2,0:T(8,128)(2,1)S(1)}, bf16[1,128,640]{1,2,0:T(8,128)(2,1)}, u32[]{:S(2)}, u32[]{:S(2)}) collective-permute-start(bf16[1,128,640]{1,2,0:T(8,128)(2,1)S(1)} %copy-done.93), channel_id=1, source_target_pairs={{6,0},{7,1},{8,2},{9,3},{10,4},{11,5},{12,6},{13,7},{14,8},{15,9},... | collective-permute-start | bytes 491528 | tf_op jit(solution)/shard_map/ppermute | solution.py:40
  3024.0 164.9 %collective-permute-start.11 = (bf16[1,128,640]{1,2,0:T(8,128)(2,1)S(1)}, bf16[1,128,640]{1,2,0:T(8,128)(2,1)}, u32[]{:S(2)}, u32[]{:S(2)}) collective-permute-start(bf16[1,128,640]{1,2,0:T(8,128)(2,1)S(1)} %get-tuple-element.1393), channel_id=1, source_target_pairs={{7,0},{8,1},{9,2},{10,3},{11,4},{12,5},{13,6},{14,7},{15,8},{23,16... | collective-permute-start | bytes 491528 | tf_op jit(solution)/shard_map/ppermute | solution.py:40
  3147.3 41.6 copy-start.92
  3188.8 54.3 copy-start.86
  3188.8 54.3 copy-start.121
  3190.4 53.6 copy-start.73
  4405.4 26.5 collective-permute-start.9
  4588.1 2738.8 %all-reduce.28.cloned.1.call-start = ((), (), s32[]{:S(2)}) async-start(), calls=%async_computation.4 | async-start | bytes 211353600
  (140 other events, 989.0 us)
Sparse Core Ops, SparseCore 0:
  44.6 658.5 all-reduce.31
  1633.2 39.4 all-gather.11
  1675.2 45.6 all-gather.9
  1724.5 554.4 all-gather.15
  2979.0 40.1 all-gather.13
  4588.3 1246.3 all-reduce.29
  5841.1 1485.7 all-reduce.27
where the time goes:
time: 7450 us; the launch traced here: 7340 us
  waiting for transfers between devices  3660 us (49%)
  local copies, waits for them, and re-layouts  1830 us (25%)
  other arithmetic  1440 us (19%)
  matrix products  248 us (3%)
  blocking collectives  104 us (1%)
    unnamed x10, waiting for transfers between devices  3250 us
    dynamic_update_slice x384, other arithmetic, ssm_local(): end_state, outputs = lax.scan(token_step, start_state, time_major)  554 us
    dynamic_update_slice x768, local copies, waits for them, and re-layouts, ssm_local(): end_state, outputs = lax.scan(token_step, start_state, time_major)  453 us
    dynamic_slice x640, local copies, waits for them, and re-layouts, ssm_local(): end_state, outputs = lax.scan(token_step, start_state, time_major)  440 us
    all_gather x1, waiting for transfers between devices, per_device(): lax.all_gather(ffn_params, ('row', 'seq'), axis=0, tiled=True)  389 us
    all_gather x1, other arithmetic, per_device(): lax.all_gather(ffn_params, ('row', 'seq'), axis=0, tiled=True)  305 us
    unnamed x364, local copies, waits for them, and re-layouts  296 us
    reduce_sum x128, other arithmetic, token_step(): (dt_t * c_t)[..., None] * b_t[:, None, :]  286 us
  transfers between devices with their start and end apart: 25, of which 7 were waited for; matrix products, arithmetic and copies ran while one was open for 8% of the time, Pallas kernels for 0%

commit v1 on v0

v1 whole, which is shorter than its diff:
```python
import functools
from functools import partial
import math

import jax
import jax.numpy as jnp
from jax import lax
from jax.experimental import pallas as pl
from jax.experimental.pallas import tpu as pltpu
from jax.sharding import PartitionSpec as P

D = 1600
HEADS = 25
GROUPS = 5
HEAD = 64
INNER = 3200
STATE = 16
CONV = 4
DT_RANK = 100
FF = 5504
REACH = 8
BLOCK = 128
RUNS = 4
SUB = 8
SPAN = 128
SIXTEEN = jnp.bfloat16
WIDE = jnp.float32


norm_eps = 1e-05


def split_flat(flat_vec, layout):
    pieces = []
    offset = 0
    for piece_shape in layout:
        piece_len = math.prod(piece_shape)
        pieces.append(flat_vec[offset : offset + piece_len].reshape(piece_shape))
        offset += piece_len
    return pieces


def mixer_layout():
    return [
        (D, HEADS * HEAD),
        (D, 2 * GROUPS * HEAD),
        (D, 2 * INNER),
        (INNER, DT_RANK + 2 * STATE),
        (DT_RANK, INNER),
        (HEADS * HEAD + INNER, D),
    ]


def ffn_layout():
    return [(D, FF), (D, FF), (FF, D)]


def small_split(flat_vec):
    width = CONV + STATE + 4
    packed_rows = flat_vec[: D * (3 + 2 * width)].reshape(D, 3 + 2 * width)
    channel_part = packed_rows[:, 3:].reshape(INNER, width)
    return packed_rows[:, 0], packed_rows[:, 1], packed_rows[:, 2], channel_part


def rms_norm(values, gain_vec):
    return (
        values * lax.rsqrt(jnp.mean(values * values, axis=-1, keepdims=True) + norm_eps) * gain_vec
    )


def silu_fn(values):
    return values / (1.0 + jnp.exp(-values))


def softplus_fn(values):
    return jnp.maximum(values, 0.0) + jnp.log1p(jnp.exp(-jnp.abs(values)))


def glu_piece(gate_pre, up_pre):
    return silu_fn(gate_pre) * up_pre


def dot_last(left, right):
    return jnp.einsum("...k,kn->...n", left, right, preferred_element_type=WIDE)


def dot_back(grads, right):
    return jnp.einsum("...n,kn->...k", grads, right, preferred_element_type=WIDE)


def dot_weight(left, grads):
    return jnp.einsum("...k,...n->kn", left, grads, preferred_element_type=WIDE)


def heads_of(shards):
    return -(-HEADS // shards)


def runs_of(shards):
    return RUNS if INNER % (RUNS * shards) == 0 else 1


def own_channels(array, axis, shards, place):
    runs = runs_of(shards)
    unit = INNER // (runs * shards)
    shape = array.shape
    cut = array.reshape(shape[:axis] + (runs, shards, unit) + shape[axis + 1 :])
    cut = lax.dynamic_index_in_dim(cut, place, axis + 1, keepdims=False)
    return cut.reshape(shape[:axis] + (runs * unit,) + shape[axis + 1 :])


def pad_heads(array, axis, shards):
    heads = heads_of(shards)
    pads = [(0, 0)] * array.ndim
    pads[axis] = (0, heads * shards - HEADS)
    padded = jnp.pad(array, pads)
    shape = padded.shape
    return padded.reshape(shape[:axis] + (shards, heads * HEAD) + shape[axis + 2 :])


def by_head(w_q, w_kv, shards):
    rows = w_q.shape[0]
    w_kv = w_kv.reshape(rows, 2, GROUPS, 1, HEAD)
    w_kv = jnp.broadcast_to(w_kv, (rows, 2, GROUPS, HEADS // GROUPS, HEAD))
    w_kv = w_kv.reshape(rows, 2, HEADS, HEAD)
    return jnp.concatenate(
        [
            pad_heads(w_q.reshape(rows, HEADS, HEAD), 1, shards),
            pad_heads(w_kv[:, 0], 1, shards),
            pad_heads(w_kv[:, 1], 1, shards),
        ],
        axis=2,
    )


def exchange(value):
    return lax.all_to_all(value, "seq", 0, 0)


def both_halves(value):
    if lax.axis_size("row") != 2:
        return lax.all_gather(value, "row", axis=0, tiled=True)
    other = lax.ppermute(value, "row", [(0, 1), (1, 0)])
    first = lax.axis_index("row") == 0
    return jnp.concatenate(
        [jnp.where(first, value, other), jnp.where(first, other, value)], axis=0
    )


def mixer_fits(length, shards):
    width = INNER // RUNS
    sizes = [math.prod(shape) for shape in mixer_layout()]
    return (
        runs_of(shards) == RUNS
        and length % width == 0
        and all(size % width == 0 for size in sizes)
        and D % shards == 0
        and (HEADS * HEAD * 2) % shards == 0
    )


def mixer_shards_whole(piece):
    shards, place = lax.axis_size("seq"), lax.axis_index("seq")
    whole = lax.all_gather(piece, ("row", "seq"), axis=0, tiled=True)
    w_q, w_kv, w_in, w_x, w_dt, w_out = split_flat(whole, mixer_layout())
    qkv = lax.dynamic_index_in_dim(by_head(w_q, w_kv, shards), place, 1, keepdims=False)
    w_in = own_channels(w_in.reshape(D, 2, INNER), 2, shards, place)
    out_heads = w_out[: HEADS * HEAD].reshape(HEADS, HEAD, D)
    out_heads = lax.dynamic_index_in_dim(pad_heads(out_heads, 0, shards), place, 0, keepdims=False)
    return (
        qkv,
        w_in.reshape(D, -1),
        own_channels(w_x, 0, shards, place),
        own_channels(w_dt, 1, shards, place),
        out_heads,
        own_channels(w_out[HEADS * HEAD :], 0, shards, place),
    )


def mixer_shards(piece):
    shards, place = lax.axis_size("seq"), lax.axis_index("seq")
    if not mixer_fits(piece.shape[0], shards):
        return mixer_shards_whole(piece)
    width = INNER // RUNS
    unit = width // shards
    mine = exchange(piece.reshape(-1, shards, unit).transpose(1, 0, 2))
    mine = both_halves(mine.reshape(-1, unit))
    part_q, part_kv, part_in, part_x, part_dt, part_out = cut_rows(
        mine, [math.prod(shape) // width for shape in mixer_layout()]
    )
    w_in = part_in.reshape(D, -1)
    w_dt = part_dt.reshape(DT_RANK, -1)
    w_x = lax.all_gather(part_x, "seq").transpose(1, 0, 2).reshape(INNER, -1)
    w_x = own_channels(w_x, 0, shards, place)
    rows = D // shards
    by_rows = exchange(
        jnp.concatenate(
            [part_q.reshape(shards, -1, unit), part_kv.reshape(shards, -1, unit)], axis=1
        )
    )
    by_rows = by_rows.transpose(1, 0, 2).reshape(-1, width)
    split = part_q.shape[0] // shards
    cut = by_head(
        by_rows[:split].reshape(rows, HEADS * HEAD),
        by_rows[split:].reshape(rows, 2 * GROUPS * HEAD),
        shards,
    )
    qkv = exchange(cut.transpose(1, 0, 2)).reshape(D, -1)
    per_row = D // width
    head_rows = heads_of(shards) * HEAD
    out_heads = part_out[: HEADS * HEAD * per_row]
    out_heads = jnp.pad(
        out_heads, ((0, (head_rows * shards - HEADS * HEAD) * per_row), (0, 0))
    ).reshape(shards, -1, unit)
    out_inner = part_out[HEADS * HEAD * per_row :].reshape(RUNS, shards, -1, unit)
    out_inner = out_inner.transpose(1, 0, 2, 3).reshape(shards, -1, unit)
    out_both = exchange(jnp.concatenate([out_heads, out_inner], axis=1))
    out_both = out_both.transpose(1, 0, 2).reshape(-1, D)
    return qkv, w_in, w_x, w_dt, out_both[:head_rows], out_both[head_rows:]


def cut_rows(array, counts):
    pieces, offset = [], 0
    for count in counts:
        pieces.append(array[offset : offset + count])
        offset += count
    return pieces


def ffn_shards(piece):
    shards, place = lax.axis_size("seq"), lax.axis_index("seq")
    unit = FF // shards
    if piece.shape[0] % FF or D % shards:
        whole = lax.all_gather(piece, ("row", "seq"), axis=0, tiled=True)
        w_gate, w_up, w_down = split_flat(whole, ffn_layout())
        return (
            lax.dynamic_slice_in_dim(w_gate, place * unit, unit, 1),
            lax.dynamic_slice_in_dim(w_up, place * unit, unit, 1),
            lax.dynamic_slice_in_dim(w_down, place * unit, unit, 0),
        )
    mine = exchange(piece.reshape(-1, shards, unit).transpose(1, 0, 2))
    mine = both_halves(mine.reshape(-1, unit))
    w_gate, w_up, part_down = cut_rows(mine, [D, D, D])
    w_down = exchange(part_down.reshape(shards, -1, unit))
    return w_gate, w_up, w_down.transpose(1, 0, 2).reshape(unit, D)


def small_shards(whole):
    shards, place = lax.axis_size("seq"), lax.axis_index("seq")
    g_one, g_attn, g_two, channel_part = small_split(whole)
    g_attn = pad_heads(g_attn.reshape(HEADS, HEAD), 0, shards)
    return (
        g_one,
        g_two,
        lax.dynamic_index_in_dim(g_attn, place, 0, keepdims=False),
        own_channels(channel_part, 0, shards, place),
    )


def tiles_of(count):
    return -(-count // 128)


def start_blocks(small_params, doc_ids):
    devices = lax.axis_size("row") * lax.axis_size("seq")
    small_rows, id_rows = tiles_of(small_params.shape[0]), tiles_of(doc_ids.shape[0])
    rows = -(-(small_rows + id_rows) // 16) * 16
    small = jnp.pad(small_params, (0, small_rows * 128 - small_params.shape[0]))
    ids = jnp.pad(doc_ids.astype(SIXTEEN), (0, (rows - small_rows) * 128 - doc_ids.shape[0]))
    block = jnp.concatenate([small.reshape(-1, 128), ids.reshape(-1, 128)], axis=0)
    every = push_gather(block, 0)
    small = every[:, :small_rows].reshape(devices, -1)[:, : small_params.shape[0]].reshape(-1)
    ids = every[:, small_rows:].reshape(devices, -1)[:, : doc_ids.shape[0]]
    ids = ids.reshape(lax.axis_size("row"), -1)
    ids = lax.dynamic_index_in_dim(ids, lax.axis_index("row"), 0, keepdims=False)
    return small.astype(WIDE), ids.astype(jnp.int32)


def end_blocks(grad_small, d_meta):
    devices = lax.axis_size("row") * lax.axis_size("seq")
    parts = grad_small.reshape(devices, -1).astype(SIXTEEN)
    small_count = parts.shape[1]
    small_rows = tiles_of(small_count)
    parts = jnp.pad(parts, ((0, 0), (0, small_rows * 128 - small_count)))
    meta = d_meta.astype(SIXTEEN).reshape(devices, -1)
    meta_count = meta.shape[1]
    rows = -(-(small_rows + tiles_of(meta_count)) // 16) * 16
    meta = jnp.pad(meta, ((0, 0), (0, (rows - small_rows) * 128 - meta_count)))
    blocks = jnp.concatenate(
        [parts.reshape(devices, -1, 128), meta.reshape(devices, -1, 128)], axis=1
    )
    own = push_scatter(blocks, 9)
    small = own[:small_rows].reshape(-1)[:small_count]
    meta = own[small_rows:].reshape(-1)[:meta_count].reshape(-1, D)
    return small, meta


def gather_seq(block):
    return lax.all_gather(block, "seq", axis=0, tiled=True)


def scatter_seq(whole):
    return lax.psum_scatter(whole.astype(SIXTEEN), "seq", scatter_dimension=0, tiled=True).astype(
        WIDE
    )


MESH = pl.DeviceIdType.MESH
ANY = pl.BlockSpec(memory_space=pl.ANY)
VMEM = pl.BlockSpec(memory_space=pltpu.VMEM)
MIB = 1024 * 1024


def greet(peers):
    barrier = pltpu.get_barrier_semaphore()
    for peer in peers:
        pl.semaphore_signal(barrier, inc=1, device_id=peer, device_id_type=MESH)
    pl.semaphore_wait(barrier, len(peers))


def ring_place(chip, chips):
    odd = chip % 2
    return odd * (chips - 1 - chip // 2) + (1 - odd) * (chip // 2)


def ring_chip(place, chips):
    place = (place + 2 * chips) % chips
    back = place // (chips // 2)
    return back * (2 * (chips - 1 - place) + 1) + (1 - back) * (2 * place)


def seq_gather_kernel(shards, parts, x_ref, out_ref, ring_send, ring_recv, pair_send, pair_recv, own_sem):
    row, me = lax.axis_index("row"), lax.axis_index("seq")
    chips = shards // 2
    core = me % 2
    place = ring_place(me // 2, chips)

    def device(spot):
        return ring_chip(spot, chips) * 2 + core

    right, left, twin = (row, device(place + 1)), (row, device(place - 1)), (row, me + 1 - 2 * core)
    greet([right, left, twin])
    rows = x_ref.shape[0] // (2 * parts)

    def cut(way, part):
        return pl.ds((way * parts + part) * rows, rows)

    own = pltpu.make_async_copy(x_ref, out_ref.at[me], own_sem)
    own.start()
    started = []

    def send(src, dst, send_sem, recv_sem, to):
        copy = pltpu.make_async_remote_copy(
            src_ref=src, dst_ref=dst, send_sem=send_sem, recv_sem=recv_sem,
            device_id=to, device_id_type=MESH,
        )
        copy.start()
        started.append(copy)
        return copy

    paths = [(way, part) for part in range(parts) for way in range(2)]
    flights = {}
    for way, part in paths:
        flights[way, part] = send(
            x_ref.at[cut(way, part)], out_ref.at[me, cut(way, part)],
            ring_send.at[way, part, 0], ring_recv.at[way, part, 0], (right, left)[way],
        )
    pairs = [send(x_ref, out_ref.at[me], pair_send.at[0, 0, chips - 1], pair_recv.at[0, 0, chips - 1], twin)]
    for step in range(chips - 1):
        for way, part in paths:
            flights[way, part].wait_recv()
            source = device(place - 1 - step if way == 0 else place + 1 + step)
            here = out_ref.at[source, cut(way, part)]
            if step < chips - 2:
                flights[way, part] = send(
                    here, here, ring_send.at[way, part, step + 1],
                    ring_recv.at[way, part, step + 1], (right, left)[way],
                )
            pairs.append(
                send(here, here, pair_send.at[way, part, step], pair_recv.at[way, part, step], twin)
            )
    own.wait()
    for copy in started:
        copy.wait_send()
    for copy in pairs:
        copy.wait_recv()


def ring_seq_gather(block, collective_id, parts=2):
    shards = lax.axis_size("seq")
    chips = shards // 2
    rows, width = block.shape
    ring = pltpu.SemaphoreType.DMA((2, parts, chips - 1))
    pair = pltpu.SemaphoreType.DMA((2, parts, chips))
    gathered = pl.pallas_call(
        functools.partial(seq_gather_kernel, shards, parts),
        out_shape=jax.ShapeDtypeStruct((shards, rows, width), block.dtype),
        in_specs=[ANY],
        out_specs=ANY,
        scratch_shapes=[ring, ring, pair, pair, pltpu.SemaphoreType.DMA],
        compiler_params=pltpu.CompilerParams(collective_id=collective_id, has_side_effects=True),
    )(block)
    return gathered.reshape(shards * rows, width)


def seq_scatter_kernel(
    shards, parts, x_ref, out_ref, mine, pair, arrived, ring_send, ring_recv, pair_send, pair_recv, own_sem
):
    row, me = lax.axis_index("row"), lax.axis_index("seq")
    chips = shards // 2
    core = me % 2
    place = ring_place(me // 2, chips)

    def device(spot, core):
        return ring_chip(spot, chips) * 2 + core

    right = (row, device(place + 1, core))
    left = (row, device(place - 1, core))
    twin = (row, me + 1 - 2 * core)
    greet([right, left, twin])
    rows = x_ref.shape[1] // (2 * parts)

    def cut(way, part):
        return pl.ds((way * parts + part) * rows, rows)

    order = []
    for far in range(1, chips // 2 + 1):
        order += [-far, far] if 2 * far < chips else [far]
    order.append(0)
    waits = {}
    started = []
    for spot in order:
        slot = spot % chips
        load = pltpu.make_async_copy(x_ref.at[device(place + spot, core)], mine.at[slot], own_sem.at[slot])
        load.start()
        copy = pltpu.make_async_remote_copy(
            src_ref=x_ref.at[device(place + spot, 1 - core)],
            dst_ref=pair.at[slot], send_sem=pair_send.at[slot], recv_sem=pair_recv.at[slot],
            device_id=twin, device_id_type=MESH,
        )
        copy.start()
        started.append(copy)
        waits[slot] = (load, copy)

    def ready(slot):
        if slot in waits:
            load, copy = waits.pop(slot)
            load.wait()
            copy.wait_recv()

    flights = {}
    for step in range(chips):
        for part in range(parts):
            for way in range(2):
                slot = (-1 - step if way == 0 else 1 + step) % chips
                ready(slot)
                here = cut(way, part)
                total = mine[slot, here, :].astype(WIDE) + pair[slot, here, :].astype(WIDE)
                if step:
                    flights[way, part].wait_recv()
                    total = total + arrived[way, step - 1, pl.ds(part * rows, rows), :].astype(WIDE)
                if step == chips - 1:
                    out_ref[here, :] = total
                    continue
                mine[slot, here, :] = total.astype(mine.dtype)
                copy = pltpu.make_async_remote_copy(
                    src_ref=mine.at[slot, here], dst_ref=arrived.at[way, step, pl.ds(part * rows, rows)],
                    send_sem=ring_send.at[way, part, step], recv_sem=ring_recv.at[way, part, step],
                    device_id=(right, left)[way], device_id_type=MESH,
                )
                copy.start()
                started.append(copy)
                flights[way, part] = copy
    for copy in started:
        copy.wait_send()


def ring_seq_scatter(whole, collective_id, parts=2):
    shards = lax.axis_size("seq")
    chips = shards // 2
    length, width = whole.shape
    rows = length // shards
    ring = pltpu.SemaphoreType.DMA((2, parts, chips - 1))
    pair = pltpu.SemaphoreType.DMA((chips,))
    return pl.pallas_call(
        functools.partial(seq_scatter_kernel, shards, parts),
        out_shape=jax.ShapeDtypeStruct((rows, width), WIDE),
        in_specs=[ANY],
        out_specs=VMEM,
        scratch_shapes=[
            pltpu.VMEM((chips, rows, width), SIXTEEN),
            pltpu.VMEM((chips, rows, width), SIXTEEN),
            pltpu.VMEM((2, chips - 1, rows // 2, width), SIXTEEN),
            ring, ring, pair, pair, pair,
        ],
        compiler_params=pltpu.CompilerParams(
            collective_id=collective_id, has_side_effects=True, vmem_limit_bytes=56 * MIB
        ),
    )(whole.astype(SIXTEEN).reshape(shards, rows, width))


def bits_of(shards):
    bits = shards.bit_length() - 1
    assert 1 << bits == shards
    return bits


def partner_of(me, bit):
    return me + (1 - 2 * ((me // (1 << bit)) % 2)) * (1 << bit)


def seq_sum_kernel(bits, x_ref, out_ref, total, staged, arrived, send_sem, recv_sem, back_send, back_recv):
    row, me = lax.axis_index("row"), lax.axis_index("seq")
    partners = [(row, partner_of(me, bit)) for bit in range(bits)]
    greet(partners)
    length = x_ref.shape[1]
    total[...] = x_ref[...].astype(WIDE)
    begin = 0
    started = []
    for bit in range(bits):
        half = length >> (bit + 1)
        upper = (me // (1 << bit)) % 2
        kept = pl.multiple_of(begin + upper * half, 128)
        given = pl.multiple_of(begin + (1 - upper) * half, 128)
        staged[:, half : 2 * half] = total[:, pl.ds(given, half)].astype(SIXTEEN)
        copy = pltpu.make_async_remote_copy(
            src_ref=staged.at[:, half : 2 * half], dst_ref=arrived.at[:, half : 2 * half],
            send_sem=send_sem.at[bit], recv_sem=recv_sem.at[bit],
            device_id=partners[bit], device_id_type=MESH,
        )
        copy.start()
        started.append(copy)
        copy.wait_recv()
        total[:, pl.ds(kept, half)] += arrived[:, half : 2 * half].astype(WIDE)
        begin = kept
    half = length >> bits
    out_ref[:, pl.ds(pl.multiple_of(begin, 128), half)] = total[
        :, pl.ds(pl.multiple_of(begin, 128), half)
    ].astype(SIXTEEN)
    for bit in range(bits - 1, -1, -1):
        half = length >> (bit + 1)
        here = out_ref.at[:, pl.ds(pl.multiple_of(begin, 128), half)]
        copy = pltpu.make_async_remote_copy(
            src_ref=here, dst_ref=here, send_sem=back_send.at[bit], recv_sem=back_recv.at[bit],
            device_id=partners[bit], device_id_type=MESH,
        )
        copy.start()
        started.append(copy)
        copy.wait_recv()
        begin = begin - ((me // (1 << bit)) % 2) * half
    for copy in started:
        copy.wait_send()


def seq_sum(values, collective_id):
    bits = bits_of(lax.axis_size("seq"))
    rows, length = values.shape
    sems = pltpu.SemaphoreType.DMA((bits,))
    return pl.pallas_call(
        functools.partial(seq_sum_kernel, bits),
        out_shape=jax.ShapeDtypeStruct((rows, length), SIXTEEN),
        in_specs=[VMEM],
        out_specs=VMEM,
        scratch_shapes=[
            pltpu.VMEM((rows, length), WIDE),
            pltpu.VMEM((rows, length), SIXTEEN),
            pltpu.VMEM((rows, length), SIXTEEN),
            sems, sems, sems, sems,
        ],
        compiler_params=pltpu.CompilerParams(
            collective_id=collective_id, has_side_effects=True, vmem_limit_bytes=48 * MIB
        ),
    )(values)


def seq_sum_small_kernel(bits, x_ref, out_ref, arrived, staged, send_sem, recv_sem):
    row, me = lax.axis_index("row"), lax.axis_index("seq")
    partners = [(row, partner_of(me, bit)) for bit in range(bits)]
    greet(partners)
    total = x_ref[...]
    copies = []
    for bit in range(bits):
        staged[bit] = total
        copy = pltpu.make_async_remote_copy(
            src_ref=staged.at[bit], dst_ref=arrived.at[bit], send_sem=send_sem.at[bit],
            recv_sem=recv_sem.at[bit], device_id=partners[bit], device_id_type=MESH,
        )
        copy.start()
        copies.append(copy)
        copy.wait_recv()
        total = total + arrived[bit]
    out_ref[...] = total
    for copy in copies:
        copy.wait_send()


def seq_sum_small(values, collective_id):
    bits = bits_of(lax.axis_size("seq"))
    shape = values.shape
    tiles = values.reshape(-1, 128)
    sems = pltpu.SemaphoreType.DMA((bits,))
    slots = pltpu.VMEM((bits,) + tiles.shape, WIDE)
    return pl.pallas_call(
        functools.partial(seq_sum_small_kernel, bits),
        out_shape=jax.ShapeDtypeStruct(tiles.shape, WIDE),
        in_specs=[VMEM],
        out_specs=VMEM,
        scratch_shapes=[slots, slots, sems, sems],
        compiler_params=pltpu.CompilerParams(collective_id=collective_id, has_side_effects=True),
    )(tiles).reshape(shape)


def all_peers(rows, shards):
    me = lax.axis_index("row") * shards + lax.axis_index("seq")
    count = rows * shards
    ahead = [(me + far) % count for far in range(1, count)]
    return me, count, [(other, (other // shards, other % shards)) for other in ahead]


def push_gather_kernel(rows, shards, x_ref, out_ref, send_sem, recv_sem):
    me, count, peers = all_peers(rows, shards)
    greet([device for _, device in peers])
    copies = []
    for far, (_, device) in enumerate(peers):
        copy = pltpu.make_async_remote_copy(
            src_ref=x_ref, dst_ref=out_ref.at[me], send_sem=send_sem.at[far],
            recv_sem=recv_sem.at[far], device_id=device, device_id_type=MESH,
        )
        copy.start()
        copies.append(copy)
    out_ref[me] = x_ref[...]
    for copy in copies:
        copy.wait()


def push_gather(block, collective_id):
    rows, shards = lax.axis_size("row"), lax.axis_size("seq")
    sems = pltpu.SemaphoreType.DMA((rows * shards - 1,))
    return pl.pallas_call(
        functools.partial(push_gather_kernel, rows, shards),
        out_shape=jax.ShapeDtypeStruct((rows * shards,) + block.shape, block.dtype),
        in_specs=[VMEM],
        out_specs=VMEM,
        scratch_shapes=[sems, sems],
        compiler_params=pltpu.CompilerParams(collective_id=collective_id, has_side_effects=True),
    )(block)


def push_scatter_kernel(rows, shards, x_ref, out_ref, arrived, send_sem, recv_sem):
    me, count, peers = all_peers(rows, shards)
    greet([device for _, device in peers])
    copies = []
    for far, (other, device) in enumerate(peers):
        copy = pltpu.make_async_remote_copy(
            src_ref=x_ref.at[other], dst_ref=arrived.at[far], send_sem=send_sem.at[far],
            recv_sem=recv_sem.at[far], device_id=device, device_id_type=MESH,
        )
        copy.start()
        copies.append(copy)
    total = x_ref[me].astype(WIDE)
    for far, copy in enumerate(copies):
        copy.wait_recv()
        total = total + arrived[far].astype(WIDE)
    out_ref[...] = total
    for copy in copies:
        copy.wait_send()


def push_scatter(blocks, collective_id):
    rows, shards = lax.axis_size("row"), lax.axis_size("seq")
    count = rows * shards
    sems = pltpu.SemaphoreType.DMA((count - 1,))
    return pl.pallas_call(
        functools.partial(push_scatter_kernel, rows, shards),
        out_shape=jax.ShapeDtypeStruct(blocks.shape[1:], WIDE),
        in_specs=[VMEM],
        out_specs=VMEM,
        scratch_shapes=[pltpu.VMEM((count - 1,) + blocks.shape[1:], blocks.dtype), sems, sems],
        compiler_params=pltpu.CompilerParams(
            collective_id=collective_id, has_side_effects=True, vmem_limit_bytes=32 * MIB
        ),
    )(blocks)


def conv_piece(extended, conv_w, conv_b, lag_masks):
    length = extended.shape[0] - (CONV - 1)
    summed = conv_b
    for j in range(CONV):
        summed = (
            summed + conv_w[j] * extended[CONV - 1 - j : CONV - 1 - j + length] * lag_masks[j]
        )
    return silu_fn(summed)


def nt_dot(left, right):
    return lax.dot_general(left, right, (((1,), (1,)), ((), ())), preferred_element_type=WIDE)


def seen_keys(block, first_row):
    window = (REACH + 1) * BLOCK
    k_pos = (block - REACH) * BLOCK + lax.broadcasted_iota(jnp.int32, (window, BLOCK), 0)
    q_pos = block * BLOCK + lax.broadcasted_iota(jnp.int32, (window, BLOCK), 1)
    return (k_pos >= first_row) & (k_pos <= q_pos) & (k_pos > q_pos - REACH * BLOCK)


def attend_forward_kernel(heads, first_ref, q_ref, kv_ref, turned_ref, meta_ref, meta_turned_ref, out_ref, total_ref):
    block = pl.program_id(0)
    span = pl.ds(pl.multiple_of(block * BLOCK, BLOCK), (REACH + 1) * BLOCK)
    seen = seen_keys(block, first_ref[0])
    outs, totals = [], []
    for h in range(heads):
        cut = slice(h * HEAD, (h + 1) * HEAD)
        v_cut = slice((heads + h) * HEAD, (heads + h + 1) * HEAD)
        query = q_ref[:, cut] * SIXTEEN(HEAD ** (-0.5))
        near = jnp.where(seen, nt_dot(kv_ref[span, cut], query), -1e30)
        meta = nt_dot(meta_ref[:, cut], query)
        top = jnp.maximum(
            jnp.max(near, axis=0, keepdims=True), jnp.max(meta, axis=0, keepdims=True)
        )
        near = jnp.exp(near - top)
        meta = jnp.exp(meta - top)
        total = jnp.sum(near, axis=0, keepdims=True) + jnp.sum(meta, axis=0, keepdims=True)
        out = jnp.dot(turned_ref[v_cut, span], near.astype(SIXTEEN), preferred_element_type=WIDE)
        out += jnp.dot(meta_turned_ref[v_cut, :], meta.astype(SIXTEEN), preferred_element_type=WIDE)
        outs.append(out / total)
        totals.append(top + jnp.log(total))
    out_ref[...] = jnp.concatenate(outs, axis=0).T
    total_ref[0] = jnp.concatenate(totals, axis=0)


def attend_backward_kernel(
    heads, first_ref, q_ref, kv_ref, turned_ref, meta_ref, meta_turned_ref, out_ref, total_ref, do_ref,
    dq_ref, dkv_ref, dmeta_ref,
):
    block = pl.program_id(0)

    @pl.when(block == 0)
    def _():
        dkv_ref[...] = jnp.zeros_like(dkv_ref)
        dmeta_ref[...] = jnp.zeros_like(dmeta_ref)

    span = pl.ds(pl.multiple_of(block * BLOCK, BLOCK), (REACH + 1) * BLOCK)
    seen = seen_keys(block, first_ref[0])
    d_out = do_ref[...]
    row_sums = (d_out * out_ref[...]).T
    d_half = d_out.astype(SIXTEEN)
    d_queries, near_k, near_v, meta_k, meta_v = [], [], [], [], []
    for h in range(heads):
        cut = slice(h * HEAD, (h + 1) * HEAD)
        v_cut = slice((heads + h) * HEAD, (heads + h + 1) * HEAD)
        query = q_ref[:, cut] * SIXTEEN(HEAD ** (-0.5))
        do = d_half[:, cut]
        total = total_ref[0, h : h + 1, :]
        mean = jnp.sum(row_sums[cut], axis=0, keepdims=True)
        near = jnp.where(seen, jnp.exp(nt_dot(kv_ref[span, cut], query) - total), 0.0)
        meta = jnp.exp(nt_dot(meta_ref[:, cut], query) - total)
        d_near = (near * (nt_dot(kv_ref[span, v_cut], do) - mean)).astype(SIXTEEN)
        d_meta = (meta * (nt_dot(meta_ref[:, v_cut], do) - mean)).astype(SIXTEEN)
        near_v.append(jnp.dot(near.astype(SIXTEEN), do, preferred_element_type=WIDE))
        meta_v.append(jnp.dot(meta.astype(SIXTEEN), do, preferred_element_type=WIDE))
        near_k.append(jnp.dot(d_near, query, preferred_element_type=WIDE))
        meta_k.append(jnp.dot(d_meta, query, preferred_element_type=WIDE))
        d_query = jnp.dot(turned_ref[cut, span], d_near, preferred_element_type=WIDE)
        d_query += jnp.dot(meta_turned_ref[cut, :], d_meta, preferred_element_type=WIDE)
        d_queries.append(d_query * HEAD ** (-0.5))
    dq_ref[...] = jnp.concatenate(d_queries, axis=0).T.astype(SIXTEEN)
    dkv_ref[span, :] += jnp.concatenate(near_k + near_v, axis=1)
    dmeta_ref[...] += jnp.concatenate(meta_k + meta_v, axis=1)


def attend_operands(queries, kv_rows, doc_first):
    length = doc_first.shape[0]
    count = length // BLOCK
    near = jnp.pad(kv_rows[:length], ((REACH * BLOCK, 0), (0, 0)))
    meta = kv_rows[length:]
    arrays = (doc_first.reshape(count, 1, BLOCK), queries, near, near.T, meta, meta.T)
    width = queries.shape[1]

    def whole(array):
        return pl.BlockSpec(array.shape, lambda i: (0,) * array.ndim)

    specs = [
        pl.BlockSpec((1, 1, BLOCK), lambda i: (i, 0, 0)),
        pl.BlockSpec((BLOCK, width), lambda i: (i, 0)),
    ] + [whole(a) for a in arrays[2:]]
    return arrays, specs, count, width


def attend_forward(queries, kv_rows, doc_first):
    arrays, specs, count, width = attend_operands(queries, kv_rows, doc_first)
    heads = width // HEAD
    return pl.pallas_call(
        lambda *refs: attend_forward_kernel(heads, *refs),
        grid=(count,),
        in_specs=specs,
        out_specs=[
            pl.BlockSpec((BLOCK, width), lambda i: (i, 0)),
            pl.BlockSpec((1, heads, BLOCK), lambda i: (i, 0, 0)),
        ],
        out_shape=[
            jax.ShapeDtypeStruct(queries.shape, WIDE),
            jax.ShapeDtypeStruct((count, heads, BLOCK), WIDE),
        ],
        compiler_params=pltpu.CompilerParams(vmem_limit_bytes=48 * MIB),
    )(*arrays)


def attend_backward(queries, kv_rows, doc_first, out, log_total, d_out):
    arrays, specs, count, width = attend_operands(queries, kv_rows, doc_first)
    heads = width // HEAD
    near, meta = arrays[2], arrays[4]
    row_spec = pl.BlockSpec((BLOCK, width), lambda i: (i, 0))
    d_queries, d_near, d_meta = pl.pallas_call(
        lambda *refs: attend_backward_kernel(heads, *refs),
        grid=(count,),
        in_specs=specs
        + [row_spec, pl.BlockSpec((1, heads, BLOCK), lambda i: (i, 0, 0)), row_spec],
        out_specs=[
            row_spec,
            pl.BlockSpec(near.shape, lambda i: (0, 0)),
            pl.BlockSpec(meta.shape, lambda i: (0, 0)),
        ],
        out_shape=[
            jax.ShapeDtypeStruct(queries.shape, SIXTEEN),
            jax.ShapeDtypeStruct(near.shape, WIDE),
            jax.ShapeDtypeStruct(meta.shape, WIDE),
        ],
        compiler_params=pltpu.CompilerParams(vmem_limit_bytes=48 * MIB),
    )(*arrays, out, log_total, d_out)
    return d_queries, jnp.concatenate([d_near[REACH * BLOCK :], d_meta], axis=0).astype(SIXTEEN)


def step_sum():
    rows = lax.broadcasted_iota(jnp.int32, (SUB, SUB * STATE), 0)
    cols = lax.broadcasted_iota(jnp.int32, (SUB, SUB * STATE), 1)
    return (cols // STATE == rows).astype(SIXTEEN)


def scan_forward_kernel(keep_ref, conv_ref, delta_ref, b_ref, c_ref, a_ref, y_ref, start_ref, state_ref):
    block = pl.program_id(0)

    @pl.when(block == 0)
    def _():
        state_ref[...] = jnp.zeros_like(state_ref)

    start_ref[0] = state_ref[...]
    decay_rate = a_ref[...]
    fold = step_sum()

    def body(group, state):
        rows = pl.ds(pl.multiple_of(group * SUB, SUB), SUB)
        delta = delta_ref[rows, :]
        drive = delta * conv_ref[rows, :]
        b_tile = b_ref[group]
        c_tile = c_ref[group]
        reads = []
        for i in range(SUB):
            keep = keep_ref[block * SPAN + group * SUB + i]
            decay = jnp.exp(delta[i : i + 1, :] * decay_rate) * keep
            state = decay * state + drive[i : i + 1, :] * b_tile[:, i : i + 1]
            reads.append((state * c_tile[:, i : i + 1]).astype(SIXTEEN))
        y_ref[rows, :] = jnp.dot(
            fold, jnp.concatenate(reads, axis=0), preferred_element_type=WIDE
        )
        return state

    state_ref[...] = lax.fori_loop(0, SPAN // SUB, body, state_ref[...])


def time_tiles(values):
    return values.reshape(values.shape[0] // SUB, SUB, STATE).transpose(0, 2, 1)


def scan_forward(keep, conv_out, delta, b_in, c_read, decay_rate):
    length, lanes = conv_out.shape
    blocks = length // SPAN
    span_spec = pl.BlockSpec((SPAN, lanes), lambda i: (i, 0))
    tile_spec = pl.BlockSpec((SPAN // SUB, STATE, SUB), lambda i: (i, 0, 0))
    return pl.pallas_call(
        scan_forward_kernel,
        grid=(blocks,),
        in_specs=[
            pl.BlockSpec(memory_space=pltpu.SMEM),
            span_spec,
            span_spec,
            tile_spec,
            tile_spec,
            pl.BlockSpec((STATE, lanes), lambda i: (0, 0)),
        ],
        out_specs=[span_spec, pl.BlockSpec((1, STATE, lanes), lambda i: (i, 0, 0))],
        out_shape=[
            jax.ShapeDtypeStruct((length, lanes), WIDE),
            jax.ShapeDtypeStruct((blocks, STATE, lanes), WIDE),
        ],
        scratch_shapes=[pltpu.VMEM((STATE, lanes), WIDE)],
    )(keep, conv_out, delta, time_tiles(b_in), time_tiles(c_read), decay_rate)


def scan_backward_kernel(
    keep_ref, conv_ref, delta_ref, b_ref, c_ref, a_ref, start_ref, dy_ref,
    dconv_ref, ddelta_ref, db_ref, dc_ref, da_ref,
    state_ref, decay_ref, adjoint_ref,
):
    turn = pl.program_id(0)
    block = pl.num_programs(0) - 1 - turn

    @pl.when(turn == 0)
    def _():
        adjoint_ref[...] = jnp.zeros_like(adjoint_ref)
        da_ref[...] = jnp.zeros_like(da_ref)

    decay_rate = a_ref[...]
    fold = step_sum()
    lanes = decay_rate.shape[1]
    ones = jnp.ones((SUB, lanes), SIXTEEN)
    state_ref[0] = start_ref[0]

    def ahead(group, state):
        rows = pl.ds(pl.multiple_of(group * SUB, SUB), SUB)
        delta = delta_ref[rows, :]
        drive = delta * conv_ref[rows, :]
        b_tile = b_ref[group]
        for i in range(SUB):
            keep = keep_ref[block * SPAN + group * SUB + i]
            decay = jnp.exp(delta[i : i + 1, :] * decay_rate) * keep
            state = decay * state + drive[i : i + 1, :] * b_tile[:, i : i + 1]
            decay_ref[group * SUB + i] = decay
            state_ref[group * SUB + i + 1] = state
        return state

    lax.fori_loop(0, SPAN // SUB, ahead, start_ref[0])

    def back(step, carry):
        adjoint, da = carry
        group = SPAN // SUB - 1 - step
        rows = pl.ds(pl.multiple_of(group * SUB, SUB), SUB)
        delta = delta_ref[rows, :]
        conv = conv_ref[rows, :]
        drive = delta * conv
        dy = dy_ref[rows, :]
        b_tile = b_ref[group]
        c_tile = c_ref[group]
        by_c, by_b, by_drive, by_delta = ([None] * SUB for _ in range(4))
        for i in range(SUB - 1, -1, -1):
            index = group * SUB + i
            dy_row = dy[i : i + 1, :]
            total = adjoint + dy_row * c_tile[:, i : i + 1]
            by_c[i] = (dy_row * state_ref[index + 1]).astype(SIXTEEN)
            by_b[i] = (total * drive[i : i + 1, :]).astype(SIXTEEN)
            by_drive[i] = (total * b_tile[:, i : i + 1]).astype(SIXTEEN)
            adjoint = total * decay_ref[index]
            rate = adjoint * state_ref[index]
            by_delta[i] = (rate * decay_rate).astype(SIXTEEN)
            da = da + rate * delta[i : i + 1, :]
        def over_state(parts):
            return jnp.dot(fold, jnp.concatenate(parts, axis=0), preferred_element_type=WIDE)
        def over_lanes(parts):
            return lax.dot_general(
                ones, jnp.concatenate(parts, axis=0), (((1,), (1,)), ((), ())),
                preferred_element_type=WIDE,
            )
        d_drive = over_state(by_drive)
        dconv_ref[rows, :] = d_drive * delta
        ddelta_ref[rows, :] = over_state(by_delta) + d_drive * conv
        db_ref[group] = over_lanes(by_b)
        dc_ref[group] = over_lanes(by_c)
        return adjoint, da

    adjoint, da = lax.fori_loop(0, SPAN // SUB, back, (adjoint_ref[...], da_ref[...]))
    adjoint_ref[...] = adjoint
    da_ref[...] = da


def scan_backward(keep, conv_out, delta, b_in, c_read, decay_rate, starts, dy):
    length, lanes = conv_out.shape
    blocks = length // SPAN
    span_spec = pl.BlockSpec((SPAN, lanes), lambda i: (blocks - 1 - i, 0))
    tile_spec = pl.BlockSpec((SPAN // SUB, STATE, SUB), lambda i: (blocks - 1 - i, 0, 0))
    sums_spec = pl.BlockSpec((SPAN // SUB, SUB, SUB * STATE), lambda i: (blocks - 1 - i, 0, 0))
    whole = pl.BlockSpec((STATE, lanes), lambda i: (0, 0))
    sums = jax.ShapeDtypeStruct((length // SUB, SUB, SUB * STATE), WIDE)
    dconv, ddelta, db, dc, da = pl.pallas_call(
        scan_backward_kernel,
        grid=(blocks,),
        in_specs=[
            pl.BlockSpec(memory_space=pltpu.SMEM),
            span_spec,
            span_spec,
            tile_spec,
            tile_spec,
            whole,
            pl.BlockSpec((1, STATE, lanes), lambda i: (blocks - 1 - i, 0, 0)),
            span_spec,
        ],
        out_specs=[span_spec, span_spec, sums_spec, sums_spec, whole],
        out_shape=[
            jax.ShapeDtypeStruct((length, lanes), WIDE),
            jax.ShapeDtypeStruct((length, lanes), WIDE),
            sums,
            sums,
            jax.ShapeDtypeStruct((STATE, lanes), WIDE),
        ],
        scratch_shapes=[
            pltpu.VMEM((SPAN + 1, STATE, lanes), WIDE),
            pltpu.VMEM((SPAN, STATE, lanes), WIDE),
            pltpu.VMEM((STATE, lanes), WIDE),
        ],
        compiler_params=pltpu.CompilerParams(vmem_limit_bytes=32 * 1024 * 1024),
    )(keep, conv_out, delta, time_tiles(b_in), time_tiles(c_read), decay_rate, starts, dy)
    return dconv, ddelta, db[:, 0].reshape(length, STATE), dc[:, 0].reshape(length, STATE), da


def padded_lanes(array, lanes):
    return jnp.pad(array, ((0, 0), (0, lanes - array.shape[1])))


def rms_pull(values, scale, gain, d_normed, mean):
    d_values = scale * gain * d_normed - values * (scale * scale * scale) * mean
    return d_values, jnp.sum(d_normed * values * scale, axis=0)


def per_device(tokens, doc_ids, meta_tokens, mixer_params, small_params, ffn_params, cotangent):
    tokens, cotangent = tokens[0], cotangent[0]
    small_whole, ids = start_blocks(small_params, doc_ids[0])
    (g_one, g_two, g_attn, channel_part), small_pull = jax.vjp(small_shards, small_whole)
    (w_qkv, w_in, w_x, w_dt, w_out_a, w_out_m), mixer_pull = jax.vjp(mixer_shards, mixer_params)
    (w_gate, w_up, w_down), ffn_pull = jax.vjp(ffn_shards, ffn_params)
    channels = channel_part.shape[0]
    lanes = -(-channels // 128) * 128
    g_ssm = channel_part[:, 0]
    conv_w = channel_part[:, 1 : 1 + CONV].T
    conv_b = channel_part[:, 1 + CONV]
    dt_bias = channel_part[:, 2 + CONV]
    a_log = channel_part[:, 3 + CONV : 3 + CONV + STATE]
    d_skip = channel_part[:, 3 + CONV + STATE]

    length = ids.shape[0]
    positions = jnp.arange(length, dtype=jnp.int32)
    starts = jnp.concatenate([jnp.ones((1,), bool), ids[1:] != ids[:-1]])
    doc_first = lax.cummax(jnp.where(starts, positions, 0), axis=0)
    keep_mask = (positions != doc_first).astype(WIDE)
    lag_masks = jnp.stack(
        [(positions - j >= doc_first).astype(WIDE)[:, None] for j in range(CONV)]
    )

    tokens_f = tokens.astype(WIDE)
    normed_f, norm_pull = jax.vjp(rms_norm, tokens_f, g_one)
    meta_own = meta_tokens.astype(WIDE)
    meta_unit = rms_norm(lax.all_gather(meta_tokens, ("row", "seq"), axis=0, tiled=True).astype(WIDE), 1.0)
    normed = ring_seq_gather(normed_f.astype(SIXTEEN), 1)
    meta_normed = (meta_unit * g_one).astype(SIXTEEN)
    every = jnp.concatenate([normed, meta_normed], axis=0)
    cotangent_all = gather_seq(cotangent)

    xz = dot_last(normed, w_in).astype(SIXTEEN)
    extended = jnp.pad(xz[:, :channels], ((CONV - 1, 0), (0, 0))).astype(WIDE)
    conv_fn = partial(conv_piece, lag_masks=lag_masks)
    conv_out, conv_pull = jax.vjp(conv_fn, extended, conv_w, conv_b)
    conv_half = conv_out.astype(SIXTEEN)
    conv_f = conv_half.astype(WIDE)
    w_x_rows = jnp.pad(w_x.T, ((0, -w_x.shape[1] % 16), (0, 0)))
    projected = seq_sum(jnp.einsum("nc,tc->nt", w_x_rows, conv_half, preferred_element_type=WIDE), 2)
    rank_half = projected[:DT_RANK].T
    b_in = projected[DT_RANK : DT_RANK + STATE].T.astype(WIDE)
    c_read = projected[DT_RANK + STATE : DT_RANK + 2 * STATE].T.astype(WIDE)
    pre_dt = dot_last(rank_half, w_dt)
    delta, delta_pull = jax.vjp(lambda p, b: softplus_fn(p + b), pre_dt, dt_bias)
    a_neg, a_pull = jax.vjp(lambda a: -jnp.exp(a), a_log)
    scan_in = (
        keep_mask,
        padded_lanes(conv_f, lanes),
        padded_lanes(delta, lanes),
        b_in,
        c_read,
        padded_lanes(a_neg.T, lanes),
    )
    y_scan, scan_starts = scan_forward(*scan_in)

    def gate_piece(y, c, skip, z):
        return (y + skip * c) * silu_fn(z)

    z_in = xz[:, channels:].astype(WIDE)
    ssm_out, gate_pull = jax.vjp(gate_piece, y_scan[:, :channels], conv_f, d_skip, z_in)

    own_heads = g_attn.shape[0]
    queries = dot_last(normed, w_qkv[:, :own_heads]).astype(SIXTEEN)
    kv_rows = dot_last(every, w_qkv[:, own_heads:]).astype(SIXTEEN)
    attn_out, log_total = attend_forward(queries, kv_rows, doc_first)

    squares = jnp.stack([jnp.sum(attn_out * attn_out, axis=1), jnp.sum(ssm_out * ssm_out, axis=1)])
    squares = seq_sum_small(squares, 3)
    scale_a = lax.rsqrt(squares[0] / (HEADS * HEAD) + norm_eps)[:, None]
    scale_m = lax.rsqrt(squares[1] / INNER + norm_eps)[:, None]
    mixed = 0.5 * jnp.concatenate(
        [attn_out * scale_a * g_attn, ssm_out * scale_m * g_ssm], axis=1
    )
    mixed = mixed.astype(SIXTEEN)
    w_out = jnp.concatenate([w_out_a, w_out_m], axis=0)
    hidden = tokens_f + ring_seq_scatter(dot_last(mixed, w_out), 4)

    second_f, second_pull = jax.vjp(rms_norm, hidden, g_two)
    second = ring_seq_gather(second_f.astype(SIXTEEN), 5)
    gate_pre = dot_last(second, w_gate)
    up_pre = dot_last(second, w_up)
    act_f, act_pull = jax.vjp(glu_piece, gate_pre, up_pre)
    act = act_f.astype(SIXTEEN)
    d_gate, d_up = act_pull(dot_back(cotangent_all, w_down))
    d_gate, d_up = d_gate.astype(SIXTEEN), d_up.astype(SIXTEEN)
    d_second = ring_seq_scatter(dot_back(d_gate, w_gate) + dot_back(d_up, w_up), 6)
    block_out = (hidden + scatter_seq(dot_last(act, w_down))).astype(SIXTEEN)
    (grad_ffn,) = ffn_pull(
        (
            dot_weight(second, d_gate).astype(SIXTEEN),
            dot_weight(second, d_up).astype(SIXTEEN),
            dot_weight(act, cotangent_all).astype(SIXTEEN),
        )
    )
    d_hidden, grad_g_two = second_pull(d_second)
    d_hidden = d_hidden + cotangent.astype(WIDE)

    d_branch = ring_seq_gather(d_hidden.astype(SIXTEEN), 7)
    grad_out = dot_weight(mixed, d_branch)
    d_mixed = 0.5 * dot_back(d_branch, w_out)
    d_mix_a, d_mix_m = d_mixed[:, :own_heads], d_mixed[:, own_heads:]
    means = jnp.stack(
        [jnp.sum(attn_out * g_attn * d_mix_a, axis=1), jnp.sum(ssm_out * g_ssm * d_mix_m, axis=1)]
    )
    means = seq_sum_small(means, 8)
    d_attn, grad_g_attn = rms_pull(
        attn_out, scale_a, g_attn, d_mix_a, means[0][:, None] / (HEADS * HEAD)
    )
    d_ssm, grad_g_ssm = rms_pull(ssm_out, scale_m, g_ssm, d_mix_m, means[1][:, None] / INNER)

    d_queries, d_kv = attend_backward(
        queries, kv_rows, doc_first, attn_out, log_total, d_attn
    )

    d_y, d_conv, grad_d_skip, d_z = gate_pull(d_ssm)
    d_conv_scan, d_delta, d_b, d_c, d_rate = scan_backward(
        *scan_in, scan_starts, padded_lanes(d_y, lanes)
    )
    d_conv = d_conv + d_conv_scan[:, :channels]
    d_pre, grad_dt_bias = delta_pull(d_delta[:, :channels])
    (grad_a_log,) = a_pull(d_rate[:, :channels].T)
    d_pre = d_pre.astype(SIXTEEN)
    grad_dt = dot_weight(rank_half, d_pre)
    d_rank = jnp.einsum("rc,tc->rt", w_dt, d_pre, preferred_element_type=WIDE)
    d_proj = jnp.concatenate([d_rank, d_b.T, d_c.T], axis=0)
    d_proj = seq_sum(jnp.pad(d_proj, ((0, -d_proj.shape[0] % 16), (0, 0))), 10)
    d_proj = d_proj[: DT_RANK + 2 * STATE].T
    grad_x = dot_weight(conv_half, d_proj)
    d_extended, grad_conv_w, grad_conv_b = conv_pull(d_conv + dot_back(d_proj, w_x))
    d_xz = jnp.concatenate([d_extended[CONV - 1 :], d_z], axis=1).astype(SIXTEEN)
    grad_in = dot_weight(normed, d_xz)
    grad_qkv = jnp.concatenate([dot_weight(normed, d_queries), dot_weight(every, d_kv)], axis=1)
    d_meta = dot_back(d_kv[length:], w_qkv[:, own_heads:])
    d_normed = (
        dot_back(d_xz, w_in)
        + dot_back(d_queries, w_qkv[:, :own_heads])
        + dot_back(d_kv[:length], w_qkv[:, own_heads:])
    )
    grad_from_norm, grad_g_one = norm_pull(ring_seq_scatter(d_normed, 11))
    grad_tokens = d_hidden + grad_from_norm
    grad_g_meta = jnp.sum(d_meta * meta_unit, axis=0)
    grads = (grad_qkv, grad_in, grad_x, grad_dt, grad_out[:own_heads], grad_out[own_heads:])
    (grad_mixer,) = mixer_pull(tuple(g.astype(SIXTEEN) for g in grads))
    grad_channels = jnp.concatenate(
        [
            grad_g_ssm[:, None],
            grad_conv_w.T,
            grad_conv_b[:, None],
            grad_dt_bias[:, None],
            grad_a_log,
            grad_d_skip[:, None],
        ],
        axis=1,
    )
    (grad_small,) = small_pull((grad_g_one + grad_g_meta, grad_g_two, grad_g_attn, grad_channels))
    grad_small, d_meta = end_blocks(grad_small, d_meta)
    _, meta_pull = jax.vjp(lambda v: rms_norm(v, g_one), meta_own)
    (grad_meta,) = meta_pull(d_meta)
    return (
        block_out[None],
        grad_tokens[None],
        grad_meta,
        grad_mixer.astype(WIDE),
        grad_small,
        grad_ffn.astype(WIDE),
    )


def solution(mesh):
    in_specs = (
        P("row", "seq", None),
        P("row", "seq"),
        P(("row", "seq"), None),
        P(("row", "seq")),
        P(("row", "seq")),
        P(("row", "seq")),
        P("row", "seq", None),
    )
    out_specs = (
        P("row", "seq", None),
        P("row", "seq", None),
        P(("row", "seq"), None),
        P(("row", "seq")),
        P(("row", "seq")),
        P(("row", "seq")),
    )
    return jax.shard_map(
        per_device, mesh=mesh, in_specs=in_specs, out_specs=out_specs, check_vma=False
    )
```

time: 7450 us -> 1530 us (0.21); the launches traced: 7340 us -> 1520 us
  waiting for transfers between devices: 3660 us -> 96.2 us
  local copies, waits for them, and re-layouts: 1830 us -> 356 us
  other arithmetic: 1440 us -> 76.3 us
  Pallas kernels: 0 us -> 656 us
  matrix products: 248 us -> 140 us
    unnamed x10 -> x4, waiting for transfers between devices: 3250 us -> 0.73 us
    pallas_call x0 -> x16, Pallas kernels: none -> 656 us  [the longest x3 142 us: ring_seq_scatter(): pl.pallas_call(functools.partial(seq_scatter_kernel, shards, parts), out_...]
    dynamic_update_slice x384 -> x0, other arithmetic: 554 us -> none  [ssm_local(): end_state, outputs = lax.scan(token_step, start_state, time_major)]
    dynamic_update_slice x768 -> x3, local copies, waits for them, and re-layouts: 453 us -> 0.71 us  [the longest x2 0.68 us: own_channels(): cut = lax.dynamic_index_in_dim(cut, place, axis + 1, keepdims=False)]
    dynamic_slice x640 -> x3, local copies, waits for them, and re-layouts: 440 us -> 1.91 us  [own_channels(): cut = lax.dynamic_index_in_dim(cut, place, axis + 1, keepdims=False)]
    all_gather x4 -> x1, waiting for transfers between devices: 389 us -> 0.01 us  [gather_seq(): return lax.all_gather(block, 'seq', axis=0, tiled=True)]
    reduce_sum x263 -> x8, other arithmetic: 372 us -> 15.1 us  [the longest x1 6.82 us: gate_piece(): return (y + skip * c) * silu_fn(z)]
    all_gather x1 -> x0, other arithmetic: 305 us -> none  [per_device(): lax.all_gather(ffn_params, ('row', 'seq'), axis=0, tiled=True)]
  transfers between devices with their start and end apart: 25 -> 19, of which waited for: 7 -> 5; matrix products, arithmetic and copies ran while one was open for 8% -> 29% of each run, Pallas kernels for 0% -> 38%
where the time goes in v1:
time: 1530 us; the launch traced here: 1520 us
  Pallas kernels  656 us (43%)
  local copies, waits for them, and re-layouts  356 us (23%)
  matrix products  140 us (9%)
  waiting for transfers between devices  96.2 us (6%)
  blocking collectives  90.5 us (6%)
  starting transfers between devices  87.5 us (6%)
  other arithmetic  76.3 us (5%)
  between operations  16.6 us (1%)
    pallas_call x3, Pallas kernels, ring_seq_scatter(): pl.pallas_call(functools.partial(seq_scatter_kernel, shards, parts), out_...  142 us
    pallas_call x3, Pallas kernels, ring_seq_gather(): pl.pallas_call(functools.partial(seq_gather_kernel, shards, parts), out_s...  130 us
    pallas_call x1, Pallas kernels, scan_backward(): pl.pallas_call(scan_backward_kernel, grid=(blocks,), in_specs=[pl.BlockSp...  95.8 us
    all_to_all x12, starting transfers between devices, exchange(): return lax.all_to_all(value, 'seq', 0, 0)  84 us
    pallas_call x1, Pallas kernels, scan_forward(): pl.pallas_call(scan_forward_kernel, grid=(blocks,), in_specs=[pl.BlockSpe...  60.9 us
    pallas_call x2, Pallas kernels, seq_sum(): pl.pallas_call(functools.partial(seq_sum_kernel, bits), out_shape=jax.Sha...  57.7 us
    pallas_call x1, Pallas kernels, push_gather(): pl.pallas_call(functools.partial(push_gather_kernel, rows, shards), out_s...  57.3 us
    dot_general x9, matrix products, dot_back(): jnp.einsum('...n,kn->...k', grads, right, preferred_element_type=WIDE)  53.9 us
  transfers between devices with their start and end apart: 19, of which 5 were waited for; matrix products, arithmetic and copies ran while one was open for 29% of the time, Pallas kernels for 38%

profile of v1, /device:TPU:0, one launch (start us, length us, event | category | flops | bytes accessed | tf_op | source)
XLA Modules:
  0.0 1518.3 jit_solution(3850010319885484261)
XLA Ops:
  7.2 12.2 reshape.557
  25.1 7.6 all-to-all-start
  34.1 57.3 %shard_map.118 = bf16[32,32,128]{2,1,0:T(8,128)(2,1)} custom-call(bf16[32,128]{1,0:T(8,128)(2,1)} %pad_maximum_fusion.18.x_ref), custom_call_target="tpu_custom_call" | custom-call | tf_op jit(solution)/shard_map/pallas_call | solution.py:639
  94.3 46.2 %all-gather.2 = bf16[32,4,1600]{2,1,0:T(4,128)(2,1)S(1)} all-gather(bf16[1,4,1600]{2,1,0:T(4,128)(2,1)S(1)} %bitcast.309), channel_id=1, replica_groups=mesh['row'=2,'seq'=16] {'row','seq'}, dimensions={0}, use_global_device_ids=true | all-gather | bytes 422400 | tf_op jit(solution)/shard_map/all_gather | solution.py:1049
  169.8 33.7 %collective-permute-done = bf16[13904,50]{0,1:T(8,128)(2,1)S(1)} collective-permute-done((bf16[13904,50]{0,1:T(8,128)(2,1)}, bf16[13904,50]{0,1:T(8,128)(2,1)S(1)}, u32[]{:S(2)}, u32[]{:S(2)}) %collective-permute-start) | collective-permute-done | bytes 1390432 | tf_op jit(solution)/shard_map/jvp()/ppermute | solution.py:143
  221.5 51.9 %shard_map.119 = bf16[16,128,1600]{2,1,0:T(8,128)(2,1)} custom-call(bf16[128,1600]{1,0:T(8,128)(2,1)} %get-tuple-element.139.x_ref), custom_call_target="tpu_custom_call" | custom-call | tf_op jit(solution)/shard_map/pallas_call | solution.py:395
  274.0 10.2 copy.489
  284.2 8.5 dot_general.115
  327.1 12.2 collective-permute-done.1
  349.2 6.8 all-to-all-start.5
  356.0 7.1 convolution_convert_fusion.2
  382.9 7.9 all-to-all-start.2
  390.8 44.3 %all-gather.3 = bf16[16,528,50]{1,2,0:T(8,128)(2,1)} all-gather(bf16[1,528,50]{1,2,0:T(8,128)(2,1)S(1)} %slice_bitcast_fusion.5), channel_id=2, replica_groups=mesh['row'=2,'seq'=16] {'seq'}, dimensions={0}, use_global_device_ids=true | all-gather | bytes 897600 | tf_op jit(solution)/shard_map/jvp()/all_gather | solution.py:193
  449.9 30.7 %shard_map.121 = bf16[144,2048]{1,0:T(8,128)(2,1)S(1)} custom-call(f32[144,2048]{1,0:T(8,128)S(1)} %fusion.62.x_ref), custom_call_target="tpu_custom_call" | custom-call | tf_op jit(solution)/shard_map/pallas_call | solution.py:559
  494.0 60.9 %shard_map.122 = (f32[2048,256]{1,0:T(8,128)}, f32[16,16,256]{2,1,0:T(8,128)}) custom-call(f32[2048]{0:T(1024)} %get-tuple-element.133.keep_ref, f32[2048,256]{1,0:T(8,128)} %pad.182.conv_ref, f32[2048,256]{1,0:T(8,128)} %pad.184.delta_ref, f32[256,16,8]{2,1,0:T(8,128)} %bitcast.255, f32[256,16,8]{2,1,0:T(8,128)} %bitcast.257, f32[16,256]{1,0:T(8,128)} %pad.185.a_ref), custom_call_target="tpu_custom_call" | custom-call | tf_op jit(solution)/shard_map/pallas_call | solution.py:879
  599.2 23.2 %shard_map.120 = (f32[2048,128]{1,0:T(8,128)S(1)}, f32[16,2,128]{2,1,0:T(2,128)S(1)}) custom-call(s32[16,1,128]{2,1,0:T(1,128)S(1)} %broadcast_maximum_fusion.refs_0_, bf16[2048,128]{1,0:T(8,128)(2,1)S(1)} %convolution_convert_fusion.7.refs_1_, bf16[3072,256]{1,0:T(8,128)(2,1)S(1)} %pad.180.clone.refs_2_, bf16[256,3072]{1,0:T(8,128)(2,1)S(1)} %pad_bitcast_fusion.refs_3_, ...), custom_call_target="tpu_custom_call" | custom-call | tf_op jit(solution)/shard_map/pallas_call | solution.py:792
  623.4 11.7 shard_map.123
  644.2 9.8 copy.452
  654.1 39.5 %shard_map.124 = f32[128,1600]{1,0:T(8,128)} custom-call(bf16[16,128,1600]{2,1,0:T(8,128)(2,1)} %bitcast.267), custom_call_target="tpu_custom_call" | custom-call | tf_op jit(solution)/shard_map/pallas_call | solution.py:485
  696.7 39.1 %shard_map.125 = bf16[16,128,1600]{2,1,0:T(8,128)(2,1)} custom-call(bf16[128,1600]{1,0:T(8,128)(2,1)} %multiply_convert_fusion.2.x_ref), custom_call_target="tpu_custom_call" | custom-call | tf_op jit(solution)/shard_map/pallas_call | solution.py:395
  735.9 7.5 fusion.87
  760.0 8.0 add_convert_fusion.1
  768.0 10.0 copy.460
  778.0 40.1 %shard_map.126 = f32[128,1600]{1,0:T(8,128)} custom-call(bf16[16,128,1600]{2,1,0:T(8,128)(2,1)} %bitcast.268), custom_call_target="tpu_custom_call" | custom-call | tf_op jit(solution)/shard_map/pallas_call | solution.py:485
  821.3 39.2 %shard_map.127 = bf16[16,128,1600]{2,1,0:T(8,128)(2,1)} custom-call(bf16[128,1600]{1,0:T(8,128)(2,1)} %fusion.86.x_ref), custom_call_target="tpu_custom_call" | custom-call | tf_op jit(solution)/shard_map/pallas_call | solution.py:395
  860.5 7.7 convolution_convert_fusion.6
  897.8 9.8 reshape.601
  918.1 34.2 %shard_map.128 = f32[32,128]{1,0:T(8,128)} custom-call(f32[32,128]{1,0:T(8,128)} %reshape.588.x_ref), custom_call_target="tpu_custom_call" | custom-call | tf_op jit(solution)/shard_map/pallas_call | solution.py:603
  953.0 6.8 multiply_reduce_fusion
  962.8 95.8 %shard_map.129 = (f32[2048,256]{1,0:T(8,128)S(1)}, f32[2048,256]{1,0:T(8,128)S(1)}, f32[256,8,128]{2,1,0:T(8,128)S(1)}, f32[256,8,128]{2,1,0:T(8,128)S(1)}, f32[16,256]{1,0:T(8,128)S(1)}) custom-call(f32[2048]{0:T(1024)S(1)} %copy-done.13, f32[2048,256]{1,0:T(8,128)S(1)} %copy-done, f32[2048,256]{1,0:T(8,128)S(1)} %copy-done.1, f32[256,16,8]{2,1,0:T(8,128)S(1)} %bitcast.256, ...), custom_call_target="tpu_custom_call" | custom-call | tf_op jit(solution)/shard_map/pallas_call | solution.py:982
  1071.0 27.0 %shard_map.130 = bf16[144,2048]{1,0:T(8,128)(2,1)S(1)} custom-call(f32[144,2048]{1,0:T(8,128)S(1)} %select_maximum_fusion.x_ref), custom_call_target="tpu_custom_call" | custom-call | tf_op jit(solution)/shard_map/pallas_call | solution.py:559
  1100.3 25.8 %shard_map.131 = (bf16[2048,128]{1,0:T(8,128)(2,1)S(1)}, f32[3072,256]{1,0:T(8,128)}, f32[128,256]{1,0:T(8,128)S(1)}) custom-call(s32[16,1,128]{2,1,0:T(1,128)S(1)} %broadcast_maximum_fusion.refs_0_, bf16[2048,128]{1,0:T(8,128)(2,1)S(1)} %convolution_convert_fusion.7.refs_1_, bf16[3072,256]{1,0:T(8,128)(2,1)S(1)} %pad.180.clone.refs_2_, ...), custom_call_target="tpu_custom_call" | custom-call | tf_op jit(solution)/shard_map/pallas_call | solution.py:813
  1140.5 6.3 fusion.14
  1173.1 9.6 copy.459
  1190.7 6.8 fusion.28
  1207.5 7.6 fusion.59
  1215.2 7.0 convolution_convert_fusion.5
  1240.3 8.1 all-to-all-start.8
  1254.5 20.4 %all-to-all-done.8 = bf16[16,280,50]{1,2,0:T(8,128)(2,1)} async-done(((bf16[16,280,50]{1,2,0:T(8,128)(2,1)}), bf16[16,280,50]{1,2,0:T(8,128)(2,1)}, u32[]{:S(2)}, u32[]{:S(2)}) %all-to-all-start.8) | async-done | bytes 448032 | tf_op jit(solution)/shard_map/transpose(jvp())/all_to_all | solution.py:137
  1291.0 13.4 add_convert_fusion
  1316.5 12.7 all-to-all-start.11
  1337.6 28.7 %all-to-all-done.11 = bf16[16,150,344]{2,1,0:T(8,128)(2,1)} async-done(((bf16[16,150,344]{2,1,0:T(8,128)(2,1)}), bf16[16,150,344]{2,1,0:T(8,128)(2,1)}, u32[]{:S(2)}, u32[]{:S(2)}) %all-to-all-start.11) | async-done | bytes 1651232 | tf_op jit(solution)/shard_map/transpose(jvp())/all_to_all | solution.py:137
  1366.4 10.5 all-to-all-start.9
  1377.1 9.6 copy.468
  1386.7 62.3 %shard_map.132 = f32[128,1600]{1,0:T(8,128)} custom-call(bf16[16,128,1600]{2,1,0:T(8,128)(2,1)} %bitcast.269), custom_call_target="tpu_custom_call" | custom-call | tf_op jit(solution)/shard_map/pallas_call | solution.py:485
  1455.0 17.4 %shard_map.133 = f32[80,128]{1,0:T(8,128)S(1)} custom-call(bf16[32,80,128]{2,1,0:T(8,128)(2,1)S(1)} %pad_maximum_fusion.15.x_ref), custom_call_target="tpu_custom_call" | custom-call | tf_op jit(solution)/shard_map/pallas_call | solution.py:673
  1487.8 7.5 copy.499
  1495.3 9.4 reshape.623
  (599 shorter events, 431.6 us)
Async XLA Ops:
  25.1 132.1 %all-to-all-start = ((bf16[16,869,50]{1,2,0:T(8,128)(2,1)}), bf16[16,869,50]{1,2,0:T(8,128)(2,1)}, u32[]{:S(2)}, u32[]{:S(2)}) async-start(bf16[16,869,50]{1,2,0:T(8,128)(2,1)} %copy.425), calls=%async_computation | async-start | bytes 3211264 | tf_op jit(solution)/shard_map/jvp()/all_to_all | solution.py:137
  32.7 61.3 %copy-start.72 = (bf16[1,128,1600]{1,2,0:T(8,128)(2,1)S(1)}, bf16[1,128,1600]{1,2,0:T(8,128)(2,1)}, u32[]{:S(2)}) copy-start(bf16[1,128,1600]{1,2,0:T(8,128)(2,1)} %param.7) | copy-start | bytes 1228804
  32.7 61.6 %copy-start.90 = (bf16[4,1600]{1,0:T(4,128)(2,1)S(1)}, bf16[4,1600]{1,0:T(4,128)(2,1)}, u32[]{:S(2)}) copy-start(bf16[4,1600]{1,0:T(4,128)(2,1)} %param.9) | copy-start | bytes 38404
  32.7 710.6 %all-gather.6.cloned.1.call-start = ((), (), s32[]{:S(2)}) async-start(), calls=%async_computation.15 | async-start | bytes 6963200 | tf_op jit(solution)/shard_map/all_gather | solution.py:299
  94.3 74.4 %copy-start.27 = (bf16[1,128,1600]{2,1,0:T(8,128)(2,1)}, bf16[1,128,1600]{2,1,0:T(8,128)(2,1)S(1)}, u32[]{:S(2)}) copy-start(bf16[1,128,1600]{2,1,0:T(8,128)(2,1)S(1)} %copy.424) | copy-start | bytes 1228804
  140.7 28.0 %copy-start.30 = (f32[128,1600]{1,0:T(8,128)}, f32[128,1600]{1,0:T(8,128)S(1)}, u32[]{:S(2)}) copy-start(f32[128,1600]{1,0:T(8,128)S(1)} %reshape.634) | copy-start | bytes 2457604
  146.1 22.6 %copy-start.75 = (f32[1600]{0:T(1024)}, f32[1600]{0:T(1024)S(1)}, u32[]{:S(2)}) copy-start(f32[1600]{0:T(1024)S(1)} %get-tuple-element.87) | copy-start | bytes 19204
  146.1 674.1 %copy-start.79 = (f32[1600]{0:T(1024)}, f32[1600]{0:T(1024)S(1)}, u32[]{:S(2)}) copy-start(f32[1600]{0:T(1024)S(1)} %get-tuple-element.85) | copy-start | bytes 19204
  157.3 56.1 %all-to-all-start.4 = ((bf16[16,150,344]{2,1,0:T(8,128)(2,1)}), bf16[16,150,344]{2,1,0:T(8,128)(2,1)}, u32[]{:S(2)}, u32[]{:S(2)}) async-start(bf16[16,150,344]{2,1,0:T(8,128)(2,1)} %copy.453), calls=%async_computation.4 | async-start | bytes 3735552 | tf_op jit(solution)/shard_map/jvp()/all_to_all | solution.py:137
  166.8 36.7 %copy-start.49 = (bf16[13904,50]{0,1:T(8,128)(2,1)S(1)}, bf16[13904,50]{0,1:T(8,128)(2,1)}, u32[]{:S(2)}) copy-start(bf16[13904,50]{0,1:T(8,128)(2,1)} %reshape.558) | copy-start | bytes 4171204
  166.8 36.7 %collective-permute-start = (bf16[13904,50]{0,1:T(8,128)(2,1)}, bf16[13904,50]{0,1:T(8,128)(2,1)S(1)}, u32[]{:S(2)}, u32[]{:S(2)}) collective-permute-start(bf16[13904,50]{0,1:T(8,128)(2,1)} %reshape.558), channel_id=1, source_target_pairs={{0,16},{16,0},{1,17},{17,1},{2,18},{18,2},{3,19},{19,3},{4,20},{20... | collective-permute-start | bytes 4171208 | tf_op jit(solution)/shard_map/jvp()/ppermute | solution.py:143
  203.7 115.5 %copy-start.38 = (bf16[13904,50]{0,1:T(8,128)(2,1)}, bf16[13904,50]{0,1:T(8,128)(2,1)S(1)}, u32[]{:S(2)}) copy-start(bf16[13904,50]{0,1:T(8,128)(2,1)S(1)} %get-tuple-element.107) | copy-start | bytes 4171204
  213.4 101.2 %all-to-all-start.1 = ((bf16[16,280,50]{1,2,0:T(8,128)(2,1)}), bf16[16,280,50]{1,2,0:T(8,128)(2,1)}, u32[]{:S(2)}, u32[]{:S(2)}) async-start(bf16[16,280,50]{1,2,0:T(8,128)(2,1)} %pad_maximum_fusion.14), calls=%async_computation.1 | async-start | bytes 1376256 | tf_op jit(solution)/shard_map/jvp()/all_to_all | solution.py:137
  221.5 51.9 %copy-start.92 = (f32[16,200]{1,0:T(8,128)S(1)}, f32[16,200]{1,0:T(8,128)}, u32[]{:S(2)}) copy-start(f32[16,200]{1,0:T(8,128)} %negate_bitcast_fusion) | copy-start | bytes 38404
  300.3 39.1 %collective-permute-start.1 = (bf16[2400,344]{0,1:T(8,128)(2,1)}, bf16[2400,344]{0,1:T(8,128)(2,1)}, u32[]{:S(2)}, u32[]{:S(2)}) collective-permute-start(bf16[2400,344]{0,1:T(8,128)(2,1)} %copy.455), channel_id=1, source_target_pairs={{0,16},{16,0},{1,17},{17,1},{2,18},{18,2},{3,19},{19,3},{4,20},{20... | collective-permute-start | bytes 4953608 | tf_op jit(solution)/shard_map/jvp()/ppermute | solution.py:143
  314.6 34.6 %all-to-all-start.3 = ((bf16[16,656,50]{1,2,0:T(8,128)(2,1)}), bf16[16,656,50]{1,2,0:T(8,128)(2,1)}, u32[]{:S(2)}, u32[]{:S(2)}) async-start(bf16[16,656,50]{1,2,0:T(8,128)(2,1)} %copy.449), calls=%async_computation.3 | async-start | bytes 2752512 | tf_op jit(solution)/shard_map/jvp()/all_to_all | solution.py:137
  349.2 33.7 %all-to-all-start.5 = ((bf16[16,100,344]{2,1,0:T(8,128)(2,1)}), bf16[16,100,344]{2,1,0:T(8,128)(2,1)}, u32[]{:S(2)}, u32[]{:S(2)}) async-start(bf16[16,100,344]{2,1,0:T(8,128)(2,1)} %copy.512), calls=%async_computation.5 | async-start | bytes 2555904 | tf_op jit(solution)/shard_map/jvp()/all_to_all | solution.py:137
  368.3 186.6 %copy-start.22 = (bf16[2048,200]{1,0:T(8,128)(2,1)}, bf16[2048,200]{1,0:T(8,128)(2,1)S(1)}, u32[]{:S(2)}) copy-start(bf16[2048,200]{1,0:T(8,128)(2,1)S(1)} %get-tuple-element.98) | copy-start | bytes 2457604
  382.9 199.7 %all-to-all-start.2 = ((bf16[16,100,384]{2,1,0:T(8,128)(2,1)}), bf16[16,100,384]{2,1,0:T(8,128)(2,1)S(1)}, u32[]{:S(2)}, u32[]{:S(2)}) async-start(bf16[16,100,384]{2,1,0:T(8,128)(2,1)} %copy.433), calls=%async_computation.2 | async-start | bytes 2555904 | tf_op jit(solution)/shard_map/jvp()/all_to_all | solution.py:137
  449.4 31.5 %copy-start.119 = (f32[200,1]{0,1:T(1,128)S(1)}, f32[200,1]{0,1:T(1,128)}, u32[]{:S(2)}) copy-start(f32[200,1]{0,1:T(1,128)} %get-tuple-element.125) | copy-start | bytes 2404
  494.0 61.0 %copy-start.103 = (f32[200,1]{0,1:T(1,128)S(1)}, f32[200,1]{0,1:T(1,128)}, u32[]{:S(2)}) copy-start(f32[200,1]{0,1:T(1,128)} %get-tuple-element.124) | copy-start | bytes 2404
  599.2 36.8 %copy-start.110 = (f32[128]{0:T(128)S(1)}, f32[128]{0:T(128)}, u32[]{:S(2)}) copy-start(f32[128]{0:T(128)} %fusion.73) | copy-start | bytes 1540
  654.1 39.5 %copy-start.28 = (bf16[1,128,1600]{2,1,0:T(8,128)(2,1)S(1)}, bf16[1,128,1600]{2,1,0:T(8,128)(2,1)}, u32[]{:S(2)}) copy-start(bf16[1,128,1600]{2,1,0:T(8,128)(2,1)} %copy-done.27) | copy-start | bytes 1228804
  694.9 125.3 %copy-start.104 = (f32[128]{0:T(128)}, f32[128]{0:T(128)S(1)}, u32[]{:S(2)}) copy-start(f32[128]{0:T(128)S(1)} %fusion.75) | copy-start | bytes 1540
  696.7 39.1 %copy-start.87 = (f32[32,128]{1,0:T(8,128)S(1)}, f32[32,128]{1,0:T(8,128)}, u32[]{:S(2)}) copy-start(f32[32,128]{1,0:T(8,128)} %shard_map.123) | copy-start | bytes 49156
  778.0 40.2 %copy-start.25 = (f32[128,1600]{1,0:T(8,128)S(1)}, f32[128,1600]{1,0:T(8,128)}, u32[]{:S(2)}) copy-start(f32[128,1600]{1,0:T(8,128)} %copy-done.24) | copy-start | bytes 2457604
  778.0 42.2 %copy-start.52 = (bf16[1,128,1600]{2,1,0:T(8,128)(2,1)S(1)}, bf16[1,128,1600]{2,1,0:T(8,128)(2,1)}, u32[]{:S(2)}) copy-start(bf16[1,128,1600]{2,1,0:T(8,128)(2,1)} %copy.461) | copy-start | bytes 1228804
  820.2 40.2 %copy-start.121 = (f32[128]{0:T(128)}, f32[128]{0:T(128)S(1)}, u32[]{:S(2)}) copy-start(f32[128]{0:T(128)S(1)} %multiply_multiply_fusion.10) | copy-start | bytes 1540
  913.0 242.7 %all-to-all-start.6 = ((bf16[16,656,50]{1,2,0:T(8,128)(2,1)}), bf16[16,656,50]{1,2,0:T(8,128)(2,1)}, u32[]{:S(2)}, u32[]{:S(2)}) async-start(bf16[16,656,50]{1,2,0:T(8,128)(2,1)} %copy.479), calls=%async_computation.7 | async-start | bytes 2752512 | tf_op jit(solution)/shard_map/transpose(jvp())/all_to_all | solution.py:137
  917.4 364.9 %reduce-scatter.7.cloned.1.call-start = ((), (), s32[]{:S(2)}) async-start(), calls=%async_computation.16 | async-start | bytes 1218560
  962.8 95.9 %copy-start.43 = (f32[2048,200]{1,0:T(8,128)S(1)}, f32[2048,200]{1,0:T(8,128)}, u32[]{:S(2)}) copy-start(f32[2048,200]{1,0:T(8,128)} %get-tuple-element.147) | copy-start | bytes 4915204
  1098.1 30.7 %copy-start.9 = (bf16[144,2048]{1,0:T(8,128)(2,1)}, bf16[144,2048]{1,0:T(8,128)(2,1)S(1)}, u32[]{:S(2)}) copy-start(bf16[144,2048]{1,0:T(8,128)(2,1)S(1)} %shard_map.130) | copy-start | bytes 1769476
  1155.7 45.6 %all-to-all-start.10 = ((bf16[16,100,344]{2,1,0:T(8,128)(2,1)}), bf16[16,100,344]{2,1,0:T(8,128)(2,1)}, u32[]{:S(2)}, u32[]{:S(2)}) async-start(bf16[16,100,344]{2,1,0:T(8,128)(2,1)} %bitcast.249), calls=%async_computation.11 | async-start | bytes 2555904 | tf_op jit(solution)/shard_map/transpose(jvp())/all_to_all | solution.py:137
  1160.3 344.5 %reduce-scatter.5.cloned.1.call-start = ((), (), s32[]{:S(2)}) async-start(), calls=%async_computation.14 | async-start | bytes 7241728 | tf_op jit(solution)/shard_map/reduce_scatter | solution.py:303
  1201.4 33.2 %all-to-all-start.7 = ((bf16[16,100,384]{2,1,0:T(8,128)(2,1)}), bf16[16,100,384]{2,1,0:T(8,128)(2,1)S(1)}, u32[]{:S(2)}, u32[]{:S(2)}) async-start(bf16[16,100,384]{2,1,0:T(8,128)(2,1)} %pad_maximum_fusion.11), calls=%async_computation.8 | async-start | bytes 2555904 | tf_op jit(solution)/shard_map/transpose(jvp())/all_to_all | solution.py:137
  1240.3 34.7 %all-to-all-start.8 = ((bf16[16,280,50]{1,2,0:T(8,128)(2,1)}), bf16[16,280,50]{1,2,0:T(8,128)(2,1)}, u32[]{:S(2)}, u32[]{:S(2)}) async-start(bf16[16,280,50]{1,2,0:T(8,128)(2,1)} %bitcast.86), calls=%async_computation.9 | async-start | bytes 1376256 | tf_op jit(solution)/shard_map/transpose(jvp())/all_to_all | solution.py:137
  1252.8 55.4 %collective-permute-start.3 = (bf16[2400,344]{0,1:T(8,128)(2,1)}, bf16[2400,344]{0,1:T(8,128)(2,1)}, u32[]{:S(2)}, u32[]{:S(2)}) collective-permute-start(bf16[2400,344]{0,1:T(8,128)(2,1)} %select_add_fusion), channel_id=1, source_target_pairs={{16,0},{0,16},{17,1},{1,17},{18,2},{2,18},{19,3},{3,19},{20,4},{4,... | collective-permute-start | bytes 4953608 | tf_op jit(solution)/shard_map/transpose(jvp())/ppermute | solution.py:143
  1289.8 39.4 %collective-permute-start.2 = (bf16[13904,50]{0,1:T(8,128)(2,1)}, bf16[13904,50]{0,1:T(8,128)(2,1)}, u32[]{:S(2)}, u32[]{:S(2)}) collective-permute-start(bf16[13904,50]{0,1:T(8,128)(2,1)} %select_add_fusion.1), channel_id=1, source_target_pairs={{16,0},{0,16},{17,1},{1,17},{18,2},{2,18},{19,3},{3,19},{20,4},{4,... | collective-permute-start | bytes 4171208 | tf_op jit(solution)/shard_map/transpose(jvp())/ppermute | solution.py:143
  1316.5 49.8 %all-to-all-start.11 = ((bf16[16,150,344]{2,1,0:T(8,128)(2,1)}), bf16[16,150,344]{2,1,0:T(8,128)(2,1)}, u32[]{:S(2)}, u32[]{:S(2)}) async-start(bf16[16,150,344]{2,1,0:T(8,128)(2,1)} %reshape.620), calls=%async_computation.12 | async-start | bytes 3735552 | tf_op jit(solution)/shard_map/transpose(jvp())/all_to_all | solution.py:137
  1337.6 39.3 %copy-start.31 = (f32[128,1600]{1,0:T(8,128)S(1)}, f32[128,1600]{1,0:T(8,128)}, u32[]{:S(2)}) copy-start(f32[128,1600]{1,0:T(8,128)} %copy-done.30) | copy-start | bytes 2457604
  1337.6 39.3 %copy-start.54 = (f32[128,1600]{1,0:T(8,128)S(1)}, f32[128,1600]{1,0:T(8,128)}, u32[]{:S(2)}) copy-start(f32[128,1600]{1,0:T(8,128)} %copy.469) | copy-start | bytes 2457604
  1337.6 39.3 %copy-start.124 = (f32[128]{0:T(128)S(1)}, f32[128]{0:T(128)}, u32[]{:S(2)}) copy-start(f32[128]{0:T(128)} %copy-done.123) | copy-start | bytes 1540
  1366.4 118.1 %all-to-all-start.9 = ((bf16[16,869,50]{1,2,0:T(8,128)(2,1)}), bf16[16,869,50]{1,2,0:T(8,128)(2,1)}, u32[]{:S(2)}, u32[]{:S(2)}) async-start(bf16[16,869,50]{1,2,0:T(8,128)(2,1)} %copy.498), calls=%async_computation.10 | async-start | bytes 3211264 | tf_op jit(solution)/shard_map/transpose(jvp())/all_to_all | solution.py:137
  1386.7 62.3 %copy-start.29 = (bf16[1,128,1600]{2,1,0:T(8,128)(2,1)S(1)}, bf16[1,128,1600]{2,1,0:T(8,128)(2,1)}, u32[]{:S(2)}) copy-start(bf16[1,128,1600]{2,1,0:T(8,128)(2,1)} %copy-done.27) | copy-start | bytes 1228804
  1386.7 62.3 %copy-start.76 = (f32[1600]{0:T(1024)S(1)}, f32[1600]{0:T(1024)}, u32[]{:S(2)}) copy-start(f32[1600]{0:T(1024)} %copy-done.75) | copy-start | bytes 19204
  1386.7 62.3 %copy-start.109 = (f32[128]{0:T(128)S(1)}, f32[128]{0:T(128)}, u32[]{:S(2)}) copy-start(f32[128]{0:T(128)} %copy-done.108) | copy-start | bytes 1540
  1386.7 64.2 %copy-start.83 = (f32[200,24]{0,1:T(8,128)S(1)}, f32[200,24]{0,1:T(8,128)}, u32[]{:S(2)}) copy-start(f32[200,24]{0,1:T(8,128)} %copy-done.81) | copy-start | bytes 57604
  1454.5 18.2 %copy-start.126 = (f32[128]{0:T(128)S(1)}, f32[128]{0:T(128)}, u32[]{:S(2)}) copy-start(f32[128]{0:T(128)} %copy-done.125) | copy-start | bytes 1540
  (109 other events, 584.6 us)
Sparse Core Ops, SparseCore 0:
  35.7 88.7 all-gather.5
  1140.5 66.7 reduce-scatter.6
  1211.2 97.9 reduce-scatter.4

commit v2 on v1

--- a/solution.py
+++ b/solution.py
@@ -156,6 +156,7 @@
         and all(size % width == 0 for size in sizes)
         and D % shards == 0
         and (HEADS * HEAD * 2) % shards == 0
+        and shards % x_turns(shards)[0] == 0
     )
 
 
@@ -172,37 +173,47 @@
         w_in.reshape(D, -1),
         own_channels(w_x, 0, shards, place),
         own_channels(w_dt, 1, shards, place),
-        out_heads,
-        own_channels(w_out[HEADS * HEAD :], 0, shards, place),
-    )
-
-
-def mixer_shards(piece):
+        jnp.concatenate([out_heads, own_channels(w_out[HEADS * HEAD :], 0, shards, place)], axis=0),
+    )
+
+
+def mixer_columns(piece):
+    shards = lax.axis_size("seq")
+    if not mixer_fits(piece.shape[0], shards):
+        return piece
+    unit = INNER // (RUNS * shards)
+    return exchange(piece.reshape(-1, shards, unit).transpose(1, 0, 2)).reshape(-1, unit)
+
+
+def mixer_shards(mine, length):
     shards, place = lax.axis_size("seq"), lax.axis_index("seq")
-    if not mixer_fits(piece.shape[0], shards):
-        return mixer_shards_whole(piece)
+    if not mixer_fits(length, shards):
+        return mixer_shards_whole(mine)
     width = INNER // RUNS
     unit = width // shards
-    mine = exchange(piece.reshape(-1, shards, unit).transpose(1, 0, 2))
-    mine = both_halves(mine.reshape(-1, unit))
+    mine = both_halves(mine)
     part_q, part_kv, part_in, part_x, part_dt, part_out = cut_rows(
         mine, [math.prod(shape) // width for shape in mixer_layout()]
     )
     w_in = part_in.reshape(D, -1)
     w_dt = part_dt.reshape(DT_RANK, -1)
-    w_x = lax.all_gather(part_x, "seq").transpose(1, 0, 2).reshape(INNER, -1)
-    w_x = own_channels(w_x, 0, shards, place)
     rows = D // shards
     by_rows = exchange(
         jnp.concatenate(
-            [part_q.reshape(shards, -1, unit), part_kv.reshape(shards, -1, unit)], axis=1
+            [
+                part_q.reshape(shards, -1, unit),
+                part_kv.reshape(shards, -1, unit),
+                x_windows(part_x, shards),
+            ],
+            axis=1,
         )
     )
     by_rows = by_rows.transpose(1, 0, 2).reshape(-1, width)
-    split = part_q.shape[0] // shards
+    split, end = part_q.shape[0] // shards, (part_q.shape[0] + part_kv.shape[0]) // shards
+    w_x = x_from_windows(by_rows[end:], place)
     cut = by_head(
         by_rows[:split].reshape(rows, HEADS * HEAD),
-        by_rows[split:].reshape(rows, 2 * GROUPS * HEAD),
+        by_rows[split:end].reshape(rows, 2 * GROUPS * HEAD),
         shards,
     )
     qkv = exchange(cut.transpose(1, 0, 2)).reshape(D, -1)
@@ -216,7 +227,34 @@
     out_inner = out_inner.transpose(1, 0, 2, 3).reshape(shards, -1, unit)
     out_both = exchange(jnp.concatenate([out_heads, out_inner], axis=1))
     out_both = out_both.transpose(1, 0, 2).reshape(-1, D)
-    return qkv, w_in, w_x, w_dt, out_both[:head_rows], out_both[head_rows:]
+    return qkv, w_in, w_x, w_dt, out_both
+
+
+def x_turns(shards):
+    width = INNER // RUNS
+    run = (width // shards) * (DT_RANK + 2 * STATE)
+    common = math.gcd(run, width)
+    return width // common, run // common
+
+
+def x_windows(part_x, shards):
+    runs, rows = x_turns(shards)
+    need = -(-rows // runs)
+    turns = part_x.reshape(-1, rows, part_x.shape[1])
+    cuts = [turns[:, (i * rows) // runs : (i * rows) // runs + need] for i in range(runs)]
+    cuts = jnp.stack(cuts, axis=1).reshape(RUNS, shards, need, part_x.shape[1])
+    return cuts.transpose(1, 0, 2, 3).reshape(shards, RUNS * need, part_x.shape[1])
+
+
+def x_from_windows(view_rows, place):
+    width = view_rows.shape[1]
+    shards = lax.axis_size("seq")
+    runs, rows = x_turns(shards)
+    columns = DT_RANK + 2 * STATE
+    count = (width // shards) * columns
+    flat = view_rows.reshape(RUNS, -1)
+    offset = (place % runs) * rows * (width // runs) % width
+    return lax.dynamic_slice_in_dim(flat, offset, count, 1).reshape(-1, columns)
 
 
 def cut_rows(array, counts):
@@ -261,19 +299,25 @@
     return -(-count // 128)
 
 
-def start_blocks(small_params, doc_ids):
+def start_blocks(small_params, doc_ids, meta_tokens):
     devices = lax.axis_size("row") * lax.axis_size("seq")
-    small_rows, id_rows = tiles_of(small_params.shape[0]), tiles_of(doc_ids.shape[0])
-    rows = -(-(small_rows + id_rows) // 16) * 16
-    small = jnp.pad(small_params, (0, small_rows * 128 - small_params.shape[0]))
-    ids = jnp.pad(doc_ids.astype(SIXTEEN), (0, (rows - small_rows) * 128 - doc_ids.shape[0]))
-    block = jnp.concatenate([small.reshape(-1, 128), ids.reshape(-1, 128)], axis=0)
+    parts = [small_params, doc_ids.astype(SIXTEEN), meta_tokens.reshape(-1)]
+    rows = [tiles_of(part.shape[0]) for part in parts]
+    rows_all = -(-sum(rows) // 16) * 16
+    tiles = [
+        jnp.pad(part, (0, count * 128 - part.shape[0])).reshape(-1, 128)
+        for part, count in zip(parts, rows)
+    ]
+    block = jnp.concatenate(tiles + [jnp.zeros((rows_all - sum(rows), 128), SIXTEEN)], axis=0)
     every = push_gather(block, 0)
-    small = every[:, :small_rows].reshape(devices, -1)[:, : small_params.shape[0]].reshape(-1)
-    ids = every[:, small_rows:].reshape(devices, -1)[:, : doc_ids.shape[0]]
-    ids = ids.reshape(lax.axis_size("row"), -1)
+    outs, begin = [], 0
+    for part, count in zip(parts, rows):
+        cut = every[:, begin : begin + count].reshape(devices, -1)[:, : part.shape[0]]
+        outs.append(cut)
+        begin += count
+    ids = outs[1].reshape(lax.axis_size("row"), -1)
     ids = lax.dynamic_index_in_dim(ids, lax.axis_index("row"), 0, keepdims=False)
-    return small.astype(WIDE), ids.astype(jnp.int32)
+    return outs[0].reshape(-1).astype(WIDE), ids.astype(jnp.int32), outs[2].reshape(-1, D)
 
 
 def end_blocks(grad_small, d_meta):
@@ -399,17 +443,21 @@
         out_specs=ANY,
         scratch_shapes=[ring, ring, pair, pair, pltpu.SemaphoreType.DMA],
         compiler_params=pltpu.CompilerParams(collective_id=collective_id, has_side_effects=True),
+        cost_estimate=pl.CostEstimate(flops=0, bytes_accessed=120 * MIB, transcendentals=0),
     )(block)
     return gathered.reshape(shards * rows, width)
 
 
-def seq_scatter_kernel(
-    shards, parts, x_ref, out_ref, mine, pair, arrived, ring_send, ring_recv, pair_send, pair_recv, own_sem
-):
+def product_scatter_kernel(shards, parts, turned, *refs):
+    terms = len(turned)
+    lefts, rights = refs[:terms], refs[terms : 2 * terms]
+    out_ref, mine, given, pair, arrived = refs[2 * terms : 2 * terms + 5]
+    ring_send, ring_recv, pair_send, pair_recv = refs[2 * terms + 5 :]
     row, me = lax.axis_index("row"), lax.axis_index("seq")
     chips = shards // 2
     core = me % 2
     place = ring_place(me // 2, chips)
+    block_rows = out_ref.shape[0]
 
     def device(spot, core):
         return ring_chip(spot, chips) * 2 + core
@@ -418,42 +466,55 @@
     left = (row, device(place - 1, core))
     twin = (row, me + 1 - 2 * core)
     greet([right, left, twin])
-    rows = x_ref.shape[1] // (2 * parts)
+    rows = block_rows // (2 * parts)
 
     def cut(way, part):
         return pl.ds((way * parts + part) * rows, rows)
 
-    order = []
-    for far in range(1, chips // 2 + 1):
-        order += [-far, far] if 2 * far < chips else [far]
-    order.append(0)
-    waits = {}
-    started = []
-    for spot in order:
-        slot = spot % chips
-        load = pltpu.make_async_copy(x_ref.at[device(place + spot, core)], mine.at[slot], own_sem.at[slot])
-        load.start()
-        copy = pltpu.make_async_remote_copy(
-            src_ref=x_ref.at[device(place + spot, 1 - core)],
-            dst_ref=pair.at[slot], send_sem=pair_send.at[slot], recv_sem=pair_recv.at[slot],
-            device_id=twin, device_id_type=MESH,
-        )
-        copy.start()
-        started.append(copy)
-        waits[slot] = (load, copy)
-
-    def ready(slot):
-        if slot in waits:
-            load, copy = waits.pop(slot)
-            load.wait()
-            copy.wait_recv()
-
-    flights = {}
+    def product(index):
+        here = pl.ds(pl.multiple_of(index * block_rows, block_rows), block_rows)
+        total = None
+        for left_ref, right_ref, turn in zip(lefts, rights, turned):
+            part = lax.dot_general(
+                left_ref[here, :], right_ref[...], (((1,), (1 if turn else 0,)), ((), ())),
+                preferred_element_type=WIDE,
+            )
+            total = part if total is None else total + part
+        return total.astype(SIXTEEN)
+
+    def pass_over(slot):
+        return pltpu.make_async_remote_copy(
+            src_ref=given.at[slot], dst_ref=pair.at[slot], send_sem=pair_send.at[slot],
+            recv_sem=pair_recv.at[slot], device_id=twin, device_id_type=MESH,
+        )
+
+    def make(far):
+        slot = far % chips
+        given[slot] = product(device(place + far, 1 - core))
+        pass_over(slot).start()
+        mine[slot] = product(device(place + far, core))
+
+    def both(step, carry):
+        make(-step)
+        make(step)
+        return carry
+
+    half = chips // 2
+    both(1, 0)
+    started, flights = [], {}
+    fresh = set(range(chips))
     for step in range(chips):
+        if step + 2 < half:
+            both(step + 2, 0)
+        elif step + 2 == half:
+            make(half)
+            make(0)
         for part in range(parts):
             for way in range(2):
                 slot = (-1 - step if way == 0 else 1 + step) % chips
-                ready(slot)
+                if slot in fresh:
+                    fresh.remove(slot)
+                    pass_over(slot).wait_recv()
                 here = cut(way, part)
                 total = mine[slot, here, :].astype(WIDE) + pair[slot, here, :].astype(WIDE)
                 if step:
@@ -462,7 +523,7 @@
                 if step == chips - 1:
                     out_ref[here, :] = total
                     continue
-                mine[slot, here, :] = total.astype(mine.dtype)
+                mine[slot, here, :] = total.astype(SIXTEEN)
                 copy = pltpu.make_async_remote_copy(
                     src_ref=mine.at[slot, here], dst_ref=arrived.at[way, step, pl.ds(part * rows, rows)],
                     send_sem=ring_send.at[way, part, step], recv_sem=ring_recv.at[way, part, step],
@@ -471,32 +532,51 @@
                 copy.start()
                 started.append(copy)
                 flights[way, part] = copy
+    for slot in range(chips):
+        pass_over(slot).wait_send()
     for copy in started:
         copy.wait_send()
 
 
-def ring_seq_scatter(whole, collective_id, parts=2):
+def padded_bytes(shape, bytes_each):
+    return -(-shape[0] // 16) * 16 * -(-shape[1] // 128) * 128 * bytes_each
+
+
+def product_scatter(terms, collective_id, parts=2):
     shards = lax.axis_size("seq")
     chips = shards // 2
-    length, width = whole.shape
+    length = terms[0][0].shape[0]
+    width = terms[0][1].shape[0 if terms[0][2] else 1]
     rows = length // shards
+    buffers = 4 * chips * padded_bytes((rows, width), 2)
+    operands = sum(padded_bytes(t[0].shape, 2) + padded_bytes(t[1].shape, 2) for t in terms)
+    if chips < 4 or buffers + operands > 40 * MIB:
+        total = 0
+        for left, right, turn in terms:
+            total = total + lax.dot_general(
+                left, right, (((1,), (1 if turn else 0,)), ((), ())), preferred_element_type=WIDE
+            )
+        return lax.psum_scatter(
+            total.astype(SIXTEEN), "seq", scatter_dimension=0, tiled=True
+        ).astype(WIDE)
     ring = pltpu.SemaphoreType.DMA((2, parts, chips - 1))
     pair = pltpu.SemaphoreType.DMA((chips,))
+    blocks = pltpu.VMEM((chips, rows, width), SIXTEEN)
     return pl.pallas_call(
-        functools.partial(seq_scatter_kernel, shards, parts),
+        functools.partial(product_scatter_kernel, shards, parts, tuple(t[2] for t in terms)),
         out_shape=jax.ShapeDtypeStruct((rows, width), WIDE),
-        in_specs=[ANY],
+        in_specs=[VMEM] * (2 * len(terms)),
         out_specs=VMEM,
         scratch_shapes=[
-            pltpu.VMEM((chips, rows, width), SIXTEEN),
-            pltpu.VMEM((chips, rows, width), SIXTEEN),
+            blocks, blocks, blocks,
             pltpu.VMEM((2, chips - 1, rows // 2, width), SIXTEEN),
-            ring, ring, pair, pair, pair,
+            ring, ring, pair, pair,
         ],
         compiler_params=pltpu.CompilerParams(
             collective_id=collective_id, has_side_effects=True, vmem_limit_bytes=56 * MIB
         ),
-    )(whole.astype(SIXTEEN).reshape(shards, rows, width))
+        cost_estimate=pl.CostEstimate(flops=0, bytes_accessed=120 * MIB, transcendentals=0),
+    )(*[t[0] for t in terms], *[t[1] for t in terms])
 
 
 def bits_of(shards):
@@ -836,7 +916,11 @@
     return (cols // STATE == rows).astype(SIXTEEN)
 
 
-def scan_forward_kernel(keep_ref, conv_ref, delta_ref, b_ref, c_ref, a_ref, y_ref, start_ref, state_ref):
+def lanes_from(tile, group):
+    return pltpu.roll(tile, (SPAN - group * SUB) % SPAN, axis=1)
+
+
+def scan_forward_kernel(keep_ref, conv_ref, delta_ref, bc_ref, a_ref, y_ref, start_ref, state_ref):
     block = pl.program_id(0)
 
     @pl.when(block == 0)
@@ -846,13 +930,15 @@
     start_ref[0] = state_ref[...]
     decay_rate = a_ref[...]
     fold = step_sum()
+    b_span = bc_ref[:STATE, :].astype(WIDE)
+    c_span = bc_ref[STATE:, :].astype(WIDE)
 
     def body(group, state):
         rows = pl.ds(pl.multiple_of(group * SUB, SUB), SUB)
         delta = delta_ref[rows, :]
         drive = delta * conv_ref[rows, :]
-        b_tile = b_ref[group]
-        c_tile = c_ref[group]
+        b_tile = lanes_from(b_span, group)
+        c_tile = lanes_from(c_span, group)
         reads = []
         for i in range(SUB):
             keep = keep_ref[block * SPAN + group * SUB + i]
@@ -864,18 +950,13 @@
         )
         return state
 
-    state_ref[...] = lax.fori_loop(0, SPAN // SUB, body, state_ref[...])
-
-
-def time_tiles(values):
-    return values.reshape(values.shape[0] // SUB, SUB, STATE).transpose(0, 2, 1)
-
-
-def scan_forward(keep, conv_out, delta, b_in, c_read, decay_rate):
+    state_ref[...] = lax.fori_loop(0, SPAN // SUB, body, state_ref[...], unroll=8)
+
+
+def scan_forward(keep, conv_out, delta, bc_rows, decay_rate):
     length, lanes = conv_out.shape
     blocks = length // SPAN
     span_spec = pl.BlockSpec((SPAN, lanes), lambda i: (i, 0))
-    tile_spec = pl.BlockSpec((SPAN // SUB, STATE, SUB), lambda i: (i, 0, 0))
     return pl.pallas_call(
         scan_forward_kernel,
         grid=(blocks,),
@@ -883,8 +964,7 @@
             pl.BlockSpec(memory_space=pltpu.SMEM),
             span_spec,
             span_spec,
-            tile_spec,
-            tile_spec,
+            pl.BlockSpec((2 * STATE, SPAN), lambda i: (0, i)),
             pl.BlockSpec((STATE, lanes), lambda i: (0, 0)),
         ],
         out_specs=[span_spec, pl.BlockSpec((1, STATE, lanes), lambda i: (i, 0, 0))],
@@ -893,12 +973,12 @@
             jax.ShapeDtypeStruct((blocks, STATE, lanes), WIDE),
         ],
         scratch_shapes=[pltpu.VMEM((STATE, lanes), WIDE)],
-    )(keep, conv_out, delta, time_tiles(b_in), time_tiles(c_read), decay_rate)
+    )(keep, conv_out, delta, bc_rows, decay_rate)
 
 
 def scan_backward_kernel(
-    keep_ref, conv_ref, delta_ref, b_ref, c_ref, a_ref, start_ref, dy_ref,
-    dconv_ref, ddelta_ref, db_ref, dc_ref, da_ref,
+    keep_ref, conv_ref, delta_ref, bc_ref, a_ref, start_ref, dy_ref,
+    dconv_ref, ddelta_ref, dbc_ref, da_ref,
     state_ref, decay_ref, adjoint_ref,
 ):
     turn = pl.program_id(0)
@@ -912,14 +992,17 @@
     decay_rate = a_ref[...]
     fold = step_sum()
     lanes = decay_rate.shape[1]
-    ones = jnp.ones((SUB, lanes), SIXTEEN)
+    ones = jnp.ones((lanes, SPAN), SIXTEEN)
+    spot = lax.broadcasted_iota(jnp.int32, (STATE, SPAN), 1)
+    b_span = bc_ref[:STATE, :].astype(WIDE)
+    c_span = bc_ref[STATE:, :].astype(WIDE)
     state_ref[0] = start_ref[0]
 
     def ahead(group, state):
         rows = pl.ds(pl.multiple_of(group * SUB, SUB), SUB)
         delta = delta_ref[rows, :]
         drive = delta * conv_ref[rows, :]
-        b_tile = b_ref[group]
+        b_tile = lanes_from(b_span, group)
         for i in range(SUB):
             keep = keep_ref[block * SPAN + group * SUB + i]
             decay = jnp.exp(delta[i : i + 1, :] * decay_rate) * keep
@@ -928,18 +1011,18 @@
             state_ref[group * SUB + i + 1] = state
         return state
 
-    lax.fori_loop(0, SPAN // SUB, ahead, start_ref[0])
+    lax.fori_loop(0, SPAN // SUB, ahead, start_ref[0], unroll=16)
 
     def back(step, carry):
-        adjoint, da = carry
+        adjoint, da, db, dc = carry
         group = SPAN // SUB - 1 - step
         rows = pl.ds(pl.multiple_of(group * SUB, SUB), SUB)
         delta = delta_ref[rows, :]
         conv = conv_ref[rows, :]
         drive = delta * conv
         dy = dy_ref[rows, :]
-        b_tile = b_ref[group]
-        c_tile = c_ref[group]
+        b_tile = lanes_from(b_span, group)
+        c_tile = lanes_from(c_span, group)
         by_c, by_b, by_drive, by_delta = ([None] * SUB for _ in range(4))
         for i in range(SUB - 1, -1, -1):
             index = group * SUB + i
@@ -952,52 +1035,54 @@
             rate = adjoint * state_ref[index]
             by_delta[i] = (rate * decay_rate).astype(SIXTEEN)
             da = da + rate * delta[i : i + 1, :]
+
         def over_state(parts):
             return jnp.dot(fold, jnp.concatenate(parts, axis=0), preferred_element_type=WIDE)
-        def over_lanes(parts):
-            return lax.dot_general(
-                ones, jnp.concatenate(parts, axis=0), (((1,), (1,)), ((), ())),
-                preferred_element_type=WIDE,
-            )
+
+        def over_lanes(parts, tile):
+            sums = jnp.dot(jnp.concatenate(parts, axis=0), ones, preferred_element_type=WIDE)
+            for i in range(SUB):
+                here = spot == group * SUB + i
+                tile = jnp.where(here, sums[i * STATE : (i + 1) * STATE, :], tile)
+            return tile
+
         d_drive = over_state(by_drive)
         dconv_ref[rows, :] = d_drive * delta
         ddelta_ref[rows, :] = over_state(by_delta) + d_drive * conv
-        db_ref[group] = over_lanes(by_b)
-        dc_ref[group] = over_lanes(by_c)
-        return adjoint, da
-
-    adjoint, da = lax.fori_loop(0, SPAN // SUB, back, (adjoint_ref[...], da_ref[...]))
+        return adjoint, da, over_lanes(by_b, db), over_lanes(by_c, dc)
+
+    none = jnp.zeros((STATE, SPAN), WIDE)
+    adjoint, da, db, dc = lax.fori_loop(
+        0, SPAN // SUB, back, (adjoint_ref[...], da_ref[...], none, none), unroll=16
+    )
     adjoint_ref[...] = adjoint
     da_ref[...] = da
-
-
-def scan_backward(keep, conv_out, delta, b_in, c_read, decay_rate, starts, dy):
+    dbc_ref[...] = jnp.concatenate([db, dc], axis=0)
+
+
+def scan_backward(keep, conv_out, delta, bc_rows, decay_rate, starts, dy):
     length, lanes = conv_out.shape
     blocks = length // SPAN
     span_spec = pl.BlockSpec((SPAN, lanes), lambda i: (blocks - 1 - i, 0))
-    tile_spec = pl.BlockSpec((SPAN // SUB, STATE, SUB), lambda i: (blocks - 1 - i, 0, 0))
-    sums_spec = pl.BlockSpec((SPAN // SUB, SUB, SUB * STATE), lambda i: (blocks - 1 - i, 0, 0))
+    rows_spec = pl.BlockSpec((2 * STATE, SPAN), lambda i: (0, blocks - 1 - i))
     whole = pl.BlockSpec((STATE, lanes), lambda i: (0, 0))
-    sums = jax.ShapeDtypeStruct((length // SUB, SUB, SUB * STATE), WIDE)
-    dconv, ddelta, db, dc, da = pl.pallas_call(
+    return pl.pallas_call(
         scan_backward_kernel,
         grid=(blocks,),
         in_specs=[
             pl.BlockSpec(memory_space=pltpu.SMEM),
             span_spec,
             span_spec,
-            tile_spec,
-            tile_spec,
+            rows_spec,
             whole,
             pl.BlockSpec((1, STATE, lanes), lambda i: (blocks - 1 - i, 0, 0)),
             span_spec,
         ],
-        out_specs=[span_spec, span_spec, sums_spec, sums_spec, whole],
+        out_specs=[span_spec, span_spec, rows_spec, whole],
         out_shape=[
             jax.ShapeDtypeStruct((length, lanes), WIDE),
             jax.ShapeDtypeStruct((length, lanes), WIDE),
-            sums,
-            sums,
+            jax.ShapeDtypeStruct((2 * STATE, length), WIDE),
             jax.ShapeDtypeStruct((STATE, lanes), WIDE),
         ],
         scratch_shapes=[
@@ -1005,9 +1090,8 @@
             pltpu.VMEM((SPAN, STATE, lanes), WIDE),
             pltpu.VMEM((STATE, lanes), WIDE),
         ],
-        compiler_params=pltpu.CompilerParams(vmem_limit_bytes=32 * 1024 * 1024),
-    )(keep, conv_out, delta, time_tiles(b_in), time_tiles(c_read), decay_rate, starts, dy)
-    return dconv, ddelta, db[:, 0].reshape(length, STATE), dc[:, 0].reshape(length, STATE), da
+        compiler_params=pltpu.CompilerParams(vmem_limit_bytes=32 * MIB),
+    )(keep, conv_out, delta, bc_rows, decay_rate, starts, dy)
 
 
 def padded_lanes(array, lanes):
@@ -1021,10 +1105,9 @@
 
 def per_device(tokens, doc_ids, meta_tokens, mixer_params, small_params, ffn_params, cotangent):
     tokens, cotangent = tokens[0], cotangent[0]
-    small_whole, ids = start_blocks(small_params, doc_ids[0])
+    small_whole, ids, meta_whole = start_blocks(small_params, doc_ids[0], meta_tokens)
     (g_one, g_two, g_attn, channel_part), small_pull = jax.vjp(small_shards, small_whole)
-    (w_qkv, w_in, w_x, w_dt, w_out_a, w_out_m), mixer_pull = jax.vjp(mixer_shards, mixer_params)
-    (w_gate, w_up, w_down), ffn_pull = jax.vjp(ffn_shards, ffn_params)
+    columns, columns_pull = jax.vjp(mixer_columns, mixer_params)
     channels = channel_part.shape[0]
     lanes = -(-channels // 128) * 128
     g_ssm = channel_part[:, 0]
@@ -1046,11 +1129,16 @@
     tokens_f = tokens.astype(WIDE)
     normed_f, norm_pull = jax.vjp(rms_norm, tokens_f, g_one)
     meta_own = meta_tokens.astype(WIDE)
-    meta_unit = rms_norm(lax.all_gather(meta_tokens, ("row", "seq"), axis=0, tiled=True).astype(WIDE), 1.0)
-    normed = ring_seq_gather(normed_f.astype(SIXTEEN), 1)
+    meta_unit = rms_norm(meta_whole.astype(WIDE), 1.0)
+    normed_own, columns = lax.optimization_barrier((normed_f.astype(SIXTEEN), columns))
+    shards_fn = partial(mixer_shards, length=mixer_params.shape[0])
+    (w_qkv, w_in, w_x, w_dt, w_out), mixer_pull = jax.vjp(shards_fn, columns)
+    normed = ring_seq_gather(normed_own, 1)
+    normed, ffn_later, cotangent_later = lax.optimization_barrier((normed, ffn_params, cotangent))
+    (w_gate, w_up, w_down), ffn_pull = jax.vjp(ffn_shards, ffn_later)
     meta_normed = (meta_unit * g_one).astype(SIXTEEN)
     every = jnp.concatenate([normed, meta_normed], axis=0)
-    cotangent_all = gather_seq(cotangent)
+    cotangent_all = gather_seq(cotangent_later)
 
     xz = dot_last(normed, w_in).astype(SIXTEEN)
     extended = jnp.pad(xz[:, :channels], ((CONV - 1, 0), (0, 0))).astype(WIDE)
@@ -1060,18 +1148,15 @@
     conv_f = conv_half.astype(WIDE)
     w_x_rows = jnp.pad(w_x.T, ((0, -w_x.shape[1] % 16), (0, 0)))
     projected = seq_sum(jnp.einsum("nc,tc->nt", w_x_rows, conv_half, preferred_element_type=WIDE), 2)
-    rank_half = projected[:DT_RANK].T
-    b_in = projected[DT_RANK : DT_RANK + STATE].T.astype(WIDE)
-    c_read = projected[DT_RANK + STATE : DT_RANK + 2 * STATE].T.astype(WIDE)
-    pre_dt = dot_last(rank_half, w_dt)
+    rank_half = projected[:DT_RANK]
+    pre_dt = jnp.einsum("rt,rc->tc", rank_half, w_dt, preferred_element_type=WIDE)
     delta, delta_pull = jax.vjp(lambda p, b: softplus_fn(p + b), pre_dt, dt_bias)
     a_neg, a_pull = jax.vjp(lambda a: -jnp.exp(a), a_log)
     scan_in = (
         keep_mask,
         padded_lanes(conv_f, lanes),
         padded_lanes(delta, lanes),
-        b_in,
-        c_read,
+        projected[DT_RANK : DT_RANK + 2 * STATE],
         padded_lanes(a_neg.T, lanes),
     )
     y_scan, scan_starts = scan_forward(*scan_in)
@@ -1095,8 +1180,7 @@
         [attn_out * scale_a * g_attn, ssm_out * scale_m * g_ssm], axis=1
     )
     mixed = mixed.astype(SIXTEEN)
-    w_out = jnp.concatenate([w_out_a, w_out_m], axis=0)
-    hidden = tokens_f + ring_seq_scatter(dot_last(mixed, w_out), 4)
+    hidden = tokens_f + product_scatter([(mixed, w_out, False)], 4)
 
     second_f, second_pull = jax.vjp(rms_norm, hidden, g_two)
     second = ring_seq_gather(second_f.astype(SIXTEEN), 5)
@@ -1106,7 +1190,7 @@
     act = act_f.astype(SIXTEEN)
     d_gate, d_up = act_pull(dot_back(cotangent_all, w_down))
     d_gate, d_up = d_gate.astype(SIXTEEN), d_up.astype(SIXTEEN)
-    d_second = ring_seq_scatter(dot_back(d_gate, w_gate) + dot_back(d_up, w_up), 6)
+    d_second = product_scatter([(d_gate, w_gate, True), (d_up, w_up, True)], 6)
     block_out = (hidden + scatter_seq(dot_last(act, w_down))).astype(SIXTEEN)
     (grad_ffn,) = ffn_pull(
         (
@@ -1136,16 +1220,16 @@
     )
 
     d_y, d_conv, grad_d_skip, d_z = gate_pull(d_ssm)
-    d_conv_scan, d_delta, d_b, d_c, d_rate = scan_backward(
+    d_conv_scan, d_delta, d_bc, d_rate = scan_backward(
         *scan_in, scan_starts, padded_lanes(d_y, lanes)
     )
     d_conv = d_conv + d_conv_scan[:, :channels]
     d_pre, grad_dt_bias = delta_pull(d_delta[:, :channels])
     (grad_a_log,) = a_pull(d_rate[:, :channels].T)
     d_pre = d_pre.astype(SIXTEEN)
-    grad_dt = dot_weight(rank_half, d_pre)
+    grad_dt = jnp.einsum("rt,tc->rc", rank_half, d_pre, preferred_element_type=WIDE)
     d_rank = jnp.einsum("rc,tc->rt", w_dt, d_pre, preferred_element_type=WIDE)
-    d_proj = jnp.concatenate([d_rank, d_b.T, d_c.T], axis=0)
+    d_proj = jnp.concatenate([d_rank, d_bc], axis=0)
     d_proj = seq_sum(jnp.pad(d_proj, ((0, -d_proj.shape[0] % 16), (0, 0))), 10)
     d_proj = d_proj[: DT_RANK + 2 * STATE].T
     grad_x = dot_weight(conv_half, d_proj)
@@ -1154,16 +1238,14 @@
     grad_in = dot_weight(normed, d_xz)
     grad_qkv = jnp.concatenate([dot_weight(normed, d_queries), dot_weight(every, d_kv)], axis=1)
     d_meta = dot_back(d_kv[length:], w_qkv[:, own_heads:])
-    d_normed = (
-        dot_back(d_xz, w_in)
-        + dot_back(d_queries, w_qkv[:, :own_heads])
-        + dot_back(d_kv[:length], w_qkv[:, own_heads:])
-    )
-    grad_from_norm, grad_g_one = norm_pull(ring_seq_scatter(d_normed, 11))
+    d_qkv = jnp.concatenate([d_queries, d_kv[:length]], axis=1)
+    d_normed = product_scatter([(d_xz, w_in, True), (d_qkv, w_qkv, True)], 11)
+    grad_from_norm, grad_g_one = norm_pull(d_normed)
     grad_tokens = d_hidden + grad_from_norm
     grad_g_meta = jnp.sum(d_meta * meta_unit, axis=0)
-    grads = (grad_qkv, grad_in, grad_x, grad_dt, grad_out[:own_heads], grad_out[own_heads:])
-    (grad_mixer,) = mixer_pull(tuple(g.astype(SIXTEEN) for g in grads))
+    grads = (grad_qkv, grad_in, grad_x, grad_dt, grad_out)
+    grads = lax.optimization_barrier(tuple(g.astype(SIXTEEN) for g in grads))
+    (grad_mixer,) = columns_pull(mixer_pull(grads)[0])
     grad_channels = jnp.concatenate(
         [
             grad_g_ssm[:, None],

time: 1530 us -> 1330 us (0.87)
  blocking collectives: 90.5 us -> 0 us
  local copies, waits for them, and re-layouts: 356 us -> 277 us
  Pallas kernels: 656 us -> 586 us
  waiting for transfers between devices: 96.2 us -> 155 us
  matrix products: 140 us -> 108 us
    all_gather x2 -> x0, blocking collectives: 90.5 us -> none  [the longest x1 46.2 us: per_device(): lax.all_gather(meta_tokens, ('row', 'seq'), axis=0, tiled=True).astype(WIDE)]
    pallas_call x1, Pallas kernels: 95.8 us -> 40.2 us  [scan_backward(): pl.pallas_call(scan_backward_kernel, grid=(blocks,), in_specs=[pl.BlockSp...]
    all_to_all x12, waiting for transfers between devices: 49.6 us -> 92.2 us  [exchange(): return lax.all_to_all(value, 'seq', 0, 0)]
    pallas_call x3, Pallas kernels: 142 us -> 184 us  [product_scatter(): pl.pallas_call(functools.partial(product_scatter_kernel, shards, parts, t...]
    pallas_call x1, Pallas kernels: 60.9 us -> 23.1 us  [scan_forward(): pl.pallas_call(scan_forward_kernel, grid=(blocks,), in_specs=[pl.BlockSpe...]
    dot_general x9 -> x4, matrix products: 53.9 us -> 17.4 us  [dot_back(): jnp.einsum('...n,kn->...k', grads, right, preferred_element_type=WIDE)]
    convert_element_type x7 -> x4, local copies, waits for them, and re-layouts: 32.7 us -> 6.06 us  [the longest x1 2.64 us: per_device(): dot_weight(second, d_gate).astype(SIXTEEN)]
    pallas_call x2, Pallas kernels: 45.8 us -> 24.5 us  [seq_sum_small(): pl.pallas_call(functools.partial(seq_sum_small_kernel, bits), out_shape=j...]
  transfers between devices with their start and end apart: 19 -> 18, of which waited for: 5 -> 9; matrix products, arithmetic and copies ran while one was open for 29% -> 25% of each run, Pallas kernels for 38% -> 30%
where the time goes in v2:
time: 1330 us
  Pallas kernels  586 us (44%)
  local copies, waits for them, and re-layouts  277 us (21%)
  waiting for transfers between devices  155 us (12%)
  matrix products  108 us (8%)
  starting transfers between devices  91.9 us (7%)
  other arithmetic  91.6 us (7%)
  between operations  16.7 us (1%)
    pallas_call x3, Pallas kernels, product_scatter(): pl.pallas_call(functools.partial(product_scatter_kernel, shards, parts, t...  184 us
    pallas_call x3, Pallas kernels, ring_seq_gather(): pl.pallas_call(functools.partial(seq_gather_kernel, shards, parts), out_s...  131 us
    all_to_all x12, waiting for transfers between devices, exchange(): return lax.all_to_all(value, 'seq', 0, 0)  92.2 us
    all_to_all x12, starting transfers between devices, exchange(): return lax.all_to_all(value, 'seq', 0, 0)  88.4 us
    pallas_call x2, Pallas kernels, seq_sum(): pl.pallas_call(functools.partial(seq_sum_kernel, bits), out_shape=jax.Sha...  65.7 us
    ppermute x4, waiting for transfers between devices, both_halves(): other = lax.ppermute(value, 'row', [(0, 1), (1, 0)])  62.6 us
    pallas_call x1, Pallas kernels, push_gather(): pl.pallas_call(functools.partial(push_gather_kernel, rows, shards), out_s...  51.1 us
    dot_general x6, matrix products, dot_last(): return jnp.einsum('...k,kn->...n', left, right, preferred_element_type=WIDE)  46.1 us
  transfers between devices with their start and end apart: 18, of which 9 were waited for; matrix products, arithmetic and copies ran while one was open for 25% of the time, Pallas kernels for 30%

profile of v2, /device:TPU:0, one launch (start us, length us, event | category | flops | bytes accessed | tf_op | source)
XLA Modules:
  0.0 1325.6 jit_solution(1802695836680232475)
XLA Ops:
  7.2 12.3 reshape.551
  25.2 7.8 all-to-all-start
  34.1 51.1 %shard_map.118 = bf16[32,80,128]{2,1,0:T(8,128)(2,1)} custom-call(bf16[80,128]{1,0:T(8,128)(2,1)} %maximum_maximum_fusion.x_ref), custom_call_target="tpu_custom_call" | custom-call | tf_op jit(solution)/shard_map/pallas_call | solution.py:719
  97.9 34.9 %collective-permute-done = bf16[13904,50]{0,1:T(8,128)(2,1)} collective-permute-done((bf16[13904,50]{0,1:T(8,128)(2,1)S(1)}, bf16[13904,50]{0,1:T(8,128)(2,1)}, u32[]{:S(2)}, u32[]{:S(2)}) %collective-permute-start) | collective-permute-done | bytes 1390432 | tf_op jit(solution)/shard_map/jvp()/ppermute | solution.py:143
  145.5 6.4 all-to-all-start.1
  153.9 52.2 %shard_map.119 = bf16[16,128,1600]{2,1,0:T(8,128)(2,1)} custom-call(bf16[128,1600]{1,0:T(8,128)(2,1)} %get-tuple-element.27.x_ref), custom_call_target="tpu_custom_call" | custom-call | bytes 125829120 | tf_op jit(solution)/shard_map/pallas_call | solution.py:439
  239.7 29.1 %all-to-all-done.4 = bf16[16,150,344]{2,1,0:T(8,128)(2,1)} async-done(((bf16[16,150,344]{2,1,0:T(8,128)(2,1)}), bf16[16,150,344]{2,1,0:T(8,128)(2,1)}, u32[]{:S(2)}, u32[]{:S(2)}) %all-to-all-start.4) | async-done | bytes 1651232 | tf_op jit(solution)/shard_map/jvp()/all_to_all | solution.py:137
  268.8 12.3 all-to-all-start.3
  290.3 7.3 convolution_convert_fusion.1
  320.4 10.8 all-to-all-done.3
  331.1 9.2 all-to-all-start.2
  347.6 38.4 %shard_map.121 = bf16[144,2048]{1,0:T(8,128)(2,1)S(1)} custom-call(f32[144,2048]{1,0:T(8,128)S(1)} %fusion.44.x_ref), custom_call_target="tpu_custom_call" | custom-call | tf_op jit(solution)/shard_map/pallas_call | solution.py:639
  390.7 23.1 %shard_map.122 = (f32[2048,256]{1,0:T(8,128)}, f32[16,16,256]{2,1,0:T(8,128)}) custom-call(f32[2048]{0:T(1024)} %get-tuple-element.178.keep_ref, f32[2048,256]{1,0:T(8,128)} %pad.186.conv_ref, f32[2048,256]{1,0:T(8,128)} %pad.188.delta_ref, bf16[32,2048]{1,0:T(8,128)(2,1)} %slice.278.bc_ref, f32[16,256]{1,0:T(8,128)} %pad.189.a_ref), custom_call_target="tpu_custom_call" | custom-call | tf_op jit(solution)/shard_map/pallas_call | solution.py:960
  454.3 23.2 %shard_map.120 = (f32[2048,128]{1,0:T(8,128)S(1)}, f32[16,2,128]{2,1,0:T(2,128)S(1)}) custom-call(s32[16,1,128]{2,1,0:T(1,128)S(1)} %broadcast_maximum_fusion.refs_0_, bf16[2048,128]{1,0:T(8,128)(2,1)S(1)} %convolution_convert_fusion.8.refs_1_, bf16[3072,256]{1,0:T(8,128)(2,1)S(1)} %pad.184.clone.refs_2_, bf16[256,3072]{1,0:T(8,128)(2,1)S(1)} %pad_bitcast_fusion.refs_3_, ...), custom_call_target="tpu_custom_call" | custom-call | tf_op jit(solution)/shard_map/pallas_call | solution.py:872
  478.5 12.3 shard_map.123
  513.2 61.7 %shard_map.124 = f32[128,1600]{1,0:T(8,128)} custom-call(bf16[2048,328]{1,0:T(8,128)(2,1)} %fusion.3.refs_0_, bf16[328,1600]{1,0:T(8,128)(2,1)} %reshape.576.refs_1_), custom_call_target="tpu_custom_call" | custom-call | bytes 125829120 | tf_op jit(solution)/shard_map/pallas_call | solution.py:565
  578.1 39.3 %shard_map.125 = bf16[16,128,1600]{2,1,0:T(8,128)(2,1)} custom-call(bf16[128,1600]{1,0:T(8,128)(2,1)} %multiply_convert_fusion.2.x_ref), custom_call_target="tpu_custom_call" | custom-call | bytes 125829120 | tf_op jit(solution)/shard_map/pallas_call | solution.py:439
  617.4 8.8 fusion.72
  636.0 6.5 fusion.73
  642.5 10.8 multiply_convert_fusion
  653.3 48.9 %shard_map.126 = f32[128,1600]{1,0:T(8,128)} custom-call(bf16[2048,344]{1,0:T(8,128)(2,1)} %get-tuple-element.138.refs_0_, bf16[2048,344]{1,0:T(8,128)(2,1)} %get-tuple-element.137.refs_1_, bf16[1600,344]{1,0:T(8,128)(2,1)} %get-tuple-element.148.refs_2_, bf16[1600,344]{1,0:T(8,128)(2,1)} %get-tuple-element.149.refs_3_), custom_call_target="tpu_custom_call" | custom-call | bytes 125829120 | tf_op jit(solution)/shard_map/pallas_call | solution.py:565
  705.3 39.0 %shard_map.127 = bf16[16,128,1600]{2,1,0:T(8,128)(2,1)} custom-call(bf16[128,1600]{1,0:T(8,128)(2,1)} %fusion.62.x_ref), custom_call_target="tpu_custom_call" | custom-call | bytes 125829120 | tf_op jit(solution)/shard_map/pallas_call | solution.py:439
  744.3 7.2 convolution_convert_fusion.6
  760.3 12.2 shard_map.128
  782.6 40.2 %shard_map.129 = (f32[2048,256]{1,0:T(8,128)S(1)}, f32[2048,256]{1,0:T(8,128)S(1)}, f32[32,2048]{1,0:T(8,128)S(1)}, f32[16,256]{1,0:T(8,128)S(1)}) custom-call(f32[2048]{0:T(1024)S(1)} %copy-done.8, f32[2048,256]{1,0:T(8,128)S(1)} %copy-done, f32[2048,256]{1,0:T(8,128)S(1)} %copy-done.1, bf16[32,2048]{1,0:T(8,128)(2,1)S(1)} %copy-done.5, ...), custom_call_target="tpu_custom_call" | custom-call | tf_op jit(solution)/shard_map/pallas_call | solution.py:1069
  826.0 27.3 %shard_map.130 = bf16[144,2048]{1,0:T(8,128)(2,1)S(1)} custom-call(f32[144,2048]{1,0:T(8,128)S(1)} %select_maximum_fusion.x_ref), custom_call_target="tpu_custom_call" | custom-call | tf_op jit(solution)/shard_map/pallas_call | solution.py:639
  855.3 25.8 %shard_map.131 = (bf16[2048,128]{1,0:T(8,128)(2,1)S(1)}, f32[3072,256]{1,0:T(8,128)}, f32[128,256]{1,0:T(8,128)S(1)}) custom-call(s32[16,1,128]{2,1,0:T(1,128)S(1)} %broadcast_maximum_fusion.refs_0_, bf16[2048,128]{1,0:T(8,128)(2,1)S(1)} %copy-done.4, bf16[3072,256]{1,0:T(8,128)(2,1)S(1)} %pad.184.clone.refs_2_, bf16[256,3072]{1,0:T(8,128)(2,1)} %copy-done.2, ...), custom_call_target="tpu_custom_call" | custom-call | tf_op jit(solution)/shard_map/pallas_call | solution.py:893
  905.3 9.1 reshape.595
  936.5 14.6 %all-to-all-done.6 = bf16[16,656,50]{1,2,0:T(8,128)(2,1)S(1)} async-done(((bf16[16,656,50]{1,2,0:T(8,128)(2,1)}), bf16[16,656,50]{1,2,0:T(8,128)(2,1)S(1)}, u32[]{:S(2)}, u32[]{:S(2)}) %all-to-all-start.6) | async-done | bytes 1049632 | tf_op jit(solution)/shard_map/transpose(jvp())/all_to_all | solution.py:137
  951.1 8.2 all-to-all-start.10
  959.3 7.1 convolution_convert_fusion.4
  971.3 14.9 %all-to-all-done.10 = bf16[16,100,344]{2,1,0:T(8,128)(2,1)S(1)} async-done(((bf16[16,100,344]{2,1,0:T(8,128)(2,1)}), bf16[16,100,344]{2,1,0:T(8,128)(2,1)S(1)}, u32[]{:S(2)}, u32[]{:S(2)}) %all-to-all-start.10) | async-done | bytes 1100832 | tf_op jit(solution)/shard_map/transpose(jvp())/all_to_all | solution.py:137
  986.2 7.9 all-to-all-start.7
  994.2 6.7 convolution_convert_fusion.3
  1020.7 8.0 convolution_convert_fusion
  1028.7 9.8 copy.673
  1059.7 6.7 all-to-all-start.8
  1066.5 7.9 pad_add_fusion
  1080.2 12.4 all-to-all-done.8
  1110.2 9.4 collective-permute-done.3
  1127.9 6.5 all-to-all-start.11
  1134.4 18.3 %collective-permute-done.2 = bf16[13904,50]{0,1:T(8,128)(2,1)} collective-permute-done((bf16[13904,50]{0,1:T(8,128)(2,1)}, bf16[13904,50]{0,1:T(8,128)(2,1)}, u32[]{:S(2)}, u32[]{:S(2)}) %collective-permute-start.2) | collective-permute-done | bytes 1390432 | tf_op jit(solution)/shard_map/transpose(jvp())/ppermute | solution.py:143
  1161.1 10.5 all-to-all-done.11
  1171.5 10.3 all-to-all-start.9
  1182.2 73.8 %shard_map.132 = f32[128,1600]{1,0:T(8,128)} custom-call(bf16[2048,400]{1,0:T(8,128)(2,1)} %pad_maximum_fusion.7.refs_0_, bf16[2048,384]{1,0:T(8,128)(2,1)} %pad_maximum_fusion.8.refs_1_, bf16[1600,400]{1,0:T(8,128)(2,1)} %reshape.567.refs_2_, bf16[1600,384]{1,0:T(8,128)(2,1)} %copy-done.32), custom_call_target="tpu_custom_call" | custom-call | bytes 125829120 | tf_op jit(solution)/shard_map/pallas_call | solution.py:565
  1262.2 17.4 %shard_map.133 = f32[80,128]{1,0:T(8,128)S(1)} custom-call(bf16[32,80,128]{2,1,0:T(8,128)(2,1)S(1)} %pad_maximum_fusion.15.x_ref), custom_call_target="tpu_custom_call" | custom-call | tf_op jit(solution)/shard_map/pallas_call | solution.py:753
  1294.9 7.5 copy.713
  1302.4 9.4 reshape.623
  (560 shorter events, 374.4 us)
Async XLA Ops:
  25.2 65.6 %all-to-all-start = ((bf16[16,869,50]{1,2,0:T(8,128)(2,1)}), bf16[16,869,50]{1,2,0:T(8,128)(2,1)}, u32[]{:S(2)}, u32[]{:S(2)}) async-start(bf16[16,869,50]{1,2,0:T(8,128)(2,1)} %copy.640), calls=%async_computation | async-start | bytes 3211264 | tf_op jit(solution)/shard_map/jvp()/all_to_all | solution.py:137
  33.2 55.9 %copy-start.22 = (bf16[1,128,1600]{2,1,0:T(8,128)(2,1)}, bf16[1,128,1600]{2,1,0:T(8,128)(2,1)S(1)}, u32[]{:S(2)}) copy-start(bf16[1,128,1600]{2,1,0:T(8,128)(2,1)S(1)} %copy.639) | copy-start | bytes 1228804
  96.3 36.5 %collective-permute-start = (bf16[13904,50]{0,1:T(8,128)(2,1)S(1)}, bf16[13904,50]{0,1:T(8,128)(2,1)}, u32[]{:S(2)}, u32[]{:S(2)}) collective-permute-start(bf16[13904,50]{0,1:T(8,128)(2,1)S(1)} %reshape.552), channel_id=1, source_target_pairs={{0,16},{16,0},{1,17},{17,1},{2,18},{18,2},{3,19},{19,3},{4,20},{20... | collective-permute-start | bytes 4171208 | tf_op jit(solution)/shard_map/jvp()/ppermute | solution.py:143
  145.5 69.6 %all-to-all-start.1 = ((bf16[16,316,50]{1,2,0:T(8,128)(2,1)}), bf16[16,316,50]{1,2,0:T(8,128)(2,1)S(1)}, u32[]{:S(2)}, u32[]{:S(2)}) async-start(bf16[16,316,50]{1,2,0:T(8,128)(2,1)} %pad_maximum_fusion.14), calls=%async_computation.1 | async-start | bytes 1376256 | tf_op jit(solution)/shard_map/jvp()/all_to_all | solution.py:137
  215.1 53.6 %all-to-all-start.4 = ((bf16[16,150,344]{2,1,0:T(8,128)(2,1)}), bf16[16,150,344]{2,1,0:T(8,128)(2,1)}, u32[]{:S(2)}, u32[]{:S(2)}) async-start(bf16[16,150,344]{2,1,0:T(8,128)(2,1)} %copy.665), calls=%async_computation.4 | async-start | bytes 3735552 | tf_op jit(solution)/shard_map/jvp()/all_to_all | solution.py:137
  219.6 416.4 %all-gather.2.cloned.1.call-start = ((), (), s32[]{:S(2)}) async-start(), calls=%async_computation.14 | async-start | bytes 7241728 | tf_op jit(solution)/shard_map/all_gather | solution.py:343
  229.6 110.7 %copy-start.80 = (f32[2048]{0:T(1024)}, f32[2048]{0:T(1024)S(1)}, u32[]{:S(2)}) copy-start(f32[2048]{0:T(1024)S(1)} %get-tuple-element.179) | copy-start | bytes 24580
  229.6 110.7 %copy-start.82 = (f32[2048]{0:T(1024)}, f32[2048]{0:T(1024)S(1)}, u32[]{:S(2)}) copy-start(f32[2048]{0:T(1024)S(1)} %get-tuple-element.180) | copy-start | bytes 24580
  229.6 110.7 %copy-start.84 = (f32[2048]{0:T(1024)}, f32[2048]{0:T(1024)S(1)}, u32[]{:S(2)}) copy-start(f32[2048]{0:T(1024)S(1)} %get-tuple-element.181) | copy-start | bytes 24580
  229.6 110.7 %copy-start.86 = (f32[2048]{0:T(1024)}, f32[2048]{0:T(1024)S(1)}, u32[]{:S(2)}) copy-start(f32[2048]{0:T(1024)S(1)} %get-tuple-element.182) | copy-start | bytes 24580
  268.8 62.3 %all-to-all-start.3 = ((bf16[16,656,50]{1,2,0:T(8,128)(2,1)}), bf16[16,656,50]{1,2,0:T(8,128)(2,1)}, u32[]{:S(2)}, u32[]{:S(2)}) async-start(bf16[16,656,50]{1,2,0:T(8,128)(2,1)} %copy.663), calls=%async_computation.3 | async-start | bytes 2752512 | tf_op jit(solution)/shard_map/jvp()/all_to_all | solution.py:137
  299.5 40.8 %copy-start.9 = (f32[2051,200]{1,0:T(8,128)}, f32[2051,200]{1,0:T(8,128)S(1)}, u32[]{:S(2)}) copy-start(f32[2051,200]{1,0:T(8,128)S(1)} %pad_convert_fusion) | copy-start | bytes 4922404
  331.1 105.2 %all-to-all-start.2 = ((bf16[16,100,384]{2,1,0:T(8,128)(2,1)}), bf16[16,100,384]{2,1,0:T(8,128)(2,1)}, u32[]{:S(2)}, u32[]{:S(2)}) async-start(bf16[16,100,384]{2,1,0:T(8,128)(2,1)} %copy.652), calls=%async_computation.2 | async-start | bytes 2555904 | tf_op jit(solution)/shard_map/jvp()/all_to_all | solution.py:137
  343.7 70.1 %copy-start.16 = (bf16[2048,200]{1,0:T(8,128)(2,1)}, bf16[2048,200]{1,0:T(8,128)(2,1)S(1)}, u32[]{:S(2)}) copy-start(bf16[2048,200]{1,0:T(8,128)(2,1)S(1)} %get-tuple-element.134) | copy-start | bytes 2457604
  347.1 39.6 %copy-start.67 = (bf16[200,132]{1,0:T(8,128)(2,1)}, bf16[200,132]{1,0:T(8,128)(2,1)S(1)}, u32[]{:S(2)}) copy-start(bf16[200,132]{1,0:T(8,128)(2,1)S(1)} %reshape.569) | copy-start | bytes 158404
  347.1 39.6 %copy-start.106 = (f32[200,1]{0,1:T(1,128)S(1)}, f32[200,1]{0,1:T(1,128)}, u32[]{:S(2)}) copy-start(f32[200,1]{0,1:T(1,128)} %get-tuple-element.170) | copy-start | bytes 2404
  423.6 71.2 %collective-permute-start.1 = (bf16[2400,344]{0,1:T(8,128)(2,1)}, bf16[2400,344]{0,1:T(8,128)(2,1)}, u32[]{:S(2)}, u32[]{:S(2)}) collective-permute-start(bf16[2400,344]{0,1:T(8,128)(2,1)} %copy.666), channel_id=1, source_target_pairs={{0,16},{16,0},{1,17},{17,1},{2,18},{18,2},{3,19},{19,3},{4,20},{20... | collective-permute-start | bytes 4953608 | tf_op jit(solution)/shard_map/jvp()/ppermute | solution.py:143
  454.3 37.5 %copy-start.96 = (f32[128]{0:T(128)S(1)}, f32[128]{0:T(128)}, u32[]{:S(2)}) copy-start(f32[128]{0:T(128)} %fusion.53) | copy-start | bytes 1540
  505.5 120.8 %all-to-all-start.5 = ((bf16[16,100,344]{2,1,0:T(8,128)(2,1)}), bf16[16,100,344]{2,1,0:T(8,128)(2,1)}, u32[]{:S(2)}, u32[]{:S(2)}) async-start(bf16[16,100,344]{2,1,0:T(8,128)(2,1)} %reshape.580), calls=%async_computation.5 | async-start | bytes 2555904 | tf_op jit(solution)/shard_map/jvp()/all_to_all | solution.py:137
  513.2 61.7 %copy-start.23 = (bf16[1,128,1600]{2,1,0:T(8,128)(2,1)S(1)}, bf16[1,128,1600]{2,1,0:T(8,128)(2,1)}, u32[]{:S(2)}) copy-start(bf16[1,128,1600]{2,1,0:T(8,128)(2,1)} %copy-done.22) | copy-start | bytes 1228804
  576.3 127.9 %copy-start.89 = (f32[128]{0:T(128)}, f32[128]{0:T(128)S(1)}, u32[]{:S(2)}) copy-start(f32[128]{0:T(128)S(1)} %fusion.55) | copy-start | bytes 1540
  578.1 39.3 %copy-start.76 = (f32[32,128]{1,0:T(8,128)S(1)}, f32[32,128]{1,0:T(8,128)}, u32[]{:S(2)}) copy-start(f32[32,128]{1,0:T(8,128)} %shard_map.123) | copy-start | bytes 49156
  653.3 48.9 %copy-start.19 = (f32[128,1600]{1,0:T(8,128)S(1)}, f32[128,1600]{1,0:T(8,128)}, u32[]{:S(2)}) copy-start(f32[128,1600]{1,0:T(8,128)} %copy-done.18) | copy-start | bytes 2457604
  653.3 51.0 %copy-start.39 = (bf16[1,128,1600]{2,1,0:T(8,128)(2,1)S(1)}, bf16[1,128,1600]{2,1,0:T(8,128)(2,1)}, u32[]{:S(2)}) copy-start(bf16[1,128,1600]{2,1,0:T(8,128)(2,1)} %copy.642) | copy-start | bytes 1228804
  704.3 40.0 %copy-start.109 = (f32[128]{0:T(128)}, f32[128]{0:T(128)S(1)}, u32[]{:S(2)}) copy-start(f32[128]{0:T(128)S(1)} %multiply_multiply_fusion.10) | copy-start | bytes 1540
  779.2 117.9 %copy-start.52 = (bf16[2048,200]{1,0:T(8,128)(2,1)}, bf16[2048,200]{1,0:T(8,128)(2,1)S(1)}, u32[]{:S(2)}) copy-start(bf16[2048,200]{1,0:T(8,128)(2,1)S(1)} %get-tuple-element.136) | copy-start | bytes 2457604
  782.6 40.2 %copy-start.35 = (f32[2048,200]{1,0:T(8,128)S(1)}, f32[2048,200]{1,0:T(8,128)}, u32[]{:S(2)}) copy-start(f32[2048,200]{1,0:T(8,128)} %get-tuple-element.192) | copy-start | bytes 4915204
  826.0 29.3 %copy-start.4 = (bf16[2048,128]{1,0:T(8,128)(2,1)S(1)}, bf16[2048,128]{1,0:T(8,128)(2,1)}, u32[]{:S(2)}) copy-start(bf16[2048,128]{1,0:T(8,128)(2,1)} %copy-done.3) | copy-start | bytes 1572868
  918.4 32.6 %all-to-all-start.6 = ((bf16[16,656,50]{1,2,0:T(8,128)(2,1)}), bf16[16,656,50]{1,2,0:T(8,128)(2,1)S(1)}, u32[]{:S(2)}, u32[]{:S(2)}) async-start(bf16[16,656,50]{1,2,0:T(8,128)(2,1)} %copy.692), calls=%async_computation.7 | async-start | bytes 2752512 | tf_op jit(solution)/shard_map/transpose(jvp())/all_to_all | solution.py:137
  951.1 35.1 %all-to-all-start.10 = ((bf16[16,100,344]{2,1,0:T(8,128)(2,1)}), bf16[16,100,344]{2,1,0:T(8,128)(2,1)S(1)}, u32[]{:S(2)}, u32[]{:S(2)}) async-start(bf16[16,100,344]{2,1,0:T(8,128)(2,1)} %bitcast.257), calls=%async_computation.11 | async-start | bytes 2555904 | tf_op jit(solution)/shard_map/transpose(jvp())/all_to_all | solution.py:137
  968.9 25.2 %copy-start.62 = (bf16[2048,344]{1,0:T(8,128)(2,1)S(1)}, bf16[2048,344]{1,0:T(8,128)(2,1)}, u32[]{:S(2)}) copy-start(bf16[2048,344]{1,0:T(8,128)(2,1)} %get-tuple-element.138.refs_0_) | copy-start | bytes 4227076
  986.2 62.7 %all-to-all-start.7 = ((bf16[16,100,384]{2,1,0:T(8,128)(2,1)}), bf16[16,100,384]{2,1,0:T(8,128)(2,1)}, u32[]{:S(2)}, u32[]{:S(2)}) async-start(bf16[16,100,384]{2,1,0:T(8,128)(2,1)} %reshape.600), calls=%async_computation.8 | async-start | bytes 2555904 | tf_op jit(solution)/shard_map/transpose(jvp())/all_to_all | solution.py:137
  994.1 317.7 %reduce-scatter.2.cloned.1.call-start = ((), (), s32[]{:S(2)}) async-start(), calls=%async_computation.13 | async-start | bytes 7241728 | tf_op jit(solution)/shard_map/reduce_scatter | solution.py:347
  1059.7 32.8 %all-to-all-start.8 = ((bf16[16,316,50]{1,2,0:T(8,128)(2,1)}), bf16[16,316,50]{1,2,0:T(8,128)(2,1)}, u32[]{:S(2)}, u32[]{:S(2)}) async-start(bf16[16,316,50]{1,2,0:T(8,128)(2,1)} %bitcast.265), calls=%async_computation.9 | async-start | bytes 1376256 | tf_op jit(solution)/shard_map/transpose(jvp())/all_to_all | solution.py:137
  1079.9 39.7 %collective-permute-start.3 = (bf16[2400,344]{0,1:T(8,128)(2,1)}, bf16[2400,344]{0,1:T(8,128)(2,1)}, u32[]{:S(2)}, u32[]{:S(2)}) collective-permute-start(bf16[2400,344]{0,1:T(8,128)(2,1)} %copy.717), channel_id=1, source_target_pairs={{16,0},{0,16},{17,1},{1,17},{18,2},{2,18},{19,3},{3,19},{20,4},{4,... | collective-permute-start | bytes 4953608 | tf_op jit(solution)/shard_map/transpose(jvp())/ppermute | solution.py:143
  1105.9 46.7 %collective-permute-start.2 = (bf16[13904,50]{0,1:T(8,128)(2,1)}, bf16[13904,50]{0,1:T(8,128)(2,1)}, u32[]{:S(2)}, u32[]{:S(2)}) collective-permute-start(bf16[13904,50]{0,1:T(8,128)(2,1)} %select_add_fusion.1), channel_id=1, source_target_pairs={{16,0},{0,16},{17,1},{1,17},{18,2},{2,18},{19,3},{3,19},{20,4},{4,... | collective-permute-start | bytes 4171208 | tf_op jit(solution)/shard_map/transpose(jvp())/ppermute | solution.py:143
  1127.9 43.6 %all-to-all-start.11 = ((bf16[16,150,344]{2,1,0:T(8,128)(2,1)}), bf16[16,150,344]{2,1,0:T(8,128)(2,1)}, u32[]{:S(2)}, u32[]{:S(2)}) async-start(bf16[16,150,344]{2,1,0:T(8,128)(2,1)} %reshape.619), calls=%async_computation.12 | async-start | bytes 3735552 | tf_op jit(solution)/shard_map/transpose(jvp())/all_to_all | solution.py:137
  1171.5 120.0 %all-to-all-start.9 = ((bf16[16,869,50]{1,2,0:T(8,128)(2,1)}), bf16[16,869,50]{1,2,0:T(8,128)(2,1)}, u32[]{:S(2)}, u32[]{:S(2)}) async-start(bf16[16,869,50]{1,2,0:T(8,128)(2,1)} %copy.712), calls=%async_computation.10 | async-start | bytes 3211264 | tf_op jit(solution)/shard_map/transpose(jvp())/all_to_all | solution.py:137
  1182.1 73.9 %copy-start.24 = (bf16[1,128,1600]{2,1,0:T(8,128)(2,1)S(1)}, bf16[1,128,1600]{2,1,0:T(8,128)(2,1)}, u32[]{:S(2)}) copy-start(bf16[1,128,1600]{2,1,0:T(8,128)(2,1)} %copy-done.22) | copy-start | bytes 1228804
  1182.1 73.9 %copy-start.70 = (f32[1600]{0:T(1024)S(1)}, f32[1600]{0:T(1024)}, u32[]{:S(2)}) copy-start(f32[1600]{0:T(1024)} %copy-done.69) | copy-start | bytes 19204
  1182.1 73.9 %copy-start.92 = (f32[128]{0:T(128)S(1)}, f32[128]{0:T(128)}, u32[]{:S(2)}) copy-start(f32[128]{0:T(128)} %copy-done.91) | copy-start | bytes 1540
  1182.1 75.4 %copy-start.115 = (f32[200]{0:T(256)S(1)}, f32[200]{0:T(256)}, u32[]{:S(2)}) copy-start(f32[200]{0:T(256)} %get-tuple-element.110) | copy-start | bytes 2404
  1182.1 75.4 %copy-start.116 = (f32[200]{0:T(256)S(1)}, f32[200]{0:T(256)}, u32[]{:S(2)}) copy-start(f32[200]{0:T(256)} %get-tuple-element.111) | copy-start | bytes 2404
  1182.1 75.4 %copy-start.117 = (f32[200]{0:T(256)S(1)}, f32[200]{0:T(256)}, u32[]{:S(2)}) copy-start(f32[200]{0:T(256)} %get-tuple-element.112) | copy-start | bytes 2404
  1182.1 75.4 %copy-start.118 = (f32[200]{0:T(256)S(1)}, f32[200]{0:T(256)}, u32[]{:S(2)}) copy-start(f32[200]{0:T(256)} %get-tuple-element.113) | copy-start | bytes 2404
  1182.2 75.6 %copy-start.114 = (f32[200]{0:T(256)S(1)}, f32[200]{0:T(256)}, u32[]{:S(2)}) copy-start(f32[200]{0:T(256)} %get-tuple-element.116) | copy-start | bytes 2404
  1182.2 76.0 %copy-start.75 = (f32[200,24]{0,1:T(8,128)S(1)}, f32[200,24]{0,1:T(8,128)}, u32[]{:S(2)}) copy-start(f32[200,24]{0,1:T(8,128)} %copy-done.74) | copy-start | bytes 57604
  1182.2 76.5 %copy-start.97 = (f32[200]{0:T(256)S(1)}, f32[200]{0:T(256)}, u32[]{:S(2)}) copy-start(f32[200]{0:T(256)} %get-tuple-element.126) | copy-start | bytes 2404
  (96 other events, 738.6 us)
Sparse Core Ops, SparseCore 0:
  229.8 104.6 all-gather.1
  1038.6 96.1 reduce-scatter.1

commit v3 on v2

--- a/solution.py
+++ b/solution.py
@@ -137,9 +137,15 @@
     return lax.all_to_all(value, "seq", 0, 0)
 
 
+def tie(*arrays):
+    return lax.optimization_barrier(arrays)
+
+
+def hold(array):
+    return lax.optimization_barrier(array)
+
+
 def both_halves(value):
-    if lax.axis_size("row") != 2:
-        return lax.all_gather(value, "row", axis=0, tiled=True)
     other = lax.ppermute(value, "row", [(0, 1), (1, 0)])
     first = lax.axis_index("row") == 0
     return jnp.concatenate(
@@ -147,17 +153,143 @@
     )
 
 
-def mixer_fits(length, shards):
-    width = INNER // RUNS
+@partial(jax.custom_vjp, nondiff_argnums=(1,))
+def cut_rows(array, counts):
+    pieces, offset = [], 0
+    for count in counts:
+        pieces.append(array[offset : offset + count])
+        offset += count
+    return tuple(pieces)
+
+
+def cut_rows_forward(array, counts):
+    return cut_rows(array, counts), None
+
+
+def cut_rows_backward(counts, _, grads):
+    return (jnp.concatenate(grads, axis=0),)
+
+
+cut_rows.defvjp(cut_rows_forward, cut_rows_backward)
+
+
+def view_width():
+    return INNER // RUNS
+
+
+def weights_fit(mixer_length, ffn_length, rows, shards):
+    width = view_width()
     sizes = [math.prod(shape) for shape in mixer_layout()]
     return (
-        runs_of(shards) == RUNS
-        and length % width == 0
+        rows == 2
+        and runs_of(shards) == RUNS
+        and mixer_length % width == 0
         and all(size % width == 0 for size in sizes)
         and D % shards == 0
+        and D % width == 0
         and (HEADS * HEAD * 2) % shards == 0
         and shards % x_turns(shards)[0] == 0
-    )
+        and ffn_length % FF == 0
+    )
+
+
+def to_columns(piece, width):
+    shards = lax.axis_size("seq")
+    unit = width // shards
+    view = hold(piece.reshape(-1, width))
+    return exchange(view.reshape(-1, shards, unit).transpose(1, 0, 2)).reshape(-1, unit)
+
+
+def full_rows(cut):
+    received = exchange(cut)
+    return hold(received.transpose(1, 0, 2).reshape(received.shape[1], -1))
+
+
+def mixer_parts(both):
+    width, shards = view_width(), lax.axis_size("seq")
+    unit = both.shape[1]
+    part_q, part_kv, part_in, part_x, part_dt, part_out = cut_rows(
+        both, tuple(math.prod(shape) // width for shape in mixer_layout())
+    )
+    q_rows = jnp.concatenate(
+        [part_q.reshape(shards, -1, unit), part_kv.reshape(shards, -1, unit)], axis=1
+    )
+    per_row = D // width
+    head_rows = heads_of(shards) * HEAD
+    out_heads, out_inner = cut_rows(part_out, (HEADS * HEAD * per_row, INNER * per_row))
+    out_heads = jnp.pad(
+        out_heads, ((0, (head_rows * shards - HEADS * HEAD) * per_row), (0, 0))
+    ).reshape(shards, -1, unit)
+    out_inner = out_inner.reshape(RUNS, shards, -1, unit)
+    out_inner = out_inner.transpose(1, 0, 2, 3).reshape(shards, -1, unit)
+    return (
+        part_in.reshape(D, -1),
+        part_dt.reshape(DT_RANK, -1),
+        q_rows,
+        x_windows(part_x, shards),
+        jnp.concatenate([out_heads, out_inner], axis=1),
+    )
+
+
+def heads_cut(q_rows):
+    shards = lax.axis_size("seq")
+    rows = D // shards
+    by_rows = full_rows(q_rows)
+    split = rows * HEADS * HEAD // view_width()
+    cut = by_head(
+        by_rows[:split].reshape(rows, HEADS * HEAD),
+        by_rows[split:].reshape(rows, 2 * GROUPS * HEAD),
+        shards,
+    )
+    return cut.transpose(1, 0, 2)
+
+
+def heads_from(cut):
+    return exchange(cut).reshape(D, -1)
+
+
+def x_from(windows):
+    return x_from_windows(full_rows(windows), lax.axis_index("seq"))
+
+
+def out_from(cut):
+    return full_rows(cut).reshape(-1, D)
+
+
+def ffn_parts(both):
+    w_gate, w_up, part_down = cut_rows(both, (D, D, D))
+    return w_gate, w_up, part_down.reshape(lax.axis_size("seq"), -1, both.shape[1])
+
+
+def down_from(cut):
+    return full_rows(cut).reshape(-1, D)
+
+
+def x_turns(shards):
+    width = INNER // RUNS
+    run = (width // shards) * (DT_RANK + 2 * STATE)
+    common = math.gcd(run, width)
+    return width // common, run // common
+
+
+def x_windows(part_x, shards):
+    runs, rows = x_turns(shards)
+    need = -(-rows // runs)
+    turns = part_x.reshape(-1, rows, part_x.shape[1])
+    cuts = [turns[:, (i * rows) // runs : (i * rows) // runs + need] for i in range(runs)]
+    cuts = jnp.stack(cuts, axis=1).reshape(RUNS, shards, need, part_x.shape[1])
+    return cuts.transpose(1, 0, 2, 3).reshape(shards, RUNS * need, part_x.shape[1])
+
+
+def x_from_windows(view_rows, place):
+    width = view_rows.shape[1]
+    shards = lax.axis_size("seq")
+    runs, rows = x_turns(shards)
+    columns = DT_RANK + 2 * STATE
+    count = (width // shards) * columns
+    flat = view_rows.reshape(RUNS, -1)
+    offset = (place % runs) * rows * (width // runs) % width
+    return lax.dynamic_slice_in_dim(flat, offset, count, 1).reshape(-1, columns)
 
 
 def mixer_shards_whole(piece):
@@ -177,110 +309,16 @@
     )
 
 
-def mixer_columns(piece):
-    shards = lax.axis_size("seq")
-    if not mixer_fits(piece.shape[0], shards):
-        return piece
-    unit = INNER // (RUNS * shards)
-    return exchange(piece.reshape(-1, shards, unit).transpose(1, 0, 2)).reshape(-1, unit)
-
-
-def mixer_shards(mine, length):
-    shards, place = lax.axis_size("seq"), lax.axis_index("seq")
-    if not mixer_fits(length, shards):
-        return mixer_shards_whole(mine)
-    width = INNER // RUNS
-    unit = width // shards
-    mine = both_halves(mine)
-    part_q, part_kv, part_in, part_x, part_dt, part_out = cut_rows(
-        mine, [math.prod(shape) // width for shape in mixer_layout()]
-    )
-    w_in = part_in.reshape(D, -1)
-    w_dt = part_dt.reshape(DT_RANK, -1)
-    rows = D // shards
-    by_rows = exchange(
-        jnp.concatenate(
-            [
-                part_q.reshape(shards, -1, unit),
-                part_kv.reshape(shards, -1, unit),
-                x_windows(part_x, shards),
-            ],
-            axis=1,
-        )
-    )
-    by_rows = by_rows.transpose(1, 0, 2).reshape(-1, width)
-    split, end = part_q.shape[0] // shards, (part_q.shape[0] + part_kv.shape[0]) // shards
-    w_x = x_from_windows(by_rows[end:], place)
-    cut = by_head(
-        by_rows[:split].reshape(rows, HEADS * HEAD),
-        by_rows[split:end].reshape(rows, 2 * GROUPS * HEAD),
-        shards,
-    )
-    qkv = exchange(cut.transpose(1, 0, 2)).reshape(D, -1)
-    per_row = D // width
-    head_rows = heads_of(shards) * HEAD
-    out_heads = part_out[: HEADS * HEAD * per_row]
-    out_heads = jnp.pad(
-        out_heads, ((0, (head_rows * shards - HEADS * HEAD) * per_row), (0, 0))
-    ).reshape(shards, -1, unit)
-    out_inner = part_out[HEADS * HEAD * per_row :].reshape(RUNS, shards, -1, unit)
-    out_inner = out_inner.transpose(1, 0, 2, 3).reshape(shards, -1, unit)
-    out_both = exchange(jnp.concatenate([out_heads, out_inner], axis=1))
-    out_both = out_both.transpose(1, 0, 2).reshape(-1, D)
-    return qkv, w_in, w_x, w_dt, out_both
-
-
-def x_turns(shards):
-    width = INNER // RUNS
-    run = (width // shards) * (DT_RANK + 2 * STATE)
-    common = math.gcd(run, width)
-    return width // common, run // common
-
-
-def x_windows(part_x, shards):
-    runs, rows = x_turns(shards)
-    need = -(-rows // runs)
-    turns = part_x.reshape(-1, rows, part_x.shape[1])
-    cuts = [turns[:, (i * rows) // runs : (i * rows) // runs + need] for i in range(runs)]
-    cuts = jnp.stack(cuts, axis=1).reshape(RUNS, shards, need, part_x.shape[1])
-    return cuts.transpose(1, 0, 2, 3).reshape(shards, RUNS * need, part_x.shape[1])
-
-
-def x_from_windows(view_rows, place):
-    width = view_rows.shape[1]
-    shards = lax.axis_size("seq")
-    runs, rows = x_turns(shards)
-    columns = DT_RANK + 2 * STATE
-    count = (width // shards) * columns
-    flat = view_rows.reshape(RUNS, -1)
-    offset = (place % runs) * rows * (width // runs) % width
-    return lax.dynamic_slice_in_dim(flat, offset, count, 1).reshape(-1, columns)
-
-
-def cut_rows(array, counts):
-    pieces, offset = [], 0
-    for count in counts:
-        pieces.append(array[offset : offset + count])
-        offset += count
-    return pieces
-
-
-def ffn_shards(piece):
-    shards, place = lax.axis_size("seq"), lax.axis_index("seq")
-    unit = FF // shards
-    if piece.shape[0] % FF or D % shards:
-        whole = lax.all_gather(piece, ("row", "seq"), axis=0, tiled=True)
-        w_gate, w_up, w_down = split_flat(whole, ffn_layout())
-        return (
-            lax.dynamic_slice_in_dim(w_gate, place * unit, unit, 1),
-            lax.dynamic_slice_in_dim(w_up, place * unit, unit, 1),
-            lax.dynamic_slice_in_dim(w_down, place * unit, unit, 0),
-        )
-    mine = exchange(piece.reshape(-1, shards, unit).transpose(1, 0, 2))
-    mine = both_halves(mine.reshape(-1, unit))
-    w_gate, w_up, part_down = cut_rows(mine, [D, D, D])
-    w_down = exchange(part_down.reshape(shards, -1, unit))
-    return w_gate, w_up, w_down.transpose(1, 0, 2).reshape(unit, D)
+def ffn_shards_whole(piece):
+    unit = FF // lax.axis_size("seq")
+    start = lax.axis_index("seq") * unit
+    whole = lax.all_gather(piece, ("row", "seq"), axis=0, tiled=True)
+    w_gate, w_up, w_down = split_flat(whole, ffn_layout())
+    return (
+        lax.dynamic_slice_in_dim(w_gate, start, unit, 1),
+        lax.dynamic_slice_in_dim(w_up, start, unit, 1),
+        lax.dynamic_slice_in_dim(w_down, start, unit, 0),
+    )
 
 
 def small_shards(whole):
@@ -353,6 +391,12 @@
 ANY = pl.BlockSpec(memory_space=pl.ANY)
 VMEM = pl.BlockSpec(memory_space=pltpu.VMEM)
 MIB = 1024 * 1024
+
+
+def takes(microseconds):
+    return pl.CostEstimate(
+        flops=0, bytes_accessed=microseconds * 3_500_000, transcendentals=0
+    )
 
 
 def greet(peers):
@@ -443,7 +487,7 @@
         out_specs=ANY,
         scratch_shapes=[ring, ring, pair, pair, pltpu.SemaphoreType.DMA],
         compiler_params=pltpu.CompilerParams(collective_id=collective_id, has_side_effects=True),
-        cost_estimate=pl.CostEstimate(flops=0, bytes_accessed=120 * MIB, transcendentals=0),
+        cost_estimate=takes(40),
     )(block)
     return gathered.reshape(shards * rows, width)
 
@@ -575,7 +619,7 @@
         compiler_params=pltpu.CompilerParams(
             collective_id=collective_id, has_side_effects=True, vmem_limit_bytes=56 * MIB
         ),
-        cost_estimate=pl.CostEstimate(flops=0, bytes_accessed=120 * MIB, transcendentals=0),
+        cost_estimate=takes(40),
     )(*[t[0] for t in terms], *[t[1] for t in terms])
 
 
@@ -650,6 +694,7 @@
         compiler_params=pltpu.CompilerParams(
             collective_id=collective_id, has_side_effects=True, vmem_limit_bytes=48 * MIB
         ),
+        cost_estimate=takes(30),
     )(values)
 
 
@@ -687,6 +732,7 @@
         out_specs=VMEM,
         scratch_shapes=[slots, slots, sems, sems],
         compiler_params=pltpu.CompilerParams(collective_id=collective_id, has_side_effects=True),
+        cost_estimate=takes(12),
     )(tiles).reshape(shape)
 
 
@@ -723,6 +769,7 @@
         out_specs=VMEM,
         scratch_shapes=[sems, sems],
         compiler_params=pltpu.CompilerParams(collective_id=collective_id, has_side_effects=True),
+        cost_estimate=takes(20),
     )(block)
 
 
@@ -759,6 +806,7 @@
         compiler_params=pltpu.CompilerParams(
             collective_id=collective_id, has_side_effects=True, vmem_limit_bytes=32 * MIB
         ),
+        cost_estimate=takes(20),
     )(blocks)
 
 
@@ -882,6 +930,7 @@
             jax.ShapeDtypeStruct((count, heads, BLOCK), WIDE),
         ],
         compiler_params=pltpu.CompilerParams(vmem_limit_bytes=48 * MIB),
+        cost_estimate=takes(24),
     )(*arrays)
 
 
@@ -906,6 +955,7 @@
             jax.ShapeDtypeStruct(meta.shape, WIDE),
         ],
         compiler_params=pltpu.CompilerParams(vmem_limit_bytes=48 * MIB),
+        cost_estimate=takes(24),
     )(*arrays, out, log_total, d_out)
     return d_queries, jnp.concatenate([d_near[REACH * BLOCK :], d_meta], axis=0).astype(SIXTEEN)
 
@@ -973,6 +1023,7 @@
             jax.ShapeDtypeStruct((blocks, STATE, lanes), WIDE),
         ],
         scratch_shapes=[pltpu.VMEM((STATE, lanes), WIDE)],
+        cost_estimate=takes(24),
     )(keep, conv_out, delta, bc_rows, decay_rate)
 
 
@@ -1091,6 +1142,7 @@
             pltpu.VMEM((STATE, lanes), WIDE),
         ],
         compiler_params=pltpu.CompilerParams(vmem_limit_bytes=32 * MIB),
+        cost_estimate=takes(40),
     )(keep, conv_out, delta, bc_rows, decay_rate, starts, dy)
 
 
@@ -1107,7 +1159,10 @@
     tokens, cotangent = tokens[0], cotangent[0]
     small_whole, ids, meta_whole = start_blocks(small_params, doc_ids[0], meta_tokens)
     (g_one, g_two, g_attn, channel_part), small_pull = jax.vjp(small_shards, small_whole)
-    columns, columns_pull = jax.vjp(mixer_columns, mixer_params)
+    rows, shards = lax.axis_size("row"), lax.axis_size("seq")
+    staged = weights_fit(mixer_params.shape[0], ffn_params.shape[0], rows, shards)
+    if staged:
+        columns, pull_columns = jax.vjp(partial(to_columns, width=view_width()), mixer_params)
     channels = channel_part.shape[0]
     lanes = -(-channels // 128) * 128
     g_ssm = channel_part[:, 0]
@@ -1130,12 +1185,20 @@
     normed_f, norm_pull = jax.vjp(rms_norm, tokens_f, g_one)
     meta_own = meta_tokens.astype(WIDE)
     meta_unit = rms_norm(meta_whole.astype(WIDE), 1.0)
-    normed_own, columns = lax.optimization_barrier((normed_f.astype(SIXTEEN), columns))
-    shards_fn = partial(mixer_shards, length=mixer_params.shape[0])
-    (w_qkv, w_in, w_x, w_dt, w_out), mixer_pull = jax.vjp(shards_fn, columns)
+    normed_own = normed_f.astype(SIXTEEN)
+    if staged:
+        normed_own, columns = tie(normed_own, columns)
+        both, pull_both = jax.vjp(both_halves, columns)
     normed = ring_seq_gather(normed_own, 1)
-    normed, ffn_later, cotangent_later = lax.optimization_barrier((normed, ffn_params, cotangent))
-    (w_gate, w_up, w_down), ffn_pull = jax.vjp(ffn_shards, ffn_later)
+    cotangent_later = cotangent
+    if staged:
+        normed, both, cotangent_later = tie(normed, both, cotangent)
+        (w_in, w_dt, q_rows, x_rows, out_rows), pull_parts = jax.vjp(mixer_parts, both)
+        w_x, pull_x = jax.vjp(x_from, x_rows)
+        by_heads, pull_rows = jax.vjp(heads_cut, q_rows)
+    else:
+        (w_qkv, w_in, w_x, w_dt, w_out), pull_mixer = jax.vjp(mixer_shards_whole, mixer_params)
+        (w_gate, w_up, w_down), pull_ffn = jax.vjp(ffn_shards_whole, ffn_params)
     meta_normed = (meta_unit * g_one).astype(SIXTEEN)
     every = jnp.concatenate([normed, meta_normed], axis=0)
     cotangent_all = gather_seq(cotangent_later)
@@ -1145,6 +1208,8 @@
     conv_fn = partial(conv_piece, lag_masks=lag_masks)
     conv_out, conv_pull = jax.vjp(conv_fn, extended, conv_w, conv_b)
     conv_half = conv_out.astype(SIXTEEN)
+    if staged:
+        conv_half, w_x = tie(conv_half, w_x)
     conv_f = conv_half.astype(WIDE)
     w_x_rows = jnp.pad(w_x.T, ((0, -w_x.shape[1] % 16), (0, 0)))
     projected = seq_sum(jnp.einsum("nc,tc->nt", w_x_rows, conv_half, preferred_element_type=WIDE), 2)
@@ -1152,6 +1217,9 @@
     pre_dt = jnp.einsum("rt,rc->tc", rank_half, w_dt, preferred_element_type=WIDE)
     delta, delta_pull = jax.vjp(lambda p, b: softplus_fn(p + b), pre_dt, dt_bias)
     a_neg, a_pull = jax.vjp(lambda a: -jnp.exp(a), a_log)
+    if staged:
+        delta, by_heads, out_rows = tie(delta, by_heads, out_rows)
+        w_qkv, pull_heads = jax.vjp(heads_from, by_heads)
     scan_in = (
         keep_mask,
         padded_lanes(conv_f, lanes),
@@ -1167,13 +1235,22 @@
     z_in = xz[:, channels:].astype(WIDE)
     ssm_out, gate_pull = jax.vjp(gate_piece, y_scan[:, :channels], conv_f, d_skip, z_in)
 
+    if staged:
+        ssm_out, w_qkv, out_rows = tie(ssm_out, w_qkv, out_rows)
+        w_out, pull_out = jax.vjp(out_from, out_rows)
     own_heads = g_attn.shape[0]
     queries = dot_last(normed, w_qkv[:, :own_heads]).astype(SIXTEEN)
     kv_rows = dot_last(every, w_qkv[:, own_heads:]).astype(SIXTEEN)
+    if staged:
+        queries, w_out, ffn_later = tie(queries, w_out, ffn_params)
+        ffn_columns, pull_ffn_columns = jax.vjp(partial(to_columns, width=FF), ffn_later)
     attn_out, log_total = attend_forward(queries, kv_rows, doc_first)
 
     squares = jnp.stack([jnp.sum(attn_out * attn_out, axis=1), jnp.sum(ssm_out * ssm_out, axis=1)])
     squares = seq_sum_small(squares, 3)
+    if staged:
+        squares, ffn_columns = tie(squares, ffn_columns)
+        ffn_both, pull_ffn_both = jax.vjp(both_halves, ffn_columns)
     scale_a = lax.rsqrt(squares[0] / (HEADS * HEAD) + norm_eps)[:, None]
     scale_m = lax.rsqrt(squares[1] / INNER + norm_eps)[:, None]
     mixed = 0.5 * jnp.concatenate(
@@ -1182,6 +1259,10 @@
     mixed = mixed.astype(SIXTEEN)
     hidden = tokens_f + product_scatter([(mixed, w_out, False)], 4)
 
+    if staged:
+        hidden, ffn_both = tie(hidden, ffn_both)
+        (w_gate, w_up, down_rows), pull_ffn_parts = jax.vjp(ffn_parts, ffn_both)
+        w_down, pull_down = jax.vjp(down_from, down_rows)
     second_f, second_pull = jax.vjp(rms_norm, hidden, g_two)
     second = ring_seq_gather(second_f.astype(SIXTEEN), 5)
     gate_pre = dot_last(second, w_gate)
@@ -1192,24 +1273,33 @@
     d_gate, d_up = d_gate.astype(SIXTEEN), d_up.astype(SIXTEEN)
     d_second = product_scatter([(d_gate, w_gate, True), (d_up, w_up, True)], 6)
     block_out = (hidden + scatter_seq(dot_last(act, w_down))).astype(SIXTEEN)
-    (grad_ffn,) = ffn_pull(
+    d_hidden, grad_g_two = second_pull(d_second)
+    d_hidden = d_hidden + cotangent.astype(WIDE)
+
+    d_branch = ring_seq_gather(d_hidden.astype(SIXTEEN), 7)
+    grads_ffn = hold(
         (
             dot_weight(second, d_gate).astype(SIXTEEN),
             dot_weight(second, d_up).astype(SIXTEEN),
             dot_weight(act, cotangent_all).astype(SIXTEEN),
         )
     )
-    d_hidden, grad_g_two = second_pull(d_second)
-    d_hidden = d_hidden + cotangent.astype(WIDE)
-
-    d_branch = ring_seq_gather(d_hidden.astype(SIXTEEN), 7)
-    grad_out = dot_weight(mixed, d_branch)
+    grad_out = hold(dot_weight(mixed, d_branch).astype(SIXTEEN))
+    if staged:
+        (d_down_rows,) = pull_down(grads_ffn[2])
     d_mixed = 0.5 * dot_back(d_branch, w_out)
     d_mix_a, d_mix_m = d_mixed[:, :own_heads], d_mixed[:, own_heads:]
     means = jnp.stack(
         [jnp.sum(attn_out * g_attn * d_mix_a, axis=1), jnp.sum(ssm_out * g_ssm * d_mix_m, axis=1)]
     )
     means = seq_sum_small(means, 8)
+    if staged:
+        means, d_down_rows, grad_gate, grad_up = tie(
+            means, d_down_rows, grads_ffn[0], grads_ffn[1]
+        )
+        (d_ffn_both,) = pull_ffn_parts((grad_gate, grad_up, d_down_rows))
+        (d_ffn_columns,) = pull_ffn_both(d_ffn_both)
+        (d_out_rows,) = pull_out(grad_out)
     d_attn, grad_g_attn = rms_pull(
         attn_out, scale_a, g_attn, d_mix_a, means[0][:, None] / (HEADS * HEAD)
     )
@@ -1219,10 +1309,23 @@
         queries, kv_rows, doc_first, attn_out, log_total, d_attn
     )
 
+    if staged:
+        d_queries, d_kv, d_ffn_columns, d_out_rows = tie(
+            d_queries, d_kv, d_ffn_columns, d_out_rows
+        )
+        (grad_ffn,) = pull_ffn_columns(d_ffn_columns)
+    grad_qkv = jnp.concatenate([dot_weight(normed, d_queries), dot_weight(every, d_kv)], axis=1)
+    grad_qkv = hold(grad_qkv.astype(SIXTEEN))
+
     d_y, d_conv, grad_d_skip, d_z = gate_pull(d_ssm)
+    if staged:
+        d_y, grad_qkv = tie(d_y, grad_qkv)
     d_conv_scan, d_delta, d_bc, d_rate = scan_backward(
         *scan_in, scan_starts, padded_lanes(d_y, lanes)
     )
+    if staged:
+        d_conv_scan, d_delta, grad_ffn, grad_qkv = tie(d_conv_scan, d_delta, grad_ffn, grad_qkv)
+        (d_by_heads,) = pull_heads(grad_qkv)
     d_conv = d_conv + d_conv_scan[:, :channels]
     d_pre, grad_dt_bias = delta_pull(d_delta[:, :channels])
     (grad_a_log,) = a_pull(d_rate[:, :channels].T)
@@ -1231,21 +1334,33 @@
     d_rank = jnp.einsum("rc,tc->rt", w_dt, d_pre, preferred_element_type=WIDE)
     d_proj = jnp.concatenate([d_rank, d_bc], axis=0)
     d_proj = seq_sum(jnp.pad(d_proj, ((0, -d_proj.shape[0] % 16), (0, 0))), 10)
+    if staged:
+        d_proj, d_by_heads = tie(d_proj, d_by_heads)
+        (d_q_rows,) = pull_rows(d_by_heads)
     d_proj = d_proj[: DT_RANK + 2 * STATE].T
-    grad_x = dot_weight(conv_half, d_proj)
+    grad_x = hold(dot_weight(conv_half, d_proj).astype(SIXTEEN))
+    if staged:
+        (d_x_rows,) = pull_x(grad_x)
     d_extended, grad_conv_w, grad_conv_b = conv_pull(d_conv + dot_back(d_proj, w_x))
     d_xz = jnp.concatenate([d_extended[CONV - 1 :], d_z], axis=1).astype(SIXTEEN)
-    grad_in = dot_weight(normed, d_xz)
-    grad_qkv = jnp.concatenate([dot_weight(normed, d_queries), dot_weight(every, d_kv)], axis=1)
+    grad_in = hold(dot_weight(normed, d_xz).astype(SIXTEEN))
+    grad_dt = grad_dt.astype(SIXTEEN)
+    if staged:
+        (d_both,) = pull_parts((grad_in, grad_dt, d_q_rows, d_x_rows, d_out_rows))
+        d_xz, d_both = tie(d_xz, d_both)
+        (d_columns,) = pull_both(d_both)
     d_meta = dot_back(d_kv[length:], w_qkv[:, own_heads:])
     d_qkv = jnp.concatenate([d_queries, d_kv[:length]], axis=1)
     d_normed = product_scatter([(d_xz, w_in, True), (d_qkv, w_qkv, True)], 11)
+    if staged:
+        d_normed, d_columns = tie(d_normed, d_columns)
+        (grad_mixer,) = pull_columns(d_columns)
+    else:
+        (grad_mixer,) = pull_mixer((grad_qkv, grad_in, grad_x, grad_dt, grad_out))
+        (grad_ffn,) = pull_ffn(grads_ffn)
     grad_from_norm, grad_g_one = norm_pull(d_normed)
     grad_tokens = d_hidden + grad_from_norm
     grad_g_meta = jnp.sum(d_meta * meta_unit, axis=0)
-    grads = (grad_qkv, grad_in, grad_x, grad_dt, grad_out)
-    grads = lax.optimization_barrier(tuple(g.astype(SIXTEEN) for g in grads))
-    (grad_mixer,) = columns_pull(mixer_pull(grads)[0])
     grad_channels = jnp.concatenate(
         [
             grad_g_ssm[:, None],
@@ -1265,9 +1380,9 @@
         block_out[None],
         grad_tokens[None],
         grad_meta,
-        grad_mixer.astype(WIDE),
+        hold(grad_mixer).astype(WIDE),
         grad_small,
-        grad_ffn.astype(WIDE),
+        hold(grad_ffn).astype(WIDE),
     )
 
 

time: 1330 us -> 1260 us (0.947)
  waiting for transfers between devices: 155 us -> 49.1 us
  Pallas kernels: 586 us -> 607 us
  matrix products: 108 us -> 124 us
    ppermute x4, waiting for transfers between devices: 62.6 us -> 0.01 us  [both_halves(): other = lax.ppermute(value, 'row', [(0, 1), (1, 0)])]
    all_to_all x12 -> x14, waiting for transfers between devices: 92.2 us -> 48.9 us  [exchange(): return lax.all_to_all(value, 'seq', 0, 0)]
    pallas_call x3, Pallas kernels: 184 us -> 144 us  [product_scatter(): pl.pallas_call(functools.partial(product_scatter_kernel, shards, parts, t...]
    pallas_call x3, Pallas kernels: 131 us -> 169 us  [ring_seq_gather(): pl.pallas_call(functools.partial(seq_gather_kernel, shards, parts), out_s...]
    convert_element_type x6 -> x1, local copies, waits for them, and re-layouts: 30.6 us -> 0.11 us  [per_device(): grad_dt = grad_dt.astype(SIXTEEN)]
    pallas_call x1, Pallas kernels: 17.4 us -> 36.8 us  [push_scatter(): pl.pallas_call(functools.partial(push_scatter_kernel, rows, shards), out_...]
    optimization_barrier x3 -> x10, local copies, waits for them, and re-layouts: 2.91 us -> 19.6 us  [the longest x7 11.4 us: hold(): return lax.optimization_barrier(array)]
    add_any x4 -> x1, other arithmetic: 14.7 us -> 0.05 us  [heads_cut(): by_rows[:split].reshape(rows, HEADS * HEAD)]
  transfers between devices with their start and end apart: 18 -> 20, of which waited for: 9 -> 2; matrix products, arithmetic and copies ran while one was open for 25% -> 28% of each run, Pallas kernels for 30% -> 45%
where the time goes in v3:
time: 1260 us; the launch traced here: 1250 us
  Pallas kernels  607 us (48%)
  local copies, waits for them, and re-layouts  274 us (22%)
  matrix products  124 us (10%)
  starting transfers between devices  94.5 us (8%)
  other arithmetic  83.2 us (7%)
  waiting for transfers between devices  49.1 us (4%)
  between operations  16.6 us (1%)
    pallas_call x3, Pallas kernels, ring_seq_gather(): pl.pallas_call(functools.partial(seq_gather_kernel, shards, parts), out_s...  169 us
    pallas_call x3, Pallas kernels, product_scatter(): pl.pallas_call(functools.partial(product_scatter_kernel, shards, parts, t...  144 us
    all_to_all x14, starting transfers between devices, exchange(): return lax.all_to_all(value, 'seq', 0, 0)  87.6 us
    pallas_call x2, Pallas kernels, seq_sum(): pl.pallas_call(functools.partial(seq_sum_kernel, bits), out_shape=jax.Sha...  70.3 us
    pallas_call x1, Pallas kernels, push_gather(): pl.pallas_call(functools.partial(push_gather_kernel, rows, shards), out_s...  51.2 us
    all_to_all x14, waiting for transfers between devices, exchange(): return lax.all_to_all(value, 'seq', 0, 0)  48.9 us
    dot_general x8, matrix products, dot_weight(): return jnp.einsum('...k,...n->kn', left, grads, preferred_element_type=WIDE)  48.8 us
    dot_general x6, matrix products, dot_last(): return jnp.einsum('...k,kn->...n', left, right, preferred_element_type=WIDE)  41.5 us
  transfers between devices with their start and end apart: 20, of which 2 were waited for; matrix products, arithmetic and copies ran while one was open for 28% of the time, Pallas kernels for 45%

profile of v3, /device:TPU:0, one launch (start us, length us, event | category | flops | bytes accessed | tf_op | source)
XLA Modules:
  0.0 1248.8 jit_solution(11003060852151215469)
XLA Ops:
  13.6 7.8 all-to-all-start
  22.5 51.2 %shard_map.118 = bf16[32,80,128]{2,1,0:T(8,128)(2,1)} custom-call(bf16[80,128]{1,0:T(8,128)(2,1)} %maximum_maximum_fusion.x_ref), custom_call_target="tpu_custom_call" | custom-call | bytes 70000000 | tf_op jit(solution)/shard_map/pallas_call | solution.py:765
  95.4 41.0 %shard_map.119 = bf16[16,128,1600]{2,1,0:T(8,128)(2,1)} custom-call(bf16[128,1600]{1,0:T(8,128)(2,1)} %get-tuple-element.60.x_ref), custom_call_target="tpu_custom_call" | custom-call | bytes 140000000 | tf_op jit(solution)/shard_map/pallas_call | solution.py:483
  160.6 7.3 convolution_convert_fusion.1
  183.7 6.4 all-to-all-start.2
  191.6 31.9 %shard_map.120 = bf16[144,2048]{1,0:T(8,128)(2,1)S(1)} custom-call(f32[144,2048]{1,0:T(8,128)S(1)} %fusion.41.x_ref), custom_call_target="tpu_custom_call" | custom-call | bytes 105000000 | tf_op jit(solution)/shard_map/pallas_call | solution.py:683
  238.4 5.0 all-to-all-start.3
  247.7 23.3 %shard_map.121 = (f32[2048,256]{1,0:T(8,128)}, f32[16,16,256]{2,1,0:T(8,128)}) custom-call(f32[2048]{0:T(1024)} %get-tuple-element.240.keep_ref, f32[2048,256]{1,0:T(8,128)} %pad.146.conv_ref, f32[2048,256]{1,0:T(8,128)} %pad.152.delta_ref, bf16[32,2048]{1,0:T(8,128)(2,1)} %slice.268.bc_ref, f32[16,256]{1,0:T(8,128)} %pad.153.a_ref), custom_call_target="tpu_custom_call" | custom-call | bytes 84000000 | tf_op jit(solution)/shard_map/pallas_call | solution.py:1010
  281.3 13.9 %all-to-all-start.4 = ((bf16[16,656,50]{1,2,0:T(8,128)(2,1)}), bf16[16,656,50]{1,2,0:T(8,128)(2,1)S(1)}, u32[]{:S(2)}, u32[]{:S(2)}) async-start(bf16[16,656,50]{1,2,0:T(8,128)(2,1)} %copy.692), calls=%async_computation.4 | async-start | bytes 2752512 | tf_op jit(solution)/shard_map/jvp()/all_to_all | solution.py:137
  295.2 4.9 convolution_convert_fusion.8.refs_1_
  300.1 45.5 %all-to-all-done.4 = bf16[16,656,50]{1,2,0:T(8,128)(2,1)S(1)} async-done(((bf16[16,656,50]{1,2,0:T(8,128)(2,1)}), bf16[16,656,50]{1,2,0:T(8,128)(2,1)S(1)}, u32[]{:S(2)}, u32[]{:S(2)}) %all-to-all-start.4) | async-done | bytes 1049632 | tf_op jit(solution)/shard_map/jvp()/all_to_all | solution.py:137
  354.3 4.5 reshape.604
  361.9 9.3 all-to-all-start.5
  371.6 5.3 fusion.2
  383.7 23.2 %shard_map.122 = (f32[2048,128]{1,0:T(8,128)S(1)}, f32[16,2,128]{2,1,0:T(2,128)S(1)}) custom-call(s32[16,1,128]{2,1,0:T(1,128)S(1)} %broadcast_maximum_fusion.refs_0_, bf16[2048,128]{1,0:T(8,128)(2,1)S(1)} %convolution_convert_fusion.8.refs_1_, bf16[3072,256]{1,0:T(8,128)(2,1)S(1)} %pad.154.clone.refs_2_, bf16[256,3072]{1,0:T(8,128)(2,1)S(1)} %pad_bitcast_fusion.refs_3_, ...), custom_call_target="tpu_custom_call" | custom-call | bytes 84000000 | tf_op jit(solution)/shard_map/pallas_call | solution.py:920
  407.9 13.5 %shard_map.123 = f32[32,128]{1,0:T(8,128)} custom-call(f32[32,128]{1,0:T(8,128)} %reshape.601.x_ref), custom_call_target="tpu_custom_call" | custom-call | bytes 42000000 | tf_op jit(solution)/shard_map/pallas_call | solution.py:728
  433.1 43.1 %shard_map.124 = f32[128,1600]{1,0:T(8,128)} custom-call(bf16[2048,328]{1,0:T(8,128)(2,1)} %fusion.3.refs_0_, bf16[328,1600]{1,0:T(8,128)(2,1)} %reshape.600.refs_1_), custom_call_target="tpu_custom_call" | custom-call | bytes 140000000 | tf_op jit(solution)/shard_map/pallas_call | solution.py:609
  490.1 4.8 all-to-all-start.6
  498.3 63.4 %shard_map.125 = bf16[16,128,1600]{2,1,0:T(8,128)(2,1)} custom-call(bf16[128,1600]{1,0:T(8,128)(2,1)} %multiply_convert_fusion.2.x_ref), custom_call_target="tpu_custom_call" | custom-call | bytes 140000000 | tf_op jit(solution)/shard_map/pallas_call | solution.py:483
  561.7 8.9 fusion.58
  570.6 7.0 fusion.60
  589.9 11.8 multiply_convert_fusion
  601.7 8.7 convolution_convert_fusion.3
  610.4 7.6 convolution_convert_fusion.4
  618.0 48.8 %shard_map.126 = f32[128,1600]{1,0:T(8,128)} custom-call(bf16[2048,344]{1,0:T(8,128)(2,1)} %copy-done.52, bf16[2048,344]{1,0:T(8,128)(2,1)} %copy-done.51, bf16[1600,344]{1,0:T(8,128)(2,1)} %get-tuple-element.204.refs_2_, bf16[1600,344]{1,0:T(8,128)(2,1)} %get-tuple-element.202.refs_3_), custom_call_target="tpu_custom_call" | custom-call | bytes 140000000 | tf_op jit(solution)/shard_map/pallas_call | solution.py:609
  668.7 6.9 convolution_convert_fusion.5
  696.0 64.2 %shard_map.127 = bf16[16,128,1600]{2,1,0:T(8,128)(2,1)} custom-call(bf16[128,1600]{1,0:T(8,128)(2,1)} %fusion.62.x_ref), custom_call_target="tpu_custom_call" | custom-call | bytes 140000000 | tf_op jit(solution)/shard_map/pallas_call | solution.py:483
  760.1 6.3 convolution_multiply_fusion
  771.1 11.9 shard_map.128
  795.1 7.1 convolution_convert_fusion.6
  810.3 4.8 all-to-all-start.8
  817.2 25.9 %shard_map.129 = (bf16[2048,128]{1,0:T(8,128)(2,1)S(1)}, f32[3072,256]{1,0:T(8,128)}, f32[128,256]{1,0:T(8,128)S(1)}) custom-call(s32[16,1,128]{2,1,0:T(1,128)S(1)} %broadcast_maximum_fusion.refs_0_, bf16[2048,128]{1,0:T(8,128)(2,1)S(1)} %convolution_convert_fusion.8.refs_1_, bf16[3072,256]{1,0:T(8,128)(2,1)S(1)} %pad.154.clone.refs_2_, ...), custom_call_target="tpu_custom_call" | custom-call | bytes 84000000 | tf_op jit(solution)/shard_map/pallas_call | solution.py:942
  854.7 6.2 all-to-all-start.9
  861.0 6.5 multiply_reduce_fusion
  867.5 5.7 convolution_convert_fusion.7
  873.3 5.2 fusion.4
  881.9 38.8 %shard_map.130 = (f32[2048,256]{1,0:T(8,128)S(1)}, f32[2048,256]{1,0:T(8,128)S(1)}, f32[32,2048]{1,0:T(8,128)S(1)}, f32[16,256]{1,0:T(8,128)S(1)}) custom-call(f32[2048]{0:T(1024)S(1)} %copy-done.10, f32[2048,256]{1,0:T(8,128)S(1)} %copy-done, f32[2048,256]{1,0:T(8,128)S(1)} %copy-done.1, bf16[32,2048]{1,0:T(8,128)(2,1)S(1)} %copy-done.5, ...), custom_call_target="tpu_custom_call" | custom-call | bytes 140000000 | tf_op jit(solution)/shard_map/pallas_call | solution.py:1120
  929.3 4.5 reshape.621
  936.0 6.0 all-to-all-start.10
  942.2 8.0 convolution_convert_fusion
  950.2 9.6 copy.705
  980.0 38.4 %shard_map.131 = bf16[144,2048]{1,0:T(8,128)(2,1)S(1)} custom-call(f32[144,2048]{1,0:T(8,128)S(1)} %select_maximum_fusion.x_ref), custom_call_target="tpu_custom_call" | custom-call | bytes 105000000 | tf_op jit(solution)/shard_map/pallas_call | solution.py:683
  1038.3 8.9 multiply_reduce_fusion.4
  1051.4 6.5 all-to-all-start.11
  1057.9 7.3 convolution_convert_fusion.2
  1085.7 5.2 concatenate.92
  1112.0 51.8 %shard_map.132 = f32[128,1600]{1,0:T(8,128)} custom-call(bf16[2048,400]{1,0:T(8,128)(2,1)} %pad_maximum_fusion.9.refs_0_, bf16[2048,384]{1,0:T(8,128)(2,1)} %pad_maximum_fusion.12.refs_1_, bf16[1600,400]{1,0:T(8,128)(2,1)} %reshape.579.refs_2_, bf16[1600,384]{1,0:T(8,128)(2,1)} %copy-done.33), custom_call_target="tpu_custom_call" | custom-call | bytes 140000000 | tf_op jit(solution)/shard_map/pallas_call | solution.py:609
  1188.9 36.8 %shard_map.133 = f32[80,128]{1,0:T(8,128)S(1)} custom-call(bf16[32,80,128]{2,1,0:T(8,128)(2,1)S(1)} %pad_maximum_fusion.18.x_ref), custom_call_target="tpu_custom_call" | custom-call | bytes 70000000 | tf_op jit(solution)/shard_map/pallas_call | solution.py:800
  (563 shorter events, 361.6 us)
Async XLA Ops:
  13.6 67.0 %all-to-all-start = ((bf16[16,869,50]{1,2,0:T(8,128)(2,1)}), bf16[16,869,50]{1,2,0:T(8,128)(2,1)}, u32[]{:S(2)}, u32[]{:S(2)}) async-start(bf16[16,869,50]{1,2,0:T(8,128)(2,1)} %bitcast.5), calls=%async_computation | async-start | bytes 3211264 | tf_op jit(solution)/shard_map/jvp()/all_to_all | solution.py:137
  21.6 57.3 %copy-start.22 = (bf16[1,128,1600]{2,1,0:T(8,128)(2,1)}, bf16[1,128,1600]{2,1,0:T(8,128)(2,1)S(1)}, u32[]{:S(2)}) copy-start(bf16[1,128,1600]{2,1,0:T(8,128)(2,1)S(1)} %copy.671) | copy-start | bytes 1228804
  86.1 50.3 %collective-permute-start = (bf16[13904,50]{0,1:T(8,128)(2,1)S(1)}, bf16[13904,50]{0,1:T(8,128)(2,1)}, u32[]{:S(2)}, u32[]{:S(2)}) collective-permute-start(bf16[13904,50]{0,1:T(8,128)(2,1)S(1)} %reshape.575), channel_id=1, source_target_pairs={{0,16},{16,0},{1,17},{17,1},{2,18},{18,2},{3,19},{19,3},{4,20},{20... | collective-permute-start | bytes 4171208 | tf_op jit(solution)/shard_map/jvp()/ppermute | solution.py:149
  90.5 45.9 %copy-start.70 = (s32[16,128]{1,0:T(8,128)}, s32[16,128]{1,0:T(8,128)S(1)}, u32[]{:S(2)}) copy-start(s32[16,128]{1,0:T(8,128)S(1)} %reduce-window.9) | copy-start | bytes 24580
  93.4 43.0 %copy-start.67 = (f32[200,24]{0,1:T(8,128)}, f32[200,24]{0,1:T(8,128)S(1)}, u32[]{:S(2)}) copy-start(f32[200,24]{0,1:T(8,128)S(1)} %reshape.578) | copy-start | bytes 57604
  93.5 42.9 %copy-start.88 = (s32[16]{0:T(128)}, s32[16]{0:T(128)S(1)}, u32[]{:S(2)}) copy-start(s32[16]{0:T(128)S(1)} %slice_reduce_fusion.4) | copy-start | bytes 196
  149.6 34.1 %all-to-all-start.1 = ((bf16[16,2,900]{2,1,0:T(2,128)(2,1)}), bf16[16,2,900]{2,1,0:T(2,128)(2,1)S(1)}, u32[]{:S(2)}, u32[]{:S(2)}) async-start(bf16[16,2,900]{2,1,0:T(2,128)(2,1)} %reshape.671), calls=%async_computation.1 | async-start | bytes 131072 | tf_op jit(solution)/shard_map/jvp()/all_to_all | solution.py:137
  169.9 53.6 %copy-start.58 = (bf16[100,200]{1,0:T(8,128)(2,1)}, bf16[100,200]{1,0:T(8,128)(2,1)S(1)}, u32[]{:S(2)}) copy-start(bf16[100,200]{1,0:T(8,128)(2,1)S(1)} %reshape.586) | copy-start | bytes 120004
  182.5 88.5 %copy-start.20 = (bf16[2048,200]{1,0:T(8,128)(2,1)}, bf16[2048,200]{1,0:T(8,128)(2,1)S(1)}, u32[]{:S(2)}) copy-start(bf16[2048,200]{1,0:T(8,128)(2,1)S(1)} %get-tuple-element.64) | copy-start | bytes 2457604
  183.7 43.0 %all-to-all-start.2 = ((bf16[16,280,50]{1,2,0:T(8,128)(2,1)}), bf16[16,280,50]{1,2,0:T(8,128)(2,1)S(1)}, u32[]{:S(2)}, u32[]{:S(2)}) async-start(bf16[16,280,50]{1,2,0:T(8,128)(2,1)} %pad_maximum_fusion.17), calls=%async_computation.2 | async-start | bytes 1376256 | tf_op jit(solution)/shard_map/jvp()/all_to_all | solution.py:137
  190.9 32.6 %copy-start.98 = (f32[200,1]{0,1:T(1,128)S(1)}, f32[200,1]{0,1:T(1,128)}, u32[]{:S(2)}) copy-start(f32[200,1]{0,1:T(1,128)} %get-tuple-element.234) | copy-start | bytes 2404
  191.1 35.7 %copy-start.63 = (bf16[200,132]{1,0:T(8,128)(2,1)}, bf16[200,132]{1,0:T(8,128)(2,1)S(1)}, u32[]{:S(2)}) copy-start(bf16[200,132]{1,0:T(8,128)(2,1)S(1)} %reshape.585) | copy-start | bytes 158404
  223.5 20.6 %copy-start.3 = (bf16[144,2048]{1,0:T(8,128)(2,1)}, bf16[144,2048]{1,0:T(8,128)(2,1)S(1)}, u32[]{:S(2)}) copy-start(bf16[144,2048]{1,0:T(8,128)(2,1)S(1)} %shard_map.120) | copy-start | bytes 1769476
  238.4 40.0 %all-to-all-start.3 = ((bf16[16,100,384]{2,1,0:T(8,128)(2,1)}), bf16[16,100,384]{2,1,0:T(8,128)(2,1)}, u32[]{:S(2)}, u32[]{:S(2)}) async-start(bf16[16,100,384]{2,1,0:T(8,128)(2,1)} %copy.691), calls=%async_computation.3 | async-start | bytes 2555904 | tf_op jit(solution)/shard_map/jvp()/all_to_all | solution.py:137
  243.4 346.5 %all-gather.2.cloned.1.call-start = ((), (), s32[]{:S(2)}) async-start(), calls=%async_computation.16 | async-start | bytes 7241728 | tf_op jit(solution)/shard_map/all_gather | solution.py:381
  247.7 23.3 %copy-start.44 = (bf16[2048,400]{1,0:T(8,128)(2,1)S(1)}, bf16[2048,400]{1,0:T(8,128)(2,1)}, u32[]{:S(2)}) copy-start(bf16[2048,400]{1,0:T(8,128)(2,1)} %copy-done.43) | copy-start | bytes 4915204
  247.7 23.3 %copy-start.82 = (f32[200,1]{0,1:T(1,128)S(1)}, f32[200,1]{0,1:T(1,128)}, u32[]{:S(2)}) copy-start(f32[200,1]{0,1:T(1,128)} %get-tuple-element.233) | copy-start | bytes 2404
  279.8 91.7 %copy-start.33 = (bf16[1600,384]{1,0:T(8,128)(2,1)}, bf16[1600,384]{1,0:T(8,128)(2,1)S(1)}, u32[]{:S(2)}) copy-start(bf16[1600,384]{1,0:T(8,128)(2,1)S(1)} %reshape.598.refs_3_) | copy-start | bytes 3686404
  281.3 64.3 %all-to-all-start.4 = ((bf16[16,656,50]{1,2,0:T(8,128)(2,1)}), bf16[16,656,50]{1,2,0:T(8,128)(2,1)S(1)}, u32[]{:S(2)}, u32[]{:S(2)}) async-start(bf16[16,656,50]{1,2,0:T(8,128)(2,1)} %copy.692), calls=%async_computation.4 | async-start | bytes 2752512 | tf_op jit(solution)/shard_map/jvp()/all_to_all | solution.py:137
  361.9 60.2 %all-to-all-start.5 = ((bf16[16,150,344]{2,1,0:T(8,128)(2,1)}), bf16[16,150,344]{2,1,0:T(8,128)(2,1)}, u32[]{:S(2)}, u32[]{:S(2)}) async-start(bf16[16,150,344]{2,1,0:T(8,128)(2,1)} %copy.697), calls=%async_computation.5 | async-start | bytes 3735552 | tf_op jit(solution)/shard_map/jvp()/all_to_all | solution.py:137
  383.7 23.5 %copy-start.2 = (bf16[256,3072]{1,0:T(8,128)(2,1)}, bf16[256,3072]{1,0:T(8,128)(2,1)S(1)}, u32[]{:S(2)}) copy-start(bf16[256,3072]{1,0:T(8,128)(2,1)S(1)} %pad_bitcast_fusion.refs_3_) | copy-start | bytes 4718596
  429.2 49.1 %collective-permute-start.1 = (bf16[2400,344]{0,1:T(8,128)(2,1)}, bf16[2400,344]{0,1:T(8,128)(2,1)}, u32[]{:S(2)}, u32[]{:S(2)}) collective-permute-start(bf16[2400,344]{0,1:T(8,128)(2,1)} %copy.698), channel_id=1, source_target_pairs={{0,16},{16,0},{1,17},{17,1},{2,18},{18,2},{3,19},{19,3},{4,20},{20... | collective-permute-start | bytes 4953608 | tf_op jit(solution)/shard_map/jvp()/ppermute | solution.py:149
  433.0 43.1 %copy-start.23 = (bf16[1,128,1600]{2,1,0:T(8,128)(2,1)S(1)}, bf16[1,128,1600]{2,1,0:T(8,128)(2,1)}, u32[]{:S(2)}) copy-start(bf16[1,128,1600]{2,1,0:T(8,128)(2,1)} %copy-done.22) | copy-start | bytes 1228804
  490.1 87.5 %all-to-all-start.6 = ((bf16[16,100,344]{2,1,0:T(8,128)(2,1)}), bf16[16,100,344]{2,1,0:T(8,128)(2,1)}, u32[]{:S(2)}, u32[]{:S(2)}) async-start(bf16[16,100,344]{2,1,0:T(8,128)(2,1)} %reshape.608), calls=%async_computation.6 | async-start | bytes 2555904 | tf_op jit(solution)/shard_map/jvp()/all_to_all | solution.py:137
  496.2 197.1 %copy-start.83 = (f32[128]{0:T(128)}, f32[128]{0:T(128)S(1)}, u32[]{:S(2)}) copy-start(f32[128]{0:T(128)S(1)} %fusion.53) | copy-start | bytes 1540
  618.0 48.8 %copy-start.17 = (f32[128,1600]{1,0:T(8,128)S(1)}, f32[128,1600]{1,0:T(8,128)}, u32[]{:S(2)}) copy-start(f32[128,1600]{1,0:T(8,128)} %convert_add_fusion) | copy-start | bytes 2457604
  618.0 50.7 %copy-start.113 = (bf16[2048,344]{1,0:T(8,128)(2,1)S(1)}, bf16[2048,344]{1,0:T(8,128)(2,1)}, u32[]{:S(2)}) copy-start(bf16[2048,344]{1,0:T(8,128)(2,1)} %get-tuple-element.201) | copy-start | bytes 4227076
  688.9 94.8 %all-to-all-start.7 = ((bf16[16,100,344]{2,1,0:T(8,128)(2,1)}), bf16[16,100,344]{2,1,0:T(8,128)(2,1)}, u32[]{:S(2)}, u32[]{:S(2)}) async-start(bf16[16,100,344]{2,1,0:T(8,128)(2,1)} %copy.713), calls=%async_computation.8 | async-start | bytes 2555904 | tf_op jit(solution)/shard_map/transpose(jvp())/all_to_all | solution.py:137
  693.4 66.8 %copy-start.102 = (f32[128]{0:T(128)}, f32[128]{0:T(128)S(1)}, u32[]{:S(2)}) copy-start(f32[128]{0:T(128)S(1)} %multiply_multiply_fusion.10) | copy-start | bytes 1540
  794.0 52.0 %collective-permute-start.2 = (bf16[2400,344]{0,1:T(8,128)(2,1)}, bf16[2400,344]{0,1:T(8,128)(2,1)}, u32[]{:S(2)}, u32[]{:S(2)}) collective-permute-start(bf16[2400,344]{0,1:T(8,128)(2,1)} %copy.716), channel_id=1, source_target_pairs={{16,0},{0,16},{17,1},{1,17},{18,2},{2,18},{19,3},{3,19},{20,4},{4,... | collective-permute-start | bytes 4953608 | tf_op jit(solution)/shard_map/transpose(jvp())/ppermute | solution.py:149
  810.3 42.9 %all-to-all-start.8 = ((bf16[16,656,50]{1,2,0:T(8,128)(2,1)}), bf16[16,656,50]{1,2,0:T(8,128)(2,1)}, u32[]{:S(2)}, u32[]{:S(2)}) async-start(bf16[16,656,50]{1,2,0:T(8,128)(2,1)} %bitcast.251), calls=%async_computation.9 | async-start | bytes 2752512 | tf_op jit(solution)/shard_map/transpose(jvp())/all_to_all | solution.py:137
  854.7 67.2 %all-to-all-start.9 = ((bf16[16,150,344]{2,1,0:T(8,128)(2,1)}), bf16[16,150,344]{2,1,0:T(8,128)(2,1)}, u32[]{:S(2)}, u32[]{:S(2)}) async-start(bf16[16,150,344]{2,1,0:T(8,128)(2,1)} %reshape.619), calls=%async_computation.10 | async-start | bytes 3735552 | tf_op jit(solution)/shard_map/transpose(jvp())/all_to_all | solution.py:137
  867.5 12.1 copy-start.37
  936.0 82.5 %all-to-all-start.10 = ((bf16[16,100,384]{2,1,0:T(8,128)(2,1)}), bf16[16,100,384]{2,1,0:T(8,128)(2,1)}, u32[]{:S(2)}, u32[]{:S(2)}) async-start(bf16[16,100,384]{2,1,0:T(8,128)(2,1)} %reshape.622), calls=%async_computation.11 | async-start | bytes 2555904 | tf_op jit(solution)/shard_map/transpose(jvp())/all_to_all | solution.py:137
  942.0 283.9 %reduce-scatter.2.cloned.1.call-start = ((), (), s32[]{:S(2)}) async-start(), calls=%async_computation.15 | async-start | bytes 7241728 | tf_op jit(solution)/shard_map/reduce_scatter | solution.py:385
  979.9 38.6 %copy-start.21 = (bf16[2048,200]{1,0:T(8,128)(2,1)S(1)}, bf16[2048,200]{1,0:T(8,128)(2,1)}, u32[]{:S(2)}) copy-start(bf16[2048,200]{1,0:T(8,128)(2,1)} %copy-done.20) | copy-start | bytes 2457604
  1021.0 30.4 %all-to-all-start.12 = ((bf16[16,2,900]{2,1,0:T(2,128)(2,1)}), bf16[16,2,900]{2,1,0:T(2,128)(2,1)S(1)}, u32[]{:S(2)}, u32[]{:S(2)}) async-start(bf16[16,2,900]{2,1,0:T(2,128)(2,1)} %reshape.673), calls=%async_computation.13 | async-start | bytes 131072 | tf_op jit(solution)/shard_map/transpose(jvp())/all_to_all | solution.py:137
  1048.1 9.8 copy-start.47
  1051.4 28.7 %all-to-all-start.11 = ((bf16[16,280,50]{1,2,0:T(8,128)(2,1)}), bf16[16,280,50]{1,2,0:T(8,128)(2,1)}, u32[]{:S(2)}, u32[]{:S(2)}) async-start(bf16[16,280,50]{1,2,0:T(8,128)(2,1)} %bitcast.258), calls=%async_computation.12 | async-start | bytes 1376256 | tf_op jit(solution)/shard_map/transpose(jvp())/all_to_all | solution.py:137
  1094.6 69.2 %collective-permute-start.3 = (bf16[13904,50]{0,1:T(8,128)(2,1)}, bf16[13904,50]{0,1:T(8,128)(2,1)}, u32[]{:S(2)}, u32[]{:S(2)}) collective-permute-start(bf16[13904,50]{0,1:T(8,128)(2,1)} %select_add_fusion.1), channel_id=1, source_target_pairs={{16,0},{0,16},{17,1},{1,17},{18,2},{2,18},{19,3},{3,19},{20,4},{4,... | collective-permute-start | bytes 4171208 | tf_op jit(solution)/shard_map/transpose(jvp())/ppermute | solution.py:149
  1112.0 51.9 %copy-start.19 = (bf16[27808,50]{0,1:T(8,128)(2,1)S(1)}, bf16[27808,50]{0,1:T(8,128)(2,1)}, u32[]{:S(2)}) copy-start(bf16[27808,50]{0,1:T(8,128)(2,1)} %concatenate.92) | copy-start | bytes 8342404
  1169.9 64.4 %all-to-all-start.13 = ((bf16[16,869,50]{1,2,0:T(8,128)(2,1)}), bf16[16,869,50]{1,2,0:T(8,128)(2,1)}, u32[]{:S(2)}, u32[]{:S(2)}) async-start(bf16[16,869,50]{1,2,0:T(8,128)(2,1)} %copy.751), calls=%async_computation.14 | async-start | bytes 3211264 | tf_op jit(solution)/shard_map/transpose(jvp())/all_to_all | solution.py:137
  1180.3 45.6 %copy-start.105 = (f32[128]{0:T(128)S(1)}, f32[128]{0:T(128)}, u32[]{:S(2)}) copy-start(f32[128]{0:T(128)} %copy-done.104) | copy-start | bytes 1540
  1180.3 45.7 %copy-start.18 = (f32[128,1600]{1,0:T(8,128)S(1)}, f32[128,1600]{1,0:T(8,128)}, u32[]{:S(2)}) copy-start(f32[128,1600]{1,0:T(8,128)} %convert_add_fusion) | copy-start | bytes 2457604
  1180.3 45.7 %copy-start.26 = (f32[128,1600]{1,0:T(8,128)S(1)}, f32[128,1600]{1,0:T(8,128)}, u32[]{:S(2)}) copy-start(f32[128,1600]{1,0:T(8,128)} %shard_map.126) | copy-start | bytes 2457604
  1180.3 45.7 %copy-start.39 = (bf16[1,128,1600]{2,1,0:T(8,128)(2,1)S(1)}, bf16[1,128,1600]{2,1,0:T(8,128)(2,1)}, u32[]{:S(2)}) copy-start(bf16[1,128,1600]{2,1,0:T(8,128)(2,1)} %copy.674) | copy-start | bytes 1228804
  1180.3 45.7 %copy-start.84 = (f32[128]{0:T(128)S(1)}, f32[128]{0:T(128)}, u32[]{:S(2)}) copy-start(f32[128]{0:T(128)} %copy-done.83) | copy-start | bytes 1540
  1180.3 45.7 %copy-start.103 = (f32[128]{0:T(128)S(1)}, f32[128]{0:T(128)}, u32[]{:S(2)}) copy-start(f32[128]{0:T(128)} %copy-done.102) | copy-start | bytes 1540
  (89 other events, 414.2 us)
Sparse Core Ops, SparseCore 0:
  246.5 103.1 all-gather.1
  960.0 92.2 reduce-scatter.1

commit v4 on v3

--- a/solution.py
+++ b/solution.py
@@ -6,6 +6,7 @@
 import jax.numpy as jnp
 from jax import lax
 from jax.experimental import pallas as pl
+from jax.experimental.layout import Layout, with_layout_constraint
 from jax.experimental.pallas import tpu as pltpu
 from jax.sharding import PartitionSpec as P
 
@@ -145,8 +146,20 @@
     return lax.optimization_barrier(array)
 
 
+@jax.custom_vjp
+def rows_major(value):
+    return with_layout_constraint(value, Layout(major_to_minor=(0, 1)))
+
+
+rows_major.defvjp(lambda value: (rows_major(value), None), lambda _, grad: (rows_major(grad),))
+
+
 def both_halves(value):
+    if value.shape[1] > 128:
+        value = rows_major(value)
     other = lax.ppermute(value, "row", [(0, 1), (1, 0)])
+    if value.shape[1] > 128:
+        other = rows_major(other)
     first = lax.axis_index("row") == 0
     return jnp.concatenate(
         [jnp.where(first, value, other), jnp.where(first, other, value)], axis=0
@@ -417,7 +430,7 @@
     return back * (2 * (chips - 1 - place) + 1) + (1 - back) * (2 * place)
 
 
-def seq_gather_kernel(shards, parts, x_ref, out_ref, ring_send, ring_recv, pair_send, pair_recv, own_sem):
+def ring_gather_loop(shards, parts, x_ref, out_ref, ring_send, ring_recv, pair_send, pair_recv, work):
     row, me = lax.axis_index("row"), lax.axis_index("seq")
     chips = shards // 2
     core = me % 2
@@ -429,67 +442,227 @@
     right, left, twin = (row, device(place + 1)), (row, device(place - 1)), (row, me + 1 - 2 * core)
     greet([right, left, twin])
     rows = x_ref.shape[0] // (2 * parts)
-
-    def cut(way, part):
-        return pl.ds((way * parts + part) * rows, rows)
-
-    own = pltpu.make_async_copy(x_ref, out_ref.at[me], own_sem)
-    own.start()
-    started = []
-
-    def send(src, dst, send_sem, recv_sem, to):
-        copy = pltpu.make_async_remote_copy(
-            src_ref=src, dst_ref=dst, send_sem=send_sem, recv_sem=recv_sem,
-            device_id=to, device_id_type=MESH,
+    paths = [(way, part) for part in range(parts) for way in range(2)]
+
+    def piece(way, part, step):
+        source = device(place - 1 - step if way == 0 else place + 1 + step)
+        return out_ref.at[source, pl.ds((way * parts + part) * rows, rows)]
+
+    def ring(way, part, step):
+        here = piece(way, part, step - 1)
+        return pltpu.make_async_remote_copy(
+            src_ref=here, dst_ref=here, send_sem=ring_send.at[way, part, step],
+            recv_sem=ring_recv.at[way, part, step], device_id=(right, left)[way], device_id_type=MESH,
         )
-        copy.start()
-        started.append(copy)
-        return copy
-
-    paths = [(way, part) for part in range(parts) for way in range(2)]
-    flights = {}
+
+    def pair(way, part, step):
+        here = piece(way, part, step - 1)
+        return pltpu.make_async_remote_copy(
+            src_ref=here, dst_ref=here, send_sem=pair_send.at[way, part, step],
+            recv_sem=pair_recv.at[way, part, step], device_id=twin, device_id_type=MESH,
+        )
+
+    out_ref[me] = x_ref[...]
     for way, part in paths:
-        flights[way, part] = send(
-            x_ref.at[cut(way, part)], out_ref.at[me, cut(way, part)],
-            ring_send.at[way, part, 0], ring_recv.at[way, part, 0], (right, left)[way],
-        )
-    pairs = [send(x_ref, out_ref.at[me], pair_send.at[0, 0, chips - 1], pair_recv.at[0, 0, chips - 1], twin)]
-    for step in range(chips - 1):
+        ring(way, part, 0).start()
+    for way, part in paths:
+        pair(way, part, 0).start()
+
+    def body(step, carry):
+        @pl.when(step < chips - 1)
+        def _():
+            for way, part in paths:
+                ring(way, part, step).wait_recv()
+
+                @pl.when(step < chips - 2)
+                def _():
+                    ring(way, part, step + 1).start()
+
+                pair(way, part, step + 1).start()
+
         for way, part in paths:
-            flights[way, part].wait_recv()
-            source = device(place - 1 - step if way == 0 else place + 1 + step)
-            here = out_ref.at[source, cut(way, part)]
-            if step < chips - 2:
-                flights[way, part] = send(
-                    here, here, ring_send.at[way, part, step + 1],
-                    ring_recv.at[way, part, step + 1], (right, left)[way],
-                )
-            pairs.append(
-                send(here, here, pair_send.at[way, part, step], pair_recv.at[way, part, step], twin)
-            )
-    own.wait()
-    for copy in started:
-        copy.wait_send()
-    for copy in pairs:
-        copy.wait_recv()
+            pair(way, part, step).wait_recv()
+        work(step, place)
+        return carry
+
+    lax.fori_loop(0, chips, body, 0)
+
+    def finish(step, carry):
+        for way, part in paths:
+            pair(way, part, step).wait_send()
+
+            @pl.when(step < chips - 1)
+            def _():
+                ring(way, part, step).wait_send()
+
+        return carry
+
+    lax.fori_loop(0, chips, finish, 0)
+
+
+def ring_semaphores(chips, parts):
+    ring = pltpu.SemaphoreType.DMA((2, parts, chips - 1))
+    pair = pltpu.SemaphoreType.DMA((2, parts, chips))
+    return [ring, ring, pair, pair]
+
+
+def seq_gather_kernel(shards, parts, x_ref, out_ref, *sems):
+    ring_gather_loop(shards, parts, x_ref, out_ref, *sems, lambda step, place: None)
+
+
+def fits_vmem(*shapes):
+    return sum(padded_bytes(shape, 2) for shape in shapes) < 48 * MIB
 
 
 def ring_seq_gather(block, collective_id, parts=2):
     shards = lax.axis_size("seq")
-    chips = shards // 2
     rows, width = block.shape
-    ring = pltpu.SemaphoreType.DMA((2, parts, chips - 1))
-    pair = pltpu.SemaphoreType.DMA((2, parts, chips))
+    if not fits_vmem((shards * rows, width)):
+        return lax.all_gather(block, "seq", axis=0, tiled=True)
     gathered = pl.pallas_call(
         functools.partial(seq_gather_kernel, shards, parts),
         out_shape=jax.ShapeDtypeStruct((shards, rows, width), block.dtype),
-        in_specs=[ANY],
-        out_specs=ANY,
-        scratch_shapes=[ring, ring, pair, pair, pltpu.SemaphoreType.DMA],
-        compiler_params=pltpu.CompilerParams(collective_id=collective_id, has_side_effects=True),
+        in_specs=[VMEM],
+        out_specs=VMEM,
+        scratch_shapes=ring_semaphores(shards // 2, parts),
+        compiler_params=pltpu.CompilerParams(
+            collective_id=collective_id, has_side_effects=True, vmem_limit_bytes=56 * MIB
+        ),
         cost_estimate=takes(40),
     )(block)
     return gathered.reshape(shards * rows, width)
+
+
+def gather_ffn_kernel(
+    shards, parts, x_ref, cot_ref, gate_ref, up_ref, down_ref,
+    out_ref, act_ref, d_gate_ref, d_up_ref, *sems,
+):
+    chips = shards // 2
+    rows = x_ref.shape[0]
+    half = rows // 2
+
+    def work(step, place):
+        back, ahead = ring_chip(place - step, chips) * 2, ring_chip(place + step, chips) * 2
+        spots = [(back, 0), (back + 1, 0), (ahead, half), (ahead + 1, half)]
+        starts = [pl.multiple_of(index * rows + first, half) for index, first in spots]
+        tokens = jnp.concatenate([out_ref[index, pl.ds(first, half), :] for index, first in spots], axis=0)
+        cot = jnp.concatenate([cot_ref[pl.ds(start, half), :] for start in starts], axis=0)
+        gate = jnp.dot(tokens, gate_ref[...], preferred_element_type=WIDE)
+        up = jnp.dot(tokens, up_ref[...], preferred_element_type=WIDE)
+        d_act = lax.dot_general(
+            cot, down_ref[...], (((1,), (1,)), ((), ())), preferred_element_type=WIDE
+        )
+        share = 1.0 / (1.0 + jnp.exp(-gate))
+        passed = gate * share
+        results = (
+            (act_ref, passed * up),
+            (d_gate_ref, d_act * up * (share * (1.0 + gate * (1.0 - share)))),
+            (d_up_ref, d_act * passed),
+        )
+        for ref, value in results:
+            value = value.astype(SIXTEEN)
+            for i, start in enumerate(starts):
+                ref[pl.ds(start, half), :] = value[i * half : (i + 1) * half]
+
+    ring_gather_loop(shards, parts, x_ref, out_ref, *sems, work)
+
+
+def gather_ffn(block, cotangent, w_gate, w_up, w_down, collective_id, parts=2):
+    shards = lax.axis_size("seq")
+    rows, width = block.shape
+    units = w_gate.shape[1]
+    if not fits_vmem((shards * rows, width), (shards * rows, width), (3 * shards * rows, units)):
+        second = ring_seq_gather(block, collective_id)
+        gate, up = dot_last(second, w_gate), dot_last(second, w_up)
+        act, pull = jax.vjp(glu_piece, gate, up)
+        d_gate, d_up = pull(dot_back(cotangent, w_down))
+        return second, act.astype(SIXTEEN), d_gate.astype(SIXTEEN), d_up.astype(SIXTEEN)
+    hidden = jax.ShapeDtypeStruct((shards * rows, units), SIXTEEN)
+    outs = pl.pallas_call(
+        functools.partial(gather_ffn_kernel, shards, parts),
+        out_shape=[jax.ShapeDtypeStruct((shards, rows, width), SIXTEEN), hidden, hidden, hidden],
+        in_specs=[VMEM] * 5,
+        out_specs=[VMEM] * 4,
+        scratch_shapes=ring_semaphores(shards // 2, parts),
+        compiler_params=pltpu.CompilerParams(
+            collective_id=collective_id, has_side_effects=True, vmem_limit_bytes=56 * MIB
+        ),
+        cost_estimate=takes(45),
+    )(block, cotangent, w_gate, w_up, w_down)
+    return (outs[0].reshape(shards * rows, width),) + tuple(outs[1:])
+
+
+def gather_beside_kernel(
+    shards, parts, x_ref, second_ref, cot_ref, act_ref, d_gate_ref, d_up_ref, down_ref,
+    out_ref, g_gate_ref, g_up_ref, g_down_ref, product_ref, *sems,
+):
+    chips = shards // 2
+    width = second_ref.shape[1]
+    block = 256
+    turns = width // block
+    share = act_ref.shape[0] // chips
+
+    def tn_dot(left, right):
+        return lax.dot_general(
+            left, right, (((0,), (0,)), ((), ())), preferred_element_type=WIDE
+        ).astype(SIXTEEN)
+
+    def columns(cut):
+        tokens = second_ref[:, cut]
+        g_gate_ref[cut, :] = tn_dot(tokens, d_gate_ref[...])
+        g_up_ref[cut, :] = tn_dot(tokens, d_up_ref[...])
+        g_down_ref[:, cut] = tn_dot(act_ref[...], cot_ref[:, cut])
+
+    def work(step, place):
+        @pl.when(step < turns)
+        def _():
+            columns(pl.ds(pl.multiple_of(step * block, block), block))
+
+        @pl.when(step == turns)
+        def _():
+            columns(slice(turns * block, width))
+
+        here = pl.ds(pl.multiple_of(step * share, share), share)
+        product_ref[here, :] = jnp.dot(
+            act_ref[here, :], down_ref[...], preferred_element_type=WIDE
+        ).astype(SIXTEEN)
+
+    ring_gather_loop(shards, parts, x_ref, out_ref, *sems, work)
+
+
+def gather_beside_ffn(block, second, cotangent, act, d_gate, d_up, w_down, collective_id, parts=2):
+    shards = lax.axis_size("seq")
+    rows, width = block.shape
+    length, units = act.shape
+    chips = shards // 2
+    if width // 256 >= chips or not fits_vmem(
+        (4 * length, width), (3 * length, units), (3 * width, units)
+    ):
+        return (
+            ring_seq_gather(block, collective_id),
+            dot_weight(second, d_gate).astype(SIXTEEN),
+            dot_weight(second, d_up).astype(SIXTEEN),
+            dot_weight(act, cotangent).astype(SIXTEEN),
+            dot_last(act, w_down).astype(SIXTEEN),
+        )
+    outs = pl.pallas_call(
+        functools.partial(gather_beside_kernel, shards, parts),
+        out_shape=[
+            jax.ShapeDtypeStruct((shards, rows, width), SIXTEEN),
+            jax.ShapeDtypeStruct((width, units), SIXTEEN),
+            jax.ShapeDtypeStruct((width, units), SIXTEEN),
+            jax.ShapeDtypeStruct((units, width), SIXTEEN),
+            jax.ShapeDtypeStruct((length, width), SIXTEEN),
+        ],
+        in_specs=[VMEM] * 7,
+        out_specs=[VMEM] * 5,
+        scratch_shapes=ring_semaphores(shards // 2, parts),
+        compiler_params=pltpu.CompilerParams(
+            collective_id=collective_id, has_side_effects=True, vmem_limit_bytes=60 * MIB
+        ),
+        cost_estimate=takes(45),
+    )(block, second, cotangent, act, d_gate, d_up, w_down)
+    return (outs[0].reshape(shards * rows, width),) + tuple(outs[1:])
 
 
 def product_scatter_kernel(shards, parts, turned, *refs):
@@ -1192,10 +1365,11 @@
     normed = ring_seq_gather(normed_own, 1)
     cotangent_later = cotangent
     if staged:
-        normed, both, cotangent_later = tie(normed, both, cotangent)
+        normed, both, cotangent_later, ffn_later = tie(normed, both, cotangent, ffn_params)
         (w_in, w_dt, q_rows, x_rows, out_rows), pull_parts = jax.vjp(mixer_parts, both)
         w_x, pull_x = jax.vjp(x_from, x_rows)
         by_heads, pull_rows = jax.vjp(heads_cut, q_rows)
+        ffn_columns, pull_ffn_columns = jax.vjp(partial(to_columns, width=FF), ffn_later)
     else:
         (w_qkv, w_in, w_x, w_dt, w_out), pull_mixer = jax.vjp(mixer_shards_whole, mixer_params)
         (w_gate, w_up, w_down), pull_ffn = jax.vjp(ffn_shards_whole, ffn_params)
@@ -1218,8 +1392,9 @@
     delta, delta_pull = jax.vjp(lambda p, b: softplus_fn(p + b), pre_dt, dt_bias)
     a_neg, a_pull = jax.vjp(lambda a: -jnp.exp(a), a_log)
     if staged:
-        delta, by_heads, out_rows = tie(delta, by_heads, out_rows)
+        delta, by_heads, out_rows, ffn_columns = tie(delta, by_heads, out_rows, ffn_columns)
         w_qkv, pull_heads = jax.vjp(heads_from, by_heads)
+        ffn_both, pull_ffn_both = jax.vjp(both_halves, ffn_columns)
     scan_in = (
         keep_mask,
         padded_lanes(conv_f, lanes),
@@ -1236,21 +1411,17 @@
     ssm_out, gate_pull = jax.vjp(gate_piece, y_scan[:, :channels], conv_f, d_skip, z_in)
 
     if staged:
-        ssm_out, w_qkv, out_rows = tie(ssm_out, w_qkv, out_rows)
+        ssm_out, w_qkv, out_rows, ffn_both = tie(ssm_out, w_qkv, out_rows, ffn_both)
         w_out, pull_out = jax.vjp(out_from, out_rows)
+        (w_gate, w_up, down_rows), pull_ffn_parts = jax.vjp(ffn_parts, ffn_both)
+        w_down, pull_down = jax.vjp(down_from, down_rows)
     own_heads = g_attn.shape[0]
     queries = dot_last(normed, w_qkv[:, :own_heads]).astype(SIXTEEN)
     kv_rows = dot_last(every, w_qkv[:, own_heads:]).astype(SIXTEEN)
-    if staged:
-        queries, w_out, ffn_later = tie(queries, w_out, ffn_params)
-        ffn_columns, pull_ffn_columns = jax.vjp(partial(to_columns, width=FF), ffn_later)
     attn_out, log_total = attend_forward(queries, kv_rows, doc_first)
 
     squares = jnp.stack([jnp.sum(attn_out * attn_out, axis=1), jnp.sum(ssm_out * ssm_out, axis=1)])
     squares = seq_sum_small(squares, 3)
-    if staged:
-        squares, ffn_columns = tie(squares, ffn_columns)
-        ffn_both, pull_ffn_both = jax.vjp(both_halves, ffn_columns)
     scale_a = lax.rsqrt(squares[0] / (HEADS * HEAD) + norm_eps)[:, None]
     scale_m = lax.rsqrt(squares[1] / INNER + norm_eps)[:, None]
     mixed = 0.5 * jnp.concatenate(
@@ -1259,31 +1430,19 @@
     mixed = mixed.astype(SIXTEEN)
     hidden = tokens_f + product_scatter([(mixed, w_out, False)], 4)
 
-    if staged:
-        hidden, ffn_both = tie(hidden, ffn_both)
-        (w_gate, w_up, down_rows), pull_ffn_parts = jax.vjp(ffn_parts, ffn_both)
-        w_down, pull_down = jax.vjp(down_from, down_rows)
     second_f, second_pull = jax.vjp(rms_norm, hidden, g_two)
-    second = ring_seq_gather(second_f.astype(SIXTEEN), 5)
-    gate_pre = dot_last(second, w_gate)
-    up_pre = dot_last(second, w_up)
-    act_f, act_pull = jax.vjp(glu_piece, gate_pre, up_pre)
-    act = act_f.astype(SIXTEEN)
-    d_gate, d_up = act_pull(dot_back(cotangent_all, w_down))
-    d_gate, d_up = d_gate.astype(SIXTEEN), d_up.astype(SIXTEEN)
+    second, act, d_gate, d_up = gather_ffn(
+        second_f.astype(SIXTEEN), cotangent_all, w_gate, w_up, w_down, 5
+    )
     d_second = product_scatter([(d_gate, w_gate, True), (d_up, w_up, True)], 6)
-    block_out = (hidden + scatter_seq(dot_last(act, w_down))).astype(SIXTEEN)
     d_hidden, grad_g_two = second_pull(d_second)
     d_hidden = d_hidden + cotangent.astype(WIDE)
 
-    d_branch = ring_seq_gather(d_hidden.astype(SIXTEEN), 7)
-    grads_ffn = hold(
-        (
-            dot_weight(second, d_gate).astype(SIXTEEN),
-            dot_weight(second, d_up).astype(SIXTEEN),
-            dot_weight(act, cotangent_all).astype(SIXTEEN),
-        )
-    )
+    d_branch, grad_gate, grad_up, grad_down, down_product = gather_beside_ffn(
+        d_hidden.astype(SIXTEEN), second, cotangent_all, act, d_gate, d_up, w_down, 7
+    )
+    grads_ffn = (grad_gate, grad_up, grad_down)
+    block_out = (hidden + scatter_seq(down_product)).astype(SIXTEEN)
     grad_out = hold(dot_weight(mixed, d_branch).astype(SIXTEEN))
     if staged:
         (d_down_rows,) = pull_down(grads_ffn[2])

time: 1260 us -> 1160 us (0.921)
  matrix products: 124 us -> 66.1 us
  waiting for transfers between devices: 49.1 us -> 11.8 us
  Pallas kernels: 607 us -> 637 us
  local copies, waits for them, and re-layouts: 274 us -> 253 us
    pallas_call x3 -> x1, Pallas kernels: 169 us -> 43.2 us  [ring_seq_gather(): pl.pallas_call(functools.partial(seq_gather_kernel, shards, parts), out_s...]
    pallas_call x0 -> x2, Pallas kernels: none -> 100 us  [the longest x1 52 us: gather_beside_ffn(): pl.pallas_call(functools.partial(gather_beside_kernel, shards, parts), ou...]
    all_to_all x14, waiting for transfers between devices: 48.9 us -> 11.1 us  [exchange(): return lax.all_to_all(value, 'seq', 0, 0)]
    pallas_call x2, Pallas kernels: 70.3 us -> 103 us  [seq_sum(): pl.pallas_call(functools.partial(seq_sum_kernel, bits), out_shape=jax.Sha...]
    dot_general x8 -> x5, matrix products: 48.8 us -> 24.6 us  [dot_weight(): return jnp.einsum('...k,...n->kn', left, grads, preferred_element_type=WIDE)]
    dot_general x6 -> x3, matrix products: 41.5 us -> 18.7 us  [dot_last(): return jnp.einsum('...k,kn->...n', left, right, preferred_element_type=WIDE)]
    dot_general x4 -> x3, matrix products: 28.1 us -> 16.7 us  [dot_back(): jnp.einsum('...n,kn->...k', grads, right, preferred_element_type=WIDE)]
    unnamed x248 -> x272, local copies, waits for them, and re-layouts: 30.2 us -> 32.9 us
  transfers between devices with their start and end apart: 20 -> 20, of which waited for: 2 -> 1; matrix products, arithmetic and copies ran while one was open for 28% -> 28% of each run, Pallas kernels for 45% -> 42%
where the time goes in v4:
time: 1160 us
  Pallas kernels  637 us (55%)
  local copies, waits for them, and re-layouts  253 us (22%)
  other arithmetic  86.7 us (7%)
  starting transfers between devices  84.1 us (7%)
  matrix products  66.1 us (6%)
  between operations  16.7 us (1%)
  waiting for transfers between devices  11.8 us (1%)
    pallas_call x3, Pallas kernels, product_scatter(): pl.pallas_call(functools.partial(product_scatter_kernel, shards, parts, t...  155 us
    pallas_call x2, Pallas kernels, seq_sum(): pl.pallas_call(functools.partial(seq_sum_kernel, bits), out_shape=jax.Sha...  103 us
    all_to_all x14, starting transfers between devices, exchange(): return lax.all_to_all(value, 'seq', 0, 0)  78.8 us
    pallas_call x1, Pallas kernels, gather_beside_ffn(): pl.pallas_call(functools.partial(gather_beside_kernel, shards, parts), ou...  52 us
    pallas_call x1, Pallas kernels, push_gather(): pl.pallas_call(functools.partial(push_gather_kernel, rows, shards), out_s...  51.2 us
    pallas_call x1, Pallas kernels, gather_ffn(): pl.pallas_call(functools.partial(gather_ffn_kernel, shards, parts), out_s...  48.3 us
    pallas_call x1, Pallas kernels, ring_seq_gather(): pl.pallas_call(functools.partial(seq_gather_kernel, shards, parts), out_s...  43.2 us
    pallas_call x1, Pallas kernels, scan_backward(): pl.pallas_call(scan_backward_kernel, grid=(blocks,), in_specs=[pl.BlockSp...  40.2 us
  transfers between devices with their start and end apart: 20, of which 1 were waited for; matrix products, arithmetic and copies ran while one was open for 28% of the time, Pallas kernels for 42%

profile of v4, /device:TPU:0, one launch (start us, length us, event | category | flops | bytes accessed | tf_op | source)
XLA Modules:
  0.0 1155.6 jit_solution(6779890806572452844)
XLA Ops:
  13.6 8.1 all-to-all-start
  22.8 51.2 %shard_map.118 = bf16[32,80,128]{2,1,0:T(8,128)(2,1)} custom-call(bf16[80,128]{1,0:T(8,128)(2,1)} %maximum_maximum_fusion.x_ref), custom_call_target="tpu_custom_call" | custom-call | bytes 70000000 | tf_op jit(solution)/shard_map/pallas_call | solution.py:938
  95.7 43.2 %shard_map.119 = bf16[16,128,1600]{2,1,0:T(8,128)(2,1)} custom-call(bf16[128,1600]{1,0:T(8,128)(2,1)} %get-tuple-element.62.x_ref), custom_call_target="tpu_custom_call" | custom-call | bytes 140000000 | tf_op jit(solution)/shard_map/pallas_call | solution.py:522
  150.4 4.2 all-to-all-start.1
  163.8 6.0 all-to-all-start.2
  169.8 8.4 convolution_convert_fusion
  186.5 11.1 all-to-all-done.2
  197.6 8.2 all-to-all-start.3
  217.3 7.5 fusion.16
  227.1 64.0 %shard_map.120 = bf16[144,2048]{1,0:T(8,128)(2,1)S(1)} custom-call(f32[144,2048]{1,0:T(8,128)S(1)} %fusion.41.x_ref), custom_call_target="tpu_custom_call" | custom-call | bytes 105000000 | tf_op jit(solution)/shard_map/pallas_call | solution.py:856
  312.5 4.8 all-to-all-start.4
  321.9 23.1 %shard_map.121 = (f32[2048,256]{1,0:T(8,128)}, f32[16,16,256]{2,1,0:T(8,128)}) custom-call(f32[2048]{0:T(1024)} %get-tuple-element.239.keep_ref, f32[2048,256]{1,0:T(8,128)} %pad.146.conv_ref, f32[2048,256]{1,0:T(8,128)} %pad.152.delta_ref, bf16[32,2048]{1,0:T(8,128)(2,1)} %slice.270.bc_ref, f32[16,256]{1,0:T(8,128)} %pad.153.a_ref), custom_call_target="tpu_custom_call" | custom-call | bytes 84000000 | tf_op jit(solution)/shard_map/pallas_call | solution.py:1183
  345.0 4.4 fusion.18
  359.8 5.3 fusion.2
  368.8 6.0 all-to-all-start.5
  379.8 5.0 convolution_convert_fusion.4.refs_1_
  384.8 23.2 %shard_map.122 = (f32[2048,128]{1,0:T(8,128)S(1)}, f32[16,2,128]{2,1,0:T(2,128)S(1)}) custom-call(s32[16,1,128]{2,1,0:T(1,128)S(1)} %broadcast_maximum_fusion.refs_0_, bf16[2048,128]{1,0:T(8,128)(2,1)S(1)} %convolution_convert_fusion.4.refs_1_, bf16[3072,256]{1,0:T(8,128)(2,1)S(1)} %copy-done.3, bf16[256,3072]{1,0:T(8,128)(2,1)S(1)} %pad_bitcast_fusion.refs_3_, ...), custom_call_target="tpu_custom_call" | custom-call | bytes 84000000 | tf_op jit(solution)/shard_map/pallas_call | solution.py:1093
  409.4 13.5 %shard_map.123 = f32[32,128]{1,0:T(8,128)} custom-call(f32[32,128]{1,0:T(8,128)} %reshape.604.x_ref), custom_call_target="tpu_custom_call" | custom-call | bytes 42000000 | tf_op jit(solution)/shard_map/pallas_call | solution.py:901
  427.9 4.6 all-to-all-start.6
  442.3 55.2 %shard_map.124 = f32[128,1600]{1,0:T(8,128)} custom-call(bf16[2048,328]{1,0:T(8,128)(2,1)} %fusion.3.refs_0_, bf16[328,1600]{1,0:T(8,128)(2,1)} %reshape.607.refs_1_), custom_call_target="tpu_custom_call" | custom-call | bytes 140000000 | tf_op jit(solution)/shard_map/pallas_call | solution.py:782
  512.0 48.3 %shard_map.125 = (bf16[16,128,1600]{2,1,0:T(8,128)(2,1)}, bf16[2048,344]{1,0:T(8,128)(2,1)}, bf16[2048,344]{1,0:T(8,128)(2,1)}, bf16[2048,344]{1,0:T(8,128)(2,1)}) custom-call(bf16[128,1600]{1,0:T(8,128)(2,1)} %multiply_convert_fusion.x_ref, bf16[2048,1600]{1,0:T(8,128)(2,1)} %all-gather.2.cloned.1.call-done.cot_ref, ...), custom_call_target="tpu_custom_call" | custom-call | bytes 157500000 | tf_op jit(solution)/shard_map/pallas_call | solution.py:581
  560.3 47.6 %shard_map.126 = f32[128,1600]{1,0:T(8,128)} custom-call(bf16[2048,344]{1,0:T(8,128)(2,1)} %get-tuple-element.80.refs_0_.d_gate_ref, bf16[2048,344]{1,0:T(8,128)(2,1)} %get-tuple-element.81.refs_1_.d_up_ref, bf16[1600,344]{1,0:T(8,128)(2,1)} %get-tuple-element.201.gate_ref.refs_2_, bf16[1600,344]{1,0:T(8,128)(2,1)} %get-tuple-element.200.up_ref.refs_3_), custom_call_target="tpu_custom_call" | custom-call | bytes 140000000 | tf_op jit(solution)/shard_map/pallas_call | solution.py:782
  611.0 52.0 %shard_map.127 = (bf16[16,128,1600]{2,1,0:T(8,128)(2,1)}, bf16[1600,344]{1,0:T(8,128)(2,1)}, bf16[1600,344]{1,0:T(8,128)(2,1)}, bf16[344,1600]{1,0:T(8,128)(2,1)}, bf16[2048,1600]{1,0:T(8,128)(2,1)}) custom-call(bf16[128,1600]{1,0:T(8,128)(2,1)} %fusion.58.x_ref, bf16[2048,1600]{1,0:T(8,128)(2,1)} %bitcast.240, ...), custom_call_target="tpu_custom_call" | custom-call | bytes 157500000 | tf_op jit(solution)/shard_map/pallas_call | solution.py:648
  676.6 6.3 convolution_multiply_fusion
  687.6 21.9 %shard_map.128 = f32[32,128]{1,0:T(8,128)} custom-call(f32[32,128]{1,0:T(8,128)} %reshape.613.x_ref), custom_call_target="tpu_custom_call" | custom-call | bytes 42000000 | tf_op jit(solution)/shard_map/pallas_call | solution.py:901
  712.9 4.1 select_add_fusion
  721.4 6.1 convolution_convert_fusion.2
  732.4 4.4 all-to-all-start.8
  739.1 25.9 %shard_map.129 = (bf16[2048,128]{1,0:T(8,128)(2,1)S(1)}, f32[3072,256]{1,0:T(8,128)}, f32[128,256]{1,0:T(8,128)S(1)}) custom-call(s32[16,1,128]{2,1,0:T(1,128)S(1)} %broadcast_maximum_fusion.refs_0_, bf16[2048,128]{1,0:T(8,128)(2,1)S(1)} %copy-done.6, bf16[3072,256]{1,0:T(8,128)(2,1)S(1)} %copy-done.4, bf16[256,3072]{1,0:T(8,128)(2,1)} %copy-done.2, ...), custom_call_target="tpu_custom_call" | custom-call | bytes 84000000 | tf_op jit(solution)/shard_map/pallas_call | solution.py:1115
  771.7 4.4 add_add_fusion
  778.9 6.3 all-to-all-start.9
  785.2 6.4 multiply_reduce_fusion
  791.7 5.7 convolution_convert_fusion.3
  797.4 5.2 fusion.4
  806.1 40.2 %shard_map.130 = (f32[2048,256]{1,0:T(8,128)S(1)}, f32[2048,256]{1,0:T(8,128)S(1)}, f32[32,2048]{1,0:T(8,128)S(1)}, f32[16,256]{1,0:T(8,128)S(1)}) custom-call(f32[2048]{0:T(1024)S(1)} %copy-done.10, f32[2048,256]{1,0:T(8,128)S(1)} %copy-done, f32[2048,256]{1,0:T(8,128)S(1)} %copy-done.1, bf16[32,2048]{1,0:T(8,128)(2,1)S(1)} %copy-done.7, ...), custom_call_target="tpu_custom_call" | custom-call | bytes 140000000 | tf_op jit(solution)/shard_map/pallas_call | solution.py:1293
  850.6 4.3 reshape.621
  854.9 4.5 reshape.622
  861.7 6.1 all-to-all-start.10
  890.3 38.9 %shard_map.131 = bf16[144,2048]{1,0:T(8,128)(2,1)S(1)} custom-call(f32[144,2048]{1,0:T(8,128)S(1)} %select_maximum_fusion.x_ref), custom_call_target="tpu_custom_call" | custom-call | bytes 105000000 | tf_op jit(solution)/shard_map/pallas_call | solution.py:856
  931.7 5.4 all-to-all-start.12
  943.4 9.2 multiply_reduce_fusion.4
  956.9 6.4 all-to-all-start.11
  963.3 7.4 convolution_convert_fusion.1
  973.4 4.1 reshape.632
  992.4 5.3 concatenate.92
  1018.7 51.8 %shard_map.132 = f32[128,1600]{1,0:T(8,128)} custom-call(bf16[2048,400]{1,0:T(8,128)(2,1)} %pad_maximum_fusion.9.refs_0_, bf16[2048,384]{1,0:T(8,128)(2,1)} %pad_maximum_fusion.12.refs_1_, bf16[1600,400]{1,0:T(8,128)(2,1)} %reshape.581.refs_2_, bf16[1600,384]{1,0:T(8,128)(2,1)} %copy-done.35), custom_call_target="tpu_custom_call" | custom-call | bytes 140000000 | tf_op jit(solution)/shard_map/pallas_call | solution.py:782
  1076.6 4.5 all-to-all-start.13
  1095.7 36.9 %shard_map.133 = f32[80,128]{1,0:T(8,128)S(1)} custom-call(bf16[32,80,128]{2,1,0:T(8,128)(2,1)S(1)} %pad_maximum_fusion.18.x_ref), custom_call_target="tpu_custom_call" | custom-call | bytes 70000000 | tf_op jit(solution)/shard_map/pallas_call | solution.py:973
  (577 shorter events, 312.7 us)
Async XLA Ops:
  13.6 67.3 %all-to-all-start = ((bf16[16,869,50]{1,2,0:T(8,128)(2,1)}), bf16[16,869,50]{1,2,0:T(8,128)(2,1)}, u32[]{:S(2)}, u32[]{:S(2)}) async-start(bf16[16,869,50]{1,2,0:T(8,128)(2,1)} %bitcast.5), calls=%async_computation | async-start | bytes 3211264 | tf_op jit(solution)/shard_map/jvp()/all_to_all | solution.py:138
  21.9 57.3 %copy-start.22 = (bf16[1,128,1600]{2,1,0:T(8,128)(2,1)}, bf16[1,128,1600]{2,1,0:T(8,128)(2,1)S(1)}, u32[]{:S(2)}) copy-start(bf16[1,128,1600]{2,1,0:T(8,128)(2,1)S(1)} %copy.505) | copy-start | bytes 1228804
  79.2 530.8 %copy-start.71 = (f32[1600]{0:T(1024)}, f32[1600]{0:T(1024)S(1)}, u32[]{:S(2)}) copy-start(f32[1600]{0:T(1024)S(1)} %get-tuple-element.185) | copy-start | bytes 19204
  86.4 52.5 %collective-permute-start = (bf16[13904,50]{0,1:T(8,128)(2,1)S(1)}, bf16[13904,50]{0,1:T(8,128)(2,1)}, u32[]{:S(2)}, u32[]{:S(2)}) collective-permute-start(bf16[13904,50]{0,1:T(8,128)(2,1)S(1)} %reshape.577), channel_id=1, source_target_pairs={{0,16},{16,0},{1,17},{17,1},{2,18},{18,2},{3,19},{19,3},{4,20},{20... | collective-permute-start | bytes 4171208 | tf_op jit(solution)/shard_map/jvp()/ppermute | solution.py:160
  90.8 48.1 %copy-start.77 = (s32[16,128]{1,0:T(8,128)}, s32[16,128]{1,0:T(8,128)S(1)}, u32[]{:S(2)}) copy-start(s32[16,128]{1,0:T(8,128)S(1)} %reduce-window.9) | copy-start | bytes 24580
  93.7 45.3 %copy-start.73 = (f32[200,24]{0,1:T(8,128)}, f32[200,24]{0,1:T(8,128)S(1)}, u32[]{:S(2)}) copy-start(f32[200,24]{0,1:T(8,128)S(1)} %reshape.580) | copy-start | bytes 57604
  93.8 45.1 %copy-start.98 = (s32[16]{0:T(128)}, s32[16]{0:T(128)S(1)}, u32[]{:S(2)}) copy-start(s32[16]{0:T(128)S(1)} %slice_reduce_fusion.4) | copy-start | bytes 196
  95.7 121.5 %copy-start.83 = (f32[2048]{0:T(1024)}, f32[2048]{0:T(1024)S(1)}, u32[]{:S(2)}) copy-start(f32[2048]{0:T(1024)S(1)} %get-tuple-element.240) | copy-start | bytes 24580
  150.4 13.4 %all-to-all-start.1 = ((bf16[16,2,900]{2,1,0:T(2,128)(2,1)}), bf16[16,2,900]{2,1,0:T(2,128)(2,1)}, u32[]{:S(2)}, u32[]{:S(2)}) async-start(bf16[16,2,900]{2,1,0:T(2,128)(2,1)} %reshape.672), calls=%async_computation.1 | async-start | bytes 131072 | tf_op jit(solution)/shard_map/jvp()/all_to_all | solution.py:138
  154.6 357.4 %all-gather.2.cloned.1.call-start = ((), (), s32[]{:S(2)}) async-start(), calls=%async_computation.15 | async-start | bytes 7241728 | tf_op jit(solution)/shard_map/all_gather | solution.py:394
  163.8 33.8 %all-to-all-start.2 = ((bf16[16,280,50]{1,2,0:T(8,128)(2,1)}), bf16[16,280,50]{1,2,0:T(8,128)(2,1)}, u32[]{:S(2)}, u32[]{:S(2)}) async-start(bf16[16,280,50]{1,2,0:T(8,128)(2,1)} %pad_maximum_fusion.17), calls=%async_computation.2 | async-start | bytes 1376256 | tf_op jit(solution)/shard_map/jvp()/all_to_all | solution.py:138
  186.5 20.4 %copy-start.31 = (bf16[27808,50]{0,1:T(8,128)(2,1)S(1)}, bf16[27808,50]{0,1:T(8,128)(2,1)}, u32[]{:S(2)}) copy-start(bf16[27808,50]{0,1:T(8,128)(2,1)} %copy-done.30) | copy-start | bytes 8342404
  197.6 104.9 %all-to-all-start.3 = ((bf16[16,150,344]{2,1,0:T(8,128)(2,1)}), bf16[16,150,344]{2,1,0:T(8,128)(2,1)}, u32[]{:S(2)}, u32[]{:S(2)}) async-start(bf16[16,150,344]{2,1,0:T(8,128)(2,1)} %copy.525), calls=%async_computation.3 | async-start | bytes 3735552 | tf_op jit(solution)/shard_map/jvp()/all_to_all | solution.py:138
  224.8 120.2 %copy-start.17 = (bf16[2048,200]{1,0:T(8,128)(2,1)}, bf16[2048,200]{1,0:T(8,128)(2,1)S(1)}, u32[]{:S(2)}) copy-start(bf16[2048,200]{1,0:T(8,128)(2,1)S(1)} %get-tuple-element.66) | copy-start | bytes 2457604
  226.4 64.7 %copy-start.58 = (bf16[100,200]{1,0:T(8,128)(2,1)S(1)}, bf16[100,200]{1,0:T(8,128)(2,1)}, u32[]{:S(2)}) copy-start(bf16[100,200]{1,0:T(8,128)(2,1)} %reshape.588) | copy-start | bytes 120004
  226.4 64.7 %copy-start.111 = (f32[200,1]{0,1:T(1,128)S(1)}, f32[200,1]{0,1:T(1,128)}, u32[]{:S(2)}) copy-start(f32[200,1]{0,1:T(1,128)} %get-tuple-element.231) | copy-start | bytes 2404
  226.6 67.8 %copy-start.65 = (bf16[200,132]{1,0:T(8,128)(2,1)}, bf16[200,132]{1,0:T(8,128)(2,1)S(1)}, u32[]{:S(2)}) copy-start(bf16[200,132]{1,0:T(8,128)(2,1)S(1)} %reshape.587) | copy-start | bytes 158404
  309.3 40.1 %collective-permute-start.1 = (bf16[2400,344]{0,1:T(8,128)(2,1)}, bf16[2400,344]{0,1:T(8,128)(2,1)}, u32[]{:S(2)}, u32[]{:S(2)}) collective-permute-start(bf16[2400,344]{0,1:T(8,128)(2,1)} %copy.527), channel_id=1, source_target_pairs={{0,16},{16,0},{1,17},{17,1},{2,18},{18,2},{3,19},{19,3},{4,20},{20... | collective-permute-start | bytes 4953608 | tf_op jit(solution)/shard_map/jvp()/ppermute | solution.py:160
  312.5 44.7 %all-to-all-start.4 = ((bf16[16,100,384]{2,1,0:T(8,128)(2,1)}), bf16[16,100,384]{2,1,0:T(8,128)(2,1)}, u32[]{:S(2)}, u32[]{:S(2)}) async-start(bf16[16,100,384]{2,1,0:T(8,128)(2,1)} %copy.526), calls=%async_computation.4 | async-start | bytes 2555904 | tf_op jit(solution)/shard_map/jvp()/all_to_all | solution.py:138
  321.9 23.1 %copy-start.91 = (f32[200,1]{0,1:T(1,128)S(1)}, f32[200,1]{0,1:T(1,128)}, u32[]{:S(2)}) copy-start(f32[200,1]{0,1:T(1,128)} %get-tuple-element.230) | copy-start | bytes 2404
  368.8 59.1 %all-to-all-start.5 = ((bf16[16,656,50]{1,2,0:T(8,128)(2,1)}), bf16[16,656,50]{1,2,0:T(8,128)(2,1)}, u32[]{:S(2)}, u32[]{:S(2)}) async-start(bf16[16,656,50]{1,2,0:T(8,128)(2,1)} %copy.532), calls=%async_computation.5 | async-start | bytes 2752512 | tf_op jit(solution)/shard_map/jvp()/all_to_all | solution.py:138
  384.8 23.6 %copy-start.5 = (bf16[2048,128]{1,0:T(8,128)(2,1)}, bf16[2048,128]{1,0:T(8,128)(2,1)S(1)}, u32[]{:S(2)}) copy-start(bf16[2048,128]{1,0:T(8,128)(2,1)S(1)} %convolution_convert_fusion.4.refs_1_) | copy-start | bytes 1572868
  384.8 23.6 %copy-start.12 = (f32[2048,200]{1,0:T(8,128)S(1)}, f32[2048,200]{1,0:T(8,128)}, u32[]{:S(2)}) copy-start(f32[2048,200]{1,0:T(8,128)} %fusion.18) | copy-start | bytes 4915204
  427.9 72.0 %all-to-all-start.6 = ((bf16[16,100,344]{2,1,0:T(8,128)(2,1)}), bf16[16,100,344]{2,1,0:T(8,128)(2,1)}, u32[]{:S(2)}, u32[]{:S(2)}) async-start(bf16[16,100,344]{2,1,0:T(8,128)(2,1)} %reshape.608), calls=%async_computation.6 | async-start | bytes 2555904 | tf_op jit(solution)/shard_map/jvp()/all_to_all | solution.py:138
  442.3 55.2 %copy-start.23 = (bf16[1,128,1600]{2,1,0:T(8,128)(2,1)S(1)}, bf16[1,128,1600]{2,1,0:T(8,128)(2,1)}, u32[]{:S(2)}) copy-start(bf16[1,128,1600]{2,1,0:T(8,128)(2,1)} %copy-done.22) | copy-start | bytes 1228804
  498.9 111.1 %copy-start.19 = (f32[128,1600]{1,0:T(8,128)}, f32[128,1600]{1,0:T(8,128)S(1)}, u32[]{:S(2)}) copy-start(f32[128,1600]{1,0:T(8,128)S(1)} %get-tuple-element.195) | copy-start | bytes 2457604
  498.9 111.1 %copy-start.93 = (f32[128]{0:T(128)}, f32[128]{0:T(128)S(1)}, u32[]{:S(2)}) copy-start(f32[128]{0:T(128)S(1)} %fusion.53) | copy-start | bytes 1540
  560.3 49.7 %copy-start.41 = (bf16[1,128,1600]{2,1,0:T(8,128)(2,1)S(1)}, bf16[1,128,1600]{2,1,0:T(8,128)(2,1)}, u32[]{:S(2)}) copy-start(bf16[1,128,1600]{2,1,0:T(8,128)(2,1)} %copy.508) | copy-start | bytes 1228804
  610.0 53.0 %copy-start.115 = (f32[128]{0:T(128)}, f32[128]{0:T(128)S(1)}, u32[]{:S(2)}) copy-start(f32[128]{0:T(128)S(1)} %multiply_multiply_fusion.10) | copy-start | bytes 1540
  672.7 37.5 %all-to-all-start.7 = ((bf16[16,100,344]{2,1,0:T(8,128)(2,1)}), bf16[16,100,344]{2,1,0:T(8,128)(2,1)S(1)}, u32[]{:S(2)}, u32[]{:S(2)}) async-start(bf16[16,100,344]{2,1,0:T(8,128)(2,1)} %copy.536), calls=%async_computation.8 | async-start | bytes 2555904 | tf_op jit(solution)/shard_map/transpose(jvp())/all_to_all | solution.py:138
  720.9 46.9 %collective-permute-start.2 = (bf16[2400,344]{0,1:T(8,128)(2,1)}, bf16[2400,344]{0,1:T(8,128)(2,1)}, u32[]{:S(2)}, u32[]{:S(2)}) collective-permute-start(bf16[2400,344]{0,1:T(8,128)(2,1)} %copy.539), channel_id=1, source_target_pairs={{16,0},{0,16},{17,1},{1,17},{18,2},{2,18},{19,3},{3,19},{20,4},{4,... | collective-permute-start | bytes 4953608 | tf_op jit(solution)/shard_map/transpose(jvp())/ppermute | solution.py:160
  732.4 43.7 %all-to-all-start.8 = ((bf16[16,656,50]{1,2,0:T(8,128)(2,1)}), bf16[16,656,50]{1,2,0:T(8,128)(2,1)}, u32[]{:S(2)}, u32[]{:S(2)}) async-start(bf16[16,656,50]{1,2,0:T(8,128)(2,1)} %bitcast.55), calls=%async_computation.9 | async-start | bytes 2752512 | tf_op jit(solution)/shard_map/transpose(jvp())/all_to_all | solution.py:138
  778.9 68.7 %all-to-all-start.9 = ((bf16[16,150,344]{2,1,0:T(8,128)(2,1)}), bf16[16,150,344]{2,1,0:T(8,128)(2,1)}, u32[]{:S(2)}, u32[]{:S(2)}) async-start(bf16[16,150,344]{2,1,0:T(8,128)(2,1)} %reshape.620), calls=%async_computation.10 | async-start | bytes 3735552 | tf_op jit(solution)/shard_map/transpose(jvp())/all_to_all | solution.py:138
  861.7 67.5 %all-to-all-start.10 = ((bf16[16,100,384]{2,1,0:T(8,128)(2,1)}), bf16[16,100,384]{2,1,0:T(8,128)(2,1)}, u32[]{:S(2)}, u32[]{:S(2)}) async-start(bf16[16,100,384]{2,1,0:T(8,128)(2,1)} %reshape.623), calls=%async_computation.11 | async-start | bytes 2555904 | tf_op jit(solution)/shard_map/transpose(jvp())/all_to_all | solution.py:138
  867.8 264.9 %reduce-scatter.2.cloned.1.call-start = ((), (), s32[]{:S(2)}) async-start(), calls=%async_computation.16 | async-start | bytes 7241728 | tf_op jit(solution)/shard_map/reduce_scatter | solution.py:398
  890.2 39.0 %copy-start.18 = (bf16[2048,200]{1,0:T(8,128)(2,1)S(1)}, bf16[2048,200]{1,0:T(8,128)(2,1)}, u32[]{:S(2)}) copy-start(bf16[2048,200]{1,0:T(8,128)(2,1)} %copy-done.17) | copy-start | bytes 2457604
  931.7 25.2 %all-to-all-start.12 = ((bf16[16,2,900]{2,1,0:T(2,128)(2,1)}), bf16[16,2,900]{2,1,0:T(2,128)(2,1)S(1)}, u32[]{:S(2)}, u32[]{:S(2)}) async-start(bf16[16,2,900]{2,1,0:T(2,128)(2,1)} %reshape.674), calls=%async_computation.13 | async-start | bytes 131072 | tf_op jit(solution)/shard_map/transpose(jvp())/all_to_all | solution.py:138
  956.9 28.9 %all-to-all-start.11 = ((bf16[16,280,50]{1,2,0:T(8,128)(2,1)}), bf16[16,280,50]{1,2,0:T(8,128)(2,1)}, u32[]{:S(2)}, u32[]{:S(2)}) async-start(bf16[16,280,50]{1,2,0:T(8,128)(2,1)} %bitcast.64), calls=%async_computation.12 | async-start | bytes 1376256 | tf_op jit(solution)/shard_map/transpose(jvp())/all_to_all | solution.py:138
  1001.3 69.2 %collective-permute-start.3 = (bf16[13904,50]{0,1:T(8,128)(2,1)}, bf16[13904,50]{0,1:T(8,128)(2,1)}, u32[]{:S(2)}, u32[]{:S(2)}) collective-permute-start(bf16[13904,50]{0,1:T(8,128)(2,1)} %select_add_fusion.1), channel_id=1, source_target_pairs={{16,0},{0,16},{17,1},{1,17},{18,2},{2,18},{19,3},{3,19},{20,4},{4,... | collective-permute-start | bytes 4171208 | tf_op jit(solution)/shard_map/transpose(jvp())/ppermute | solution.py:160
  1018.7 51.8 %copy-start.16 = (bf16[27808,50]{0,1:T(8,128)(2,1)S(1)}, bf16[27808,50]{0,1:T(8,128)(2,1)}, u32[]{:S(2)}) copy-start(bf16[27808,50]{0,1:T(8,128)(2,1)} %concatenate.92) | copy-start | bytes 8342404
  1076.6 64.5 %all-to-all-start.13 = ((bf16[16,869,50]{1,2,0:T(8,128)(2,1)}), bf16[16,869,50]{1,2,0:T(8,128)(2,1)}, u32[]{:S(2)}, u32[]{:S(2)}) async-start(bf16[16,869,50]{1,2,0:T(8,128)(2,1)} %copy.574), calls=%async_computation.14 | async-start | bytes 3211264 | tf_op jit(solution)/shard_map/transpose(jvp())/all_to_all | solution.py:138
  1087.1 45.6 %copy-start.118 = (f32[128]{0:T(128)S(1)}, f32[128]{0:T(128)}, u32[]{:S(2)}) copy-start(f32[128]{0:T(128)} %copy-done.117) | copy-start | bytes 1540
  1087.1 45.7 %copy-start.20 = (f32[128,1600]{1,0:T(8,128)S(1)}, f32[128,1600]{1,0:T(8,128)}, u32[]{:S(2)}) copy-start(f32[128,1600]{1,0:T(8,128)} %copy-done.19) | copy-start | bytes 2457604
  1087.1 45.7 %copy-start.26 = (f32[128,1600]{1,0:T(8,128)S(1)}, f32[128,1600]{1,0:T(8,128)}, u32[]{:S(2)}) copy-start(f32[128,1600]{1,0:T(8,128)} %shard_map.126) | copy-start | bytes 2457604
  1087.1 45.7 %copy-start.42 = (bf16[1,128,1600]{2,1,0:T(8,128)(2,1)S(1)}, bf16[1,128,1600]{2,1,0:T(8,128)(2,1)}, u32[]{:S(2)}) copy-start(bf16[1,128,1600]{2,1,0:T(8,128)(2,1)} %copy.508) | copy-start | bytes 1228804
  1087.1 45.7 %copy-start.72 = (f32[1600]{0:T(1024)S(1)}, f32[1600]{0:T(1024)}, u32[]{:S(2)}) copy-start(f32[1600]{0:T(1024)} %copy-done.71) | copy-start | bytes 19204
  1087.1 45.7 %copy-start.94 = (f32[128]{0:T(128)S(1)}, f32[128]{0:T(128)}, u32[]{:S(2)}) copy-start(f32[128]{0:T(128)} %copy-done.93) | copy-start | bytes 1540
  1087.1 45.7 %copy-start.116 = (f32[128]{0:T(128)S(1)}, f32[128]{0:T(128)}, u32[]{:S(2)}) copy-start(f32[128]{0:T(128)} %copy-done.115) | copy-start | bytes 1540
  (102 other events, 400.0 us)
Sparse Core Ops, SparseCore 0:
  161.7 111.6 all-gather.1
  872.6 94.2 reduce-scatter.1

commit v5 on v4

--- a/solution.py
+++ b/solution.py
@@ -6,7 +6,6 @@
 import jax.numpy as jnp
 from jax import lax
 from jax.experimental import pallas as pl
-from jax.experimental.layout import Layout, with_layout_constraint
 from jax.experimental.pallas import tpu as pltpu
 from jax.sharding import PartitionSpec as P
 
@@ -146,24 +145,37 @@
     return lax.optimization_barrier(array)
 
 
+def hand_on(array, after):
+    return pl.pallas_call(
+        lambda *refs: None,
+        out_shape=jax.ShapeDtypeStruct(array.shape, array.dtype),
+        in_specs=[ANY, ANY],
+        out_specs=ANY,
+        input_output_aliases={0: 0},
+    )(array, after)
+
+
+def other_row(value):
+    return lax.ppermute(value, "row", [(0, 1), (1, 0)])
+
+
+def in_turn(first_row, one, two):
+    return jnp.where(first_row, one, two), jnp.where(first_row, two, one)
+
+
 @jax.custom_vjp
-def rows_major(value):
-    return with_layout_constraint(value, Layout(major_to_minor=(0, 1)))
-
-
-rows_major.defvjp(lambda value: (rows_major(value), None), lambda _, grad: (rows_major(grad),))
-
-
 def both_halves(value):
-    if value.shape[1] > 128:
-        value = rows_major(value)
-    other = lax.ppermute(value, "row", [(0, 1), (1, 0)])
-    if value.shape[1] > 128:
-        other = rows_major(other)
-    first = lax.axis_index("row") == 0
-    return jnp.concatenate(
-        [jnp.where(first, value, other), jnp.where(first, other, value)], axis=0
-    )
+    first_row = lax.axis_index("row") == 0
+    return jnp.concatenate(in_turn(first_row, value, other_row(value)), axis=0)
+
+
+def both_halves_backward(_, grad):
+    half = grad.shape[0] // 2
+    own, other = in_turn(lax.axis_index("row") == 0, grad[:half], grad[half:])
+    return (own + other_row(other),)
+
+
+both_halves.defvjp(lambda value: (both_halves(value), None), both_halves_backward)
 
 
 @partial(jax.custom_vjp, nondiff_argnums=(1,))
@@ -225,7 +237,12 @@
         both, tuple(math.prod(shape) // width for shape in mixer_layout())
     )
     q_rows = jnp.concatenate(
-        [part_q.reshape(shards, -1, unit), part_kv.reshape(shards, -1, unit)], axis=1
+        [
+            part_q.reshape(shards, -1, unit),
+            part_kv.reshape(shards, -1, unit),
+            x_windows(part_x, shards),
+        ],
+        axis=1,
     )
     per_row = D // width
     head_rows = heads_of(shards) * HEAD
@@ -239,7 +256,6 @@
         part_in.reshape(D, -1),
         part_dt.reshape(DT_RANK, -1),
         q_rows,
-        x_windows(part_x, shards),
         jnp.concatenate([out_heads, out_inner], axis=1),
     )
 
@@ -249,33 +265,37 @@
     rows = D // shards
     by_rows = full_rows(q_rows)
     split = rows * HEADS * HEAD // view_width()
+    end = split + rows * 2 * GROUPS * HEAD // view_width()
     cut = by_head(
         by_rows[:split].reshape(rows, HEADS * HEAD),
-        by_rows[split:].reshape(rows, 2 * GROUPS * HEAD),
+        by_rows[split:end].reshape(rows, 2 * GROUPS * HEAD),
         shards,
     )
-    return cut.transpose(1, 0, 2)
+    return cut.transpose(1, 0, 2), x_from_windows(by_rows[end:], lax.axis_index("seq"))
 
 
 def heads_from(cut):
     return exchange(cut).reshape(D, -1)
 
 
-def x_from(windows):
-    return x_from_windows(full_rows(windows), lax.axis_index("seq"))
-
-
-def out_from(cut):
-    return full_rows(cut).reshape(-1, D)
+def out_from(received):
+    rows = received.shape[1]
+    return hold(received.transpose(1, 0, 2).reshape(rows, -1)).reshape(-1, D)
+
+
+def ffn_blocks(piece):
+    shards = lax.axis_size("seq")
+    return piece.reshape(-1, shards, FF // shards).transpose(1, 0, 2)
 
 
 def ffn_parts(both):
-    w_gate, w_up, part_down = cut_rows(both, (D, D, D))
-    return w_gate, w_up, part_down.reshape(lax.axis_size("seq"), -1, both.shape[1])
+    unit = both.shape[2]
+    w_gate, w_up, part_down = cut_rows(both.reshape(-1, unit), (D, D, D))
+    return w_gate, w_up, part_down.reshape(lax.axis_size("seq"), -1, unit)
 
 
 def down_from(cut):
-    return full_rows(cut).reshape(-1, D)
+    return exchange(cut).transpose(1, 0, 2).reshape(-1, D)
 
 
 def x_turns(shards):
@@ -806,7 +826,8 @@
     return me + (1 - 2 * ((me // (1 << bit)) % 2)) * (1 << bit)
 
 
-def seq_sum_kernel(bits, x_ref, out_ref, total, staged, arrived, send_sem, recv_sem, back_send, back_recv):
+def seq_sum_kernel(bits, waits, x_ref, *refs):
+    out_ref, total, staged, arrived, send_sem, recv_sem, back_send, back_recv = refs[waits:]
     row, me = lax.axis_index("row"), lax.axis_index("seq")
     partners = [(row, partner_of(me, bit)) for bit in range(bits)]
     greet(partners)
@@ -849,14 +870,14 @@
         copy.wait_send()
 
 
-def seq_sum(values, collective_id):
+def seq_sum(values, collective_id, after=()):
     bits = bits_of(lax.axis_size("seq"))
     rows, length = values.shape
     sems = pltpu.SemaphoreType.DMA((bits,))
     return pl.pallas_call(
-        functools.partial(seq_sum_kernel, bits),
+        functools.partial(seq_sum_kernel, bits, len(after)),
         out_shape=jax.ShapeDtypeStruct((rows, length), SIXTEEN),
-        in_specs=[VMEM],
+        in_specs=[VMEM] + [ANY] * len(after),
         out_specs=VMEM,
         scratch_shapes=[
             pltpu.VMEM((rows, length), WIDE),
@@ -868,42 +889,58 @@
             collective_id=collective_id, has_side_effects=True, vmem_limit_bytes=48 * MIB
         ),
         cost_estimate=takes(30),
-    )(values)
-
-
-def seq_sum_small_kernel(bits, x_ref, out_ref, arrived, staged, send_sem, recv_sem):
+    )(values, *after)
+
+
+def seq_sum_small_kernel(groups, x_ref, out_ref, arrived, staged, send_sem, recv_sem):
     row, me = lax.axis_index("row"), lax.axis_index("seq")
-    partners = [(row, partner_of(me, bit)) for bit in range(bits)]
-    greet(partners)
+    phases = []
+    for size, stride in groups:
+        spot = (me // stride) % size
+        phases.append(
+            [(row, me + ((spot + far) % size - spot) * stride) for far in range(1, size)]
+        )
+    greet([peer for peers in phases for peer in peers])
     total = x_ref[...]
-    copies = []
-    for bit in range(bits):
-        staged[bit] = total
-        copy = pltpu.make_async_remote_copy(
-            src_ref=staged.at[bit], dst_ref=arrived.at[bit], send_sem=send_sem.at[bit],
-            recv_sem=recv_sem.at[bit], device_id=partners[bit], device_id_type=MESH,
-        )
-        copy.start()
-        copies.append(copy)
-        copy.wait_recv()
-        total = total + arrived[bit]
+    copies, slot = [], 0
+    for phase, peers in enumerate(phases):
+        staged[phase] = total
+        flights = []
+        for peer in peers:
+            copy = pltpu.make_async_remote_copy(
+                src_ref=staged.at[phase], dst_ref=arrived.at[slot], send_sem=send_sem.at[slot],
+                recv_sem=recv_sem.at[slot], device_id=peer, device_id_type=MESH,
+            )
+            copy.start()
+            flights.append((copy, slot))
+            slot += 1
+        for copy, here in flights:
+            copy.wait_recv()
+            total = total + arrived[here]
+        copies += flights
     out_ref[...] = total
-    for copy in copies:
+    for copy, _ in copies:
         copy.wait_send()
 
 
 def seq_sum_small(values, collective_id):
     bits = bits_of(lax.axis_size("seq"))
+    low = 1 << (bits // 2)
+    groups = ((low, 1), ((1 << bits) // low, low))
+    count = sum(size - 1 for size, _ in groups)
     shape = values.shape
     tiles = values.reshape(-1, 128)
-    sems = pltpu.SemaphoreType.DMA((bits,))
-    slots = pltpu.VMEM((bits,) + tiles.shape, WIDE)
+    sems = pltpu.SemaphoreType.DMA((count,))
     return pl.pallas_call(
-        functools.partial(seq_sum_small_kernel, bits),
+        functools.partial(seq_sum_small_kernel, groups),
         out_shape=jax.ShapeDtypeStruct(tiles.shape, WIDE),
         in_specs=[VMEM],
         out_specs=VMEM,
-        scratch_shapes=[slots, slots, sems, sems],
+        scratch_shapes=[
+            pltpu.VMEM((count,) + tiles.shape, WIDE),
+            pltpu.VMEM((len(groups),) + tiles.shape, WIDE),
+            sems, sems,
+        ],
         compiler_params=pltpu.CompilerParams(collective_id=collective_id, has_side_effects=True),
         cost_estimate=takes(12),
     )(tiles).reshape(shape)
@@ -1004,29 +1041,36 @@
     return (k_pos >= first_row) & (k_pos <= q_pos) & (k_pos > q_pos - REACH * BLOCK)
 
 
-def attend_forward_kernel(heads, first_ref, q_ref, kv_ref, turned_ref, meta_ref, meta_turned_ref, out_ref, total_ref):
-    block = pl.program_id(0)
-    span = pl.ds(pl.multiple_of(block * BLOCK, BLOCK), (REACH + 1) * BLOCK)
-    seen = seen_keys(block, first_ref[0])
-    outs, totals = [], []
-    for h in range(heads):
-        cut = slice(h * HEAD, (h + 1) * HEAD)
-        v_cut = slice((heads + h) * HEAD, (heads + h + 1) * HEAD)
-        query = q_ref[:, cut] * SIXTEEN(HEAD ** (-0.5))
-        near = jnp.where(seen, nt_dot(kv_ref[span, cut], query), -1e30)
-        meta = nt_dot(meta_ref[:, cut], query)
-        top = jnp.maximum(
-            jnp.max(near, axis=0, keepdims=True), jnp.max(meta, axis=0, keepdims=True)
-        )
-        near = jnp.exp(near - top)
-        meta = jnp.exp(meta - top)
-        total = jnp.sum(near, axis=0, keepdims=True) + jnp.sum(meta, axis=0, keepdims=True)
-        out = jnp.dot(turned_ref[v_cut, span], near.astype(SIXTEEN), preferred_element_type=WIDE)
-        out += jnp.dot(meta_turned_ref[v_cut, :], meta.astype(SIXTEEN), preferred_element_type=WIDE)
-        outs.append(out / total)
-        totals.append(top + jnp.log(total))
-    out_ref[...] = jnp.concatenate(outs, axis=0).T
-    total_ref[0] = jnp.concatenate(totals, axis=0)
+PER = 4
+
+
+def attend_forward_kernel(heads, waits, *refs):
+    first_ref, q_ref, kv_ref, turned_ref, meta_ref, meta_turned_ref = refs[:6]
+    out_ref, total_ref = refs[6 + waits : 8 + waits]
+    for sub in range(PER):
+        block = pl.program_id(0) * PER + sub
+        here = slice(sub * BLOCK, (sub + 1) * BLOCK)
+        span = pl.ds(pl.multiple_of(block * BLOCK, BLOCK), (REACH + 1) * BLOCK)
+        seen = seen_keys(block, first_ref[sub])
+        outs, totals = [], []
+        for h in range(heads):
+            cut = slice(h * HEAD, (h + 1) * HEAD)
+            v_cut = slice((heads + h) * HEAD, (heads + h + 1) * HEAD)
+            query = q_ref[here, cut] * SIXTEEN(HEAD ** (-0.5))
+            near = jnp.where(seen, nt_dot(kv_ref[span, cut], query), -1e30)
+            meta = nt_dot(meta_ref[:, cut], query)
+            top = jnp.maximum(
+                jnp.max(near, axis=0, keepdims=True), jnp.max(meta, axis=0, keepdims=True)
+            )
+            near = jnp.exp(near - top)
+            meta = jnp.exp(meta - top)
+            total = jnp.sum(near, axis=0, keepdims=True) + jnp.sum(meta, axis=0, keepdims=True)
+            out = jnp.dot(turned_ref[v_cut, span], near.astype(SIXTEEN), preferred_element_type=WIDE)
+            out += jnp.dot(meta_turned_ref[v_cut, :], meta.astype(SIXTEEN), preferred_element_type=WIDE)
+            outs.append(out / total)
+            totals.append(top + jnp.log(total))
+        out_ref[here, :] = jnp.concatenate(outs, axis=0).T
+        total_ref[sub] = jnp.concatenate(totals, axis=0)
 
 
 def attend_backward_kernel(
@@ -1087,24 +1131,31 @@
     return arrays, specs, count, width
 
 
-def attend_forward(queries, kv_rows, doc_first):
+def attend_forward(queries, kv_rows, doc_first, through=()):
     arrays, specs, count, width = attend_operands(queries, kv_rows, doc_first)
     heads = width // HEAD
+    specs = [
+        pl.BlockSpec((PER, 1, BLOCK), lambda i: (i, 0, 0)),
+        pl.BlockSpec((PER * BLOCK, width), lambda i: (i, 0)),
+    ] + specs[2:]
     return pl.pallas_call(
-        lambda *refs: attend_forward_kernel(heads, *refs),
-        grid=(count,),
-        in_specs=specs,
+        lambda *refs: attend_forward_kernel(heads, len(through), *refs),
+        grid=(count // PER,),
+        in_specs=specs + [ANY] * len(through),
         out_specs=[
-            pl.BlockSpec((BLOCK, width), lambda i: (i, 0)),
-            pl.BlockSpec((1, heads, BLOCK), lambda i: (i, 0, 0)),
-        ],
+            pl.BlockSpec((PER * BLOCK, width), lambda i: (i, 0)),
+            pl.BlockSpec((PER, heads, BLOCK), lambda i: (i, 0, 0)),
+        ]
+        + [ANY] * len(through),
         out_shape=[
             jax.ShapeDtypeStruct(queries.shape, WIDE),
             jax.ShapeDtypeStruct((count, heads, BLOCK), WIDE),
-        ],
+        ]
+        + [jax.ShapeDtypeStruct(x.shape, x.dtype) for x in through],
+        input_output_aliases={6 + i: 2 + i for i in range(len(through))},
         compiler_params=pltpu.CompilerParams(vmem_limit_bytes=48 * MIB),
         cost_estimate=takes(24),
-    )(*arrays)
+    )(*arrays, *through)
 
 
 def attend_backward(queries, kv_rows, doc_first, out, log_total, d_out):
@@ -1130,7 +1181,7 @@
         compiler_params=pltpu.CompilerParams(vmem_limit_bytes=48 * MIB),
         cost_estimate=takes(24),
     )(*arrays, out, log_total, d_out)
-    return d_queries, jnp.concatenate([d_near[REACH * BLOCK :], d_meta], axis=0).astype(SIXTEEN)
+    return d_queries, d_near[REACH * BLOCK :].astype(SIXTEEN), d_meta.astype(SIXTEEN)
 
 
 def step_sum():
@@ -1143,7 +1194,10 @@
     return pltpu.roll(tile, (SPAN - group * SUB) % SPAN, axis=1)
 
 
-def scan_forward_kernel(keep_ref, conv_ref, delta_ref, bc_ref, a_ref, y_ref, start_ref, state_ref):
+def scan_forward_kernel(waits, *refs):
+    keep_ref, conv_ref, delta_ref, bc_ref, a_ref = refs[:5]
+    y_ref, start_ref, kept_ref = refs[5 + waits : 8 + waits]
+    state_ref = refs[-1]
     block = pl.program_id(0)
 
     @pl.when(block == 0)
@@ -1167,6 +1221,7 @@
             keep = keep_ref[block * SPAN + group * SUB + i]
             decay = jnp.exp(delta[i : i + 1, :] * decay_rate) * keep
             state = decay * state + drive[i : i + 1, :] * b_tile[:, i : i + 1]
+            kept_ref[group * SUB + i] = state.astype(SIXTEEN)
             reads.append((state * c_tile[:, i : i + 1]).astype(SIXTEEN))
         y_ref[rows, :] = jnp.dot(
             fold, jnp.concatenate(reads, axis=0), preferred_element_type=WIDE
@@ -1176,12 +1231,13 @@
     state_ref[...] = lax.fori_loop(0, SPAN // SUB, body, state_ref[...], unroll=8)
 
 
-def scan_forward(keep, conv_out, delta, bc_rows, decay_rate):
+def scan_forward(keep, conv_out, delta, bc_rows, decay_rate, after=(), through=()):
     length, lanes = conv_out.shape
+    waits = len(after) + len(through)
     blocks = length // SPAN
     span_spec = pl.BlockSpec((SPAN, lanes), lambda i: (i, 0))
     return pl.pallas_call(
-        scan_forward_kernel,
+        functools.partial(scan_forward_kernel, waits),
         grid=(blocks,),
         in_specs=[
             pl.BlockSpec(memory_space=pltpu.SMEM),
@@ -1189,21 +1245,30 @@
             span_spec,
             pl.BlockSpec((2 * STATE, SPAN), lambda i: (0, i)),
             pl.BlockSpec((STATE, lanes), lambda i: (0, 0)),
-        ],
-        out_specs=[span_spec, pl.BlockSpec((1, STATE, lanes), lambda i: (i, 0, 0))],
+        ]
+        + [ANY] * waits,
+        out_specs=[
+            span_spec,
+            pl.BlockSpec((1, STATE, lanes), lambda i: (i, 0, 0)),
+            pl.BlockSpec((SPAN, STATE, lanes), lambda i: (i, 0, 0)),
+        ]
+        + [ANY] * len(through),
         out_shape=[
             jax.ShapeDtypeStruct((length, lanes), WIDE),
             jax.ShapeDtypeStruct((blocks, STATE, lanes), WIDE),
-        ],
+            jax.ShapeDtypeStruct((length, STATE, lanes), SIXTEEN),
+        ]
+        + [jax.ShapeDtypeStruct(x.shape, x.dtype) for x in through],
+        input_output_aliases={5 + len(after) + i: 3 + i for i in range(len(through))},
         scratch_shapes=[pltpu.VMEM((STATE, lanes), WIDE)],
         cost_estimate=takes(24),
-    )(keep, conv_out, delta, bc_rows, decay_rate)
+    )(keep, conv_out, delta, bc_rows, decay_rate, *after, *through)
 
 
 def scan_backward_kernel(
-    keep_ref, conv_ref, delta_ref, bc_ref, a_ref, start_ref, dy_ref,
+    keep_ref, conv_ref, delta_ref, bc_ref, a_ref, start_ref, kept_ref, dy_ref,
     dconv_ref, ddelta_ref, dbc_ref, da_ref,
-    state_ref, decay_ref, adjoint_ref,
+    adjoint_ref,
 ):
     turn = pl.program_id(0)
     block = pl.num_programs(0) - 1 - turn
@@ -1220,23 +1285,6 @@
     spot = lax.broadcasted_iota(jnp.int32, (STATE, SPAN), 1)
     b_span = bc_ref[:STATE, :].astype(WIDE)
     c_span = bc_ref[STATE:, :].astype(WIDE)
-    state_ref[0] = start_ref[0]
-
-    def ahead(group, state):
-        rows = pl.ds(pl.multiple_of(group * SUB, SUB), SUB)
-        delta = delta_ref[rows, :]
-        drive = delta * conv_ref[rows, :]
-        b_tile = lanes_from(b_span, group)
-        for i in range(SUB):
-            keep = keep_ref[block * SPAN + group * SUB + i]
-            decay = jnp.exp(delta[i : i + 1, :] * decay_rate) * keep
-            state = decay * state + drive[i : i + 1, :] * b_tile[:, i : i + 1]
-            decay_ref[group * SUB + i] = decay
-            state_ref[group * SUB + i + 1] = state
-        return state
-
-    lax.fori_loop(0, SPAN // SUB, ahead, start_ref[0], unroll=16)
-
     def back(step, carry):
         adjoint, da, db, dc = carry
         group = SPAN // SUB - 1 - step
@@ -1247,16 +1295,20 @@
         dy = dy_ref[rows, :]
         b_tile = lanes_from(b_span, group)
         c_tile = lanes_from(c_span, group)
+        before = kept_ref[jnp.maximum(group * SUB - 1, 0)].astype(WIDE)
+        before = jnp.where(group == 0, start_ref[0], before)
+        states = [before] + [kept_ref[group * SUB + i].astype(WIDE) for i in range(SUB)]
         by_c, by_b, by_drive, by_delta = ([None] * SUB for _ in range(4))
         for i in range(SUB - 1, -1, -1):
-            index = group * SUB + i
+            keep = keep_ref[block * SPAN + group * SUB + i]
+            decay = jnp.exp(delta[i : i + 1, :] * decay_rate) * keep
             dy_row = dy[i : i + 1, :]
             total = adjoint + dy_row * c_tile[:, i : i + 1]
-            by_c[i] = (dy_row * state_ref[index + 1]).astype(SIXTEEN)
+            by_c[i] = (dy_row * states[i + 1]).astype(SIXTEEN)
             by_b[i] = (total * drive[i : i + 1, :]).astype(SIXTEEN)
             by_drive[i] = (total * b_tile[:, i : i + 1]).astype(SIXTEEN)
-            adjoint = total * decay_ref[index]
-            rate = adjoint * state_ref[index]
+            adjoint = total * decay
+            rate = adjoint * states[i]
             by_delta[i] = (rate * decay_rate).astype(SIXTEEN)
             da = da + rate * delta[i : i + 1, :]
 
@@ -1284,7 +1336,7 @@
     dbc_ref[...] = jnp.concatenate([db, dc], axis=0)
 
 
-def scan_backward(keep, conv_out, delta, bc_rows, decay_rate, starts, dy):
+def scan_backward(keep, conv_out, delta, bc_rows, decay_rate, starts, kept, dy):
     length, lanes = conv_out.shape
     blocks = length // SPAN
     span_spec = pl.BlockSpec((SPAN, lanes), lambda i: (blocks - 1 - i, 0))
@@ -1300,6 +1352,7 @@
             rows_spec,
             whole,
             pl.BlockSpec((1, STATE, lanes), lambda i: (blocks - 1 - i, 0, 0)),
+            pl.BlockSpec((SPAN, STATE, lanes), lambda i: (blocks - 1 - i, 0, 0)),
             span_spec,
         ],
         out_specs=[span_spec, span_spec, rows_spec, whole],
@@ -1310,13 +1363,11 @@
             jax.ShapeDtypeStruct((STATE, lanes), WIDE),
         ],
         scratch_shapes=[
-            pltpu.VMEM((SPAN + 1, STATE, lanes), WIDE),
-            pltpu.VMEM((SPAN, STATE, lanes), WIDE),
             pltpu.VMEM((STATE, lanes), WIDE),
         ],
         compiler_params=pltpu.CompilerParams(vmem_limit_bytes=32 * MIB),
         cost_estimate=takes(40),
-    )(keep, conv_out, delta, bc_rows, decay_rate, starts, dy)
+    )(keep, conv_out, delta, bc_rows, decay_rate, starts, kept, dy)
 
 
 def padded_lanes(array, lanes):
@@ -1331,20 +1382,11 @@
 def per_device(tokens, doc_ids, meta_tokens, mixer_params, small_params, ffn_params, cotangent):
     tokens, cotangent = tokens[0], cotangent[0]
     small_whole, ids, meta_whole = start_blocks(small_params, doc_ids[0], meta_tokens)
-    (g_one, g_two, g_attn, channel_part), small_pull = jax.vjp(small_shards, small_whole)
+    g_one = small_shards(small_whole)[0]
     rows, shards = lax.axis_size("row"), lax.axis_size("seq")
     staged = weights_fit(mixer_params.shape[0], ffn_params.shape[0], rows, shards)
     if staged:
         columns, pull_columns = jax.vjp(partial(to_columns, width=view_width()), mixer_params)
-    channels = channel_part.shape[0]
-    lanes = -(-channels // 128) * 128
-    g_ssm = channel_part[:, 0]
-    conv_w = channel_part[:, 1 : 1 + CONV].T
-    conv_b = channel_part[:, 1 + CONV]
-    dt_bias = channel_part[:, 2 + CONV]
-    a_log = channel_part[:, 3 + CONV : 3 + CONV + STATE]
-    d_skip = channel_part[:, 3 + CONV + STATE]
-
     length = ids.shape[0]
     positions = jnp.arange(length, dtype=jnp.int32)
     starts = jnp.concatenate([jnp.ones((1,), bool), ids[1:] != ids[:-1]])
@@ -1365,14 +1407,22 @@
     normed = ring_seq_gather(normed_own, 1)
     cotangent_later = cotangent
     if staged:
-        normed, both, cotangent_later, ffn_later = tie(normed, both, cotangent, ffn_params)
-        (w_in, w_dt, q_rows, x_rows, out_rows), pull_parts = jax.vjp(mixer_parts, both)
-        w_x, pull_x = jax.vjp(x_from, x_rows)
-        by_heads, pull_rows = jax.vjp(heads_cut, q_rows)
-        ffn_columns, pull_ffn_columns = jax.vjp(partial(to_columns, width=FF), ffn_later)
+        normed, both, cotangent_later = tie(normed, both, cotangent)
+        (w_in, w_dt, q_rows, out_rows), pull_parts = jax.vjp(mixer_parts, both)
+        (by_heads, w_x), pull_rows = jax.vjp(heads_cut, q_rows)
     else:
         (w_qkv, w_in, w_x, w_dt, w_out), pull_mixer = jax.vjp(mixer_shards_whole, mixer_params)
         (w_gate, w_up, w_down), pull_ffn = jax.vjp(ffn_shards_whole, ffn_params)
+    normed, small_later = tie(normed, small_whole)
+    (_, g_two, g_attn, channel_part), small_pull = jax.vjp(small_shards, small_later)
+    channels = channel_part.shape[0]
+    lanes = -(-channels // 128) * 128
+    g_ssm = channel_part[:, 0]
+    conv_w = channel_part[:, 1 : 1 + CONV].T
+    conv_b = channel_part[:, 1 + CONV]
+    dt_bias = channel_part[:, 2 + CONV]
+    a_log = channel_part[:, 3 + CONV : 3 + CONV + STATE]
+    d_skip = channel_part[:, 3 + CONV + STATE]
     meta_normed = (meta_unit * g_one).astype(SIXTEEN)
     every = jnp.concatenate([normed, meta_normed], axis=0)
     cotangent_all = gather_seq(cotangent_later)
@@ -1383,7 +1433,9 @@
     conv_out, conv_pull = jax.vjp(conv_fn, extended, conv_w, conv_b)
     conv_half = conv_out.astype(SIXTEEN)
     if staged:
-        conv_half, w_x = tie(conv_half, w_x)
+        conv_half, by_heads, w_x, ffn_later = tie(conv_half, by_heads, w_x, ffn_params)
+        w_qkv, pull_heads = jax.vjp(heads_from, by_heads)
+        ffn_cut, pull_ffn_cut = jax.vjp(ffn_blocks, ffn_later)
     conv_f = conv_half.astype(WIDE)
     w_x_rows = jnp.pad(w_x.T, ((0, -w_x.shape[1] % 16), (0, 0)))
     projected = seq_sum(jnp.einsum("nc,tc->nt", w_x_rows, conv_half, preferred_element_type=WIDE), 2)
@@ -1392,9 +1444,9 @@
     delta, delta_pull = jax.vjp(lambda p, b: softplus_fn(p + b), pre_dt, dt_bias)
     a_neg, a_pull = jax.vjp(lambda a: -jnp.exp(a), a_log)
     if staged:
-        delta, by_heads, out_rows, ffn_columns = tie(delta, by_heads, out_rows, ffn_columns)
-        w_qkv, pull_heads = jax.vjp(heads_from, by_heads)
-        ffn_both, pull_ffn_both = jax.vjp(both_halves, ffn_columns)
+        after, through = (w_qkv, cotangent_all), (ffn_cut,)
+    else:
+        after, through = (), ()
     scan_in = (
         keep_mask,
         padded_lanes(conv_f, lanes),
@@ -1402,7 +1454,13 @@
         projected[DT_RANK : DT_RANK + 2 * STATE],
         padded_lanes(a_neg.T, lanes),
     )
-    y_scan, scan_starts = scan_forward(*scan_in)
+    y_scan, scan_starts, scan_states, *through = scan_forward(*scan_in, after, through)
+    if staged:
+        (ffn_cut,) = through
+        ffn_columns, pull_ffn_columns = jax.vjp(exchange, ffn_cut)
+        ffn_both, pull_ffn_both = jax.vjp(both_halves, ffn_columns)
+        (w_gate, w_up, down_rows), pull_ffn_parts = jax.vjp(ffn_parts, ffn_both)
+        w_down, pull_down = jax.vjp(down_from, down_rows)
 
     def gate_piece(y, c, skip, z):
         return (y + skip * c) * silu_fn(z)
@@ -1410,18 +1468,19 @@
     z_in = xz[:, channels:].astype(WIDE)
     ssm_out, gate_pull = jax.vjp(gate_piece, y_scan[:, :channels], conv_f, d_skip, z_in)
 
-    if staged:
-        ssm_out, w_qkv, out_rows, ffn_both = tie(ssm_out, w_qkv, out_rows, ffn_both)
-        w_out, pull_out = jax.vjp(out_from, out_rows)
-        (w_gate, w_up, down_rows), pull_ffn_parts = jax.vjp(ffn_parts, ffn_both)
-        w_down, pull_down = jax.vjp(down_from, down_rows)
     own_heads = g_attn.shape[0]
     queries = dot_last(normed, w_qkv[:, :own_heads]).astype(SIXTEEN)
     kv_rows = dot_last(every, w_qkv[:, own_heads:]).astype(SIXTEEN)
-    attn_out, log_total = attend_forward(queries, kv_rows, doc_first)
+    through = (out_rows.transpose(0, 2, 1),) if staged else ()
+    attn_out, log_total, *through = attend_forward(queries, kv_rows, doc_first, through)
+    if staged:
+        out_received, pull_out_exchange = jax.vjp(exchange, through[0].transpose(0, 2, 1))
 
     squares = jnp.stack([jnp.sum(attn_out * attn_out, axis=1), jnp.sum(ssm_out * ssm_out, axis=1)])
     squares = seq_sum_small(squares, 3)
+    if staged:
+        out_received = hand_on(out_received.transpose(0, 2, 1), squares).transpose(0, 2, 1)
+        w_out, pull_out = jax.vjp(out_from, out_received)
     scale_a = lax.rsqrt(squares[0] / (HEADS * HEAD) + norm_eps)[:, None]
     scale_m = lax.rsqrt(squares[1] / INNER + norm_eps)[:, None]
     mixed = 0.5 * jnp.concatenate(
@@ -1458,13 +1517,13 @@
         )
         (d_ffn_both,) = pull_ffn_parts((grad_gate, grad_up, d_down_rows))
         (d_ffn_columns,) = pull_ffn_both(d_ffn_both)
-        (d_out_rows,) = pull_out(grad_out)
+        (d_out_rows,) = pull_out_exchange(pull_out(grad_out)[0])
     d_attn, grad_g_attn = rms_pull(
         attn_out, scale_a, g_attn, d_mix_a, means[0][:, None] / (HEADS * HEAD)
     )
     d_ssm, grad_g_ssm = rms_pull(ssm_out, scale_m, g_ssm, d_mix_m, means[1][:, None] / INNER)
 
-    d_queries, d_kv = attend_backward(
+    d_queries, d_kv, d_meta_kv = attend_backward(
         queries, kv_rows, doc_first, attn_out, log_total, d_attn
     )
 
@@ -1472,15 +1531,16 @@
         d_queries, d_kv, d_ffn_columns, d_out_rows = tie(
             d_queries, d_kv, d_ffn_columns, d_out_rows
         )
-        (grad_ffn,) = pull_ffn_columns(d_ffn_columns)
-    grad_qkv = jnp.concatenate([dot_weight(normed, d_queries), dot_weight(every, d_kv)], axis=1)
+        (grad_ffn,) = pull_ffn_cut(pull_ffn_columns(d_ffn_columns)[0])
+    grad_kv = dot_weight(normed, d_kv) + dot_weight(meta_normed, d_meta_kv)
+    grad_qkv = jnp.concatenate([dot_weight(normed, d_queries), grad_kv], axis=1)
     grad_qkv = hold(grad_qkv.astype(SIXTEEN))
 
     d_y, d_conv, grad_d_skip, d_z = gate_pull(d_ssm)
     if staged:
         d_y, grad_qkv = tie(d_y, grad_qkv)
     d_conv_scan, d_delta, d_bc, d_rate = scan_backward(
-        *scan_in, scan_starts, padded_lanes(d_y, lanes)
+        *scan_in, scan_starts, scan_states, padded_lanes(d_y, lanes)
     )
     if staged:
         d_conv_scan, d_delta, grad_ffn, grad_qkv = tie(d_conv_scan, d_delta, grad_ffn, grad_qkv)
@@ -1492,25 +1552,26 @@
     grad_dt = jnp.einsum("rt,tc->rc", rank_half, d_pre, preferred_element_type=WIDE)
     d_rank = jnp.einsum("rc,tc->rt", w_dt, d_pre, preferred_element_type=WIDE)
     d_proj = jnp.concatenate([d_rank, d_bc], axis=0)
-    d_proj = seq_sum(jnp.pad(d_proj, ((0, -d_proj.shape[0] % 16), (0, 0))), 10)
+    d_proj = seq_sum(jnp.pad(d_proj, ((0, -d_proj.shape[0] % 16), (0, 0))), 10, (block_out,))
     if staged:
         d_proj, d_by_heads = tie(d_proj, d_by_heads)
-        (d_q_rows,) = pull_rows(d_by_heads)
     d_proj = d_proj[: DT_RANK + 2 * STATE].T
     grad_x = hold(dot_weight(conv_half, d_proj).astype(SIXTEEN))
     if staged:
-        (d_x_rows,) = pull_x(grad_x)
+        (d_q_rows,) = pull_rows((d_by_heads, grad_x))
     d_extended, grad_conv_w, grad_conv_b = conv_pull(d_conv + dot_back(d_proj, w_x))
     d_xz = jnp.concatenate([d_extended[CONV - 1 :], d_z], axis=1).astype(SIXTEEN)
     grad_in = hold(dot_weight(normed, d_xz).astype(SIXTEEN))
     grad_dt = grad_dt.astype(SIXTEEN)
     if staged:
-        (d_both,) = pull_parts((grad_in, grad_dt, d_q_rows, d_x_rows, d_out_rows))
+        (d_both,) = pull_parts((grad_in, grad_dt, d_q_rows, d_out_rows))
         d_xz, d_both = tie(d_xz, d_both)
         (d_columns,) = pull_both(d_both)
-    d_meta = dot_back(d_kv[length:], w_qkv[:, own_heads:])
-    d_qkv = jnp.concatenate([d_queries, d_kv[:length]], axis=1)
-    d_normed = product_scatter([(d_xz, w_in, True), (d_qkv, w_qkv, True)], 11)
+    w_q, w_kv = w_qkv[:, :own_heads], w_qkv[:, own_heads:]
+    d_meta = dot_back(d_meta_kv, w_kv)
+    d_normed = product_scatter(
+        [(d_xz, w_in, True), (d_queries, w_q, True), (d_kv, w_kv, True)], 11
+    )
     if staged:
         d_normed, d_columns = tie(d_normed, d_columns)
         (grad_mixer,) = pull_columns(d_columns)

time: 1160 us -> 1120 us (0.966)
  Pallas kernels: 637 us -> 615 us
    reshape x7 -> x16, local copies, waits for them, and re-layouts: 13.4 us -> 46.6 us  [the longest x3 12.4 us: ffn_blocks(): return piece.reshape(-1, shards, FF // shards).transpose(1, 0, 2)]
    pallas_call x6 -> x7, Pallas kernels: 185 us -> 163 us  [the longest x2 71.4 us: seq_sum(): pl.pallas_call(functools.partial(seq_sum_kernel, bits, len(after)), out_s...]
    add_any x4 -> x0, other arithmetic: 14.2 us -> none  [the longest x2 7.75 us: both_halves(): jnp.where(first, value, other)]
    all_to_all x14 -> x12, starting transfers between devices: 78.8 us -> 72.6 us  [exchange(): return lax.all_to_all(value, 'seq', 0, 0)]
    dot_general x5 -> x6, matrix products: 24.6 us -> 23.7 us  [dot_weight(): return jnp.einsum('...k,...n->kn', left, grads, preferred_element_type=WIDE)]
    unnamed x272 -> x250, local copies, waits for them, and re-layouts: 32.9 us -> 32.7 us
  transfers between devices with their start and end apart: 20 -> 18, of which waited for: 1 -> 2; matrix products, arithmetic and copies ran while one was open for 28% -> 25% of each run, Pallas kernels for 42% -> 40%
where the time goes in v5:
time: 1120 us; the launch traced here: 1110 us
  Pallas kernels  615 us (55%)
  local copies, waits for them, and re-layouts  256 us (23%)
  starting transfers between devices  79.8 us (7%)
  other arithmetic  79.3 us (7%)
  matrix products  62.8 us (6%)
  between operations  16.5 us (1%)
    pallas_call x3, Pallas kernels, product_scatter(): pl.pallas_call(functools.partial(product_scatter_kernel, shards, parts, t...  162 us
    all_to_all x12, starting transfers between devices, exchange(): return lax.all_to_all(value, 'seq', 0, 0)  72.6 us
    pallas_call x2, Pallas kernels, seq_sum(): pl.pallas_call(functools.partial(seq_sum_kernel, bits, len(after)), out_s...  71.4 us
    pallas_call x1, Pallas kernels, gather_beside_ffn(): pl.pallas_call(functools.partial(gather_beside_kernel, shards, parts), ou...  52.3 us
    pallas_call x1, Pallas kernels, push_gather(): pl.pallas_call(functools.partial(push_gather_kernel, rows, shards), out_s...  50.7 us
    pallas_call x1, Pallas kernels, gather_ffn(): pl.pallas_call(functools.partial(gather_ffn_kernel, shards, parts), out_s...  48.8 us
    pallas_call x2, Pallas kernels, seq_sum_small(): pl.pallas_call(functools.partial(seq_sum_small_kernel, groups), out_shape...  45.5 us
    pallas_call x1, Pallas kernels, ring_seq_gather(): pl.pallas_call(functools.partial(seq_gather_kernel, shards, parts), out_s...  43.5 us
  transfers between devices with their start and end apart: 18, of which 2 were waited for; matrix products, arithmetic and copies ran while one was open for 25% of the time, Pallas kernels for 40%

profile of v5, /device:TPU:0, one launch (start us, length us, event | category | flops | bytes accessed | tf_op | source)
XLA Modules:
  0.0 1113.7 jit_solution(1790656690179827998)
XLA Ops:
  13.6 7.5 all-to-all-start
  22.8 50.7 %shard_map.118 = bf16[32,80,128]{2,1,0:T(8,128)(2,1)} custom-call(bf16[80,128]{1,0:T(8,128)(2,1)} %maximum_maximum_fusion.x_ref), custom_call_target="tpu_custom_call" | custom-call | bytes 70000000 | tf_op jit(solution)/shard_map/pallas_call | solution.py:975
  88.2 43.5 %shard_map.119 = bf16[16,128,1600]{2,1,0:T(8,128)(2,1)} custom-call(bf16[128,1600]{1,0:T(8,128)(2,1)} %get-tuple-element.60.x_ref), custom_call_target="tpu_custom_call" | custom-call | bytes 140000000 | tf_op jit(solution)/shard_map/pallas_call | solution.py:542
  147.9 4.5 all-to-all-start.1
  159.1 7.3 convolution_convert_fusion
  188.7 9.4 all-to-all-start.2
  201.9 42.1 %shard_map.121 = bf16[144,2048]{1,0:T(8,128)(2,1)S(1)} custom-call(f32[144,2048]{1,0:T(8,128)S(1)} %fusion.40.x_ref), custom_call_target="tpu_custom_call" | custom-call | bytes 105000000 | tf_op jit(solution)/shard_map/pallas_call | solution.py:877
  248.7 5.2 reshape.594
  257.8 23.8 %shard_map.122 = (f32[2048,256]{1,0:T(8,128)}, f32[16,16,256]{2,1,0:T(8,128)}, bf16[2048,16,256]{2,1,0:T(8,128)(2,1)}, bf16[16,150,344]{2,1,0:T(8,128)(2,1)}) custom-call(f32[2048]{0:T(1024)} %get-tuple-element.232.refs_0_.keep_ref, f32[2048,256]{1,0:T(8,128)} %pad.154.refs_1_.conv_ref, ...), custom_call_target="tpu_custom_call", output_to_operand_aliasing={{3}: (7, {})} | custom-call | bytes 84000000 | tf_op jit(solution)/shard_map/pallas_call | solution.py:1239
  281.6 4.6 all-to-all-start.4
  295.6 5.3 fusion.4
  307.0 5.0 convolution_convert_fusion.4.refs_1_
  312.0 22.4 %shard_map.120 = (f32[2048,128]{1,0:T(8,128)S(1)}, f32[16,2,128]{2,1,0:T(2,128)S(1)}, bf16[16,50,656]{2,1,0:T(8,128)(2,1)S(1)}) custom-call(s32[16,1,128]{2,1,0:T(1,128)S(1)} %broadcast_maximum_fusion.refs_0_, bf16[2048,128]{1,0:T(8,128)(2,1)S(1)} %convolution_convert_fusion.4.refs_1_, ...), custom_call_target="tpu_custom_call", output_to_operand_aliasing={{2}: (6, {})} | custom-call | bytes 84000000 | tf_op jit(solution)/shard_map/pallas_call | solution.py:1141
  336.3 6.0 all-to-all-start.3
  348.3 4.8 multiply_reduce_fusion.7
  353.7 24.1 %shard_map.123 = f32[32,128]{1,0:T(8,128)} custom-call(f32[32,128]{1,0:T(8,128)} %reshape.595.x_ref), custom_call_target="tpu_custom_call" | custom-call | bytes 42000000 | tf_op jit(solution)/shard_map/pallas_call | solution.py:934
  393.4 5.2 reshape.600
  398.7 4.0 fusion.65
  404.9 6.0 all-to-all-start.5
  414.4 61.7 %shard_map.125 = f32[128,1600]{1,0:T(8,128)} custom-call(bf16[2048,328]{1,0:T(8,128)(2,1)} %fusion.7.refs_0_, bf16[328,1600]{1,0:T(8,128)(2,1)} %reshape.599.refs_1_), custom_call_target="tpu_custom_call" | custom-call | bytes 140000000 | tf_op jit(solution)/shard_map/pallas_call | solution.py:802
  481.8 4.2 reshape.658
  488.8 48.8 %shard_map.126 = (bf16[16,128,1600]{2,1,0:T(8,128)(2,1)}, bf16[2048,344]{1,0:T(8,128)(2,1)}, bf16[2048,344]{1,0:T(8,128)(2,1)}, bf16[2048,344]{1,0:T(8,128)(2,1)}) custom-call(bf16[128,1600]{1,0:T(8,128)(2,1)} %multiply_convert_fusion.x_ref, bf16[2048,1600]{1,0:T(8,128)(2,1)} %all-gather.2.cloned.1.call-done.refs_6_.cot_ref, ...), custom_call_target="tpu_custom_call" | custom-call | bytes 157500000 | tf_op jit(solution)/shard_map/pallas_call | solution.py:601
  537.6 47.6 %shard_map.127 = f32[128,1600]{1,0:T(8,128)} custom-call(bf16[2048,344]{1,0:T(8,128)(2,1)} %get-tuple-element.75.refs_0_.d_gate_ref, bf16[2048,344]{1,0:T(8,128)(2,1)} %get-tuple-element.76.refs_1_.d_up_ref, bf16[1600,344]{1,0:T(8,128)(2,1)} %get-tuple-element.196.gate_ref.refs_2_, bf16[1600,344]{1,0:T(8,128)(2,1)} %get-tuple-element.195.up_ref.refs_3_), custom_call_target="tpu_custom_call" | custom-call | bytes 140000000 | tf_op jit(solution)/shard_map/pallas_call | solution.py:802
  588.4 52.3 %shard_map.128 = (bf16[16,128,1600]{2,1,0:T(8,128)(2,1)}, bf16[1600,344]{1,0:T(8,128)(2,1)}, bf16[1600,344]{1,0:T(8,128)(2,1)}, bf16[344,1600]{1,0:T(8,128)(2,1)}, bf16[2048,1600]{1,0:T(8,128)(2,1)}) custom-call(bf16[128,1600]{1,0:T(8,128)(2,1)} %fusion.61.x_ref, bf16[2048,1600]{1,0:T(8,128)(2,1)} %bitcast.250, ...), custom_call_target="tpu_custom_call" | custom-call | bytes 157500000 | tf_op jit(solution)/shard_map/pallas_call | solution.py:668
  644.1 4.5 reshape.607
  651.2 4.4 all-to-all-start.6
  656.4 6.5 convolution_multiply_fusion
  667.5 21.4 %shard_map.129 = f32[32,128]{1,0:T(8,128)} custom-call(f32[32,128]{1,0:T(8,128)} %reshape.605.x_ref), custom_call_target="tpu_custom_call" | custom-call | bytes 42000000 | tf_op jit(solution)/shard_map/pallas_call | solution.py:934
  692.1 5.0 broadcast_select_fusion.2
  704.8 6.6 convolution_convert_fusion.2
  719.6 4.4 all-to-all-start.7
  730.0 26.0 %shard_map.130 = (bf16[2048,128]{1,0:T(8,128)(2,1)S(1)}, f32[3072,256]{1,0:T(8,128)}, f32[128,256]{1,0:T(8,128)S(1)}) custom-call(s32[16,1,128]{2,1,0:T(1,128)S(1)} %broadcast_maximum_fusion.refs_0_, bf16[2048,128]{1,0:T(8,128)(2,1)S(1)} %copy-done.5, bf16[3072,256]{1,0:T(8,128)(2,1)S(1)} %pad.152.clone.refs_2_, bf16[256,3072]{1,0:T(8,128)(2,1)} %pad_bitcast_fusion.refs_3_, ...), custom_call_target="tpu_custom_call" | custom-call | bytes 84000000 | tf_op jit(solution)/shard_map/pallas_call | solution.py:1166
  765.7 8.8 all-to-all-start.8
  774.6 6.9 multiply_reduce_fusion
  781.5 5.8 fusion.72
  793.8 34.9 %shard_map.131 = (f32[2048,256]{1,0:T(8,128)S(1)}, f32[2048,256]{1,0:T(8,128)S(1)}, f32[32,2048]{1,0:T(8,128)S(1)}, f32[16,256]{1,0:T(8,128)S(1)}) custom-call(f32[2048]{0:T(1024)S(1)} %copy-done.11, f32[2048,256]{1,0:T(8,128)S(1)} %copy-done, f32[2048,256]{1,0:T(8,128)S(1)} %copy-done.1, bf16[32,2048]{1,0:T(8,128)(2,1)S(1)} %copy-done.6, ...), custom_call_target="tpu_custom_call" | custom-call | bytes 140000000 | tf_op jit(solution)/shard_map/pallas_call | solution.py:1345
  833.1 5.5 reshape.611
  840.9 6.2 all-to-all-start.9
  868.9 29.3 %shard_map.132 = bf16[144,2048]{1,0:T(8,128)(2,1)S(1)} custom-call(f32[144,2048]{1,0:T(8,128)S(1)} %select_maximum_fusion.x_ref, bf16[128,1600]{1,0:T(8,128)(2,1)S(1)} %add_convert_fusion.refs_0_), custom_call_target="tpu_custom_call" | custom-call | bytes 105000000 | tf_op jit(solution)/shard_map/pallas_call | solution.py:877
  914.1 6.4 all-to-all-start.10
  920.6 8.5 multiply_reduce_fusion.4
  931.0 7.4 convolution_convert_fusion.1
  941.1 4.1 reshape.623
  958.2 5.3 concatenate.84
  976.3 53.0 %shard_map.133 = f32[128,1600]{1,0:T(8,128)} custom-call(bf16[2048,400]{1,0:T(8,128)(2,1)} %pad_maximum_fusion.2.refs_0_, bf16[2048,128]{1,0:T(8,128)(2,1)} %copy-done.7, bf16[2048,256]{1,0:T(8,128)(2,1)} %slice.447.refs_2_, bf16[1600,400]{1,0:T(8,128)(2,1)} %reshape.575.refs_3_, bf16[1600,128]{1,0:T(8,128)(2,1)} %slice.346.refs_4_, ...), custom_call_target="tpu_custom_call" | custom-call | bytes 140000000 | tf_op jit(solution)/shard_map/pallas_call | solution.py:802
  1031.3 3.7 reshape.642
  1037.8 4.5 all-to-all-start.11
  1060.3 33.5 %shard_map.134 = f32[80,128]{1,0:T(8,128)S(1)} custom-call(bf16[32,80,128]{2,1,0:T(8,128)(2,1)S(1)} %pad_maximum_fusion.8.x_ref), custom_call_target="tpu_custom_call" | custom-call | bytes 70000000 | tf_op jit(solution)/shard_map/pallas_call | solution.py:1010
  (548 shorter events, 298.8 us)
Async XLA Ops:
  13.6 67.9 %all-to-all-start = ((bf16[16,869,50]{1,2,0:T(8,128)(2,1)}), bf16[16,869,50]{1,2,0:T(8,128)(2,1)S(1)}, u32[]{:S(2)}, u32[]{:S(2)}) async-start(bf16[16,869,50]{1,2,0:T(8,128)(2,1)} %bitcast.252), calls=%async_computation | async-start | bytes 3211264 | tf_op jit(solution)/shard_map/jvp()/all_to_all | solution.py:137
  21.1 236.7 %all-gather.2.cloned.1.call-start = ((), (), s32[]{:S(2)}) async-start(), calls=%async_computation.13 | async-start | bytes 7241728 | tf_op jit(solution)/shard_map/all_gather | solution.py:414
  21.9 57.9 %copy-start.26 = (bf16[1,128,1600]{2,1,0:T(8,128)(2,1)}, bf16[1,128,1600]{2,1,0:T(8,128)(2,1)S(1)}, u32[]{:S(2)}) copy-start(bf16[1,128,1600]{2,1,0:T(8,128)(2,1)S(1)} %copy.455) | copy-start | bytes 1228804
  85.6 46.1 %collective-permute-start = (bf16[13904,50]{0,1:T(8,128)(2,1)S(1)}, bf16[13904,50]{0,1:T(8,128)(2,1)S(1)}, u32[]{:S(2)}, u32[]{:S(2)}) collective-permute-start(bf16[13904,50]{0,1:T(8,128)(2,1)S(1)} %reshape.570), channel_id=1, source_target_pairs={{0,16},{16,0},{1,17},{17,1},{2,18},{18,2},{3,19},{19,3},{4,20},{20... | collective-permute-start | bytes 4171208 | tf_op jit(solution)/shard_map/jvp()/ppermute | solution.py:159
  136.6 37.3 %copy-start.77 = (f32[2048]{0:T(1024)}, f32[2048]{0:T(1024)S(1)}, u32[]{:S(2)}) copy-start(f32[2048]{0:T(1024)S(1)} %get-tuple-element.233) | copy-start | bytes 24580
  136.6 37.3 %copy-start.79 = (f32[2048]{0:T(1024)}, f32[2048]{0:T(1024)S(1)}, u32[]{:S(2)}) copy-start(f32[2048]{0:T(1024)S(1)} %get-tuple-element.234) | copy-start | bytes 24580
  136.6 37.3 %copy-start.81 = (f32[2048]{0:T(1024)}, f32[2048]{0:T(1024)S(1)}, u32[]{:S(2)}) copy-start(f32[2048]{0:T(1024)S(1)} %get-tuple-element.235) | copy-start | bytes 24580
  136.6 37.3 %copy-start.83 = (f32[2048]{0:T(1024)}, f32[2048]{0:T(1024)S(1)}, u32[]{:S(2)}) copy-start(f32[2048]{0:T(1024)S(1)} %get-tuple-element.236) | copy-start | bytes 24580
  147.9 29.9 %all-to-all-start.1 = ((bf16[16,316,50]{1,2,0:T(8,128)(2,1)}), bf16[16,316,50]{1,2,0:T(8,128)(2,1)}, u32[]{:S(2)}, u32[]{:S(2)}) async-start(bf16[16,316,50]{1,2,0:T(8,128)(2,1)} %pad_maximum_fusion.7), calls=%async_computation.1 | async-start | bytes 1376256 | tf_op jit(solution)/shard_map/jvp()/all_to_all | solution.py:137
  172.9 26.4 %copy-start.70 = (f32[200,24]{0,1:T(8,128)}, f32[200,24]{0,1:T(8,128)S(1)}, u32[]{:S(2)}) copy-start(f32[200,24]{0,1:T(8,128)S(1)} %reshape.574) | copy-start | bytes 57604
  177.8 23.7 %copy-start.23 = (bf16[2048,200]{1,0:T(8,128)(2,1)}, bf16[2048,200]{1,0:T(8,128)(2,1)S(1)}, u32[]{:S(2)}) copy-start(bf16[2048,200]{1,0:T(8,128)(2,1)S(1)} %get-tuple-element.68) | copy-start | bytes 2457604
  185.3 16.1 %copy-start.61 = (bf16[200,132]{1,0:T(8,128)(2,1)}, bf16[200,132]{1,0:T(8,128)(2,1)S(1)}, u32[]{:S(2)}) copy-start(bf16[200,132]{1,0:T(8,128)(2,1)S(1)} %reshape.588) | copy-start | bytes 158404
  188.7 67.0 %all-to-all-start.2 = ((bf16[16,100,384]{2,1,0:T(8,128)(2,1)}), bf16[16,100,384]{2,1,0:T(8,128)(2,1)}, u32[]{:S(2)}, u32[]{:S(2)}) async-start(bf16[16,100,384]{2,1,0:T(8,128)(2,1)} %copy.472), calls=%async_computation.2 | async-start | bytes 2555904 | tf_op jit(solution)/shard_map/jvp()/all_to_all | solution.py:137
  281.6 54.6 %all-to-all-start.4 = ((bf16[16,150,344]{2,1,0:T(8,128)(2,1)}), bf16[16,150,344]{2,1,0:T(8,128)(2,1)}, u32[]{:S(2)}, u32[]{:S(2)}) async-start(bf16[16,150,344]{2,1,0:T(8,128)(2,1)} %get-tuple-element.74), calls=%async_computation.4 | async-start | bytes 3735552 | tf_op jit(solution)/shard_map/jvp()/all_to_all | solution.py:137
  336.3 42.8 %all-to-all-start.3 = ((bf16[16,656,50]{1,2,0:T(8,128)(2,1)}), bf16[16,656,50]{1,2,0:T(8,128)(2,1)}, u32[]{:S(2)}, u32[]{:S(2)}) async-start(bf16[16,656,50]{1,2,0:T(8,128)(2,1)} %bitcast.239), calls=%async_computation.3 | async-start | bytes 2752512 | tf_op jit(solution)/shard_map/jvp()/all_to_all | solution.py:137
  345.3 42.8 %collective-permute-start.1 = (bf16[16,150,344]{2,0,1:T(8,128)(2,1)}, bf16[16,150,344]{2,0,1:T(8,128)(2,1)}, u32[]{:S(2)}, u32[]{:S(2)}) collective-permute-start(bf16[16,150,344]{2,0,1:T(8,128)(2,1)} %copy.483), channel_id=1, source_target_pairs={{0,16},{16,0},{1,17},{17,1},{2,18},{18,2},{3,19},{19,3},{4,20},{20... | collective-permute-start | bytes 4953608 | tf_op jit(solution)/shard_map/jvp()/ppermute | solution.py:159
  347.8 239.5 %copy-start.68 = (f32[1600]{0:T(1024)}, f32[1600]{0:T(1024)S(1)}, u32[]{:S(2)}) copy-start(f32[1600]{0:T(1024)S(1)} %get-tuple-element.175) | copy-start | bytes 19204
  387.3 276.7 %copy-start.72 = (f32[2048]{0:T(1024)}, f32[2048]{0:T(1024)S(1)}, u32[]{:S(2)}) copy-start(f32[2048]{0:T(1024)S(1)} %get-tuple-element.231) | copy-start | bytes 24580
  404.9 74.3 %all-to-all-start.5 = ((bf16[16,100,344]{2,1,0:T(8,128)(2,1)}), bf16[16,100,344]{2,1,0:T(8,128)(2,1)}, u32[]{:S(2)}, u32[]{:S(2)}) async-start(bf16[16,100,344]{2,1,0:T(8,128)(2,1)} %reshape.601), calls=%async_computation.5 | async-start | bytes 2555904 | tf_op jit(solution)/shard_map/jvp()/all_to_all | solution.py:137
  414.4 61.7 %copy-start.27 = (bf16[1,128,1600]{2,1,0:T(8,128)(2,1)S(1)}, bf16[1,128,1600]{2,1,0:T(8,128)(2,1)}, u32[]{:S(2)}) copy-start(bf16[1,128,1600]{2,1,0:T(8,128)(2,1)} %copy-done.26) | copy-start | bytes 1228804
  477.4 109.9 %copy-start.90 = (f32[128]{0:T(128)}, f32[128]{0:T(128)S(1)}, u32[]{:S(2)}) copy-start(f32[128]{0:T(128)S(1)} %fusion.54) | copy-start | bytes 1540
  537.6 47.7 %copy-start.19 = (f32[128,1600]{1,0:T(8,128)S(1)}, f32[128,1600]{1,0:T(8,128)}, u32[]{:S(2)}) copy-start(f32[128,1600]{1,0:T(8,128)} %copy-done.18) | copy-start | bytes 2457604
  537.6 49.7 %copy-start.42 = (bf16[1,128,1600]{2,1,0:T(8,128)(2,1)S(1)}, bf16[1,128,1600]{2,1,0:T(8,128)(2,1)}, u32[]{:S(2)}) copy-start(bf16[1,128,1600]{2,1,0:T(8,128)(2,1)} %copy.458) | copy-start | bytes 1228804
  587.3 53.3 %copy-start.112 = (f32[128]{0:T(128)}, f32[128]{0:T(128)S(1)}, u32[]{:S(2)}) copy-start(f32[128]{0:T(128)S(1)} %multiply_multiply_fusion.10) | copy-start | bytes 1540
  651.2 38.5 %all-to-all-start.6 = ((bf16[16,100,344]{2,1,0:T(8,128)(2,1)}), bf16[16,100,344]{2,1,0:T(8,128)(2,1)}, u32[]{:S(2)}, u32[]{:S(2)}) async-start(bf16[16,100,344]{2,1,0:T(8,128)(2,1)} %bitcast.254), calls=%async_computation.7 | async-start | bytes 2555904 | tf_op jit(solution)/shard_map/transpose(jvp())/all_to_all | solution.py:137
  655.6 212.2 %reduce-scatter.2.cloned.1.call-start = ((), (), s32[]{:S(2)}) async-start(), calls=%async_computation.14 | async-start | bytes 7241728 | tf_op jit(solution)/shard_map/reduce_scatter | solution.py:418
  703.1 56.6 %collective-permute-start.2 = (bf16[16,150,344]{2,0,1:T(8,128)(2,1)}, bf16[16,150,344]{2,0,1:T(8,128)(2,1)}, u32[]{:S(2)}, u32[]{:S(2)}) collective-permute-start(bf16[16,150,344]{2,0,1:T(8,128)(2,1)} %copy.491), channel_id=1, source_target_pairs={{0,16},{16,0},{1,17},{17,1},{2,18},{18,2},{3,19},{19,3},{4,20},{20... | collective-permute-start | bytes 4953608 | tf_op jit(solution)/shard_map/transpose(jvp())/ppermute | solution.py:1461
  719.6 46.2 %all-to-all-start.7 = ((bf16[16,656,50]{1,2,0:T(8,128)(2,1)}), bf16[16,656,50]{1,2,0:T(8,128)(2,1)}, u32[]{:S(2)}, u32[]{:S(2)}) async-start(bf16[16,656,50]{1,2,0:T(8,128)(2,1)} %bitcast.253), calls=%async_computation.8 | async-start | bytes 2752512 | tf_op jit(solution)/shard_map/transpose(jvp())/all_to_all | solution.py:137
  762.9 11.6 %copy-start.17 = (f32[2048,200]{1,0:T(8,128)S(1)}, f32[2048,200]{1,0:T(8,128)}, u32[]{:S(2)}) copy-start(f32[2048,200]{1,0:T(8,128)} %get-tuple-element.186) | copy-start | bytes 4915204
  762.9 11.6 %copy-start.73 = (f32[2048]{0:T(1024)S(1)}, f32[2048]{0:T(1024)}, u32[]{:S(2)}) copy-start(f32[2048]{0:T(1024)} %copy-done.72) | copy-start | bytes 24580
  762.9 11.6 %copy-start.85 = (f32[2048]{0:T(1024)S(1)}, f32[2048]{0:T(1024)}, u32[]{:S(2)}) copy-start(f32[2048]{0:T(1024)} %get-tuple-element.227) | copy-start | bytes 24580
  762.9 11.6 %copy-start.86 = (f32[1,2048]{1,0:T(1,128)S(1)}, f32[1,2048]{1,0:T(1,128)}, u32[]{:S(2)}) copy-start(f32[1,2048]{1,0:T(1,128)} %get-tuple-element.229) | copy-start | bytes 24580
  762.9 11.6 %copy-start.88 = (f32[200,1]{0,1:T(1,128)S(1)}, f32[200,1]{0,1:T(1,128)}, u32[]{:S(2)}) copy-start(f32[200,1]{0,1:T(1,128)} %get-tuple-element.223) | copy-start | bytes 2404
  765.7 64.3 %all-to-all-start.8 = ((bf16[16,150,344]{2,1,0:T(8,128)(2,1)}), bf16[16,150,344]{2,1,0:T(8,128)(2,1)}, u32[]{:S(2)}, u32[]{:S(2)}) async-start(bf16[16,150,344]{2,1,0:T(8,128)(2,1)} %copy_add_fusion), calls=%async_computation.9 | async-start | bytes 3735552 | tf_op jit(solution)/shard_map/transpose(jvp())/all_to_all | solution.py:137
  774.5 13.2 %slice-start = ((s8[6815744]{0:T(1024)(128)(4,1)}), s8[4194304]{0:T(1024)(128)(4,1)S(1)}, s32[]{:S(2)}) async-start(s8[6815744]{0:T(1024)(128)(4,1)} %bitcast.247), calls=%async_computation.15 | async-start | bytes 8388608
  840.9 57.3 %all-to-all-start.9 = ((bf16[16,100,384]{2,1,0:T(8,128)(2,1)}), bf16[16,100,384]{2,1,0:T(8,128)(2,1)}, u32[]{:S(2)}, u32[]{:S(2)}) async-start(bf16[16,100,384]{2,1,0:T(8,128)(2,1)} %reshape.612), calls=%async_computation.10 | async-start | bytes 2555904 | tf_op jit(solution)/shard_map/transpose(jvp())/all_to_all | solution.py:137
  909.6 10.9 copy-start.82
  914.1 37.9 %all-to-all-start.10 = ((bf16[16,316,50]{1,2,0:T(8,128)(2,1)}), bf16[16,316,50]{1,2,0:T(8,128)(2,1)}, u32[]{:S(2)}, u32[]{:S(2)}) async-start(bf16[16,316,50]{1,2,0:T(8,128)(2,1)} %bitcast.259), calls=%async_computation.11 | async-start | bytes 1376256 | tf_op jit(solution)/shard_map/transpose(jvp())/all_to_all | solution.py:137
  967.2 62.1 %collective-permute-start.3 = (bf16[13904,50]{0,1:T(8,128)(2,1)}, bf16[13904,50]{0,1:T(8,128)(2,1)}, u32[]{:S(2)}, u32[]{:S(2)}) collective-permute-start(bf16[13904,50]{0,1:T(8,128)(2,1)} %broadcast_select_fusion.4), channel_id=1, source_target_pairs={{0,16},{16,0},{1,17},{17,1},{2,18},{18,2},{3,19},{19,3},{4,20},{20... | collective-permute-start | bytes 4171208 | tf_op jit(solution)/shard_map/transpose(jvp())/ppermute | solution.py:1406
  976.3 53.1 %copy-start.22 = (bf16[27808,50]{0,1:T(8,128)(2,1)S(1)}, bf16[27808,50]{0,1:T(8,128)(2,1)}, u32[]{:S(2)}) copy-start(bf16[27808,50]{0,1:T(8,128)(2,1)} %concatenate.84) | copy-start | bytes 8342404
  1037.8 61.4 %all-to-all-start.11 = ((bf16[16,869,50]{1,2,0:T(8,128)(2,1)}), bf16[16,869,50]{1,2,0:T(8,128)(2,1)}, u32[]{:S(2)}, u32[]{:S(2)}) async-start(bf16[16,869,50]{1,2,0:T(8,128)(2,1)} %copy.525), calls=%async_computation.12 | async-start | bytes 3211264 | tf_op jit(solution)/shard_map/transpose(jvp())/all_to_all | solution.py:137
  1051.6 42.2 %copy-start.110 = (f32[128]{0:T(128)S(1)}, f32[128]{0:T(128)}, u32[]{:S(2)}) copy-start(f32[128]{0:T(128)} %copy-done.109) | copy-start | bytes 1540
  1051.6 42.3 %copy-start.21 = (f32[128,1600]{1,0:T(8,128)S(1)}, f32[128,1600]{1,0:T(8,128)}, u32[]{:S(2)}) copy-start(f32[128,1600]{1,0:T(8,128)} %copy-done.18) | copy-start | bytes 2457604
  1051.6 42.3 %copy-start.32 = (f32[128,1600]{1,0:T(8,128)S(1)}, f32[128,1600]{1,0:T(8,128)}, u32[]{:S(2)}) copy-start(f32[128,1600]{1,0:T(8,128)} %shard_map.127) | copy-start | bytes 2457604
  1051.6 42.3 %copy-start.43 = (bf16[1,128,1600]{2,1,0:T(8,128)(2,1)S(1)}, bf16[1,128,1600]{2,1,0:T(8,128)(2,1)}, u32[]{:S(2)}) copy-start(bf16[1,128,1600]{2,1,0:T(8,128)(2,1)} %copy.458) | copy-start | bytes 1228804
  1051.6 42.3 %copy-start.69 = (f32[1600]{0:T(1024)S(1)}, f32[1600]{0:T(1024)}, u32[]{:S(2)}) copy-start(f32[1600]{0:T(1024)} %copy-done.68) | copy-start | bytes 19204
  1051.6 42.3 %copy-start.91 = (f32[128]{0:T(128)S(1)}, f32[128]{0:T(128)}, u32[]{:S(2)}) copy-start(f32[128]{0:T(128)} %copy-done.90) | copy-start | bytes 1540
  1051.7 42.3 %copy-start.113 = (f32[128]{0:T(128)S(1)}, f32[128]{0:T(128)}, u32[]{:S(2)}) copy-start(f32[128]{0:T(128)} %copy-done.112) | copy-start | bytes 1540
  (89 other events, 375.5 us)
Sparse Core Ops, SparseCore 0:
  132.6 68.3 all-gather.1
  660.4 105.9 reduce-scatter.1

commit v6 on v5

--- a/solution.py
+++ b/solution.py
@@ -145,14 +145,14 @@
     return lax.optimization_barrier(array)
 
 
-def hand_on(array, after):
+def hand_on(array, *after):
     return pl.pallas_call(
         lambda *refs: None,
         out_shape=jax.ShapeDtypeStruct(array.shape, array.dtype),
-        in_specs=[ANY, ANY],
+        in_specs=[ANY] * (1 + len(after)),
         out_specs=ANY,
         input_output_aliases={0: 0},
-    )(array, after)
+    )(array, *after)
 
 
 def other_row(value):
@@ -169,9 +169,13 @@
     return jnp.concatenate(in_turn(first_row, value, other_row(value)), axis=0)
 
 
+def row_parts(grad):
+    half = grad.shape[0] // 2
+    return in_turn(lax.axis_index("row") == 0, grad[:half], grad[half:])
+
+
 def both_halves_backward(_, grad):
-    half = grad.shape[0] // 2
-    own, other = in_turn(lax.axis_index("row") == 0, grad[:half], grad[half:])
+    own, other = row_parts(grad)
     return (own + other_row(other),)
 
 
@@ -294,8 +298,8 @@
     return w_gate, w_up, part_down.reshape(lax.axis_size("seq"), -1, unit)
 
 
-def down_from(cut):
-    return exchange(cut).transpose(1, 0, 2).reshape(-1, D)
+def down_from(received):
+    return received.transpose(1, 0, 2).reshape(-1, D)
 
 
 def x_turns(shards):
@@ -450,7 +454,9 @@
     return back * (2 * (chips - 1 - place) + 1) + (1 - back) * (2 * place)
 
 
-def ring_gather_loop(shards, parts, x_ref, out_ref, ring_send, ring_recv, pair_send, pair_recv, work):
+def ring_gather_loop(
+    shards, parts, x_ref, out_ref, ring_send, ring_recv, pair_send, pair_recv, work, begin=None
+):
     row, me = lax.axis_index("row"), lax.axis_index("seq")
     chips = shards // 2
     core = me % 2
@@ -487,6 +493,8 @@
         ring(way, part, 0).start()
     for way, part in paths:
         pair(way, part, 0).start()
+    if begin is not None:
+        begin()
 
     def body(step, carry):
         @pl.when(step < chips - 1)
@@ -613,11 +621,18 @@
 
 
 def gather_beside_kernel(
-    shards, parts, x_ref, second_ref, cot_ref, act_ref, d_gate_ref, d_up_ref, down_ref,
-    out_ref, g_gate_ref, g_up_ref, g_down_ref, product_ref, *sems,
+    shards, parts, x_ref, second_any, cot_any, act_ref, d_gate_ref, d_up_ref, down_ref, mixed_ref, w_out_ref,
+    out_ref, g_gate_ref, g_up_ref, g_down_ref, product_ref, d_mixed_ref, g_out_ref,
+    second_ref, cot_ref, total_ref, load_sem, *sems,
 ):
     chips = shards // 2
     width = second_ref.shape[1]
+    rows = x_ref.shape[0]
+    half = rows // 2
+    loads = [
+        pltpu.make_async_copy(second_any, second_ref, load_sem.at[0]),
+        pltpu.make_async_copy(cot_any, cot_ref, load_sem.at[1]),
+    ]
     block = 256
     turns = width // block
     share = act_ref.shape[0] // chips
@@ -633,7 +648,36 @@
         g_up_ref[cut, :] = tn_dot(tokens, d_up_ref[...])
         g_down_ref[:, cut] = tn_dot(act_ref[...], cot_ref[:, cut])
 
+    def begin():
+        for load in loads:
+            load.start()
+
     def work(step, place):
+        @pl.when(step == 0)
+        def _():
+            for load in loads:
+                load.wait()
+
+        back, ahead = ring_chip(place - step, chips) * 2, ring_chip(place + step, chips) * 2
+        spots = [(back, 0), (back + 1, 0), (ahead, half), (ahead + 1, half)]
+        starts = [pl.multiple_of(index * rows + first, half) for index, first in spots]
+        grads = jnp.concatenate([out_ref[index, pl.ds(first, half), :] for index, first in spots], axis=0)
+        mixed = jnp.concatenate([mixed_ref[pl.ds(start, half), :] for start in starts], axis=0)
+        d_mixed = lax.dot_general(
+            grads, w_out_ref[...], (((1,), (1,)), ((), ())), preferred_element_type=WIDE
+        )
+        for i, start in enumerate(starts):
+            d_mixed_ref[pl.ds(start, half), :] = d_mixed[i * half : (i + 1) * half]
+        part = lax.dot_general(mixed, grads, (((0,), (0,)), ((), ())), preferred_element_type=WIDE)
+
+        @pl.when(step == 0)
+        def _():
+            total_ref[...] = part
+
+        @pl.when(step > 0)
+        def _():
+            total_ref[...] += part
+
         @pl.when(step < turns)
         def _():
             columns(pl.ds(pl.multiple_of(step * block, block), block))
@@ -647,23 +691,30 @@
             act_ref[here, :], down_ref[...], preferred_element_type=WIDE
         ).astype(SIXTEEN)
 
-    ring_gather_loop(shards, parts, x_ref, out_ref, *sems, work)
-
-
-def gather_beside_ffn(block, second, cotangent, act, d_gate, d_up, w_down, collective_id, parts=2):
+    ring_gather_loop(shards, parts, x_ref, out_ref, *sems, work, begin)
+    g_out_ref[...] = total_ref[...].astype(SIXTEEN)
+
+
+def gather_beside_ffn(
+    block, second, cotangent, act, d_gate, d_up, w_down, mixed, w_out, collective_id, parts=2
+):
     shards = lax.axis_size("seq")
     rows, width = block.shape
     length, units = act.shape
     chips = shards // 2
     if width // 256 >= chips or not fits_vmem(
-        (4 * length, width), (3 * length, units), (3 * width, units)
+        (4 * length, width), (3 * length, units), (3 * width, units), (4 * mixed.shape[1], width),
+        (3 * length, mixed.shape[1])
     ):
+        gathered = ring_seq_gather(block, collective_id)
         return (
-            ring_seq_gather(block, collective_id),
+            gathered,
             dot_weight(second, d_gate).astype(SIXTEEN),
             dot_weight(second, d_up).astype(SIXTEEN),
             dot_weight(act, cotangent).astype(SIXTEEN),
             dot_last(act, w_down).astype(SIXTEEN),
+            dot_back(gathered, w_out),
+            dot_weight(mixed, gathered).astype(SIXTEEN),
         )
     outs = pl.pallas_call(
         functools.partial(gather_beside_kernel, shards, parts),
@@ -673,15 +724,23 @@
             jax.ShapeDtypeStruct((width, units), SIXTEEN),
             jax.ShapeDtypeStruct((units, width), SIXTEEN),
             jax.ShapeDtypeStruct((length, width), SIXTEEN),
+            jax.ShapeDtypeStruct(mixed.shape, WIDE),
+            jax.ShapeDtypeStruct(w_out.shape, SIXTEEN),
         ],
-        in_specs=[VMEM] * 7,
-        out_specs=[VMEM] * 5,
-        scratch_shapes=ring_semaphores(shards // 2, parts),
+        in_specs=[VMEM, ANY, ANY] + [VMEM] * 6,
+        out_specs=[VMEM] * 7,
+        scratch_shapes=[
+            pltpu.VMEM(second.shape, SIXTEEN),
+            pltpu.VMEM(cotangent.shape, SIXTEEN),
+            pltpu.VMEM(w_out.shape, WIDE),
+            pltpu.SemaphoreType.DMA((2,)),
+        ]
+        + ring_semaphores(chips, parts),
         compiler_params=pltpu.CompilerParams(
             collective_id=collective_id, has_side_effects=True, vmem_limit_bytes=60 * MIB
         ),
         cost_estimate=takes(45),
-    )(block, second, cotangent, act, d_gate, d_up, w_down)
+    )(block, second, cotangent, act, d_gate, d_up, w_down, mixed, w_out)
     return (outs[0].reshape(shards * rows, width),) + tuple(outs[1:])
 
 
@@ -1073,10 +1132,10 @@
         total_ref[sub] = jnp.concatenate(totals, axis=0)
 
 
-def attend_backward_kernel(
-    heads, first_ref, q_ref, kv_ref, turned_ref, meta_ref, meta_turned_ref, out_ref, total_ref, do_ref,
-    dq_ref, dkv_ref, dmeta_ref,
-):
+def attend_backward_kernel(heads, waits, *refs):
+    first_ref, q_ref, kv_ref, turned_ref, meta_ref, meta_turned_ref = refs[:6]
+    out_ref, total_ref, do_ref = refs[6:9]
+    dq_ref, dkv_ref, dmeta_ref = refs[9 + waits : 12 + waits]
     block = pl.program_id(0)
 
     @pl.when(block == 0)
@@ -1158,30 +1217,34 @@
     )(*arrays, *through)
 
 
-def attend_backward(queries, kv_rows, doc_first, out, log_total, d_out):
+def attend_backward(queries, kv_rows, doc_first, out, log_total, d_out, through=()):
     arrays, specs, count, width = attend_operands(queries, kv_rows, doc_first)
     heads = width // HEAD
     near, meta = arrays[2], arrays[4]
     row_spec = pl.BlockSpec((BLOCK, width), lambda i: (i, 0))
-    d_queries, d_near, d_meta = pl.pallas_call(
-        lambda *refs: attend_backward_kernel(heads, *refs),
+    d_queries, d_near, d_meta, *through = pl.pallas_call(
+        lambda *refs: attend_backward_kernel(heads, len(through), *refs),
         grid=(count,),
         in_specs=specs
-        + [row_spec, pl.BlockSpec((1, heads, BLOCK), lambda i: (i, 0, 0)), row_spec],
+        + [row_spec, pl.BlockSpec((1, heads, BLOCK), lambda i: (i, 0, 0)), row_spec]
+        + [ANY] * len(through),
         out_specs=[
             row_spec,
             pl.BlockSpec(near.shape, lambda i: (0, 0)),
             pl.BlockSpec(meta.shape, lambda i: (0, 0)),
-        ],
+        ]
+        + [ANY] * len(through),
         out_shape=[
             jax.ShapeDtypeStruct(queries.shape, SIXTEEN),
             jax.ShapeDtypeStruct(near.shape, WIDE),
             jax.ShapeDtypeStruct(meta.shape, WIDE),
-        ],
+        ]
+        + [jax.ShapeDtypeStruct(x.shape, x.dtype) for x in through],
+        input_output_aliases={9 + i: 3 + i for i in range(len(through))},
         compiler_params=pltpu.CompilerParams(vmem_limit_bytes=48 * MIB),
         cost_estimate=takes(24),
-    )(*arrays, out, log_total, d_out)
-    return d_queries, d_near[REACH * BLOCK :].astype(SIXTEEN), d_meta.astype(SIXTEEN)
+    )(*arrays, out, log_total, d_out, *through)
+    return d_queries, d_near[REACH * BLOCK :].astype(SIXTEEN), d_meta.astype(SIXTEEN), *through
 
 
 def step_sum():
@@ -1265,11 +1328,9 @@
     )(keep, conv_out, delta, bc_rows, decay_rate, *after, *through)
 
 
-def scan_backward_kernel(
-    keep_ref, conv_ref, delta_ref, bc_ref, a_ref, start_ref, kept_ref, dy_ref,
-    dconv_ref, ddelta_ref, dbc_ref, da_ref,
-    adjoint_ref,
-):
+def scan_backward_kernel(waits, *refs):
+    keep_ref, conv_ref, delta_ref, bc_ref, a_ref, start_ref, kept_ref, dy_ref = refs[:8]
+    dconv_ref, ddelta_ref, dbc_ref, da_ref, adjoint_ref = refs[8 + waits :]
     turn = pl.program_id(0)
     block = pl.num_programs(0) - 1 - turn
 
@@ -1336,14 +1397,14 @@
     dbc_ref[...] = jnp.concatenate([db, dc], axis=0)
 
 
-def scan_backward(keep, conv_out, delta, bc_rows, decay_rate, starts, kept, dy):
+def scan_backward(keep, conv_out, delta, bc_rows, decay_rate, starts, kept, dy, after=()):
     length, lanes = conv_out.shape
     blocks = length // SPAN
     span_spec = pl.BlockSpec((SPAN, lanes), lambda i: (blocks - 1 - i, 0))
     rows_spec = pl.BlockSpec((2 * STATE, SPAN), lambda i: (0, blocks - 1 - i))
     whole = pl.BlockSpec((STATE, lanes), lambda i: (0, 0))
     return pl.pallas_call(
-        scan_backward_kernel,
+        functools.partial(scan_backward_kernel, len(after)),
         grid=(blocks,),
         in_specs=[
             pl.BlockSpec(memory_space=pltpu.SMEM),
@@ -1354,7 +1415,8 @@
             pl.BlockSpec((1, STATE, lanes), lambda i: (blocks - 1 - i, 0, 0)),
             pl.BlockSpec((SPAN, STATE, lanes), lambda i: (blocks - 1 - i, 0, 0)),
             span_spec,
-        ],
+        ]
+        + [ANY] * len(after),
         out_specs=[span_spec, span_spec, rows_spec, whole],
         out_shape=[
             jax.ShapeDtypeStruct((length, lanes), WIDE),
@@ -1367,7 +1429,7 @@
         ],
         compiler_params=pltpu.CompilerParams(vmem_limit_bytes=32 * MIB),
         cost_estimate=takes(40),
-    )(keep, conv_out, delta, bc_rows, decay_rate, starts, kept, dy)
+    )(keep, conv_out, delta, bc_rows, decay_rate, starts, kept, dy, *after)
 
 
 def padded_lanes(array, lanes):
@@ -1460,7 +1522,8 @@
         ffn_columns, pull_ffn_columns = jax.vjp(exchange, ffn_cut)
         ffn_both, pull_ffn_both = jax.vjp(both_halves, ffn_columns)
         (w_gate, w_up, down_rows), pull_ffn_parts = jax.vjp(ffn_parts, ffn_both)
-        w_down, pull_down = jax.vjp(down_from, down_rows)
+        down_received, pull_down_exchange = jax.vjp(exchange, down_rows)
+        w_down, pull_down = jax.vjp(down_from, down_received)
 
     def gate_piece(y, c, skip, z):
         return (y + skip * c) * silu_fn(z)
@@ -1497,41 +1560,35 @@
     d_hidden, grad_g_two = second_pull(d_second)
     d_hidden = d_hidden + cotangent.astype(WIDE)
 
-    d_branch, grad_gate, grad_up, grad_down, down_product = gather_beside_ffn(
-        d_hidden.astype(SIXTEEN), second, cotangent_all, act, d_gate, d_up, w_down, 7
+    _, grad_gate, grad_up, grad_down, down_product, d_mixed, grad_out = gather_beside_ffn(
+        d_hidden.astype(SIXTEEN), second, cotangent_all, act, d_gate, d_up, w_down, mixed, w_out, 7
     )
     grads_ffn = (grad_gate, grad_up, grad_down)
     block_out = (hidden + scatter_seq(down_product)).astype(SIXTEEN)
-    grad_out = hold(dot_weight(mixed, d_branch).astype(SIXTEEN))
-    if staged:
-        (d_down_rows,) = pull_down(grads_ffn[2])
-    d_mixed = 0.5 * dot_back(d_branch, w_out)
+    d_mixed = 0.5 * d_mixed
     d_mix_a, d_mix_m = d_mixed[:, :own_heads], d_mixed[:, own_heads:]
     means = jnp.stack(
         [jnp.sum(attn_out * g_attn * d_mix_a, axis=1), jnp.sum(ssm_out * g_ssm * d_mix_m, axis=1)]
     )
     means = seq_sum_small(means, 8)
-    if staged:
-        means, d_down_rows, grad_gate, grad_up = tie(
-            means, d_down_rows, grads_ffn[0], grads_ffn[1]
-        )
-        (d_ffn_both,) = pull_ffn_parts((grad_gate, grad_up, d_down_rows))
-        (d_ffn_columns,) = pull_ffn_both(d_ffn_both)
-        (d_out_rows,) = pull_out_exchange(pull_out(grad_out)[0])
     d_attn, grad_g_attn = rms_pull(
         attn_out, scale_a, g_attn, d_mix_a, means[0][:, None] / (HEADS * HEAD)
     )
     d_ssm, grad_g_ssm = rms_pull(ssm_out, scale_m, g_ssm, d_mix_m, means[1][:, None] / INNER)
 
-    d_queries, d_kv, d_meta_kv = attend_backward(
-        queries, kv_rows, doc_first, attn_out, log_total, d_attn
-    )
-
+    through = ()
     if staged:
-        d_queries, d_kv, d_ffn_columns, d_out_rows = tie(
-            d_queries, d_kv, d_ffn_columns, d_out_rows
-        )
-        (grad_ffn,) = pull_ffn_cut(pull_ffn_columns(d_ffn_columns)[0])
+        d_down_cut = hand_on(pull_down(grad_down)[0], means)
+        (d_down_rows,) = pull_down_exchange(d_down_cut)
+        through = (pull_out(grad_out)[0].transpose(0, 2, 1),)
+    d_queries, d_kv, d_meta_kv, *through = attend_backward(
+        queries, kv_rows, doc_first, attn_out, log_total, d_attn, through
+    )
+
+    if staged:
+        (d_ffn_both,) = pull_ffn_parts((grad_gate, grad_up, d_down_rows))
+        d_ffn_own, d_ffn_other = row_parts(d_ffn_both)
+        (d_out_rows,) = pull_out_exchange(through[0].transpose(0, 2, 1))
     grad_kv = dot_weight(normed, d_kv) + dot_weight(meta_normed, d_meta_kv)
     grad_qkv = jnp.concatenate([dot_weight(normed, d_queries), grad_kv], axis=1)
     grad_qkv = hold(grad_qkv.astype(SIXTEEN))
@@ -1539,12 +1596,13 @@
     d_y, d_conv, grad_d_skip, d_z = gate_pull(d_ssm)
     if staged:
         d_y, grad_qkv = tie(d_y, grad_qkv)
+    after = (d_ffn_other,) if staged else ()
     d_conv_scan, d_delta, d_bc, d_rate = scan_backward(
-        *scan_in, scan_starts, scan_states, padded_lanes(d_y, lanes)
+        *scan_in, scan_starts, scan_states, padded_lanes(d_y, lanes), after
     )
     if staged:
-        d_conv_scan, d_delta, grad_ffn, grad_qkv = tie(d_conv_scan, d_delta, grad_ffn, grad_qkv)
-        (d_by_heads,) = pull_heads(grad_qkv)
+        d_ffn_columns = d_ffn_own + other_row(d_ffn_other)
+        d_out_rows = hand_on(d_out_rows.transpose(0, 2, 1), d_delta).transpose(0, 2, 1)
     d_conv = d_conv + d_conv_scan[:, :channels]
     d_pre, grad_dt_bias = delta_pull(d_delta[:, :channels])
     (grad_a_log,) = a_pull(d_rate[:, :channels].T)
@@ -1554,7 +1612,9 @@
     d_proj = jnp.concatenate([d_rank, d_bc], axis=0)
     d_proj = seq_sum(jnp.pad(d_proj, ((0, -d_proj.shape[0] % 16), (0, 0))), 10, (block_out,))
     if staged:
-        d_proj, d_by_heads = tie(d_proj, d_by_heads)
+        d_proj = hand_on(d_proj, d_ffn_columns)
+        (d_by_heads,) = pull_heads(hand_on(grad_qkv, d_proj))
+        (grad_ffn,) = pull_ffn_cut(pull_ffn_columns(d_ffn_columns)[0])
     d_proj = d_proj[: DT_RANK + 2 * STATE].T
     grad_x = hold(dot_weight(conv_half, d_proj).astype(SIXTEEN))
     if staged:

time: 1120 us -> 1110 us (level)
  local copies, waits for them, and re-layouts: 256 us -> 234 us
  Pallas kernels: 615 us -> 630 us
  matrix products: 62.8 us -> 50.9 us
    pallas_call x3, Pallas kernels: 162 us -> 190 us  [product_scatter(): pl.pallas_call(functools.partial(product_scatter_kernel, shards, parts, t...]
    dot_general x6 -> x5, matrix products: 23.7 us -> 18.6 us  [dot_weight(): return jnp.einsum('...k,...n->kn', left, grads, preferred_element_type=WIDE)]
    unnamed x250 -> x254, local copies, waits for them, and re-layouts: 32.7 us -> 32.4 us
  transfers between devices with their start and end apart: 18 -> 18, of which waited for: 2 -> 2; matrix products, arithmetic and copies ran while one was open for 25% -> 26% of each run, Pallas kernels for 40% -> 42%
where the time goes in v6:
time: 1110 us; the launch traced here: 1100 us
  Pallas kernels  630 us (57%)
  local copies, waits for them, and re-layouts  234 us (21%)
  starting transfers between devices  82.7 us (7%)
  other arithmetic  81.9 us (7%)
  matrix products  50.9 us (5%)
  between operations  16.5 us (1%)
    pallas_call x3, Pallas kernels, product_scatter(): pl.pallas_call(functools.partial(product_scatter_kernel, shards, parts, t...  190 us
    all_to_all x12, starting transfers between devices, exchange(): return lax.all_to_all(value, 'seq', 0, 0)  76.9 us
    pallas_call x2, Pallas kernels, seq_sum(): pl.pallas_call(functools.partial(seq_sum_kernel, bits, len(after)), out_s...  71 us
    pallas_call x1, Pallas kernels, gather_beside_ffn(): pl.pallas_call(functools.partial(gather_beside_kernel, shards, parts), ou...  52.7 us
    pallas_call x1, Pallas kernels, push_gather(): pl.pallas_call(functools.partial(push_gather_kernel, rows, shards), out_s...  50.8 us
    pallas_call x1, Pallas kernels, gather_ffn(): pl.pallas_call(functools.partial(gather_ffn_kernel, shards, parts), out_s...  48.5 us
    pallas_call x1, Pallas kernels, ring_seq_gather(): pl.pallas_call(functools.partial(seq_gather_kernel, shards, parts), out_s...  43.5 us
    pallas_call x1, Pallas kernels, scan_backward(): pl.pallas_call(functools.partial(scan_backward_kernel, len(after)), grid=...  35 us
  transfers between devices with their start and end apart: 18, of which 2 were waited for; matrix products, arithmetic and copies ran while one was open for 26% of the time, Pallas kernels for 42%

profile of v6, /device:TPU:0, one launch (start us, length us, event | category | flops | bytes accessed | tf_op | source)
XLA Modules:
  0.0 1100.8 jit_solution(6050886128588130127)
XLA Ops:
  13.6 7.5 all-to-all-start
  22.6 50.8 %shard_map.118 = bf16[32,80,128]{2,1,0:T(8,128)(2,1)} custom-call(bf16[80,128]{1,0:T(8,128)(2,1)} %maximum_maximum_fusion.x_ref), custom_call_target="tpu_custom_call" | custom-call | bytes 70000000 | tf_op jit(solution)/shard_map/pallas_call | solution.py:1034
  88.2 43.5 %shard_map.119 = bf16[16,128,1600]{2,1,0:T(8,128)(2,1)} custom-call(bf16[128,1600]{1,0:T(8,128)(2,1)} %get-tuple-element.48.x_ref), custom_call_target="tpu_custom_call" | custom-call | bytes 140000000 | tf_op jit(solution)/shard_map/pallas_call | solution.py:550
  147.9 4.8 all-to-all-start.1
  159.5 7.3 convolution_convert_fusion
  175.4 7.5 fusion.20
  193.9 6.4 all-to-all-start.2
  204.1 41.8 %shard_map.121 = bf16[144,2048]{1,0:T(8,128)(2,1)S(1)} custom-call(f32[144,2048]{1,0:T(8,128)S(1)} %fusion.40.x_ref), custom_call_target="tpu_custom_call" | custom-call | bytes 105000000 | tf_op jit(solution)/shard_map/pallas_call | solution.py:936
  250.7 5.2 reshape.595
  259.9 23.8 %shard_map.122 = (f32[2048,256]{1,0:T(8,128)}, f32[16,16,256]{2,1,0:T(8,128)}, bf16[2048,16,256]{2,1,0:T(8,128)(2,1)}, bf16[16,150,344]{2,1,0:T(8,128)(2,1)}) custom-call(f32[2048]{0:T(1024)} %get-tuple-element.208.refs_0_, f32[2048,256]{1,0:T(8,128)} %pad.154.refs_1_, f32[2048,256]{1,0:T(8,128)} %pad.156.refs_2_, ...), custom_call_target="tpu_custom_call", output_to_operand_aliasing={{3}: (7, {})} | custom-call | bytes 84000000 | tf_op jit(solution)/shard_map/pallas_call | solution.py:1302
  283.7 4.6 all-to-all-start.4
  297.6 5.3 fusion.4
  310.4 5.0 convolution_convert_fusion.3.refs_1_
  315.4 22.5 %shard_map.120 = (f32[2048,128]{1,0:T(8,128)S(1)}, f32[16,2,128]{2,1,0:T(2,128)S(1)}, bf16[16,50,656]{2,1,0:T(8,128)(2,1)S(1)}) custom-call(s32[16,1,128]{2,1,0:T(1,128)S(1)} %broadcast_maximum_fusion.refs_0_, bf16[2048,128]{1,0:T(8,128)(2,1)S(1)} %convolution_convert_fusion.3.refs_1_, ...), custom_call_target="tpu_custom_call", output_to_operand_aliasing={{2}: (6, {})} | custom-call | bytes 84000000 | tf_op jit(solution)/shard_map/pallas_call | solution.py:1200
  339.8 6.0 all-to-all-start.3
  351.5 4.5 multiply_reduce_fusion.7
  356.6 24.7 %shard_map.123 = f32[32,128]{1,0:T(8,128)} custom-call(f32[32,128]{1,0:T(8,128)} %reshape.596.x_ref), custom_call_target="tpu_custom_call" | custom-call | bytes 42000000 | tf_op jit(solution)/shard_map/pallas_call | solution.py:993
  397.0 5.2 reshape.601
  402.2 3.9 fusion.65
  407.2 5.9 all-to-all-start.5
  416.8 61.5 %shard_map.125 = f32[128,1600]{1,0:T(8,128)} custom-call(bf16[2048,328]{1,0:T(8,128)(2,1)} %fusion.7.refs_0_.mixed_ref, bf16[328,1600]{1,0:T(8,128)(2,1)} %reshape.600.refs_1_.w_out_ref), custom_call_target="tpu_custom_call" | custom-call | bytes 140000000 | tf_op jit(solution)/shard_map/pallas_call | solution.py:861
  483.2 4.2 reshape.658
  490.3 48.5 %shard_map.126 = (bf16[16,128,1600]{2,1,0:T(8,128)(2,1)}, bf16[2048,344]{1,0:T(8,128)(2,1)}, bf16[2048,344]{1,0:T(8,128)(2,1)}, bf16[2048,344]{1,0:T(8,128)(2,1)}) custom-call(bf16[128,1600]{1,0:T(8,128)(2,1)} %multiply_convert_fusion.x_ref, bf16[2048,1600]{1,0:T(8,128)(2,1)} %all-gather.2.cloned.1.call-done.refs_6_.cot_ref.cot_any, ...), custom_call_target="tpu_custom_call" | custom-call | bytes 157500000 | tf_op jit(solution)/shard_map/pallas_call | solution.py:609
  538.9 47.6 %shard_map.127 = f32[128,1600]{1,0:T(8,128)} custom-call(bf16[2048,344]{1,0:T(8,128)(2,1)} %get-tuple-element.63.refs_0_.d_gate_ref, bf16[2048,344]{1,0:T(8,128)(2,1)} %get-tuple-element.64.refs_1_.d_up_ref, bf16[1600,344]{1,0:T(8,128)(2,1)} %get-tuple-element.172.gate_ref.refs_2_, bf16[1600,344]{1,0:T(8,128)(2,1)} %get-tuple-element.171.up_ref.refs_3_), custom_call_target="tpu_custom_call" | custom-call | bytes 140000000 | tf_op jit(solution)/shard_map/pallas_call | solution.py:861
  589.0 52.7 %shard_map.128 = (bf16[16,128,1600]{2,1,0:T(8,128)(2,1)}, bf16[1600,344]{1,0:T(8,128)(2,1)}, bf16[1600,344]{1,0:T(8,128)(2,1)}, bf16[344,1600]{1,0:T(8,128)(2,1)...) custom-call(bf16[128,1600]{1,0:T(8,128)(2,1)} %fusion.61.x_ref, ...), custom_call_target="tpu_custom_call" | custom-call | bytes 157500000 | tf_op jit(solution)/shard_map/pallas_call | solution.py:719
  648.2 9.7 shard_map.129
  661.7 3.9 reshape.608
  667.0 4.7 all-to-all-start.6
  678.9 26.1 %shard_map.130 = (bf16[2048,128]{1,0:T(8,128)(2,1)S(1)}, f32[3072,256]{1,0:T(8,128)}, f32[128,256]{1,0:T(8,128)S(1)}, bf16[16,50,656]{2,1,0:T(8,128)(2,1)}) custom-call(s32[16,1,128]{2,1,0:T(1,128)S(1)} %broadcast_maximum_fusion.refs_0_, bf16[2048,128]{1,0:T(8,128)(2,1)S(1)} %copy-done.12, ...), custom_call_target="tpu_custom_call", output_to_operand_aliasing={{3}: (9, {})} | custom-call | bytes 84000000 | tf_op jit(solution)/shard_map/pallas_call | solution.py:1225
  705.0 5.9 convolution_convert_fusion.2
  715.8 3.9 multiply_reduce_fusion
  721.2 4.4 broadcast_select_fusion.2
  733.5 13.3 %all-to-all-start.9 = ((bf16[16,656,50]{1,2,0:T(8,128)(2,1)}), bf16[16,656,50]{1,2,0:T(8,128)(2,1)}, u32[]{:S(2)}, u32[]{:S(2)}) async-start(bf16[16,656,50]{1,2,0:T(8,128)(2,1)} %bitcast.68), calls=%async_computation.10 | async-start | bytes 2752512 | tf_op jit(solution)/shard_map/transpose(jvp())/all_to_all | solution.py:137
  754.6 35.0 %shard_map.132 = (f32[2048,256]{1,0:T(8,128)S(1)}, f32[2048,256]{1,0:T(8,128)S(1)}, f32[32,2048]{1,0:T(8,128)S(1)}, f32[16,256]{1,0:T(8,128)S(1)}) custom-call(f32[2048]{0:T(1024)S(1)} %copy-done.17, f32[2048,256]{1,0:T(8,128)S(1)} %copy-done, f32[2048,256]{1,0:T(8,128)S(1)} %copy-done.1, bf16[32,2048]{1,0:T(8,128)(2,1)S(1)} %copy-done.13, ...), custom_call_target="tpu_custom_call" | custom-call | bytes 140000000 | tf_op jit(solution)/shard_map/pallas_call | solution.py:1406
  798.1 29.2 %shard_map.133.refs_0_ = bf16[144,2048]{1,0:T(8,128)(2,1)S(1)} custom-call(f32[144,2048]{1,0:T(8,128)S(1)} %select_maximum_fusion.x_ref, bf16[128,1600]{1,0:T(8,128)(2,1)S(1)} %add_convert_fusion.refs_0_), custom_call_target="tpu_custom_call" | custom-call | bytes 105000000 | tf_op jit(solution)/shard_map/pallas_call | solution.py:936
  830.4 4.8 all-to-all-start.7
  848.5 9.6 multiply_reduce_fusion.4
  868.9 8.0 all-to-all-start.8
  876.9 7.6 convolution_convert_fusion.1
  887.9 6.1 reshape.622
  894.0 4.6 copy.509
  904.5 5.8 concatenate.84
  910.3 3.6 broadcast_select_fusion.4
  926.6 6.4 all-to-all-start.11
  933.0 80.5 %shard_map.137 = f32[128,1600]{1,0:T(8,128)} custom-call(bf16[2048,400]{1,0:T(8,128)(2,1)} %pad_maximum_fusion.2.refs_0_, bf16[2048,128]{1,0:T(8,128)(2,1)} %copy-done.14, bf16[2048,256]{1,0:T(8,128)(2,1)} %slice.450.refs_2_, bf16[1600,400]{1,0:T(8,128)(2,1)} %reshape.576.refs_3_, bf16[1600,128]{1,0:T(8,128)(2,1)} %slice.348.refs_4_, ...), custom_call_target="tpu_custom_call" | custom-call | bytes 140000000 | tf_op jit(solution)/shard_map/pallas_call | solution.py:861
  1022.3 4.5 all-to-all-start.10
  1029.1 4.6 reshape.645
  1047.6 31.9 %shard_map.138 = f32[80,128]{1,0:T(8,128)S(1)} custom-call(bf16[32,80,128]{2,1,0:T(8,128)(2,1)S(1)} %pad_maximum_fusion.8.x_ref), custom_call_target="tpu_custom_call" | custom-call | bytes 70000000 | tf_op jit(solution)/shard_map/pallas_call | solution.py:1069
  (555 shorter events, 269.4 us)
Async XLA Ops:
  13.6 8.2 copy-start.78
  13.6 8.3 copy-start.116
  13.6 8.4 copy-start.92
  13.6 67.9 %all-to-all-start = ((bf16[16,869,50]{1,2,0:T(8,128)(2,1)}), bf16[16,869,50]{1,2,0:T(8,128)(2,1)S(1)}, u32[]{:S(2)}, u32[]{:S(2)}) async-start(bf16[16,869,50]{1,2,0:T(8,128)(2,1)} %bitcast.252), calls=%async_computation | async-start | bytes 3211264 | tf_op jit(solution)/shard_map/jvp()/all_to_all | solution.py:137
  21.1 238.8 %all-gather.2.cloned.1.call-start = ((), (), s32[]{:S(2)}) async-start(), calls=%async_computation.13 | async-start | bytes 7241728 | tf_op jit(solution)/shard_map/all_gather | solution.py:418
  21.7 58.0 %copy-start.32 = (bf16[1,128,1600]{2,1,0:T(8,128)(2,1)}, bf16[1,128,1600]{2,1,0:T(8,128)(2,1)S(1)}, u32[]{:S(2)}) copy-start(bf16[1,128,1600]{2,1,0:T(8,128)(2,1)S(1)} %copy.453) | copy-start | bytes 1228804
  85.6 46.1 %collective-permute-start = (bf16[13904,50]{0,1:T(8,128)(2,1)S(1)}, bf16[13904,50]{0,1:T(8,128)(2,1)S(1)}, u32[]{:S(2)}, u32[]{:S(2)}) collective-permute-start(bf16[13904,50]{0,1:T(8,128)(2,1)S(1)} %reshape.571), channel_id=1, source_target_pairs={{0,16},{16,0},{1,17},{17,1},{2,18},{18,2},{3,19},{19,3},{4,20},{20... | collective-permute-start | bytes 4171208 | tf_op jit(solution)/shard_map/jvp()/ppermute | solution.py:159
  132.5 10.7 copy-start.41
  136.6 38.8 %copy-start.80 = (f32[2048]{0:T(1024)}, f32[2048]{0:T(1024)S(1)}, u32[]{:S(2)}) copy-start(f32[2048]{0:T(1024)S(1)} %get-tuple-element.209) | copy-start | bytes 24580
  136.6 38.8 %copy-start.82 = (f32[2048]{0:T(1024)}, f32[2048]{0:T(1024)S(1)}, u32[]{:S(2)}) copy-start(f32[2048]{0:T(1024)S(1)} %get-tuple-element.210) | copy-start | bytes 24580
  136.6 38.8 %copy-start.84 = (f32[2048]{0:T(1024)}, f32[2048]{0:T(1024)S(1)}, u32[]{:S(2)}) copy-start(f32[2048]{0:T(1024)S(1)} %get-tuple-element.211) | copy-start | bytes 24580
  136.6 38.8 %copy-start.86 = (f32[2048]{0:T(1024)}, f32[2048]{0:T(1024)S(1)}, u32[]{:S(2)}) copy-start(f32[2048]{0:T(1024)S(1)} %get-tuple-element.212) | copy-start | bytes 24580
  147.9 35.1 %all-to-all-start.1 = ((bf16[16,316,50]{1,2,0:T(8,128)(2,1)}), bf16[16,316,50]{1,2,0:T(8,128)(2,1)}, u32[]{:S(2)}, u32[]{:S(2)}) async-start(bf16[16,316,50]{1,2,0:T(8,128)(2,1)} %pad_maximum_fusion.7), calls=%async_computation.1 | async-start | bytes 1376256 | tf_op jit(solution)/shard_map/jvp()/all_to_all | solution.py:137
  173.3 28.2 %copy-start.75 = (f32[200,24]{0,1:T(8,128)}, f32[200,24]{0,1:T(8,128)S(1)}, u32[]{:S(2)}) copy-start(f32[200,24]{0,1:T(8,128)S(1)} %reshape.575) | copy-start | bytes 57604
  174.8 8.1 copy-start.97
  174.8 8.1 copy-start.99
  174.8 8.1 copy-start.101
  174.9 8.1 copy-start.103
  183.0 20.6 %copy-start.27 = (bf16[2048,200]{1,0:T(8,128)(2,1)}, bf16[2048,200]{1,0:T(8,128)(2,1)S(1)}, u32[]{:S(2)}) copy-start(bf16[2048,200]{1,0:T(8,128)(2,1)S(1)} %get-tuple-element.56) | copy-start | bytes 2457604
  193.9 63.8 %all-to-all-start.2 = ((bf16[16,100,384]{2,1,0:T(8,128)(2,1)}), bf16[16,100,384]{2,1,0:T(8,128)(2,1)}, u32[]{:S(2)}, u32[]{:S(2)}) async-start(bf16[16,100,384]{2,1,0:T(8,128)(2,1)} %copy.470), calls=%async_computation.2 | async-start | bytes 2555904 | tf_op jit(solution)/shard_map/jvp()/all_to_all | solution.py:137
  283.7 56.1 %all-to-all-start.4 = ((bf16[16,150,344]{2,1,0:T(8,128)(2,1)}), bf16[16,150,344]{2,1,0:T(8,128)(2,1)}, u32[]{:S(2)}, u32[]{:S(2)}) async-start(bf16[16,150,344]{2,1,0:T(8,128)(2,1)} %get-tuple-element.62), calls=%async_computation.4 | async-start | bytes 3735552 | tf_op jit(solution)/shard_map/jvp()/all_to_all | solution.py:137
  306.6 8.8 copy-start.4
  339.8 42.8 %all-to-all-start.3 = ((bf16[16,656,50]{1,2,0:T(8,128)(2,1)}), bf16[16,656,50]{1,2,0:T(8,128)(2,1)}, u32[]{:S(2)}, u32[]{:S(2)}) async-start(bf16[16,656,50]{1,2,0:T(8,128)(2,1)} %bitcast.238), calls=%async_computation.3 | async-start | bytes 2752512 | tf_op jit(solution)/shard_map/jvp()/all_to_all | solution.py:137
  348.9 42.8 %collective-permute-start.1 = (bf16[16,150,344]{2,0,1:T(8,128)(2,1)}, bf16[16,150,344]{2,0,1:T(8,128)(2,1)}, u32[]{:S(2)}, u32[]{:S(2)}) collective-permute-start(bf16[16,150,344]{2,0,1:T(8,128)(2,1)} %copy.481), channel_id=1, source_target_pairs={{0,16},{16,0},{1,17},{17,1},{2,18},{18,2},{3,19},{19,3},{4,20},{20... | collective-permute-start | bytes 4953608 | tf_op jit(solution)/shard_map/jvp()/ppermute | solution.py:159
  407.2 73.4 %all-to-all-start.5 = ((bf16[16,100,344]{2,1,0:T(8,128)(2,1)}), bf16[16,100,344]{2,1,0:T(8,128)(2,1)}, u32[]{:S(2)}, u32[]{:S(2)}) async-start(bf16[16,100,344]{2,1,0:T(8,128)(2,1)} %reshape.602), calls=%async_computation.5 | async-start | bytes 2555904 | tf_op jit(solution)/shard_map/jvp()/all_to_all | solution.py:137
  413.2 383.6 %reduce-scatter.2.cloned.1.call-start = ((), (), s32[]{:S(2)}) async-start(), calls=%async_computation.14 | async-start | bytes 7241728 | tf_op jit(solution)/shard_map/reduce_scatter | solution.py:422
  416.8 61.5 %copy-start.33 = (bf16[1,128,1600]{2,1,0:T(8,128)(2,1)S(1)}, bf16[1,128,1600]{2,1,0:T(8,128)(2,1)}, u32[]{:S(2)}) copy-start(bf16[1,128,1600]{2,1,0:T(8,128)(2,1)} %copy-done.32) | copy-start | bytes 1228804
  479.6 108.3 %copy-start.22 = (f32[128,1600]{1,0:T(8,128)}, f32[128,1600]{1,0:T(8,128)S(1)}, u32[]{:S(2)}) copy-start(f32[128,1600]{1,0:T(8,128)S(1)} %get-tuple-element.160) | copy-start | bytes 2457604
  538.9 49.1 %copy-start.49 = (bf16[1,128,1600]{2,1,0:T(8,128)(2,1)S(1)}, bf16[1,128,1600]{2,1,0:T(8,128)(2,1)}, u32[]{:S(2)}) copy-start(bf16[1,128,1600]{2,1,0:T(8,128)(2,1)} %copy.456) | copy-start | bytes 1228804
  588.0 53.8 %copy-start.109 = (f32[128]{0:T(128)}, f32[128]{0:T(128)S(1)}, u32[]{:S(2)}) copy-start(f32[128]{0:T(128)S(1)} %multiply_multiply_fusion.10) | copy-start | bytes 1540
  646.7 12.5 %copy-start.63 = (bf16[344,1600]{1,0:T(8,128)(2,1)S(1)}, bf16[344,1600]{1,0:T(8,128)(2,1)}, u32[]{:S(2)}) copy-start(bf16[344,1600]{1,0:T(8,128)(2,1)} %get-tuple-element.78) | copy-start | bytes 3302404
  667.0 52.7 %all-to-all-start.6 = ((bf16[16,100,344]{2,1,0:T(8,128)(2,1)}), bf16[16,100,344]{2,1,0:T(8,128)(2,1)}, u32[]{:S(2)}, u32[]{:S(2)}) async-start(bf16[16,100,344]{2,1,0:T(8,128)(2,1)} %shard_map.131), calls=%async_computation.7 | async-start | bytes 2555904 | tf_op jit(solution)/shard_map/transpose(jvp())/all_to_all | solution.py:137
  678.9 32.0 %slice-start = ((s8[6815744]{0:T(1024)(128)(4,1)}), s8[4194304]{0:T(1024)(128)(4,1)S(1)}, s32[]{:S(2)}) async-start(s8[6815744]{0:T(1024)(128)(4,1)} %bitcast.247), calls=%async_computation.15 | async-start | bytes 8388608
  728.9 63.7 %collective-permute-start.2 = (bf16[16,150,344]{2,0,1:T(8,128)(2,1)}, bf16[16,150,344]{2,0,1:T(8,128)(2,1)}, u32[]{:S(2)}, u32[]{:S(2)}) collective-permute-start(bf16[16,150,344]{2,0,1:T(8,128)(2,1)} %copy.489), channel_id=1, source_target_pairs={{0,16},{16,0},{1,17},{17,1},{2,18},{18,2},{3,19},{19,3},{4,20},{20... | collective-permute-start | bytes 4953608 | tf_op jit(solution)/shard_map/ppermute | solution.py:159
  733.5 96.9 %all-to-all-start.9 = ((bf16[16,656,50]{1,2,0:T(8,128)(2,1)}), bf16[16,656,50]{1,2,0:T(8,128)(2,1)}, u32[]{:S(2)}, u32[]{:S(2)}) async-start(bf16[16,656,50]{1,2,0:T(8,128)(2,1)} %bitcast.68), calls=%async_computation.10 | async-start | bytes 2752512 | tf_op jit(solution)/shard_map/transpose(jvp())/all_to_all | solution.py:137
  754.6 35.1 %copy-start.44 = (f32[2048,200]{1,0:T(8,128)S(1)}, f32[2048,200]{1,0:T(8,128)}, u32[]{:S(2)}) copy-start(f32[2048,200]{1,0:T(8,128)} %get-tuple-element.222) | copy-start | bytes 4915204
  830.4 31.6 %all-to-all-start.7 = ((bf16[16,100,384]{2,1,0:T(8,128)(2,1)}), bf16[16,100,384]{2,1,0:T(8,128)(2,1)}, u32[]{:S(2)}, u32[]{:S(2)}) async-start(bf16[16,100,384]{2,1,0:T(8,128)(2,1)} %reshape.613), calls=%async_computation.8 | async-start | bytes 2555904 | tf_op jit(solution)/shard_map/transpose(jvp())/all_to_all | solution.py:137
  867.5 9.4 copy-start.53
  868.9 33.1 %all-to-all-start.8 = ((bf16[16,316,50]{1,2,0:T(8,128)(2,1)}), bf16[16,316,50]{1,2,0:T(8,128)(2,1)S(1)}, u32[]{:S(2)}, u32[]{:S(2)}) async-start(bf16[16,316,50]{1,2,0:T(8,128)(2,1)} %bitcast.257), calls=%async_computation.9 | async-start | bytes 1376256 | tf_op jit(solution)/shard_map/transpose(jvp())/all_to_all | solution.py:137
  913.9 99.5 %collective-permute-start.3 = (bf16[13904,50]{0,1:T(8,128)(2,1)}, bf16[13904,50]{0,1:T(8,128)(2,1)}, u32[]{:S(2)}, u32[]{:S(2)}) collective-permute-start(bf16[13904,50]{0,1:T(8,128)(2,1)} %broadcast_select_fusion.4), channel_id=1, source_target_pairs={{0,16},{16,0},{1,17},{17,1},{2,18},{18,2},{3,19},{19,3},{4,20},{20... | collective-permute-start | bytes 4171208 | tf_op jit(solution)/shard_map/transpose(jvp())/ppermute | solution.py:1468
  926.6 95.7 %all-to-all-start.11 = ((bf16[16,150,344]{2,1,0:T(8,128)(2,1)}), bf16[16,150,344]{2,1,0:T(8,128)(2,1)}, u32[]{:S(2)}, u32[]{:S(2)}) async-start(bf16[16,150,344]{2,1,0:T(8,128)(2,1)} %copy_add_fusion.refs_1_), calls=%async_computation.12 | async-start | bytes 3735552 | tf_op jit(solution)/shard_map/transpose(jvp())/all_to_all | solution.py:137
  933.0 80.5 %copy-start.26 = (bf16[27808,50]{0,1:T(8,128)(2,1)S(1)}, bf16[27808,50]{0,1:T(8,128)(2,1)}, u32[]{:S(2)}) copy-start(bf16[27808,50]{0,1:T(8,128)(2,1)} %concatenate.84) | copy-start | bytes 8342404
  1022.3 63.7 %all-to-all-start.10 = ((bf16[16,869,50]{1,2,0:T(8,128)(2,1)}), bf16[16,869,50]{1,2,0:T(8,128)(2,1)}, u32[]{:S(2)}, u32[]{:S(2)}) async-start(bf16[16,869,50]{1,2,0:T(8,128)(2,1)} %copy.521), calls=%async_computation.11 | async-start | bytes 3211264 | tf_op jit(solution)/shard_map/transpose(jvp())/all_to_all | solution.py:137
  1043.3 36.3 %copy-start.107 = (f32[128]{0:T(128)S(1)}, f32[128]{0:T(128)}, u32[]{:S(2)}) copy-start(f32[128]{0:T(128)} %copy-done.106) | copy-start | bytes 1540
  1043.3 36.3 %copy-start.23 = (f32[128,1600]{1,0:T(8,128)S(1)}, f32[128,1600]{1,0:T(8,128)}, u32[]{:S(2)}) copy-start(f32[128,1600]{1,0:T(8,128)} %copy-done.22) | copy-start | bytes 2457604
  1043.3 36.3 %copy-start.38 = (f32[128,1600]{1,0:T(8,128)S(1)}, f32[128,1600]{1,0:T(8,128)}, u32[]{:S(2)}) copy-start(f32[128,1600]{1,0:T(8,128)} %shard_map.127) | copy-start | bytes 2457604
  1043.4 36.3 %copy-start.50 = (bf16[1,128,1600]{2,1,0:T(8,128)(2,1)S(1)}, bf16[1,128,1600]{2,1,0:T(8,128)(2,1)}, u32[]{:S(2)}) copy-start(bf16[1,128,1600]{2,1,0:T(8,128)(2,1)} %copy.456) | copy-start | bytes 1228804
  1043.4 36.3 %copy-start.110 = (f32[128]{0:T(128)S(1)}, f32[128]{0:T(128)}, u32[]{:S(2)}) copy-start(f32[128]{0:T(128)} %copy-done.109) | copy-start | bytes 1540
  (91 other events, 283.2 us)
Sparse Core Ops, SparseCore 0:
  132.7 68.6 all-gather.1
  641.9 110.3 reduce-scatter.1

commit v7 on v6

--- a/solution.py
+++ b/solution.py
@@ -542,7 +542,7 @@
     return sum(padded_bytes(shape, 2) for shape in shapes) < 48 * MIB
 
 
-def ring_seq_gather(block, collective_id, parts=2):
+def ring_seq_gather(block, collective_id, parts=4):
     shards = lax.axis_size("seq")
     rows, width = block.shape
     if not fits_vmem((shards * rows, width)):
@@ -595,7 +595,7 @@
     ring_gather_loop(shards, parts, x_ref, out_ref, *sems, work)
 
 
-def gather_ffn(block, cotangent, w_gate, w_up, w_down, collective_id, parts=2):
+def gather_ffn(block, cotangent, w_gate, w_up, w_down, collective_id, parts=4):
     shards = lax.axis_size("seq")
     rows, width = block.shape
     units = w_gate.shape[1]
@@ -696,7 +696,7 @@
 
 
 def gather_beside_ffn(
-    block, second, cotangent, act, d_gate, d_up, w_down, mixed, w_out, collective_id, parts=2
+    block, second, cotangent, act, d_gate, d_up, w_down, mixed, w_out, collective_id, parts=4
 ):
     shards = lax.axis_size("seq")
     rows, width = block.shape
@@ -838,7 +838,7 @@
     return -(-shape[0] // 16) * 16 * -(-shape[1] // 128) * 128 * bytes_each
 
 
-def product_scatter(terms, collective_id, parts=2):
+def product_scatter(terms, collective_id, parts=4):
     shards = lax.axis_size("seq")
     chips = shards // 2
     length = terms[0][0].shape[0]

time: 1110 us -> 1110 us (level)
  transfers between devices with their start and end apart: 18 -> 18, of which waited for: 2 -> 2; matrix products, arithmetic and copies ran while one was open for 26% -> 26% of each run, Pallas kernels for 42% -> 41%
where the time goes in v7:
time: 1110 us; the launch traced here: 1100 us
  Pallas kernels  629 us (57%)
  local copies, waits for them, and re-layouts  234 us (21%)
  starting transfers between devices  84.1 us (8%)
  other arithmetic  81.7 us (7%)
  matrix products  50.9 us (5%)
  between operations  16.6 us (1%)
    pallas_call x3, Pallas kernels, product_scatter(): pl.pallas_call(functools.partial(product_scatter_kernel, shards, parts, t...  188 us
    all_to_all x12, starting transfers between devices, exchange(): return lax.all_to_all(value, 'seq', 0, 0)  77.3 us
    pallas_call x2, Pallas kernels, seq_sum(): pl.pallas_call(functools.partial(seq_sum_kernel, bits, len(after)), out_s...  71 us
    pallas_call x1, Pallas kernels, gather_beside_ffn(): pl.pallas_call(functools.partial(gather_beside_kernel, shards, parts), ou...  54 us
    pallas_call x1, Pallas kernels, push_gather(): pl.pallas_call(functools.partial(push_gather_kernel, rows, shards), out_s...  50.6 us
    pallas_call x1, Pallas kernels, gather_ffn(): pl.pallas_call(functools.partial(gather_ffn_kernel, shards, parts), out_s...  49.8 us
    pallas_call x1, Pallas kernels, ring_seq_gather(): pl.pallas_call(functools.partial(seq_gather_kernel, shards, parts), out_s...  42.7 us
    pallas_call x1, Pallas kernels, scan_backward(): pl.pallas_call(functools.partial(scan_backward_kernel, len(after)), grid=...  35 us
  transfers between devices with their start and end apart: 18, of which 2 were waited for; matrix products, arithmetic and copies ran while one was open for 26% of the time, Pallas kernels for 41%

profile of v7, /device:TPU:0, one launch (start us, length us, event | category | flops | bytes accessed | tf_op | source)
XLA Modules:
  0.0 1101.1 jit_solution(7222585377555290567)
XLA Ops:
  13.6 7.5 all-to-all-start
  22.9 50.6 %shard_map.118 = bf16[32,80,128]{2,1,0:T(8,128)(2,1)} custom-call(bf16[80,128]{1,0:T(8,128)(2,1)} %maximum_maximum_fusion.x_ref), custom_call_target="tpu_custom_call" | custom-call | bytes 70000000 | tf_op jit(solution)/shard_map/pallas_call | solution.py:1034
  88.2 42.7 %shard_map.119 = bf16[16,128,1600]{2,1,0:T(8,128)(2,1)} custom-call(bf16[128,1600]{1,0:T(8,128)(2,1)} %get-tuple-element.48.x_ref), custom_call_target="tpu_custom_call" | custom-call | bytes 140000000 | tf_op jit(solution)/shard_map/pallas_call | solution.py:550
  147.1 4.7 all-to-all-start.1
  158.6 7.3 convolution_convert_fusion
  174.6 7.5 fusion.20
  193.1 6.6 all-to-all-start.2
  203.5 41.8 %shard_map.121 = bf16[144,2048]{1,0:T(8,128)(2,1)S(1)} custom-call(f32[144,2048]{1,0:T(8,128)S(1)} %fusion.40.x_ref), custom_call_target="tpu_custom_call" | custom-call | bytes 105000000 | tf_op jit(solution)/shard_map/pallas_call | solution.py:936
  250.1 5.2 reshape.595
  259.3 23.8 %shard_map.122 = (f32[2048,256]{1,0:T(8,128)}, f32[16,16,256]{2,1,0:T(8,128)}, bf16[2048,16,256]{2,1,0:T(8,128)(2,1)}, bf16[16,150,344]{2,1,0:T(8,128)(2,1)}) custom-call(f32[2048]{0:T(1024)} %get-tuple-element.208.refs_0_, f32[2048,256]{1,0:T(8,128)} %pad.154.refs_1_, f32[2048,256]{1,0:T(8,128)} %pad.156.refs_2_, ...), custom_call_target="tpu_custom_call", output_to_operand_aliasing={{3}: (7, {})} | custom-call | bytes 84000000 | tf_op jit(solution)/shard_map/pallas_call | solution.py:1302
  283.1 4.6 all-to-all-start.4
  297.0 5.3 fusion.4
  309.8 5.0 convolution_convert_fusion.3.refs_1_
  314.8 22.3 %shard_map.120 = (f32[2048,128]{1,0:T(8,128)S(1)}, f32[16,2,128]{2,1,0:T(2,128)S(1)}, bf16[16,50,656]{2,1,0:T(8,128)(2,1)S(1)}) custom-call(s32[16,1,128]{2,1,0:T(1,128)S(1)} %broadcast_maximum_fusion.refs_0_, bf16[2048,128]{1,0:T(8,128)(2,1)S(1)} %convolution_convert_fusion.3.refs_1_, ...), custom_call_target="tpu_custom_call", output_to_operand_aliasing={{2}: (6, {})} | custom-call | bytes 84000000 | tf_op jit(solution)/shard_map/pallas_call | solution.py:1200
  339.0 6.0 all-to-all-start.3
  351.0 4.5 multiply_reduce_fusion.7
  356.2 24.3 %shard_map.123 = f32[32,128]{1,0:T(8,128)} custom-call(f32[32,128]{1,0:T(8,128)} %reshape.596.x_ref), custom_call_target="tpu_custom_call" | custom-call | bytes 42000000 | tf_op jit(solution)/shard_map/pallas_call | solution.py:993
  396.1 5.2 reshape.601
  401.4 3.9 fusion.65
  406.4 5.9 all-to-all-start.5
  416.0 60.6 %shard_map.125 = f32[128,1600]{1,0:T(8,128)} custom-call(bf16[2048,328]{1,0:T(8,128)(2,1)} %fusion.7.refs_0_.mixed_ref, bf16[328,1600]{1,0:T(8,128)(2,1)} %reshape.600.refs_1_.w_out_ref), custom_call_target="tpu_custom_call" | custom-call | bytes 140000000 | tf_op jit(solution)/shard_map/pallas_call | solution.py:861
  481.6 4.2 reshape.658
  488.6 49.8 %shard_map.126 = (bf16[16,128,1600]{2,1,0:T(8,128)(2,1)}, bf16[2048,344]{1,0:T(8,128)(2,1)}, bf16[2048,344]{1,0:T(8,128)(2,1)}, bf16[2048,344]{1,0:T(8,128)(2,1)}) custom-call(bf16[128,1600]{1,0:T(8,128)(2,1)} %multiply_convert_fusion.x_ref, bf16[2048,1600]{1,0:T(8,128)(2,1)} %all-gather.2.cloned.1.call-done.refs_6_.cot_ref.cot_any, ...), custom_call_target="tpu_custom_call" | custom-call | bytes 157500000 | tf_op jit(solution)/shard_map/pallas_call | solution.py:609
  538.5 47.2 %shard_map.127 = f32[128,1600]{1,0:T(8,128)} custom-call(bf16[2048,344]{1,0:T(8,128)(2,1)} %get-tuple-element.63.refs_0_.d_gate_ref, bf16[2048,344]{1,0:T(8,128)(2,1)} %get-tuple-element.64.refs_1_.d_up_ref, bf16[1600,344]{1,0:T(8,128)(2,1)} %get-tuple-element.172.gate_ref.refs_2_, bf16[1600,344]{1,0:T(8,128)(2,1)} %get-tuple-element.171.up_ref.refs_3_), custom_call_target="tpu_custom_call" | custom-call | bytes 140000000 | tf_op jit(solution)/shard_map/pallas_call | solution.py:861
  588.3 54.0 %shard_map.128 = (bf16[16,128,1600]{2,1,0:T(8,128)(2,1)}, bf16[1600,344]{1,0:T(8,128)(2,1)}, bf16[1600,344]{1,0:T(8,128)(2,1)}, bf16[344,1600]{1,0:T(8,128)(2,1)...) custom-call(bf16[128,1600]{1,0:T(8,128)(2,1)} %fusion.61.x_ref, ...), custom_call_target="tpu_custom_call" | custom-call | bytes 157500000 | tf_op jit(solution)/shard_map/pallas_call | solution.py:719
  648.9 9.5 shard_map.129
  662.2 3.9 reshape.608
  667.4 4.9 all-to-all-start.6
  679.6 26.1 %shard_map.130 = (bf16[2048,128]{1,0:T(8,128)(2,1)S(1)}, f32[3072,256]{1,0:T(8,128)}, f32[128,256]{1,0:T(8,128)S(1)}, bf16[16,50,656]{2,1,0:T(8,128)(2,1)}) custom-call(s32[16,1,128]{2,1,0:T(1,128)S(1)} %broadcast_maximum_fusion.refs_0_, bf16[2048,128]{1,0:T(8,128)(2,1)S(1)} %copy-done.12, ...), custom_call_target="tpu_custom_call", output_to_operand_aliasing={{3}: (9, {})} | custom-call | bytes 84000000 | tf_op jit(solution)/shard_map/pallas_call | solution.py:1225
  705.7 5.9 convolution_convert_fusion.2
  716.5 3.9 multiply_reduce_fusion
  721.9 4.4 broadcast_select_fusion.2
  734.3 13.3 %all-to-all-start.9 = ((bf16[16,656,50]{1,2,0:T(8,128)(2,1)}), bf16[16,656,50]{1,2,0:T(8,128)(2,1)}, u32[]{:S(2)}, u32[]{:S(2)}) async-start(bf16[16,656,50]{1,2,0:T(8,128)(2,1)} %bitcast.68), calls=%async_computation.10 | async-start | bytes 2752512 | tf_op jit(solution)/shard_map/transpose(jvp())/all_to_all | solution.py:137
  755.3 35.0 %shard_map.132 = (f32[2048,256]{1,0:T(8,128)S(1)}, f32[2048,256]{1,0:T(8,128)S(1)}, f32[32,2048]{1,0:T(8,128)S(1)}, f32[16,256]{1,0:T(8,128)S(1)}) custom-call(f32[2048]{0:T(1024)S(1)} %copy-done.17, f32[2048,256]{1,0:T(8,128)S(1)} %copy-done, f32[2048,256]{1,0:T(8,128)S(1)} %copy-done.1, bf16[32,2048]{1,0:T(8,128)(2,1)S(1)} %copy-done.13, ...), custom_call_target="tpu_custom_call" | custom-call | bytes 140000000 | tf_op jit(solution)/shard_map/pallas_call | solution.py:1406
  798.9 29.1 %shard_map.133.refs_0_ = bf16[144,2048]{1,0:T(8,128)(2,1)S(1)} custom-call(f32[144,2048]{1,0:T(8,128)S(1)} %select_maximum_fusion.x_ref, bf16[128,1600]{1,0:T(8,128)(2,1)S(1)} %add_convert_fusion.refs_0_), custom_call_target="tpu_custom_call" | custom-call | bytes 105000000 | tf_op jit(solution)/shard_map/pallas_call | solution.py:936
  831.1 4.6 all-to-all-start.7
  849.0 9.6 multiply_reduce_fusion.4
  869.4 8.1 all-to-all-start.8
  877.5 7.6 convolution_convert_fusion.1
  888.4 6.1 reshape.622
  894.6 4.6 copy.509
  905.0 5.8 concatenate.84
  910.9 3.6 broadcast_select_fusion.4
  927.2 6.6 all-to-all-start.11
  933.9 80.1 %shard_map.137 = f32[128,1600]{1,0:T(8,128)} custom-call(bf16[2048,400]{1,0:T(8,128)(2,1)} %pad_maximum_fusion.2.refs_0_, bf16[2048,128]{1,0:T(8,128)(2,1)} %copy-done.14, bf16[2048,256]{1,0:T(8,128)(2,1)} %slice.450.refs_2_, bf16[1600,400]{1,0:T(8,128)(2,1)} %reshape.576.refs_3_, bf16[1600,128]{1,0:T(8,128)(2,1)} %slice.348.refs_4_, ...), custom_call_target="tpu_custom_call" | custom-call | bytes 140000000 | tf_op jit(solution)/shard_map/pallas_call | solution.py:861
  1022.5 4.5 all-to-all-start.10
  1029.3 4.6 reshape.645
  1047.8 31.9 %shard_map.138 = f32[80,128]{1,0:T(8,128)S(1)} custom-call(bf16[32,80,128]{2,1,0:T(8,128)(2,1)S(1)} %pad_maximum_fusion.8.x_ref), custom_call_target="tpu_custom_call" | custom-call | bytes 70000000 | tf_op jit(solution)/shard_map/pallas_call | solution.py:1069
  (555 shorter events, 270.1 us)
Async XLA Ops:
  13.6 8.4 copy-start.78
  13.6 8.5 copy-start.116
  13.6 8.6 copy-start.92
  13.6 67.9 %all-to-all-start = ((bf16[16,869,50]{1,2,0:T(8,128)(2,1)}), bf16[16,869,50]{1,2,0:T(8,128)(2,1)S(1)}, u32[]{:S(2)}, u32[]{:S(2)}) async-start(bf16[16,869,50]{1,2,0:T(8,128)(2,1)} %bitcast.252), calls=%async_computation | async-start | bytes 3211264 | tf_op jit(solution)/shard_map/jvp()/all_to_all | solution.py:137
  21.1 238.2 %all-gather.2.cloned.1.call-start = ((), (), s32[]{:S(2)}) async-start(), calls=%async_computation.13 | async-start | bytes 7241728 | tf_op jit(solution)/shard_map/all_gather | solution.py:418
  22.0 57.7 %copy-start.32 = (bf16[1,128,1600]{2,1,0:T(8,128)(2,1)}, bf16[1,128,1600]{2,1,0:T(8,128)(2,1)S(1)}, u32[]{:S(2)}) copy-start(bf16[1,128,1600]{2,1,0:T(8,128)(2,1)S(1)} %copy.453) | copy-start | bytes 1228804
  85.6 45.3 %collective-permute-start = (bf16[13904,50]{0,1:T(8,128)(2,1)S(1)}, bf16[13904,50]{0,1:T(8,128)(2,1)S(1)}, u32[]{:S(2)}, u32[]{:S(2)}) collective-permute-start(bf16[13904,50]{0,1:T(8,128)(2,1)S(1)} %reshape.571), channel_id=1, source_target_pairs={{0,16},{16,0},{1,17},{17,1},{2,18},{18,2},{3,19},{19,3},{4,20},{20... | collective-permute-start | bytes 4171208 | tf_op jit(solution)/shard_map/jvp()/ppermute | solution.py:159
  131.7 10.7 copy-start.41
  135.8 38.8 %copy-start.80 = (f32[2048]{0:T(1024)}, f32[2048]{0:T(1024)S(1)}, u32[]{:S(2)}) copy-start(f32[2048]{0:T(1024)S(1)} %get-tuple-element.209) | copy-start | bytes 24580
  135.8 38.8 %copy-start.82 = (f32[2048]{0:T(1024)}, f32[2048]{0:T(1024)S(1)}, u32[]{:S(2)}) copy-start(f32[2048]{0:T(1024)S(1)} %get-tuple-element.210) | copy-start | bytes 24580
  135.8 38.8 %copy-start.84 = (f32[2048]{0:T(1024)}, f32[2048]{0:T(1024)S(1)}, u32[]{:S(2)}) copy-start(f32[2048]{0:T(1024)S(1)} %get-tuple-element.211) | copy-start | bytes 24580
  135.8 38.8 %copy-start.86 = (f32[2048]{0:T(1024)}, f32[2048]{0:T(1024)S(1)}, u32[]{:S(2)}) copy-start(f32[2048]{0:T(1024)S(1)} %get-tuple-element.212) | copy-start | bytes 24580
  147.1 35.1 %all-to-all-start.1 = ((bf16[16,316,50]{1,2,0:T(8,128)(2,1)}), bf16[16,316,50]{1,2,0:T(8,128)(2,1)}, u32[]{:S(2)}, u32[]{:S(2)}) async-start(bf16[16,316,50]{1,2,0:T(8,128)(2,1)} %pad_maximum_fusion.7), calls=%async_computation.1 | async-start | bytes 1376256 | tf_op jit(solution)/shard_map/jvp()/all_to_all | solution.py:137
  172.4 28.5 %copy-start.75 = (f32[200,24]{0,1:T(8,128)}, f32[200,24]{0,1:T(8,128)S(1)}, u32[]{:S(2)}) copy-start(f32[200,24]{0,1:T(8,128)S(1)} %reshape.575) | copy-start | bytes 57604
  174.0 8.1 copy-start.97
  174.0 8.1 copy-start.99
  174.0 8.1 copy-start.101
  174.0 8.1 copy-start.103
  182.2 20.9 %copy-start.27 = (bf16[2048,200]{1,0:T(8,128)(2,1)}, bf16[2048,200]{1,0:T(8,128)(2,1)S(1)}, u32[]{:S(2)}) copy-start(bf16[2048,200]{1,0:T(8,128)(2,1)S(1)} %get-tuple-element.56) | copy-start | bytes 2457604
  193.1 64.0 %all-to-all-start.2 = ((bf16[16,100,384]{2,1,0:T(8,128)(2,1)}), bf16[16,100,384]{2,1,0:T(8,128)(2,1)}, u32[]{:S(2)}, u32[]{:S(2)}) async-start(bf16[16,100,384]{2,1,0:T(8,128)(2,1)} %copy.470), calls=%async_computation.2 | async-start | bytes 2555904 | tf_op jit(solution)/shard_map/jvp()/all_to_all | solution.py:137
  283.1 55.9 %all-to-all-start.4 = ((bf16[16,150,344]{2,1,0:T(8,128)(2,1)}), bf16[16,150,344]{2,1,0:T(8,128)(2,1)}, u32[]{:S(2)}, u32[]{:S(2)}) async-start(bf16[16,150,344]{2,1,0:T(8,128)(2,1)} %get-tuple-element.62), calls=%async_computation.4 | async-start | bytes 3735552 | tf_op jit(solution)/shard_map/jvp()/all_to_all | solution.py:137
  306.0 8.8 copy-start.4
  339.0 42.8 %all-to-all-start.3 = ((bf16[16,656,50]{1,2,0:T(8,128)(2,1)}), bf16[16,656,50]{1,2,0:T(8,128)(2,1)}, u32[]{:S(2)}, u32[]{:S(2)}) async-start(bf16[16,656,50]{1,2,0:T(8,128)(2,1)} %bitcast.238), calls=%async_computation.3 | async-start | bytes 2752512 | tf_op jit(solution)/shard_map/jvp()/all_to_all | solution.py:137
  348.1 42.8 %collective-permute-start.1 = (bf16[16,150,344]{2,0,1:T(8,128)(2,1)}, bf16[16,150,344]{2,0,1:T(8,128)(2,1)}, u32[]{:S(2)}, u32[]{:S(2)}) collective-permute-start(bf16[16,150,344]{2,0,1:T(8,128)(2,1)} %copy.481), channel_id=1, source_target_pairs={{0,16},{16,0},{1,17},{17,1},{2,18},{18,2},{3,19},{19,3},{4,20},{20... | collective-permute-start | bytes 4953608 | tf_op jit(solution)/shard_map/jvp()/ppermute | solution.py:159
  406.4 72.6 %all-to-all-start.5 = ((bf16[16,100,344]{2,1,0:T(8,128)(2,1)}), bf16[16,100,344]{2,1,0:T(8,128)(2,1)}, u32[]{:S(2)}, u32[]{:S(2)}) async-start(bf16[16,100,344]{2,1,0:T(8,128)(2,1)} %reshape.602), calls=%async_computation.5 | async-start | bytes 2555904 | tf_op jit(solution)/shard_map/jvp()/all_to_all | solution.py:137
  412.4 385.2 %reduce-scatter.2.cloned.1.call-start = ((), (), s32[]{:S(2)}) async-start(), calls=%async_computation.14 | async-start | bytes 7241728 | tf_op jit(solution)/shard_map/reduce_scatter | solution.py:422
  416.0 60.6 %copy-start.33 = (bf16[1,128,1600]{2,1,0:T(8,128)(2,1)S(1)}, bf16[1,128,1600]{2,1,0:T(8,128)(2,1)}, u32[]{:S(2)}) copy-start(bf16[1,128,1600]{2,1,0:T(8,128)(2,1)} %copy-done.32) | copy-start | bytes 1228804
  478.0 109.2 %copy-start.22 = (f32[128,1600]{1,0:T(8,128)}, f32[128,1600]{1,0:T(8,128)S(1)}, u32[]{:S(2)}) copy-start(f32[128,1600]{1,0:T(8,128)S(1)} %get-tuple-element.160) | copy-start | bytes 2457604
  538.5 48.7 %copy-start.49 = (bf16[1,128,1600]{2,1,0:T(8,128)(2,1)S(1)}, bf16[1,128,1600]{2,1,0:T(8,128)(2,1)}, u32[]{:S(2)}) copy-start(bf16[1,128,1600]{2,1,0:T(8,128)(2,1)} %copy.456) | copy-start | bytes 1228804
  587.2 55.1 %copy-start.109 = (f32[128]{0:T(128)}, f32[128]{0:T(128)S(1)}, u32[]{:S(2)}) copy-start(f32[128]{0:T(128)S(1)} %multiply_multiply_fusion.10) | copy-start | bytes 1540
  647.4 12.3 %copy-start.63 = (bf16[344,1600]{1,0:T(8,128)(2,1)S(1)}, bf16[344,1600]{1,0:T(8,128)(2,1)}, u32[]{:S(2)}) copy-start(bf16[344,1600]{1,0:T(8,128)(2,1)} %get-tuple-element.78) | copy-start | bytes 3302404
  667.4 52.9 %all-to-all-start.6 = ((bf16[16,100,344]{2,1,0:T(8,128)(2,1)}), bf16[16,100,344]{2,1,0:T(8,128)(2,1)}, u32[]{:S(2)}, u32[]{:S(2)}) async-start(bf16[16,100,344]{2,1,0:T(8,128)(2,1)} %shard_map.131), calls=%async_computation.7 | async-start | bytes 2555904 | tf_op jit(solution)/shard_map/transpose(jvp())/all_to_all | solution.py:137
  679.6 32.0 %slice-start = ((s8[6815744]{0:T(1024)(128)(4,1)}), s8[4194304]{0:T(1024)(128)(4,1)S(1)}, s32[]{:S(2)}) async-start(s8[6815744]{0:T(1024)(128)(4,1)} %bitcast.247), calls=%async_computation.15 | async-start | bytes 8388608
  729.6 63.8 %collective-permute-start.2 = (bf16[16,150,344]{2,0,1:T(8,128)(2,1)}, bf16[16,150,344]{2,0,1:T(8,128)(2,1)}, u32[]{:S(2)}, u32[]{:S(2)}) collective-permute-start(bf16[16,150,344]{2,0,1:T(8,128)(2,1)} %copy.489), channel_id=1, source_target_pairs={{0,16},{16,0},{1,17},{17,1},{2,18},{18,2},{3,19},{19,3},{4,20},{20... | collective-permute-start | bytes 4953608 | tf_op jit(solution)/shard_map/ppermute | solution.py:159
  734.3 96.9 %all-to-all-start.9 = ((bf16[16,656,50]{1,2,0:T(8,128)(2,1)}), bf16[16,656,50]{1,2,0:T(8,128)(2,1)}, u32[]{:S(2)}, u32[]{:S(2)}) async-start(bf16[16,656,50]{1,2,0:T(8,128)(2,1)} %bitcast.68), calls=%async_computation.10 | async-start | bytes 2752512 | tf_op jit(solution)/shard_map/transpose(jvp())/all_to_all | solution.py:137
  755.3 35.1 %copy-start.44 = (f32[2048,200]{1,0:T(8,128)S(1)}, f32[2048,200]{1,0:T(8,128)}, u32[]{:S(2)}) copy-start(f32[2048,200]{1,0:T(8,128)} %get-tuple-element.222) | copy-start | bytes 4915204
  831.1 31.4 %all-to-all-start.7 = ((bf16[16,100,384]{2,1,0:T(8,128)(2,1)}), bf16[16,100,384]{2,1,0:T(8,128)(2,1)}, u32[]{:S(2)}, u32[]{:S(2)}) async-start(bf16[16,100,384]{2,1,0:T(8,128)(2,1)} %reshape.613), calls=%async_computation.8 | async-start | bytes 2555904 | tf_op jit(solution)/shard_map/transpose(jvp())/all_to_all | solution.py:137
  868.0 9.5 copy-start.53
  869.4 33.1 %all-to-all-start.8 = ((bf16[16,316,50]{1,2,0:T(8,128)(2,1)}), bf16[16,316,50]{1,2,0:T(8,128)(2,1)S(1)}, u32[]{:S(2)}, u32[]{:S(2)}) async-start(bf16[16,316,50]{1,2,0:T(8,128)(2,1)} %bitcast.257), calls=%async_computation.9 | async-start | bytes 1376256 | tf_op jit(solution)/shard_map/transpose(jvp())/all_to_all | solution.py:137
  914.5 99.4 %collective-permute-start.3 = (bf16[13904,50]{0,1:T(8,128)(2,1)}, bf16[13904,50]{0,1:T(8,128)(2,1)}, u32[]{:S(2)}, u32[]{:S(2)}) collective-permute-start(bf16[13904,50]{0,1:T(8,128)(2,1)} %broadcast_select_fusion.4), channel_id=1, source_target_pairs={{0,16},{16,0},{1,17},{17,1},{2,18},{18,2},{3,19},{19,3},{4,20},{20... | collective-permute-start | bytes 4171208 | tf_op jit(solution)/shard_map/transpose(jvp())/ppermute | solution.py:1468
  927.2 95.3 %all-to-all-start.11 = ((bf16[16,150,344]{2,1,0:T(8,128)(2,1)}), bf16[16,150,344]{2,1,0:T(8,128)(2,1)}, u32[]{:S(2)}, u32[]{:S(2)}) async-start(bf16[16,150,344]{2,1,0:T(8,128)(2,1)} %copy_add_fusion.refs_1_), calls=%async_computation.12 | async-start | bytes 3735552 | tf_op jit(solution)/shard_map/transpose(jvp())/all_to_all | solution.py:137
  933.8 80.1 %copy-start.26 = (bf16[27808,50]{0,1:T(8,128)(2,1)S(1)}, bf16[27808,50]{0,1:T(8,128)(2,1)}, u32[]{:S(2)}) copy-start(bf16[27808,50]{0,1:T(8,128)(2,1)} %concatenate.84) | copy-start | bytes 8342404
  1022.5 63.7 %all-to-all-start.10 = ((bf16[16,869,50]{1,2,0:T(8,128)(2,1)}), bf16[16,869,50]{1,2,0:T(8,128)(2,1)}, u32[]{:S(2)}, u32[]{:S(2)}) async-start(bf16[16,869,50]{1,2,0:T(8,128)(2,1)} %copy.521), calls=%async_computation.11 | async-start | bytes 3211264 | tf_op jit(solution)/shard_map/transpose(jvp())/all_to_all | solution.py:137
  1043.5 36.3 %copy-start.107 = (f32[128]{0:T(128)S(1)}, f32[128]{0:T(128)}, u32[]{:S(2)}) copy-start(f32[128]{0:T(128)} %copy-done.106) | copy-start | bytes 1540
  1043.5 36.3 %copy-start.23 = (f32[128,1600]{1,0:T(8,128)S(1)}, f32[128,1600]{1,0:T(8,128)}, u32[]{:S(2)}) copy-start(f32[128,1600]{1,0:T(8,128)} %copy-done.22) | copy-start | bytes 2457604
  1043.6 36.3 %copy-start.38 = (f32[128,1600]{1,0:T(8,128)S(1)}, f32[128,1600]{1,0:T(8,128)}, u32[]{:S(2)}) copy-start(f32[128,1600]{1,0:T(8,128)} %shard_map.127) | copy-start | bytes 2457604
  1043.6 36.3 %copy-start.50 = (bf16[1,128,1600]{2,1,0:T(8,128)(2,1)S(1)}, bf16[1,128,1600]{2,1,0:T(8,128)(2,1)}, u32[]{:S(2)}) copy-start(bf16[1,128,1600]{2,1,0:T(8,128)(2,1)} %copy.456) | copy-start | bytes 1228804
  1043.6 36.3 %copy-start.110 = (f32[128]{0:T(128)S(1)}, f32[128]{0:T(128)}, u32[]{:S(2)}) copy-start(f32[128]{0:T(128)} %copy-done.109) | copy-start | bytes 1540
  (91 other events, 285.5 us)
Sparse Core Ops, SparseCore 0:
  131.9 70.8 all-gather.1
  642.5 110.6 reduce-scatter.1
